TPU v7x, 32 devices: a whole 2x2x4 slice. The times are simulated.
32 devices in a mesh: dp: 2 (over y), expert: 16 (over z, x, core).
Axes of the slice: x: 2, y: 2, z: 4, core: 2. Of those that a mesh axis runs over, the one named last changes fastest.
Arguments:
- attention: bfloat16 [4096, 1536], P(('dp', 'expert')), may hold values from -6 to 6
- residual: bfloat16 [4096, 1536], P(('dp', 'expert')), may hold values from -6 to 6
- out_weight: bfloat16 [1536, 1536], P(('dp', 'expert')), may hold values from -0.15625 to 0.15625
- gate_weight: bfloat16 [16, 1536, 512], P('expert', 'dp'), may hold values from -0.15625 to 0.15625
- up_weight: bfloat16 [16, 1536, 512], P('expert', 'dp'), may hold values from -0.15625 to 0.15625
- down_weight: bfloat16 [16, 512, 1536], P('expert'), may hold values from -0.25 to 0.25
- routes: int32 [4096, 8], P(('dp', 'expert')), may hold values from 0 to 15, all different within a row; in each aligned block of 128 rows (0 to 127, 128 to 255, ...) at most 80 rows name the same one
- router_scores: float32 [4096, 8], P(('dp', 'expert')), may hold values from 0.05 to 1
- norm_gain: float32 [1536], replicated, may hold values from 0.5 to 1.5
Outputs:
- normed: bfloat16 [4096, 1536], P(('dp', 'expert'))
Inputs may be any that keep to these rules, and one draw needn't show every extreme that they name: `routes`: in each aligned block of 128 rows (the rows of one device) no expert is named by more than 80 rows, a bound that some block reaches; a row names 8 different experts.
All inputs are finite; a program needn't handle non-finite values.
Results may differ from a plain program's by a relative error of at most 0.0053.
Values may be sent and summed in bfloat16 or wider, within the bound.
No kernel may reach another device: no remote copies, remote signals or barrier semaphores. Data moves between devices by JAX's collectives and lax.ppermute only.
A program may use at most 64 MiB of HBM per device.

v0:
```python
import jax
import jax.numpy as jnp
from jax import lax
from jax.sharding import PartitionSpec as P


def body(
    attention,
    residual,
    out_weight,
    gate_weight,
    up_weight,
    down_weight,
    routes,
    router_scores,
    norm_gain,
):
    token_count, feature_count = attention.shape
    chosen = routes.shape[1]
    full_weight = lax.all_gather(out_weight, ("dp", "expert"), axis=0, tiled=True)
    projected = jnp.dot(attention, full_weight, preferred_element_type=jnp.float32)
    stream = (residual.astype(jnp.float32) + projected).astype(jnp.bfloat16)
    gate_full, up_full = (
        lax.all_gather(gate_weight, "dp", axis=1, tiled=True),
        lax.all_gather(up_weight, "dp", axis=1, tiled=True),
    )
    gate_mat = gate_full[0]
    up_mat = up_full[0]
    down_mat = down_weight[0]
    peers = lax.axis_size("expert")
    capacity = min(token_count, token_count * chosen * 5 // (4 * peers))
    pairs = routes.reshape(-1)
    onehot = (pairs[:, None] == jnp.arange(peers, dtype=jnp.int32)[None, :]).astype(jnp.int32)
    earlier = jnp.cumsum(onehot, axis=0) - onehot
    position = jnp.sum(earlier * onehot, axis=1)
    target = pairs * capacity + position
    token_index = jnp.arange(token_count * chosen, dtype=jnp.int32) // chosen
    table = jnp.full((peers * capacity,), token_count, jnp.int32).at[target].set(token_index)
    padded = jnp.concatenate([stream, jnp.zeros((1, feature_count), jnp.bfloat16)], axis=0)
    outgoing = padded[table].reshape(peers, capacity, feature_count)
    received = lax.all_to_all(outgoing, "expert", split_axis=0, concat_axis=0, tiled=True)
    rows_in = received.reshape(-1, feature_count)
    gate_act = jnp.dot(rows_in, gate_mat, preferred_element_type=jnp.float32)
    up_act = jnp.dot(rows_in, up_mat, preferred_element_type=jnp.float32)
    expert_hidden = (jax.nn.silu(gate_act) * up_act).astype(jnp.bfloat16)
    expert_out = jnp.dot(expert_hidden, down_mat, preferred_element_type=jnp.float32).astype(
        jnp.bfloat16
    )
    answered = lax.all_to_all(
        expert_out.reshape(received.shape), "expert", split_axis=0, concat_axis=0, tiled=True
    )
    picked = answered.reshape(-1, feature_count)[target].reshape(token_count, chosen, feature_count)
    combine = router_scores / jnp.sum(router_scores, axis=1, keepdims=True)
    mixture = jnp.zeros((token_count, feature_count), jnp.float32)
    for choice_index in range(chosen):
        mixture = mixture + combine[:, choice_index : choice_index + 1] * picked[
            :, choice_index
        ].astype(jnp.float32)
    total = stream.astype(jnp.float32) + mixture
    scale = lax.rsqrt(jnp.mean(total * total, axis=1, keepdims=True) + 1e-06)
    return (total * scale * norm_gain[None, :]).astype(jnp.bfloat16)


def solution(mesh):
    in_specs = (
        P(("dp", "expert"), None),
        P(("dp", "expert"), None),
        P(("dp", "expert"), None),
        P("expert", "dp", None),
        P("expert", "dp", None),
        P("expert", None, None),
        P(("dp", "expert"), None),
        P(("dp", "expert"), None),
        P(),
    )
    out_specs = P(("dp", "expert"), None)
    return jax.shard_map(body, mesh=mesh, in_specs=in_specs, out_specs=out_specs, check_vma=False)
```

profile of v0, /device:TPU:11, one launch (start us, length us, event | category | flops | bytes accessed | tf_op | source)
XLA Modules:
  0.0 317.4 jit_solution(5070370519651938139)
XLA Ops:
  7.4 0.0 copy-start
  7.4 0.0 all-gather.4.cloned.1.call-start
  7.4 0.7 all-gather.4.cloned.1.call-update
  8.1 0.8 copy.13
  8.9 0.1 eq.29
  9.0 0.1 eq.25
  9.1 4.5 %reduce-window.6 = s32[16,8,128]{2,1,0:T(8,128)S(1)} reduce-window(s32[16,8,128]{2,1,0:T(8,128)S(1)} %fusion.19, s32[]{:T(128)} %constant.35.clone.1), window={size=1x1x128 pad=0_0x0_0x127_0}, to_apply=%region_1.2 | reduce-window | flops 2080768 | bytes 131076 | tf_op jit(solution)/shard_map/reduce-window
  13.6 0.1 slice.76
  13.7 0.1 copy.15
  13.8 0.1 copy.16
  13.9 0.7 broadcast_multiply_fusion
  14.6 0.1 copy.12
  14.7 0.1 mul.129
  14.8 0.1 broadcast_add_fusion
  15.0 4.3 %scatter_custom_fusion = s32[1280]{0:T(1024)S(1)} fusion(s32[1024]{0:T(1024)S(1)} %bitcast.110, s32[1024]{0:T(1024)S(1)} %add_select_fusion, s32[]{:T(128)} %constant.33.clone.1), kind=kCustom, calls=%fused_computation.55 | custom fusion | bytes 5124 | tf_op jit(solution)/shard_map/scatter | solution.py:38
  19.3 57.3 %all-gather.4.cloned.1.call-done = bf16[1536,1536]{1,0:T(8,128)(2,1)} async-done(((bf16[48,1536]{1,0:T(8,128)(2,1)}), bf16[1536,1536]{1,0:T(8,128)(2,1)}) %all-gather.4.cloned.1.call-update) | async-done | bytes 4718608 | tf_op jit(solution)/shard_map/all_gather | solution.py:20
  76.6 3.3 %fusion.1 = bf16[128,1536]{1,0:T(8,128)(2,1)S(1)} fusion(bf16[128,1536]{1,0:T(8,128)(2,1)} %param.9, bf16[1536,1536]{1,0:T(8,128)(2,1)} %all-gather.4.cloned.1.call-done, bf16[128,1536]{1,0:T(8,128)(2,1)} %param.10), kind=kOutput, calls=%fused_computation.7 | convolution fusion | flops 604569600 | bytes 5898240 | tf_op jit(solution)/shard_map/dot_general | solution.py:21
  80.0 5.5 %gather_fusion = bf16[1280,1536]{1,0:T(8,128)(2,1)} fusion(bf16[129,1536]{1,0:T(8,128)(2,1)S(1)} %concatenate.3, s32[2048]{0:T(1024)S(1)} %pad_clamp_fusion), kind=kCustom, calls=%fused_computation | custom fusion | bytes 7869440 | tf_op jit(solution)/shard_map/gather | solution.py:40
  85.5 4.4 %all-to-all-start = ((bf16[16,80,1536]{2,1,0:T(8,128)(2,1)}), bf16[16,80,1536]{2,1,0:T(8,128)(2,1)}, u32[]{:S(2)}, u32[]{:S(2)}) async-start(bf16[16,80,1536]{2,1,0:T(8,128)(2,1)} %bitcast.105), calls=%async_computation | async-start | bytes 7864320 | tf_op jit(solution)/shard_map/all_to_all | solution.py:41
  89.9 0.0 all-gather.6.cloned.1.call-start
  90.0 0.5 all-gather.6.cloned.1.call-update
  90.5 0.0 all-gather.8.cloned.1.call-start
  90.5 0.5 all-gather.8.cloned.1.call-update
  91.1 28.3 %all-gather.6.cloned.1.call-done = bf16[1,1536,512]{2,1,0:T(8,128)(2,1)} async-done(((bf16[1,768,512]{2,1,0:T(8,128)(2,1)}), bf16[1,1536,512]{2,1,0:T(8,128)(2,1)}) %all-gather.6.cloned.1.call-update) | async-done | bytes 1572880 | tf_op jit(solution)/shard_map/all_gather | solution.py:24
  119.4 57.3 %all-to-all-done = bf16[16,80,1536]{2,1,0:T(8,128)(2,1)} async-done(((bf16[16,80,1536]{2,1,0:T(8,128)(2,1)}), bf16[16,80,1536]{2,1,0:T(8,128)(2,1)}, u32[]{:S(2)}, u32[]{:S(2)}) %all-to-all-start) | async-done | bytes 3932192 | tf_op jit(solution)/shard_map/all_to_all | solution.py:41
  176.7 6.3 %fusion.4 = f32[1280,512]{1,0:T(8,128)} fusion(bf16[1280,1536]{1,0:T(8,128)(2,1)} %bitcast.6, bf16[1,1536,512]{2,1,0:T(8,128)(2,1)} %all-gather.6.cloned.1.call-done), kind=kOutput, calls=%fused_computation.10 | convolution fusion | flops 2013265920 | bytes 8126464 | tf_op jit(solution)/shard_map/dot_general | solution.py:43
  183.0 0.0 all-gather.8.cloned.1.call-done
  183.0 0.0 copy-done
  183.0 9.7 %convolution_convert_fusion = bf16[1280,1536]{1,0:T(8,128)(2,1)} fusion(bf16[1,512,1536]{2,1,0:T(8,128)(2,1)S(1)} %copy-done, bf16[1280,1536]{1,0:T(8,128)(2,1)} %bitcast.6, f32[1280,512]{1,0:T(8,128)} %fusion.4, bf16[1,1536,512]{2,1,0:T(8,128)(2,1)} %all-gather.8.cloned.1.call-done), kind=kOutput, calls=%fused_computation.3 | convolution fusion | flops 4032430080 | bytes 13631488 | tf_op jit(solution)/shard_map/dot_general | solution.py:46
  192.7 0.0 copy-start.1
  192.7 5.0 %all-to-all-start.1 = ((bf16[16,80,1536]{2,1,0:T(8,128)(2,1)}), bf16[16,80,1536]{2,1,0:T(8,128)(2,1)}, u32[]{:S(2)}, u32[]{:S(2)}) async-start(bf16[16,80,1536]{2,1,0:T(8,128)(2,1)} %bitcast.106), calls=%async_computation.1 | async-start | bytes 7864320 | tf_op jit(solution)/shard_map/all_to_all | solution.py:49
  197.7 0.0 copy-done.1
  197.8 86.8 %all-to-all-done.1 = bf16[16,80,1536]{2,1,0:T(8,128)(2,1)} async-done(((bf16[16,80,1536]{2,1,0:T(8,128)(2,1)}), bf16[16,80,1536]{2,1,0:T(8,128)(2,1)}, u32[]{:S(2)}, u32[]{:S(2)}) %all-to-all-start.1) | async-done | bytes 3932192 | tf_op jit(solution)/shard_map/all_to_all | solution.py:49
  284.6 9.9 %gather_fusion.1 = bf16[1024,1536]{1,0:T(8,128)(2,1)} fusion(bf16[1280,1536]{1,0:T(8,128)(2,1)} %bitcast.11, s32[1024]{0:T(1024)S(1)} %broadcast_clamp_fusion), kind=kCustom, calls=%fused_computation.1 | custom fusion | bytes 6295552 | tf_op jit(solution)/shard_map/gather | solution.py:52
  294.5 13.6 %fusion.27 = (bf16[128,1,1536]{2,1,0:T(2,128)(2,1)S(1)}, bf16[128,1,1536]{2,1,0:T(2,128)(2,1)S(1)}, bf16[128,1,1536]{2,1,0:T(2,128)(2,1)S(1)}, bf16[128,1,1536]{...) fusion(bf16[128,8,1536]{2,1,0:T(8,128)(2,1)} %bitcast.104), kind=kLoop, calls=%fused_computation.71 | loop fusion | bytes 6291456 | tf_op jit(solution)/shard_map/slice | solution.py:56
  308.1 0.0 copy-start.2
  308.1 0.9 multiply_reduce_fusion
  309.0 0.0 copy-done.2
  309.0 0.9 multiply_convert_fusion
  (14 shorter events, 0.2 us)
Async XLA Ops:
  7.4 175.7 %copy-start = (bf16[1,512,1536]{2,1,0:T(8,128)(2,1)S(1)}, bf16[1,512,1536]{2,1,0:T(8,128)(2,1)}, u32[]{:S(2)}) copy-start(bf16[1,512,1536]{2,1,0:T(8,128)(2,1)} %param.14) | copy-start | bytes 4718596
  7.4 69.3 %all-gather.4.cloned.1.call-start = ((), (), s32[]{:S(2)}) async-start(), calls=%async_computation.2 | async-start | bytes 4866048 | tf_op jit(solution)/shard_map/all_gather | solution.py:20
  85.5 91.2 %all-to-all-start = ((bf16[16,80,1536]{2,1,0:T(8,128)(2,1)}), bf16[16,80,1536]{2,1,0:T(8,128)(2,1)}, u32[]{:S(2)}, u32[]{:S(2)}) async-start(bf16[16,80,1536]{2,1,0:T(8,128)(2,1)} %bitcast.105), calls=%async_computation | async-start | bytes 7864320 | tf_op jit(solution)/shard_map/all_to_all | solution.py:41
  89.9 29.5 %all-gather.6.cloned.1.call-start = ((), (), s32[]{:S(2)}) async-start(), calls=%async_computation.3 | async-start | bytes 2359296 | tf_op jit(solution)/shard_map/all_gather | solution.py:24
  90.5 92.5 %all-gather.8.cloned.1.call-start = ((), (), s32[]{:S(2)}) async-start(), calls=%async_computation.4 | async-start | bytes 2359296 | tf_op jit(solution)/shard_map/all_gather | solution.py:25
  192.7 5.1 %copy-start.1 = (f32[128,8]{0,1:T(8,128)S(1)}, f32[128,8]{0,1:T(8,128)}, u32[]{:S(2)}) copy-start(f32[128,8]{0,1:T(8,128)} %param.16) | copy-start | bytes 12292
  192.7 91.9 %all-to-all-start.1 = ((bf16[16,80,1536]{2,1,0:T(8,128)(2,1)}), bf16[16,80,1536]{2,1,0:T(8,128)(2,1)}, u32[]{:S(2)}, u32[]{:S(2)}) async-start(bf16[16,80,1536]{2,1,0:T(8,128)(2,1)} %bitcast.106), calls=%async_computation.1 | async-start | bytes 7864320 | tf_op jit(solution)/shard_map/all_to_all | solution.py:49
  308.1 0.9 copy-start.2
Sparse Core Ops, SparseCore 0:
  11.1 65.5 all-gather.3
Sparse Core Ops, SparseCore 1:
  91.9 27.4 all-gather.5
  120.8 27.0 all-gather.7
where the time goes:
time: 318 us; the launch traced here: 317 us
  waiting for transfers between devices  231 us (73%)
  local copies, waits for them, and re-layouts  34.8 us (11%)
  matrix products  19.3 us (6%)
  between operations  15 us (5%)
  starting transfers between devices  9.56 us (3%)
  other arithmetic  7.21 us (2%)
    all_to_all x1, waiting for transfers between devices, body(): lax.all_to_all(expert_out.reshape(received.shape), 'expert', split_axis=0...  86.8 us
    all_gather x1, waiting for transfers between devices, body(): lax.all_gather(out_weight, ('dp', 'expert'), axis=0, tiled=True)  57.3 us
    all_to_all x1, waiting for transfers between devices, body(): lax.all_to_all(outgoing, 'expert', split_axis=0, concat_axis=0, tiled=True)  57.3 us
    all_gather x1, waiting for transfers between devices, body(): lax.all_gather(gate_weight, 'dp', axis=1, tiled=True)  28.3 us
    slice x1, local copies, waits for them, and re-layouts, body(): picked[:, choice_index].astype(jnp.float32)  13.6 us
    gather x1, local copies, waits for them, and re-layouts, body(): answered.reshape(-1, feature_count)[target]  9.92 us
    dot_general x1, matrix products, body(): jnp.dot(expert_hidden, down_mat, preferred_element_type=jnp.float32)  9.66 us
  transfers between devices with their start and end apart: 5, of which 4 were waited for; matrix products, arithmetic and copies ran while one was open for 6% of the time, Pallas kernels for 0%

commit v1 on v0

v1 whole, which is shorter than its diff:
```python
import functools

import jax
import jax.numpy as jnp
import numpy as np
from jax import lax
from jax.experimental import pallas as pl
from jax.experimental.pallas import tpu as pltpu
from jax.sharding import PartitionSpec as P

BF16 = jnp.bfloat16
F32 = jnp.float32


def expert_kernel(place_ref, *refs):
    own_a, own_b, near_a, near_b, gate_a, gate_b, up_a, up_b, down, own_mix, near_mix, own_out, near_out = refs
    expert = place_ref[1]

    def weight(ref):
        lane = lax.broadcasted_iota(jnp.int32, ref.shape, 1)
        return jnp.sum(jnp.where(lane == expert, ref[...], 0.0), axis=1, keepdims=True)

    first = jnp.concatenate([own_a[...], near_a[...]], axis=0)
    second = jnp.concatenate([own_b[...], near_b[...]], axis=0)
    dot = functools.partial(jnp.dot, preferred_element_type=F32)
    gate_act = dot(first, gate_a[...]) + dot(second, gate_b[...])
    up_act = dot(first, up_a[...]) + dot(second, up_b[...])
    hidden = (jax.nn.silu(gate_act) * up_act).astype(BF16)
    result = dot(hidden, down[...])
    rows = own_a.shape[0]
    own_out[...] = result[:rows] * weight(own_mix)
    near_out[...] = (result[rows:] * weight(near_mix)).astype(BF16)


def run_expert(place, block, weights, mix):
    rows = mix.shape[0] // 2
    half = weights[0].shape[0]
    width = weights[4].shape[1]

    def picked(shape, near):
        if near:
            return pl.BlockSpec(shape, lambda i, place: (1 - place[0], 0))
        return pl.BlockSpec(shape, lambda i, place: (place[0], 0))

    def whole(array):
        return pl.BlockSpec(array.shape, lambda i, place: (0, 0))

    if len(block) == 2:
        first, second = block
        tokens = (first, second, first, second)
        token_specs = [picked((rows, half), near) for near in (False, False, True, True)]
    else:
        tokens = block
        token_specs = [whole(array) for array in block]
    mix_specs = [picked((rows, mix.shape[1]), False), picked((rows, mix.shape[1]), True)]
    flops = 2 * 2 * rows * (2 * half * 2 * weights[0].shape[1] + weights[4].shape[0] * width)
    return pl.pallas_call(
        expert_kernel,
        grid_spec=pltpu.PrefetchScalarGridSpec(
            num_scalar_prefetch=1,
            grid=(1,),
            in_specs=token_specs + [whole(array) for array in weights] + mix_specs,
            out_specs=[pl.BlockSpec((rows, width), lambda i, place: (0, 0))] * 2,
        ),
        out_shape=[
            jax.ShapeDtypeStruct((rows, width), F32),
            jax.ShapeDtypeStruct((rows, width), BF16),
        ],
        compiler_params=pltpu.CompilerParams(vmem_limit_bytes=32 * 1024 * 1024),
        cost_estimate=pl.CostEstimate(flops=flops, bytes_accessed=8 * 1024 * 1024, transcendentals=0),
    )(place, *tokens, *weights, mix, mix)


def body(
    attention,
    residual,
    out_weight,
    gate_weight,
    up_weight,
    down_weight,
    routes,
    router_scores,
    norm_gain,
):
    token_count, width = attention.shape
    half = width // 2
    groups = lax.axis_size("dp")
    peers = lax.axis_size("expert")
    chips = peers // 2
    far = chips // 2
    group = lax.axis_index("dp")
    expert = lax.axis_index("expert")
    core = expert % 2
    ring = list(range(0, chips, 2)) + list(range(chips - 1, 0, -2))
    ring_of = np.argsort(np.array(ring))
    at = jnp.asarray(ring_of, jnp.int32)[expert // 2]
    pair_at = jnp.asarray(ring, jnp.int32)
    forth = [(2 * ring[k] + c, 2 * ring[(k + 1) % chips] + c) for k in range(chips) for c in range(2)]
    back = [(b, a) for a, b in forth]
    across = [(e, e ^ 1) for e in range(peers)]

    def swap(x):
        return lax.ppermute(x, "expert", across)

    def go(x):
        return lax.ppermute(x, "expert", forth)

    def come(x):
        return lax.ppermute(x, "expert", back)

    def columns(x, which):
        return lax.dynamic_slice(x, (0, which * half), (x.shape[0], half))

    def paired(mine, other):
        return jnp.where(core == 0, jnp.concatenate([mine, other], 0), jnp.concatenate([other, mine], 0))

    combine = router_scores / jnp.sum(router_scores, axis=1, keepdims=True)
    named = routes[:, :, None] == jnp.arange(peers, dtype=jnp.int32)[None, None, :]
    dense = jnp.sum(jnp.where(named, combine[:, :, None], 0.0), axis=1)
    mix_all = lax.all_gather(dense, "expert", axis=0, tiled=True).reshape(chips, 2 * token_count, peers)

    tokens = paired(attention, swap(attention))
    base = paired(columns(residual, core), swap(columns(residual, 1 - core)))
    if groups == 2:
        mine = jnp.concatenate([columns(out_weight, core), swap(columns(out_weight, 1 - core))], axis=0)
        other = lax.ppermute(mine, "dp", [(0, 1), (1, 0)])
        parts = [(mine, 0, 0), (other, 0, 1)]
        mine_f = mine_b = mine
        other_f = other_b = other
        for step in range(1, far + 1):
            mine_f = go(mine_f)
            parts.append((mine_f, -step, 0))
            other_b = come(other_b)
            parts.append((other_b, step, 1))
            if step < far:
                mine_b = come(mine_b)
                parts.append((mine_b, step, 0))
                other_f = go(other_f)
                parts.append((other_f, -step, 1))
        rows = out_weight.shape[0]
        starts = []
        for _, offset, other_group in parts:
            pair = pair_at[(at + offset) % chips]
            of_group = (group + other_group) % 2
            for c in (core, 1 - core):
                starts.append(((of_group * chips + pair) * 2 + c) * rows)
        order = (jnp.stack(starts)[:, None] + jnp.arange(rows, dtype=jnp.int32)[None, :]).reshape(-1)
        place_matrix = (jnp.arange(width, dtype=jnp.int32)[:, None] == order[None, :]).astype(BF16)
        tokens = jnp.dot(tokens, place_matrix, preferred_element_type=F32).astype(BF16)
        half_weight = jnp.concatenate([p[0] for p in parts], axis=0)
        near_first = core == group
        flip = [(0, 1), (1, 0)]

        def halves(x):
            x = x[0]
            y = lax.ppermute(x, "dp", flip)
            return jnp.where(near_first, x, y), jnp.where(near_first, y, x)

    else:
        half_weight = columns(lax.all_gather(out_weight, ("dp", "expert"), axis=0, tiled=True), core)

        def halves(x):
            x = lax.all_gather(x, "dp", axis=1, tiled=True)[0]
            return (
                lax.dynamic_slice(x, (core * half, 0), (half, x.shape[1])),
                lax.dynamic_slice(x, ((1 - core) * half, 0), (half, x.shape[1])),
            )

    projected = jnp.dot(tokens, half_weight, preferred_element_type=F32)
    stream = (base.astype(F32) + projected).astype(BF16)

    gate = halves(gate_weight)
    up = halves(up_weight)
    weights = (*gate, *up, down_weight[0])
    place = jnp.stack([core, expert]).astype(jnp.int32)

    def experts(block, offset):
        return run_expert(place, block, weights, mix_all[pair_at[(at + offset) % chips]])

    out = {}
    stream_near = swap(stream)
    out[0] = experts((stream, stream_near), 0)
    f = b = stream
    for step in range(1, far):
        f, b = go(f), come(b)
        out[-step] = experts((f, swap(f)), -step)
        out[step] = experts((b, swap(b)), step)
    f = go(lax.dynamic_slice(f, (core * token_count, 0), (token_count, half)))
    b = come(lax.dynamic_slice(b, ((1 - core) * token_count, 0), (token_count, half)))
    out[far] = experts((f, swap(b), b, swap(f)), far)

    shared = {offset: (own, swap(near)) for offset, (own, near) in out.items()}
    cut = token_count // 2

    def term(offset, part):
        own, near = shared[offset]
        rows = slice(part * cut, (part + 1) * cut)
        return own[rows] + near[rows].astype(F32)

    def chain(move, sign, part, distance):
        total = term(distance if distance == far else sign * distance, part).astype(BF16)
        total = move(total)
        for left in range(distance - 1, 0, -1):
            total = move((term(sign * left, part) + total.astype(F32)).astype(BF16))
        return total.astype(F32)

    mixture = jnp.concatenate(
        [
            term(0, 0) + chain(go, 1, 0, far) + chain(come, -1, 0, far - 1),
            term(0, 1) + chain(come, -1, 1, far) + chain(go, 1, 1, far - 1),
        ],
        axis=0,
    )
    own_rows = lax.dynamic_slice(stream, (core * token_count, 0), (token_count, half))
    near_rows = lax.dynamic_slice(stream_near, (core * token_count, 0), (token_count, half))
    whole_rows = jnp.where(
        core == 0,
        jnp.concatenate([own_rows, near_rows], axis=1),
        jnp.concatenate([near_rows, own_rows], axis=1),
    )
    total = whole_rows.astype(F32) + mixture
    scale = lax.rsqrt(jnp.mean(total * total, axis=1, keepdims=True) + 1e-06)
    return (total * scale * norm_gain[None, :]).astype(BF16)


def solution(mesh):
    in_specs = (
        P(("dp", "expert"), None),
        P(("dp", "expert"), None),
        P(("dp", "expert"), None),
        P("expert", "dp", None),
        P("expert", "dp", None),
        P("expert", None, None),
        P(("dp", "expert"), None),
        P(("dp", "expert"), None),
        P(),
    )
    out_specs = P(("dp", "expert"), None)
    return jax.shard_map(body, mesh=mesh, in_specs=in_specs, out_specs=out_specs, check_vma=False)
```

time: 318 us -> 201 us (0.63)
  the two profiles are of different devices: /device:TPU:11 before, /device:TPU:0 now
where the time goes in v1:
time: 201 us; the launch traced here: 199 us
  waiting for transfers between devices  52.1 us (26%)
  starting transfers between devices  47.4 us (24%)
  between operations  31.7 us (16%)
  blocking collectives  22.4 us (11%)
  local copies, waits for them, and re-layouts  20.1 us (10%)
  Pallas kernels  16.2 us (8%)
  other arithmetic  4.78 us (2%)
  matrix products  4.62 us (2%)
    ppermute x18, waiting for transfers between devices, go(): return lax.ppermute(x, 'expert', forth)  34 us
    all_gather x1, blocking collectives, body(): lax.all_gather(dense, 'expert', axis=0, tiled=True)  22.4 us
    ppermute x18, starting transfers between devices, go(): return lax.ppermute(x, 'expert', forth)  19.7 us
    ppermute x18, starting transfers between devices, come(): return lax.ppermute(x, 'expert', back)  17.3 us
    pallas_call x8, Pallas kernels, run_expert(): pl.pallas_call(expert_kernel, grid_spec=pltpu.PrefetchScalarGridSpec(num_...  16.2 us
    ppermute x18, waiting for transfers between devices, come(): return lax.ppermute(x, 'expert', back)  15.6 us
    unnamed x30, local copies, waits for them, and re-layouts  11.6 us
    ppermute x20, starting transfers between devices, swap(): return lax.ppermute(x, 'expert', across)  5.75 us
  transfers between devices with their start and end apart: 59, of which 25 were waited for; matrix products, arithmetic and copies ran while one was open for 11% of the time, Pallas kernels for 8%

profile of v1, /device:TPU:0, one launch (start us, length us, event | category | flops | bytes accessed | tf_op | source)
XLA Modules:
  0.0 199.4 jit_solution(14456630110687332405)
XLA Ops:
  0.0 1.6 constant_dynamic-update-slice_fusion.16
  2.1 1.0 constant_dynamic-slice_fusion.7
  3.6 1.2 dynamic_slice.95
  11.2 1.7 fusion.18
  23.0 2.6 %collective-permute-start.3 = (bf16[96,768]{1,0:T(8,128)(2,1)S(1)}, bf16[96,768]{1,0:T(8,128)(2,1)S(1)}, u32[]{:S(2)}, u32[]{:S(2)}) collective-permute-start(bf16[96,768]{1,0:T(8,128)(2,1)S(1)} %pad_maximum_fusion), channel_id=1, source_target_pairs={{0,16},{16,0},{1,17},{17,1},{2,18},{18,2},{3,19},{19,3},{4,20},{20... | collective-permute-start | bytes 442376 | tf_op jit(solution)/shard_map/ppermute | solution.py:126
  25.8 1.6 collective-permute-start.4
  28.4 1.7 collective-permute-done.3
  30.1 1.7 collective-permute-start.5
  32.5 0.8 collective-permute-start.7
  34.0 1.6 collective-permute-start.8
  36.2 1.1 collective-permute-start.10
  37.9 0.7 constant_dynamic-update-slice_fusion.11
  39.2 1.6 collective-permute-start.9
  42.9 1.5 collective-permute-start.12
  44.5 1.4 collective-permute-start.14
  46.6 0.7 constant_dynamic-update-slice_fusion.7
  47.3 1.6 collective-permute-start.13
  50.6 1.8 collective-permute-done.13
  52.4 1.1 collective-permute-start.16
  53.5 0.7 constant_dynamic-update-slice_fusion.4
  54.2 1.0 collective-permute-start.17
  55.1 0.7 constant_dynamic-update-slice_fusion.3
  56.6 1.0 collective-permute-done.16
  58.2 1.1 collective-permute-done.17
  60.0 4.6 %fusion.3.refs_0_.refs_2_ = bf16[256,768]{1,0:T(8,128)(2,1)S(1)} fusion(bf16[1536,768]{1,0:T(8,128)(2,1)} %constant_dynamic-update-slice_fusion, s32[1536]{0:T(1024)S(1)} %add.570, bf16[128,1536]{1,0:T(8,128)(2,1)S(1)} %collective-permute-done.1, bf16[128,1536]{1,0:T(8,128)(2,1)S(1)} %copy-done.6, pred[]{:T(512)S(6)} %eq.76, ...), kind=kOutput, calls=%fused_computation.5 | convolution fusion | flops 1820590080 | bytes 3938305 | tf_op jit(solution)/shard_map/dot_general | solution.py:169
  64.6 1.6 collective-permute-start.31
  66.7 6.6 %collective-permute-done.31.refs_0_.refs_2_ = bf16[256,768]{1,0:T(8,128)(2,1)S(1)} collective-permute-done((bf16[256,768]{1,0:T(8,128)(2,1)S(1)}, bf16[256,768]{1,0:T(8,128)(2,1)S(1)}, u32[]{:S(2)}, u32[]{:S(2)}) %collective-permute-start.31) | collective-permute-done | bytes 393248 | tf_op jit(solution)/shard_map/ppermute | solution.py:106
  73.3 2.5 %collective-permute-start.32 = (bf16[256,768]{1,0:T(8,128)(2,1)S(1)}, bf16[256,768]{1,0:T(8,128)(2,1)S(1)}, u32[]{:S(2)}, u32[]{:S(2)}) collective-permute-start(bf16[256,768]{1,0:T(8,128)(2,1)S(1)} %collective-permute-done.31.refs_0_.refs_2_), channel_id=1, source_target_pairs={{0,4},{1,5},{4,8},{5,9},{8,12},{9,13},{12,14},{13,15},{14,10},{15,... | collective-permute-start | bytes 1179656 | tf_op jit(solution)/shard_map/ppermute | solution.py:106
  75.8 1.7 collective-permute-start.19
  77.9 6.1 %collective-permute-done.32.refs_0_.refs_2_ = bf16[256,768]{1,0:T(8,128)(2,1)S(1)} collective-permute-done((bf16[256,768]{1,0:T(8,128)(2,1)S(1)}, bf16[256,768]{1,0:T(8,128)(2,1)S(1)}, u32[]{:S(2)}, u32[]{:S(2)}) %collective-permute-start.32) | collective-permute-done | bytes 393248 | tf_op jit(solution)/shard_map/ppermute | solution.py:106
  84.0 2.5 %collective-permute-start.33 = (bf16[256,768]{1,0:T(8,128)(2,1)S(1)}, bf16[256,768]{1,0:T(8,128)(2,1)S(1)}, u32[]{:S(2)}, u32[]{:S(2)}) collective-permute-start(bf16[256,768]{1,0:T(8,128)(2,1)S(1)} %collective-permute-done.32.refs_0_.refs_2_), channel_id=1, source_target_pairs={{0,4},{1,5},{4,8},{5,9},{8,12},{9,13},{12,14},{13,15},{14,10},{15,... | collective-permute-start | bytes 1179656 | tf_op jit(solution)/shard_map/ppermute | solution.py:106
  86.5 22.4 %all_gather.3 = f32[2048,16]{0,1:T(8,128)} all-gather(f32[128,16]{0,1:T(8,128)S(1)} %select_reduce_fusion), channel_id=1, replica_groups=mesh['dp'=2,'expert'=16] {'expert'}, dimensions={0}, use_global_device_ids=true | all-gather | bytes 139264 | tf_op jit(solution)/shard_map/all_gather | solution.py:120
  118.9 2.2 %copy.22 = f32[2048,16]{1,0:T(8,128)} copy(f32[2048,16]{0,1:T(8,128)} %all_gather.3) | data formatting | bytes 262144 | tf_op jit(solution)/shard_map/reshape | solution.py:120
  126.2 1.4 dynamic-slice_bitcast_fusion.7
  128.1 2.2 %collective-permute-start.35 = (bf16[128,768]{1,0:T(8,128)(2,1)S(1)}, bf16[128,768]{1,0:T(8,128)(2,1)S(1)}, u32[]{:S(2)}, u32[]{:S(2)}) collective-permute-start(bf16[128,768]{1,0:T(8,128)(2,1)S(1)} %constant_dynamic-slice_fusion), channel_id=1, source_target_pairs={{4,0},{5,1},{8,4},{9,5},{12,8},{13,9},{14,12},{15,13},{10,14},{11,... | collective-permute-start | bytes 589832 | tf_op jit(solution)/shard_map/ppermute | solution.py:109
  130.3 1.2 broadcast_select_fusion.2
  132.2 3.1 %collective-permute-done.35.refs_2_ = bf16[128,768]{1,0:T(8,128)(2,1)S(1)} collective-permute-done((bf16[128,768]{1,0:T(8,128)(2,1)S(1)}, bf16[128,768]{1,0:T(8,128)(2,1)S(1)}, u32[]{:S(2)}, u32[]{:S(2)}) %collective-permute-start.35) | collective-permute-done | bytes 196640 | tf_op jit(solution)/shard_map/ppermute | solution.py:109
  135.8 1.2 broadcast_select_fusion
  137.2 2.0 %shard_map.109 = (f32[128,1536]{1,0:T(8,128)S(1)}, bf16[128,1536]{1,0:T(8,128)(2,1)S(1)}) custom-call(s32[2]{0:T(128)S(1)} %pad_add_fusion.place_ref, bf16[256,768]{1,0:T(8,128)(2,1)S(1)} %fusion.3.refs_0_.refs_2_, bf16[256,768]{1,0:T(8,128)(2,1)S(1)} %collective-permute-done.18.refs_1_.refs_3_, bf16[256,768]{1,0:T(8,128)(2,1)S(1)} %fusion.3.refs_0_.refs_2_, ...), custom_call_target="tpu_custom_call" | custom-call | flops 1207959552 | bytes 8388608 | tf_op jit(solution)/shard_map/pallas_call | solution.py:57
  139.9 2.0 %shard_map.113 = (f32[128,1536]{1,0:T(8,128)S(1)}, bf16[128,1536]{1,0:T(8,128)(2,1)S(1)}) custom-call(s32[2]{0:T(128)S(1)} %pad_add_fusion.place_ref, bf16[128,768]{1,0:T(8,128)(2,1)S(1)} %collective-permute-done.34.refs_0_, bf16[128,768]{1,0:T(8,128)(2,1)S(1)} %collective-permute-done.36.refs_1_, bf16[128,768]{1,0:T(8,128)(2,1)S(1)} %collective-permute-done.35.refs_2_, ...), custom_call_target="tpu_custom_call" | custom-call | flops 1207959552 | bytes 8388608 | tf_op jit(solution)/shard_map/pallas_call | solution.py:57
  142.4 2.0 %shard_map.114 = (f32[128,1536]{1,0:T(8,128)S(1)}, bf16[128,1536]{1,0:T(8,128)(2,1)S(1)}) custom-call(s32[2]{0:T(128)S(1)} %pad_add_fusion.place_ref, bf16[256,768]{1,0:T(8,128)(2,1)S(1)} %collective-permute-done.31.refs_0_.refs_2_, bf16[256,768]{1,0:T(8,128)(2,1)S(1)} %collective-permute-done.43.refs_1_.refs_3_, ...), custom_call_target="tpu_custom_call" | custom-call | flops 1207959552 | bytes 8388608 | tf_op jit(solution)/shard_map/pallas_call | solution.py:57
  144.6 2.0 %shard_map.110 = (f32[128,1536]{1,0:T(8,128)S(1)}, bf16[128,1536]{1,0:T(8,128)(2,1)S(1)}) custom-call(s32[2]{0:T(128)S(1)} %pad_add_fusion.place_ref, bf16[256,768]{1,0:T(8,128)(2,1)S(1)} %collective-permute-done.22.refs_0_.refs_2_, bf16[256,768]{1,0:T(8,128)(2,1)S(1)} %collective-permute-done.23.refs_1_.refs_3_, ...), custom_call_target="tpu_custom_call" | custom-call | flops 1207959552 | bytes 8388608 | tf_op jit(solution)/shard_map/pallas_call | solution.py:57
  147.1 2.0 %shard_map.115 = (f32[128,1536]{1,0:T(8,128)S(1)}, bf16[128,1536]{1,0:T(8,128)(2,1)S(1)}) custom-call(s32[2]{0:T(128)S(1)} %pad_add_fusion.place_ref, bf16[256,768]{1,0:T(8,128)(2,1)S(1)} %collective-permute-done.32.refs_0_.refs_2_, bf16[256,768]{1,0:T(8,128)(2,1)S(1)} %collective-permute-done.45.refs_1_.refs_3_, ...), custom_call_target="tpu_custom_call" | custom-call | flops 1207959552 | bytes 8388608 | tf_op jit(solution)/shard_map/pallas_call | solution.py:57
  149.3 2.0 %shard_map.116 = (f32[128,1536]{1,0:T(8,128)S(1)}, bf16[128,1536]{1,0:T(8,128)(2,1)S(1)}) custom-call(s32[2]{0:T(128)S(1)} %pad_add_fusion.place_ref, bf16[256,768]{1,0:T(8,128)(2,1)S(1)} %collective-permute-done.33.refs_0_.refs_2_, bf16[256,768]{1,0:T(8,128)(2,1)S(1)} %collective-permute-done.47.refs_1_.refs_3_, ...), custom_call_target="tpu_custom_call" | custom-call | flops 1207959552 | bytes 8388608 | tf_op jit(solution)/shard_map/pallas_call | solution.py:57
  151.9 1.8 collective-permute-start.52
  153.7 2.0 %shard_map.111 = (f32[128,1536]{1,0:T(8,128)S(1)}, bf16[128,1536]{1,0:T(8,128)(2,1)S(1)}) custom-call(s32[2]{0:T(128)S(1)} %pad_add_fusion.place_ref, bf16[256,768]{1,0:T(8,128)(2,1)S(1)} %collective-permute-done.25.refs_0_.refs_2_, bf16[256,768]{1,0:T(8,128)(2,1)S(1)} %collective-permute-done.26.refs_1_.refs_3_, ...), custom_call_target="tpu_custom_call" | custom-call | flops 1207959552 | bytes 8388608 | tf_op jit(solution)/shard_map/pallas_call | solution.py:57
  155.8 2.0 %shard_map.112 = (f32[128,1536]{1,0:T(8,128)S(1)}, bf16[128,1536]{1,0:T(8,128)(2,1)S(1)}) custom-call(s32[2]{0:T(128)S(1)} %pad_add_fusion.place_ref, bf16[256,768]{1,0:T(8,128)(2,1)S(1)} %collective-permute-done.28.refs_0_.refs_2_, bf16[256,768]{1,0:T(8,128)(2,1)S(1)} %collective-permute-done.29.refs_1_.refs_3_, ...), custom_call_target="tpu_custom_call" | custom-call | flops 1207959552 | bytes 8388608 | tf_op jit(solution)/shard_map/pallas_call | solution.py:57
  159.0 0.8 collective-permute-done.30
  159.8 1.3 collective-permute-start.49
  161.1 4.2 %collective-permute-done.39 = bf16[64,1536]{1,0:T(8,128)(2,1)S(1)} collective-permute-done((bf16[64,1536]{1,0:T(8,128)(2,1)S(1)}, bf16[64,1536]{1,0:T(8,128)(2,1)S(1)}, u32[]{:S(2)}, u32[]{:S(2)}) %collective-permute-start.39) | collective-permute-done | bytes 196640 | tf_op jit(solution)/shard_map/ppermute | solution.py:106
  165.3 1.3 collective-permute-start.53
  167.6 3.6 %collective-permute-done.53 = bf16[64,1536]{1,0:T(8,128)(2,1)S(1)} collective-permute-done((bf16[64,1536]{1,0:T(8,128)(2,1)S(1)}, bf16[64,1536]{1,0:T(8,128)(2,1)S(1)}, u32[]{:S(2)}, u32[]{:S(2)}) %collective-permute-start.53) | collective-permute-done | bytes 196640 | tf_op jit(solution)/shard_map/ppermute | solution.py:109
  171.8 3.2 %collective-permute-done.40 = bf16[64,1536]{1,0:T(8,128)(2,1)S(1)} collective-permute-done((bf16[64,1536]{1,0:T(8,128)(2,1)S(1)}, bf16[64,1536]{1,0:T(8,128)(2,1)S(1)}, u32[]{:S(2)}, u32[]{:S(2)}) %collective-permute-start.40) | collective-permute-done | bytes 196640 | tf_op jit(solution)/shard_map/ppermute | solution.py:106
  175.0 3.3 %collective-permute-done.56 = bf16[64,1536]{1,0:T(8,128)(2,1)S(1)} collective-permute-done((bf16[64,1536]{1,0:T(8,128)(2,1)S(1)}, bf16[64,1536]{1,0:T(8,128)(2,1)S(1)}, u32[]{:S(2)}, u32[]{:S(2)}) %collective-permute-start.56) | collective-permute-done | bytes 196640 | tf_op jit(solution)/shard_map/ppermute | solution.py:106
  178.8 1.8 collective-permute-start.41
  181.3 3.6 %collective-permute-done.54 = bf16[64,1536]{1,0:T(8,128)(2,1)S(1)} collective-permute-done((bf16[64,1536]{1,0:T(8,128)(2,1)S(1)}, bf16[64,1536]{1,0:T(8,128)(2,1)S(1)}, u32[]{:S(2)}, u32[]{:S(2)}) %collective-permute-start.54) | collective-permute-done | bytes 196640 | tf_op jit(solution)/shard_map/ppermute | solution.py:109
  185.2 1.5 collective-permute-done.41
  186.7 2.1 %collective-permute-done.57 = bf16[64,1536]{1,0:T(8,128)(2,1)S(1)} collective-permute-done((bf16[64,1536]{1,0:T(8,128)(2,1)S(1)}, bf16[64,1536]{1,0:T(8,128)(2,1)S(1)}, u32[]{:S(2)}, u32[]{:S(2)}) %collective-permute-start.57) | collective-permute-done | bytes 196640 | tf_op jit(solution)/shard_map/ppermute | solution.py:106
  189.0 1.8 collective-permute-start.42
  190.8 1.1 collective-permute-start.58
  191.9 0.9 collective-permute-start.55
  192.9 3.1 %collective-permute-done.42 = bf16[64,1536]{1,0:T(8,128)(2,1)S(1)} collective-permute-done((bf16[64,1536]{1,0:T(8,128)(2,1)S(1)}, bf16[64,1536]{1,0:T(8,128)(2,1)S(1)}, u32[]{:S(2)}, u32[]{:S(2)}) %collective-permute-start.42) | collective-permute-done | bytes 196640 | tf_op jit(solution)/shard_map/ppermute | solution.py:106
  196.0 2.1 %collective-permute-done.58 = bf16[64,1536]{1,0:T(8,128)(2,1)S(1)} collective-permute-done((bf16[64,1536]{1,0:T(8,128)(2,1)S(1)}, bf16[64,1536]{1,0:T(8,128)(2,1)S(1)}, u32[]{:S(2)}, u32[]{:S(2)}) %collective-permute-start.58) | collective-permute-done | bytes 196640 | tf_op jit(solution)/shard_map/ppermute | solution.py:106
  198.5 0.9 multiply_convert_fusion
  (125 shorter events, 22.4 us)
Async XLA Ops:
  1.6 21.4 %collective-permute-start.2 = (bf16[48,768]{1,0:T(8,128)(2,1)S(1)}, bf16[48,768]{1,0:T(8,128)(2,1)S(1)}, u32[]{:S(2)}, u32[]{:S(2)}) collective-permute-start(bf16[48,768]{1,0:T(8,128)(2,1)S(1)} %get-tuple-element.69), channel_id=1, source_target_pairs={{0,1},{1,0},{2,3},{3,2},{4,5},{5,4},{6,7},{7,6},{8,9},{9,8},{10,11... | collective-permute-start | bytes 221192 | tf_op jit(solution)/shard_map/ppermute | solution.py:103
  2.0 58.0 %collective-permute-start.1 = (bf16[128,1536]{1,0:T(8,128)(2,1)}, bf16[128,1536]{1,0:T(8,128)(2,1)S(1)}, u32[]{:S(2)}, u32[]{:S(2)}) collective-permute-start(bf16[128,1536]{1,0:T(8,128)(2,1)} %param.11), channel_id=1, source_target_pairs={{0,1},{1,0},{2,3},{3,2},{4,5},{5,4},{6,7},{7,6},{8,9},{9,8},{10,11... | collective-permute-start | bytes 1179656 | tf_op jit(solution)/shard_map/ppermute | solution.py:103
  3.1 56.9 %collective-permute-start = (bf16[128,768]{1,0:T(8,128)(2,1)S(1)}, bf16[128,768]{1,0:T(8,128)(2,1)S(1)}, u32[]{:S(2)}, u32[]{:S(2)}) collective-permute-start(bf16[128,768]{1,0:T(8,128)(2,1)S(1)} %get-tuple-element.68), channel_id=1, source_target_pairs={{0,1},{1,0},{2,3},{3,2},{4,5},{5,4},{6,7},{7,6},{8,9},{9,8},{10,11... | collective-permute-start | bytes 589832 | tf_op jit(solution)/shard_map/ppermute | solution.py:103
  23.0 37.0 %copy-start.6 = (bf16[128,1536]{1,0:T(8,128)(2,1)S(1)}, bf16[128,1536]{1,0:T(8,128)(2,1)}, u32[]{:S(2)}) copy-start(bf16[128,1536]{1,0:T(8,128)(2,1)} %param.11) | copy-start | bytes 1179652
  23.0 7.1 %collective-permute-start.3 = (bf16[96,768]{1,0:T(8,128)(2,1)S(1)}, bf16[96,768]{1,0:T(8,128)(2,1)S(1)}, u32[]{:S(2)}, u32[]{:S(2)}) collective-permute-start(bf16[96,768]{1,0:T(8,128)(2,1)S(1)} %pad_maximum_fusion), channel_id=1, source_target_pairs={{0,16},{16,0},{1,17},{17,1},{2,18},{18,2},{3,19},{19,3},{4,20},{20... | collective-permute-start | bytes 442376 | tf_op jit(solution)/shard_map/ppermute | solution.py:126
  25.8 6.7 %collective-permute-start.4 = (bf16[96,768]{1,0:T(8,128)(2,1)S(1)}, bf16[96,768]{1,0:T(8,128)(2,1)S(1)}, u32[]{:S(2)}, u32[]{:S(2)}) collective-permute-start(bf16[96,768]{1,0:T(8,128)(2,1)S(1)} %pad_maximum_fusion), channel_id=1, source_target_pairs={{0,4},{1,5},{4,8},{5,9},{8,12},{9,13},{12,14},{13,15},{14,10},{15,... | collective-permute-start | bytes 442376 | tf_op jit(solution)/shard_map/ppermute | solution.py:106
  27.3 6.6 %collective-permute-start.6 = (bf16[96,768]{1,0:T(8,128)(2,1)S(1)}, bf16[96,768]{1,0:T(8,128)(2,1)S(1)}, u32[]{:S(2)}, u32[]{:S(2)}) collective-permute-start(bf16[96,768]{1,0:T(8,128)(2,1)S(1)} %pad_maximum_fusion), channel_id=1, source_target_pairs={{4,0},{5,1},{8,4},{9,5},{12,8},{13,9},{14,12},{15,13},{10,14},{11,... | collective-permute-start | bytes 442376 | tf_op jit(solution)/shard_map/ppermute | solution.py:109
  30.1 6.1 %collective-permute-start.5 = (bf16[96,768]{1,0:T(8,128)(2,1)S(1)}, bf16[96,768]{1,0:T(8,128)(2,1)S(1)}, u32[]{:S(2)}, u32[]{:S(2)}) collective-permute-start(bf16[96,768]{1,0:T(8,128)(2,1)S(1)} %collective-permute-done.3), channel_id=1, source_target_pairs={{4,0},{5,1},{8,4},{9,5},{12,8},{13,9},{14,12},{15,13},{10,14},{11,... | collective-permute-start | bytes 442376 | tf_op jit(solution)/shard_map/ppermute | solution.py:109
  32.5 6.7 %collective-permute-start.7 = (bf16[96,768]{1,0:T(8,128)(2,1)S(1)}, bf16[96,768]{1,0:T(8,128)(2,1)S(1)}, u32[]{:S(2)}, u32[]{:S(2)}) collective-permute-start(bf16[96,768]{1,0:T(8,128)(2,1)S(1)} %collective-permute-done.3), channel_id=1, source_target_pairs={{0,4},{1,5},{4,8},{5,9},{8,12},{9,13},{12,14},{13,15},{14,10},{15,... | collective-permute-start | bytes 442376 | tf_op jit(solution)/shard_map/ppermute | solution.py:106
  34.0 7.5 %collective-permute-start.8 = (bf16[96,768]{1,0:T(8,128)(2,1)S(1)}, bf16[96,768]{1,0:T(8,128)(2,1)S(1)}, u32[]{:S(2)}, u32[]{:S(2)}) collective-permute-start(bf16[96,768]{1,0:T(8,128)(2,1)S(1)} %collective-permute-done.4), channel_id=1, source_target_pairs={{0,4},{1,5},{4,8},{5,9},{8,12},{9,13},{12,14},{13,15},{14,10},{15,... | collective-permute-start | bytes 442376 | tf_op jit(solution)/shard_map/ppermute | solution.py:106
  36.2 6.8 %collective-permute-start.10 = (bf16[96,768]{1,0:T(8,128)(2,1)S(1)}, bf16[96,768]{1,0:T(8,128)(2,1)S(1)}, u32[]{:S(2)}, u32[]{:S(2)}) collective-permute-start(bf16[96,768]{1,0:T(8,128)(2,1)S(1)} %collective-permute-done.6), channel_id=1, source_target_pairs={{4,0},{5,1},{8,4},{9,5},{12,8},{13,9},{14,12},{15,13},{10,14},{11,... | collective-permute-start | bytes 442376 | tf_op jit(solution)/shard_map/ppermute | solution.py:109
  39.2 5.3 %collective-permute-start.9 = (bf16[96,768]{1,0:T(8,128)(2,1)S(1)}, bf16[96,768]{1,0:T(8,128)(2,1)S(1)}, u32[]{:S(2)}, u32[]{:S(2)}) collective-permute-start(bf16[96,768]{1,0:T(8,128)(2,1)S(1)} %collective-permute-done.5), channel_id=1, source_target_pairs={{4,0},{5,1},{8,4},{9,5},{12,8},{13,9},{14,12},{15,13},{10,14},{11,... | collective-permute-start | bytes 442376 | tf_op jit(solution)/shard_map/ppermute | solution.py:109
  41.5 5.8 %collective-permute-start.11 = (bf16[96,768]{1,0:T(8,128)(2,1)S(1)}, bf16[96,768]{1,0:T(8,128)(2,1)S(1)}, u32[]{:S(2)}, u32[]{:S(2)}) collective-permute-start(bf16[96,768]{1,0:T(8,128)(2,1)S(1)} %collective-permute-done.7), channel_id=1, source_target_pairs={{0,4},{1,5},{4,8},{5,9},{8,12},{9,13},{12,14},{13,15},{14,10},{15,... | collective-permute-start | bytes 442376 | tf_op jit(solution)/shard_map/ppermute | solution.py:106
  42.9 6.6 %collective-permute-start.12 = (bf16[96,768]{1,0:T(8,128)(2,1)S(1)}, bf16[96,768]{1,0:T(8,128)(2,1)S(1)}, u32[]{:S(2)}, u32[]{:S(2)}) collective-permute-start(bf16[96,768]{1,0:T(8,128)(2,1)S(1)} %collective-permute-done.8), channel_id=1, source_target_pairs={{0,4},{1,5},{4,8},{5,9},{8,12},{9,13},{12,14},{13,15},{14,10},{15,... | collective-permute-start | bytes 442376 | tf_op jit(solution)/shard_map/ppermute | solution.py:106
  44.5 9.6 %collective-permute-start.14 = (bf16[96,768]{1,0:T(8,128)(2,1)S(1)}, bf16[96,768]{1,0:T(8,128)(2,1)S(1)}, u32[]{:S(2)}, u32[]{:S(2)}) collective-permute-start(bf16[96,768]{1,0:T(8,128)(2,1)S(1)} %collective-permute-done.10), channel_id=1, source_target_pairs={{4,0},{5,1},{8,4},{9,5},{12,8},{13,9},{14,12},{15,13},{10,14},{11,... | collective-permute-start | bytes 442376 | tf_op jit(solution)/shard_map/ppermute | solution.py:109
  47.3 5.1 %collective-permute-start.13 = (bf16[96,768]{1,0:T(8,128)(2,1)S(1)}, bf16[96,768]{1,0:T(8,128)(2,1)S(1)}, u32[]{:S(2)}, u32[]{:S(2)}) collective-permute-start(bf16[96,768]{1,0:T(8,128)(2,1)S(1)} %collective-permute-done.9), channel_id=1, source_target_pairs={{4,0},{5,1},{8,4},{9,5},{12,8},{13,9},{14,12},{15,13},{10,14},{11,... | collective-permute-start | bytes 442376 | tf_op jit(solution)/shard_map/ppermute | solution.py:109
  49.5 6.4 %collective-permute-start.15 = (bf16[96,768]{1,0:T(8,128)(2,1)S(1)}, bf16[96,768]{1,0:T(8,128)(2,1)S(1)}, u32[]{:S(2)}, u32[]{:S(2)}) collective-permute-start(bf16[96,768]{1,0:T(8,128)(2,1)S(1)} %collective-permute-done.11), channel_id=1, source_target_pairs={{0,4},{1,5},{4,8},{5,9},{8,12},{9,13},{12,14},{13,15},{14,10},{15,... | collective-permute-start | bytes 442376 | tf_op jit(solution)/shard_map/ppermute | solution.py:106
  52.4 5.1 %collective-permute-start.16 = (bf16[96,768]{1,0:T(8,128)(2,1)S(1)}, bf16[96,768]{1,0:T(8,128)(2,1)S(1)}, u32[]{:S(2)}, u32[]{:S(2)}) collective-permute-start(bf16[96,768]{1,0:T(8,128)(2,1)S(1)} %collective-permute-done.12), channel_id=1, source_target_pairs={{0,4},{1,5},{4,8},{5,9},{8,12},{9,13},{12,14},{13,15},{14,10},{15,... | collective-permute-start | bytes 442376 | tf_op jit(solution)/shard_map/ppermute | solution.py:106
  54.2 5.1 %collective-permute-start.17 = (bf16[96,768]{1,0:T(8,128)(2,1)S(1)}, bf16[96,768]{1,0:T(8,128)(2,1)S(1)}, u32[]{:S(2)}, u32[]{:S(2)}) collective-permute-start(bf16[96,768]{1,0:T(8,128)(2,1)S(1)} %collective-permute-done.13), channel_id=1, source_target_pairs={{4,0},{5,1},{8,4},{9,5},{12,8},{13,9},{14,12},{15,13},{10,14},{11,... | collective-permute-start | bytes 442376 | tf_op jit(solution)/shard_map/ppermute | solution.py:109
  60.0 15.8 %copy-start.1 = (bf16[1,768,512]{2,1,0:T(8,128)(2,1)S(1)}, bf16[1,768,512]{2,1,0:T(8,128)(2,1)}, u32[]{:S(2)}) copy-start(bf16[1,768,512]{2,1,0:T(8,128)(2,1)} %param.14) | copy-start | bytes 2359300
  60.0 17.9 %copy-start.3 = (f32[128,8]{0,1:T(8,128)S(1)}, f32[128,8]{0,1:T(8,128)}, u32[]{:S(2)}) copy-start(f32[128,8]{0,1:T(8,128)} %param.18) | copy-start | bytes 12292
  60.0 26.4 %copy-start.5 = (s32[128,8]{0,1:T(8,128)S(1)}, s32[128,8]{0,1:T(8,128)}, u32[]{:S(2)}) copy-start(s32[128,8]{0,1:T(8,128)} %param.17) | copy-start | bytes 12292
  64.6 8.6 %collective-permute-start.31 = (bf16[256,768]{1,0:T(8,128)(2,1)S(1)}, bf16[256,768]{1,0:T(8,128)(2,1)S(1)}, u32[]{:S(2)}, u32[]{:S(2)}) collective-permute-start(bf16[256,768]{1,0:T(8,128)(2,1)S(1)} %fusion.3.refs_0_.refs_2_), channel_id=1, source_target_pairs={{0,4},{1,5},{4,8},{5,9},{8,12},{9,13},{12,14},{13,15},{14,10},{15,... | collective-permute-start | bytes 1179656 | tf_op jit(solution)/shard_map/ppermute | solution.py:106
  66.2 9.6 %collective-permute-start.22 = (bf16[256,768]{1,0:T(8,128)(2,1)S(1)}, bf16[256,768]{1,0:T(8,128)(2,1)S(1)}, u32[]{:S(2)}, u32[]{:S(2)}) collective-permute-start(bf16[256,768]{1,0:T(8,128)(2,1)S(1)} %fusion.3.refs_0_.refs_2_), channel_id=1, source_target_pairs={{4,0},{5,1},{8,4},{9,5},{12,8},{13,9},{14,12},{15,13},{10,14},{11,... | collective-permute-start | bytes 1179656 | tf_op jit(solution)/shard_map/ppermute | solution.py:109
  73.3 10.7 %collective-permute-start.32 = (bf16[256,768]{1,0:T(8,128)(2,1)S(1)}, bf16[256,768]{1,0:T(8,128)(2,1)S(1)}, u32[]{:S(2)}, u32[]{:S(2)}) collective-permute-start(bf16[256,768]{1,0:T(8,128)(2,1)S(1)} %collective-permute-done.31.refs_0_.refs_2_), channel_id=1, source_target_pairs={{0,4},{1,5},{4,8},{5,9},{8,12},{9,13},{12,14},{13,15},{14,10},{15,... | collective-permute-start | bytes 1179656 | tf_op jit(solution)/shard_map/ppermute | solution.py:106
  75.8 10.7 %collective-permute-start.25 = (bf16[256,768]{1,0:T(8,128)(2,1)S(1)}, bf16[256,768]{1,0:T(8,128)(2,1)S(1)}, u32[]{:S(2)}, u32[]{:S(2)}) collective-permute-start(bf16[256,768]{1,0:T(8,128)(2,1)S(1)} %collective-permute-done.22.refs_0_.refs_2_), channel_id=1, source_target_pairs={{4,0},{5,1},{8,4},{9,5},{12,8},{13,9},{14,12},{15,13},{10,14},{11,... | collective-permute-start | bytes 1179656 | tf_op jit(solution)/shard_map/ppermute | solution.py:109
  75.8 54.6 %collective-permute-start.19 = (bf16[768,512]{1,0:T(8,128)(2,1)S(1)}, bf16[768,512]{1,0:T(8,128)(2,1)}, u32[]{:S(2)}, u32[]{:S(2)}) collective-permute-start(bf16[768,512]{1,0:T(8,128)(2,1)S(1)} %bitcast.78), channel_id=1, source_target_pairs={{0,16},{16,0},{1,17},{17,1},{2,18},{18,2},{3,19},{19,3},{4,20},{20... | collective-permute-start | bytes 2359304 | tf_op jit(solution)/shard_map/ppermute | solution.py:156
  77.5 54.2 %collective-permute-start.20 = (bf16[768,512]{1,0:T(8,128)(2,1)}, bf16[768,512]{1,0:T(8,128)(2,1)}, u32[]{:S(2)}, u32[]{:S(2)}) collective-permute-start(bf16[768,512]{1,0:T(8,128)(2,1)} %bitcast.79), channel_id=1, source_target_pairs={{0,16},{16,0},{1,17},{17,1},{2,18},{18,2},{3,19},{19,3},{4,20},{20... | collective-permute-start | bytes 2359304 | tf_op jit(solution)/shard_map/ppermute | solution.py:156
  84.0 44.0 %collective-permute-start.33 = (bf16[256,768]{1,0:T(8,128)(2,1)S(1)}, bf16[256,768]{1,0:T(8,128)(2,1)S(1)}, u32[]{:S(2)}, u32[]{:S(2)}) collective-permute-start(bf16[256,768]{1,0:T(8,128)(2,1)S(1)} %collective-permute-done.32.refs_0_.refs_2_), channel_id=1, source_target_pairs={{0,4},{1,5},{4,8},{5,9},{8,12},{9,13},{12,14},{13,15},{14,10},{15,... | collective-permute-start | bytes 1179656 | tf_op jit(solution)/shard_map/ppermute | solution.py:106
  86.5 41.6 %collective-permute-start.28 = (bf16[256,768]{1,0:T(8,128)(2,1)S(1)}, bf16[256,768]{1,0:T(8,128)(2,1)S(1)}, u32[]{:S(2)}, u32[]{:S(2)}) collective-permute-start(bf16[256,768]{1,0:T(8,128)(2,1)S(1)} %collective-permute-done.25.refs_0_.refs_2_), channel_id=1, source_target_pairs={{4,0},{5,1},{8,4},{9,5},{12,8},{13,9},{14,12},{15,13},{10,14},{11,... | collective-permute-start | bytes 1179656 | tf_op jit(solution)/shard_map/ppermute | solution.py:109
  127.6 8.3 %copy-start.2 = (bf16[1,768,512]{2,1,0:T(8,128)(2,1)S(1)}, bf16[1,768,512]{2,1,0:T(8,128)(2,1)}, u32[]{:S(2)}) copy-start(bf16[1,768,512]{2,1,0:T(8,128)(2,1)} %param.15) | copy-start | bytes 2359300
  127.6 9.5 %collective-permute-start.18 = (bf16[256,768]{1,0:T(8,128)(2,1)S(1)}, bf16[256,768]{1,0:T(8,128)(2,1)S(1)}, u32[]{:S(2)}, u32[]{:S(2)}) collective-permute-start(bf16[256,768]{1,0:T(8,128)(2,1)S(1)} %fusion.3.refs_0_.refs_2_), channel_id=1, source_target_pairs={{0,1},{1,0},{2,3},{3,2},{4,5},{5,4},{6,7},{7,6},{8,9},{9,8},{10,11... | collective-permute-start | bytes 1179656 | tf_op jit(solution)/shard_map/ppermute | solution.py:103
  128.0 7.3 %collective-permute-start.34 = (bf16[128,768]{1,0:T(8,128)(2,1)S(1)}, bf16[128,768]{1,0:T(8,128)(2,1)S(1)}, u32[]{:S(2)}, u32[]{:S(2)}) collective-permute-start(bf16[128,768]{1,0:T(8,128)(2,1)S(1)} %constant_dynamic-slice_fusion.1), channel_id=1, source_target_pairs={{0,4},{1,5},{4,8},{5,9},{8,12},{9,13},{12,14},{13,15},{14,10},{15,... | collective-permute-start | bytes 589832 | tf_op jit(solution)/shard_map/ppermute | solution.py:106
  128.1 7.2 %collective-permute-start.35 = (bf16[128,768]{1,0:T(8,128)(2,1)S(1)}, bf16[128,768]{1,0:T(8,128)(2,1)S(1)}, u32[]{:S(2)}, u32[]{:S(2)}) collective-permute-start(bf16[128,768]{1,0:T(8,128)(2,1)S(1)} %constant_dynamic-slice_fusion), channel_id=1, source_target_pairs={{4,0},{5,1},{8,4},{9,5},{12,8},{13,9},{14,12},{15,13},{10,14},{11,... | collective-permute-start | bytes 589832 | tf_op jit(solution)/shard_map/ppermute | solution.py:109
  131.6 10.3 %collective-permute-start.43 = (bf16[256,768]{1,0:T(8,128)(2,1)S(1)}, bf16[256,768]{1,0:T(8,128)(2,1)S(1)}, u32[]{:S(2)}, u32[]{:S(2)}) collective-permute-start(bf16[256,768]{1,0:T(8,128)(2,1)S(1)} %collective-permute-done.31.refs_0_.refs_2_), channel_id=1, source_target_pairs={{0,1},{1,0},{2,3},{3,2},{4,5},{5,4},{6,7},{7,6},{8,9},{9,8},{10,11... | collective-permute-start | bytes 1179656 | tf_op jit(solution)/shard_map/ppermute | solution.py:103
  131.7 12.7 %collective-permute-start.23 = (bf16[256,768]{1,0:T(8,128)(2,1)S(1)}, bf16[256,768]{1,0:T(8,128)(2,1)S(1)}, u32[]{:S(2)}, u32[]{:S(2)}) collective-permute-start(bf16[256,768]{1,0:T(8,128)(2,1)S(1)} %collective-permute-done.22.refs_0_.refs_2_), channel_id=1, source_target_pairs={{0,1},{1,0},{2,3},{3,2},{4,5},{5,4},{6,7},{7,6},{8,9},{9,8},{10,11... | collective-permute-start | bytes 1179656 | tf_op jit(solution)/shard_map/ppermute | solution.py:103
  135.3 3.9 %collective-permute-start.36 = (bf16[128,768]{1,0:T(8,128)(2,1)S(1)}, bf16[128,768]{1,0:T(8,128)(2,1)S(1)}, u32[]{:S(2)}, u32[]{:S(2)}) collective-permute-start(bf16[128,768]{1,0:T(8,128)(2,1)S(1)} %collective-permute-done.35.refs_2_), channel_id=1, source_target_pairs={{0,1},{1,0},{2,3},{3,2},{4,5},{5,4},{6,7},{7,6},{8,9},{9,8},{10,11... | collective-permute-start | bytes 589832 | tf_op jit(solution)/shard_map/ppermute | solution.py:103
  135.3 4.5 %collective-permute-start.37 = (bf16[128,768]{1,0:T(8,128)(2,1)S(1)}, bf16[128,768]{1,0:T(8,128)(2,1)S(1)}, u32[]{:S(2)}, u32[]{:S(2)}) collective-permute-start(bf16[128,768]{1,0:T(8,128)(2,1)S(1)} %collective-permute-done.34.refs_0_), channel_id=1, source_target_pairs={{0,1},{1,0},{2,3},{3,2},{4,5},{5,4},{6,7},{7,6},{8,9},{9,8},{10,11... | collective-permute-start | bytes 589832 | tf_op jit(solution)/shard_map/ppermute | solution.py:103
  137.1 9.5 %collective-permute-start.45 = (bf16[256,768]{1,0:T(8,128)(2,1)S(1)}, bf16[256,768]{1,0:T(8,128)(2,1)S(1)}, u32[]{:S(2)}, u32[]{:S(2)}) collective-permute-start(bf16[256,768]{1,0:T(8,128)(2,1)S(1)} %collective-permute-done.32.refs_0_.refs_2_), channel_id=1, source_target_pairs={{0,1},{1,0},{2,3},{3,2},{4,5},{5,4},{6,7},{7,6},{8,9},{9,8},{10,11... | collective-permute-start | bytes 1179656 | tf_op jit(solution)/shard_map/ppermute | solution.py:103
  139.2 53.6 %collective-permute-start.21 = (bf16[128,1536]{1,0:T(8,128)(2,1)S(1)}, bf16[128,1536]{1,0:T(8,128)(2,1)S(1)}, u32[]{:S(2)}, u32[]{:S(2)}) collective-permute-start(bf16[128,1536]{1,0:T(8,128)(2,1)S(1)} %get-tuple-element.22), channel_id=1, source_target_pairs={{0,1},{1,0},{2,3},{3,2},{4,5},{5,4},{6,7},{7,6},{8,9},{9,8},{10,11... | collective-permute-start | bytes 1179656 | tf_op jit(solution)/shard_map/ppermute | solution.py:103
  139.8 9.4 %collective-permute-start.47 = (bf16[256,768]{1,0:T(8,128)(2,1)S(1)}, bf16[256,768]{1,0:T(8,128)(2,1)S(1)}, u32[]{:S(2)}, u32[]{:S(2)}) collective-permute-start(bf16[256,768]{1,0:T(8,128)(2,1)S(1)} %collective-permute-done.33.refs_0_.refs_2_), channel_id=1, source_target_pairs={{0,1},{1,0},{2,3},{3,2},{4,5},{5,4},{6,7},{7,6},{8,9},{9,8},{10,11... | collective-permute-start | bytes 1179656 | tf_op jit(solution)/shard_map/ppermute | solution.py:103
  141.9 9.5 %collective-permute-start.38 = (bf16[128,1536]{1,0:T(8,128)(2,1)S(1)}, bf16[128,1536]{1,0:T(8,128)(2,1)S(1)}, u32[]{:S(2)}, u32[]{:S(2)}) collective-permute-start(bf16[128,1536]{1,0:T(8,128)(2,1)S(1)} %get-tuple-element.30), channel_id=1, source_target_pairs={{0,1},{1,0},{2,3},{3,2},{4,5},{5,4},{6,7},{7,6},{8,9},{9,8},{10,11... | collective-permute-start | bytes 1179656 | tf_op jit(solution)/shard_map/ppermute | solution.py:103
  144.4 34.4 %collective-permute-start.44 = (bf16[128,1536]{1,0:T(8,128)(2,1)S(1)}, bf16[128,1536]{1,0:T(8,128)(2,1)S(1)}, u32[]{:S(2)}, u32[]{:S(2)}) collective-permute-start(bf16[128,1536]{1,0:T(8,128)(2,1)S(1)} %get-tuple-element.32), channel_id=1, source_target_pairs={{0,1},{1,0},{2,3},{3,2},{4,5},{5,4},{6,7},{7,6},{8,9},{9,8},{10,11... | collective-permute-start | bytes 1179656 | tf_op jit(solution)/shard_map/ppermute | solution.py:103
  146.6 5.3 %collective-permute-start.26 = (bf16[256,768]{1,0:T(8,128)(2,1)S(1)}, bf16[256,768]{1,0:T(8,128)(2,1)S(1)}, u32[]{:S(2)}, u32[]{:S(2)}) collective-permute-start(bf16[256,768]{1,0:T(8,128)(2,1)S(1)} %collective-permute-done.25.refs_0_.refs_2_), channel_id=1, source_target_pairs={{0,1},{1,0},{2,3},{3,2},{4,5},{5,4},{6,7},{7,6},{8,9},{9,8},{10,11... | collective-permute-start | bytes 1179656 | tf_op jit(solution)/shard_map/ppermute | solution.py:103
  149.2 6.6 %collective-permute-start.29 = (bf16[256,768]{1,0:T(8,128)(2,1)S(1)}, bf16[256,768]{1,0:T(8,128)(2,1)S(1)}, u32[]{:S(2)}, u32[]{:S(2)}) collective-permute-start(bf16[256,768]{1,0:T(8,128)(2,1)S(1)} %collective-permute-done.28.refs_0_.refs_2_), channel_id=1, source_target_pairs={{0,1},{1,0},{2,3},{3,2},{4,5},{5,4},{6,7},{7,6},{8,9},{9,8},{10,11... | collective-permute-start | bytes 1179656 | tf_op jit(solution)/shard_map/ppermute | solution.py:103
  151.4 6.5 %collective-permute-start.48 = (bf16[128,1536]{1,0:T(8,128)(2,1)S(1)}, bf16[128,1536]{1,0:T(8,128)(2,1)S(1)}, u32[]{:S(2)}, u32[]{:S(2)}) collective-permute-start(bf16[128,1536]{1,0:T(8,128)(2,1)S(1)} %get-tuple-element.36), channel_id=1, source_target_pairs={{0,1},{1,0},{2,3},{3,2},{4,5},{5,4},{6,7},{7,6},{8,9},{9,8},{10,11... | collective-permute-start | bytes 1179656 | tf_op jit(solution)/shard_map/ppermute | solution.py:103
  151.9 7.0 %collective-permute-start.52 = (bf16[64,1536]{1,0:T(8,128)(2,1)S(1)}, bf16[64,1536]{1,0:T(8,128)(2,1)S(1)}, u32[]{:S(2)}, u32[]{:S(2)}) collective-permute-start(bf16[64,1536]{1,0:T(8,128)(2,1)S(1)} %get-tuple-element.52), channel_id=1, source_target_pairs={{4,0},{5,1},{8,4},{9,5},{12,8},{13,9},{14,12},{15,13},{10,14},{11,... | collective-permute-start | bytes 589832 | tf_op jit(solution)/shard_map/ppermute | solution.py:109
  155.7 11.0 %collective-permute-start.46 = (bf16[128,1536]{1,0:T(8,128)(2,1)S(1)}, bf16[128,1536]{1,0:T(8,128)(2,1)S(1)}, u32[]{:S(2)}, u32[]{:S(2)}) collective-permute-start(bf16[128,1536]{1,0:T(8,128)(2,1)S(1)} %get-tuple-element.34), channel_id=1, source_target_pairs={{0,1},{1,0},{2,3},{3,2},{4,5},{5,4},{6,7},{7,6},{8,9},{9,8},{10,11... | collective-permute-start | bytes 1179656 | tf_op jit(solution)/shard_map/ppermute | solution.py:103
  157.9 1.9 collective-permute-start.30
  158.9 6.4 %collective-permute-start.39 = (bf16[64,1536]{1,0:T(8,128)(2,1)S(1)}, bf16[64,1536]{1,0:T(8,128)(2,1)S(1)}, u32[]{:S(2)}, u32[]{:S(2)}) collective-permute-start(bf16[64,1536]{1,0:T(8,128)(2,1)S(1)} %get-tuple-element.51), channel_id=1, source_target_pairs={{0,4},{1,5},{4,8},{5,9},{8,12},{9,13},{12,14},{13,15},{14,10},{15,... | collective-permute-start | bytes 589832 | tf_op jit(solution)/shard_map/ppermute | solution.py:106
  159.8 7.5 %collective-permute-start.49 = (bf16[64,1536]{1,0:T(8,128)(2,1)S(1)}, bf16[64,1536]{1,0:T(8,128)(2,1)S(1)}, u32[]{:S(2)}, u32[]{:S(2)}) collective-permute-start(bf16[64,1536]{1,0:T(8,128)(2,1)S(1)} %get-tuple-element.57), channel_id=1, source_target_pairs={{4,0},{5,1},{8,4},{9,5},{12,8},{13,9},{14,12},{15,13},{10,14},{11,... | collective-permute-start | bytes 589832 | tf_op jit(solution)/shard_map/ppermute | solution.py:109
  165.3 5.9 %collective-permute-start.53 = (bf16[64,1536]{1,0:T(8,128)(2,1)S(1)}, bf16[64,1536]{1,0:T(8,128)(2,1)S(1)}, u32[]{:S(2)}, u32[]{:S(2)}) collective-permute-start(bf16[64,1536]{1,0:T(8,128)(2,1)S(1)} %get-tuple-element.58), channel_id=1, source_target_pairs={{4,0},{5,1},{8,4},{9,5},{12,8},{13,9},{14,12},{15,13},{10,14},{11,... | collective-permute-start | bytes 589832 | tf_op jit(solution)/shard_map/ppermute | solution.py:109
  166.8 4.9 %collective-permute-start.27 = (bf16[128,1536]{1,0:T(8,128)(2,1)S(1)}, bf16[128,1536]{1,0:T(8,128)(2,1)S(1)}, u32[]{:S(2)}, u32[]{:S(2)}) collective-permute-start(bf16[128,1536]{1,0:T(8,128)(2,1)S(1)} %get-tuple-element.26), channel_id=1, source_target_pairs={{0,1},{1,0},{2,3},{3,2},{4,5},{5,4},{6,7},{7,6},{8,9},{9,8},{10,11... | collective-permute-start | bytes 1179656 | tf_op jit(solution)/shard_map/ppermute | solution.py:103
  167.2 7.8 %collective-permute-start.40 = (bf16[64,1536]{1,0:T(8,128)(2,1)S(1)}, bf16[64,1536]{1,0:T(8,128)(2,1)S(1)}, u32[]{:S(2)}, u32[]{:S(2)}) collective-permute-start(bf16[64,1536]{1,0:T(8,128)(2,1)S(1)} %get-tuple-element.49), channel_id=1, source_target_pairs={{0,4},{1,5},{4,8},{5,9},{8,12},{9,13},{12,14},{13,15},{14,10},{15,... | collective-permute-start | bytes 589832 | tf_op jit(solution)/shard_map/ppermute | solution.py:106
  171.2 7.2 %collective-permute-start.56 = (bf16[64,1536]{1,0:T(8,128)(2,1)S(1)}, bf16[64,1536]{1,0:T(8,128)(2,1)S(1)}, u32[]{:S(2)}, u32[]{:S(2)}) collective-permute-start(bf16[64,1536]{1,0:T(8,128)(2,1)S(1)} %get-tuple-element.50), channel_id=1, source_target_pairs={{0,4},{1,5},{4,8},{5,9},{8,12},{9,13},{12,14},{13,15},{14,10},{15,... | collective-permute-start | bytes 589832 | tf_op jit(solution)/shard_map/ppermute | solution.py:106
  171.7 13.5 %collective-permute-start.24 = (bf16[128,1536]{1,0:T(8,128)(2,1)S(1)}, bf16[128,1536]{1,0:T(8,128)(2,1)S(1)}, u32[]{:S(2)}, u32[]{:S(2)}) collective-permute-start(bf16[128,1536]{1,0:T(8,128)(2,1)S(1)} %get-tuple-element.24), channel_id=1, source_target_pairs={{0,1},{1,0},{2,3},{3,2},{4,5},{5,4},{6,7},{7,6},{8,9},{9,8},{10,11... | collective-permute-start | bytes 1179656 | tf_op jit(solution)/shard_map/ppermute | solution.py:103
  175.0 6.1 %collective-permute-start.50 = (bf16[64,1536]{1,0:T(8,128)(2,1)S(1)}, bf16[64,1536]{1,0:T(8,128)(2,1)S(1)}, u32[]{:S(2)}, u32[]{:S(2)}) collective-permute-start(bf16[64,1536]{1,0:T(8,128)(2,1)S(1)} %get-tuple-element.55), channel_id=1, source_target_pairs={{4,0},{5,1},{8,4},{9,5},{12,8},{13,9},{14,12},{15,13},{10,14},{11,... | collective-permute-start | bytes 589832 | tf_op jit(solution)/shard_map/ppermute | solution.py:109
  178.4 6.5 %collective-permute-start.54 = (bf16[64,1536]{1,0:T(8,128)(2,1)S(1)}, bf16[64,1536]{1,0:T(8,128)(2,1)S(1)}, u32[]{:S(2)}, u32[]{:S(2)}) collective-permute-start(bf16[64,1536]{1,0:T(8,128)(2,1)S(1)} %get-tuple-element.56), channel_id=1, source_target_pairs={{4,0},{5,1},{8,4},{9,5},{12,8},{13,9},{14,12},{15,13},{10,14},{11,... | collective-permute-start | bytes 589832 | tf_op jit(solution)/shard_map/ppermute | solution.py:109
  178.8 7.9 %collective-permute-start.41 = (bf16[64,1536]{1,0:T(8,128)(2,1)S(1)}, bf16[64,1536]{1,0:T(8,128)(2,1)S(1)}, u32[]{:S(2)}, u32[]{:S(2)}) collective-permute-start(bf16[64,1536]{1,0:T(8,128)(2,1)S(1)} %get-tuple-element.47), channel_id=1, source_target_pairs={{0,4},{1,5},{4,8},{5,9},{8,12},{9,13},{12,14},{13,15},{14,10},{15,... | collective-permute-start | bytes 589832 | tf_op jit(solution)/shard_map/ppermute | solution.py:106
  181.1 7.8 %collective-permute-start.57 = (bf16[64,1536]{1,0:T(8,128)(2,1)S(1)}, bf16[64,1536]{1,0:T(8,128)(2,1)S(1)}, u32[]{:S(2)}, u32[]{:S(2)}) collective-permute-start(bf16[64,1536]{1,0:T(8,128)(2,1)S(1)} %get-tuple-element.48), channel_id=1, source_target_pairs={{0,4},{1,5},{4,8},{5,9},{8,12},{9,13},{12,14},{13,15},{14,10},{15,... | collective-permute-start | bytes 589832 | tf_op jit(solution)/shard_map/ppermute | solution.py:106
  185.0 7.8 %collective-permute-start.51 = (bf16[64,1536]{1,0:T(8,128)(2,1)S(1)}, bf16[64,1536]{1,0:T(8,128)(2,1)S(1)}, u32[]{:S(2)}, u32[]{:S(2)}) collective-permute-start(bf16[64,1536]{1,0:T(8,128)(2,1)S(1)} %get-tuple-element.53), channel_id=1, source_target_pairs={{4,0},{5,1},{8,4},{9,5},{12,8},{13,9},{14,12},{15,13},{10,14},{11,... | collective-permute-start | bytes 589832 | tf_op jit(solution)/shard_map/ppermute | solution.py:109
  189.0 7.0 %collective-permute-start.42 = (bf16[64,1536]{1,0:T(8,128)(2,1)S(1)}, bf16[64,1536]{1,0:T(8,128)(2,1)S(1)}, u32[]{:S(2)}, u32[]{:S(2)}) collective-permute-start(bf16[64,1536]{1,0:T(8,128)(2,1)S(1)} %get-tuple-element.45), channel_id=1, source_target_pairs={{0,4},{1,5},{4,8},{5,9},{8,12},{9,13},{12,14},{13,15},{14,10},{15,... | collective-permute-start | bytes 589832 | tf_op jit(solution)/shard_map/ppermute | solution.py:106
  190.8 7.3 %collective-permute-start.58 = (bf16[64,1536]{1,0:T(8,128)(2,1)S(1)}, bf16[64,1536]{1,0:T(8,128)(2,1)S(1)}, u32[]{:S(2)}, u32[]{:S(2)}) collective-permute-start(bf16[64,1536]{1,0:T(8,128)(2,1)S(1)} %get-tuple-element.46), channel_id=1, source_target_pairs={{0,4},{1,5},{4,8},{5,9},{8,12},{9,13},{12,14},{13,15},{14,10},{15,... | collective-permute-start | bytes 589832 | tf_op jit(solution)/shard_map/ppermute | solution.py:106
  191.9 6.2 %collective-permute-start.55 = (bf16[64,1536]{1,0:T(8,128)(2,1)S(1)}, bf16[64,1536]{1,0:T(8,128)(2,1)S(1)}, u32[]{:S(2)}, u32[]{:S(2)}) collective-permute-start(bf16[64,1536]{1,0:T(8,128)(2,1)S(1)} %get-tuple-element.54), channel_id=1, source_target_pairs={{4,0},{5,1},{8,4},{9,5},{12,8},{13,9},{14,12},{15,13},{10,14},{11,... | collective-permute-start | bytes 589832 | tf_op jit(solution)/shard_map/ppermute | solution.py:109
  (2 other events, 12.2 us)

commit v2 on v0

v2 whole, which is shorter than its diff:
```python
import functools

import jax
import jax.numpy as jnp
from jax import lax
from jax.experimental import pallas as pl
from jax.experimental.pallas import tpu as pltpu
from jax.sharding import PartitionSpec as P

BF16 = jnp.bfloat16
F32 = jnp.float32
VMEM = pl.BlockSpec(memory_space=pltpu.VMEM)
SMEM = pl.BlockSpec(memory_space=pltpu.SMEM)
PIECES = 3
dot = functools.partial(jnp.dot, preferred_element_type=F32)


def ring_order(chips):
    return list(range(0, chips, 2)) + list(range(chips - 1, 0, -2))


def call(kernel, out_shape, *args, scratch=(), flops=0, name=None):
    return pl.pallas_call(
        kernel,
        in_specs=[SMEM] + [VMEM] * (len(args) - 1),
        out_specs=jax.tree.map(lambda _: VMEM, out_shape),
        out_shape=out_shape,
        scratch_shapes=list(scratch),
        compiler_params=pltpu.CompilerParams(vmem_limit_bytes=32 * 1024 * 1024),
        cost_estimate=pl.CostEstimate(flops=flops, bytes_accessed=4 * 1024 * 1024, transcendentals=0),
        name=name,
    )(*args)


def stream_kernel(layout, place, att, att_near, res, res_near, routes, scores, *refs):
    *blocks, out, full, tokens = refs
    core, expert, group = place[0], place[1], place[2]
    rows, width = att.shape
    half = width // 2
    extra = out.shape[0] - 2 * rows
    mine = pl.ds(pl.multiple_of(core * half, 128), half)
    own_rows = pl.ds(pl.multiple_of(core * rows, 16), rows)
    near_rows = pl.ds(pl.multiple_of((1 - core) * rows, 16), rows)
    tokens[own_rows, :] = att[...]
    tokens[near_rows, :] = att_near[...]
    if layout is None:
        full[...] = blocks[0][:, mine]
    else:
        chips, where = layout
        pair = lax.shift_right_logical(expert, 1)
        down = (pair & 1) == 1
        at = jnp.where(down, chips - lax.shift_right_logical(pair + 1, 1), lax.shift_right_logical(pair, 1))
        for block, (offset, other) in zip(blocks, where, strict=True):
            spot = lax.rem(at + (offset + chips), chips)
            source = jnp.where(spot < chips // 2, 2 * spot, 2 * (chips - spot) - 1)
            of_group = group if other == 0 else 1 - group
            depth = block.shape[0] // 2
            for index, c in enumerate((core, 1 - core)):
                start = ((of_group * chips + source) * 2 + c) * depth
                full[pl.ds(pl.multiple_of(start, 16), depth), :] = block[index * depth : (index + 1) * depth, :]
    projected = dot(tokens[...], full[...])
    for c in range(2):
        at_rows = slice(c * (rows + extra), c * (rows + extra) + rows)
        part = projected[c * rows : (c + 1) * rows]

        @pl.when(core == c)
        def _(at_rows=at_rows, part=part):
            out[at_rows, :] = (res[:, mine].astype(F32) + part).astype(BF16)

        @pl.when(core != c)
        def _(at_rows=at_rows, part=part):
            out[at_rows, :] = (res_near[:, mine].astype(F32) + part).astype(BF16)

    combine = scores[...] / jnp.sum(scores[...], axis=0, keepdims=True)
    named = lax.broadcasted_iota(jnp.int32, (extra, rows), 0)
    left = jnp.zeros((extra, rows), F32)
    for k in range(routes.shape[0]):
        left = left + jnp.where(routes[k : k + 1, :] == named, combine[k : k + 1, :], 0.0)
    for piece in range(PIECES):
        value = left.astype(BF16)
        out[rows : rows + extra, piece * rows : (piece + 1) * rows] = value
        left = left - value.astype(F32)


def expert_kernel(parts, place, *refs):
    *tokens, gate_a, gate_b, up_a, up_b, down, own_out, near_out = refs
    core, expert, group = place[0], place[1], place[2]
    rows = own_out.shape[0]

    def split(arrays):
        extra = arrays[0].shape[0] - rows if len(arrays) == 2 else arrays[0].shape[0] - 2 * rows
        if len(arrays) == 2:
            return arrays[0][:rows, :], arrays[1][extra:, :], arrays[0][rows:, : PIECES * rows]
        whole = arrays[0]
        return whole[:rows, :], whole[rows + extra :, :], whole[rows : rows + extra, : PIECES * rows]

    own = split(tokens[:parts])
    near = split(tokens[parts:])
    same = core == group
    first = jnp.concatenate([jnp.where(same, own[c], near[c]) for c in range(2)], axis=0)
    second = jnp.concatenate([jnp.where(same, near[c], own[c]) for c in range(2)], axis=0)
    gate_act = dot(first, gate_a[...]) + dot(second, gate_b[...])
    up_act = dot(first, up_a[...]) + dot(second, up_b[...])
    hidden = (jax.nn.silu(gate_act) * up_act).astype(BF16)
    result = dot(hidden, down[...])

    def weight(pieces):
        pieces = pieces.astype(F32)
        total = pieces[:, :rows]
        for piece in range(1, PIECES):
            total = total + pieces[:, piece * rows : (piece + 1) * rows]
        at_expert = lax.broadcasted_iota(jnp.int32, total.shape, 0) == expert
        line = jnp.sum(jnp.where(at_expert, total, 0.0), axis=0, keepdims=True)
        square = (rows, rows)
        diagonal = lax.broadcasted_iota(jnp.int32, square, 0) == lax.broadcasted_iota(jnp.int32, square, 1)
        return jnp.sum(jnp.where(diagonal, jnp.broadcast_to(line, square), 0.0), axis=1, keepdims=True)

    by_core = (jnp.where(core == 0, own[2], near[2]), jnp.where(core == 0, near[2], own[2]))
    for c in range(2):
        weighted = result[c * rows : (c + 1) * rows] * weight(by_core[c])

        @pl.when(core == c)
        def _(weighted=weighted):
            own_out[...] = weighted

        @pl.when(core != c)
        def _(weighted=weighted):
            near_out[...] = weighted.astype(BF16)


def final_kernel(place, own, near, mine, shared, first_a, first_b, second_a, second_b, gain, out):
    core = place[0]
    rows, width = out.shape
    extra = own.shape[0] - 2 * rows
    half = width // 2
    cut = rows // 2
    at_rows = pl.ds(pl.multiple_of(core * (rows + extra), 16), rows)
    own_half, near_half = own[at_rows, :].astype(F32), near[at_rows, :].astype(F32)
    stream = jnp.concatenate(
        [jnp.where(core == 0, own_half, near_half), jnp.where(core == 0, near_half, own_half)], axis=1
    )
    base = stream + mine[...] + shared[...].astype(F32)
    sums = ((first_a, first_b), (second_a, second_b))
    for index, (a, b) in enumerate(sums):
        total = base[index * cut : (index + 1) * cut] + (a[...].astype(F32) + b[...].astype(F32))
        scale = lax.rsqrt(jnp.sum(total * total, axis=1, keepdims=True) / width + 1e-06)
        out[index * cut : (index + 1) * cut, :] = (total * scale * gain[...]).astype(BF16)


def body(
    attention,
    residual,
    out_weight,
    gate_weight,
    up_weight,
    down_weight,
    routes,
    router_scores,
    norm_gain,
):
    token_count, width = attention.shape
    half = width // 2
    groups = lax.axis_size("dp")
    peers = lax.axis_size("expert")
    chips = peers // 2
    far = chips // 2
    ring = ring_order(chips)
    forth = [(2 * ring[k] + c, 2 * ring[(k + 1) % chips] + c) for k in range(chips) for c in range(2)]
    back = [(b, a) for a, b in forth]
    across = [(e, e ^ 1) for e in range(peers)]
    group = lax.axis_index("dp")
    expert = lax.axis_index("expert")
    core = expert & 1
    place = jnp.stack([core, expert, group if groups == 2 else jnp.zeros_like(group)]).astype(jnp.int32)

    def swap(x):
        return lax.ppermute(x, "expert", across)

    def go(x):
        return lax.ppermute(x, "expert", forth)

    def come(x):
        return lax.ppermute(x, "expert", back)

    if groups == 2:
        flip = [(0, 1), (1, 0)]

        def columns(which):
            return lax.dynamic_slice(
                out_weight, (0, which * half), (out_weight.shape[0], half), allow_negative_indices=False
            )

        mine = jnp.concatenate([columns(core), swap(columns(1 - core))], axis=0)
        other = lax.ppermute(mine, "dp", flip)
        blocks, layout = [mine, other], [(0, 0), (0, 1)]
        mine_f = mine_b = mine
        other_f = other_b = other
        for step in range(1, far + 1):
            mine_f, other_b = go(mine_f), come(other_b)
            blocks += [mine_f, other_b]
            layout += [(-step, 0), (step, 1)]
            if step < far:
                mine_b, other_f = come(mine_b), go(other_f)
                blocks += [mine_b, other_f]
                layout += [(step, 0), (-step, 1)]
        layout = (chips, layout)
        gate, up = gate_weight[0], up_weight[0]
        weights = (gate, lax.ppermute(gate, "dp", flip), up, lax.ppermute(up, "dp", flip), down_weight[0])
    else:
        blocks, layout = [lax.all_gather(out_weight, ("dp", "expert"), axis=0, tiled=True)], None
        gate = lax.all_gather(gate_weight, "dp", axis=1, tiled=True)[0]
        up = lax.all_gather(up_weight, "dp", axis=1, tiled=True)[0]
        weights = (gate[:half], gate[half:], up[:half], up[half:], down_weight[0])

    extra = -(-peers // 16) * 16
    block_rows = 2 * token_count + extra
    stream = call(
        functools.partial(stream_kernel, layout),
        jax.ShapeDtypeStruct((block_rows, half), BF16),
        place,
        attention,
        swap(attention),
        residual,
        swap(residual),
        routes.T,
        router_scores.T,
        *blocks,
        scratch=[pltpu.VMEM((width, half), BF16), pltpu.VMEM((2 * token_count, width), BF16)],
        flops=4 * token_count * width * half,
        name="stream",
    )

    def experts(*tokens):
        hidden = weights[0].shape[1]
        return call(
            functools.partial(expert_kernel, len(tokens) // 2),
            [
                jax.ShapeDtypeStruct((token_count, width), F32),
                jax.ShapeDtypeStruct((token_count, width), BF16),
            ],
            place,
            *tokens,
            *weights,
            flops=4 * token_count * 3 * width * hidden,
            name="experts",
        )

    out = {}
    stream_near = swap(stream)
    out[0] = experts(stream, stream_near)
    f = b = stream
    for step in range(1, far):
        f, b = go(f), come(b)
        out[-step] = experts(f, swap(f))
        out[step] = experts(b, swap(b))
    f, b = go(f[: token_count + extra]), come(b[token_count:])
    out[far] = experts(f, b, swap(f), swap(b))

    shared = {offset: (own, swap(near)) for offset, (own, near) in out.items()}
    cut = token_count // 2

    def term(offset, part):
        own, near = shared[offset]
        rows = slice(part * cut, (part + 1) * cut)
        return own[rows] + near[rows].astype(F32)

    def chain(move, sign, part, distance):
        total = move(term(distance if distance == far else sign * distance, part).astype(BF16))
        for left in range(distance - 1, 0, -1):
            total = move((term(sign * left, part) + total.astype(F32)).astype(BF16))
        return total

    return call(
        final_kernel,
        jax.ShapeDtypeStruct((token_count, width), BF16),
        place,
        stream,
        stream_near,
        *shared[0],
        chain(go, 1, 0, far),
        chain(come, -1, 0, far - 1),
        chain(go, 1, 1, far - 1),
        chain(come, -1, 1, far),
        norm_gain[None, :],
        name="final",
    )


def solution(mesh):
    in_specs = (
        P(("dp", "expert"), None),
        P(("dp", "expert"), None),
        P(("dp", "expert"), None),
        P("expert", "dp", None),
        P("expert", "dp", None),
        P("expert", None, None),
        P(("dp", "expert"), None),
        P(("dp", "expert"), None),
        P(),
    )
    out_specs = P(("dp", "expert"), None)
    return jax.shard_map(body, mesh=mesh, in_specs=in_specs, out_specs=out_specs, check_vma=False)
```

time: 318 us -> 152 us (0.48)
  the two profiles are of different devices: /device:TPU:11 before, /device:TPU:0 now
where the time goes in v2:
time: 152 us
  waiting for transfers between devices  79.7 us (52%)
  starting transfers between devices  45.5 us (30%)
  Pallas kernels  21.3 us (14%)
  local copies, waits for them, and re-layouts  4.34 us (3%)
    ppermute x18, waiting for transfers between devices, go(): return lax.ppermute(x, 'expert', forth)  54.2 us
    pallas_call x10, Pallas kernels, call(): pl.pallas_call(kernel, in_specs=[SMEM] + [VMEM] * (len(args) - 1), out_sp...  21.3 us
    ppermute x18, starting transfers between devices, come(): return lax.ppermute(x, 'expert', back)  19.7 us
    ppermute x18, starting transfers between devices, go(): return lax.ppermute(x, 'expert', forth)  16.9 us
    ppermute x18, waiting for transfers between devices, come(): return lax.ppermute(x, 'expert', back)  16.1 us
    ppermute x1, waiting for transfers between devices, body(): lax.ppermute(up, 'dp', flip)  5.96 us
    ppermute x20, starting transfers between devices, swap(): return lax.ppermute(x, 'expert', across)  3.97 us
    unnamed x16, local copies, waits for them, and re-layouts  3.38 us
  transfers between devices with their start and end apart: 59, of which 29 were waited for; matrix products, arithmetic and copies ran while one was open for 1% of the time, Pallas kernels for 12%

profile of v2, /device:TPU:0, one launch (start us, length us, event | category | flops | bytes accessed | tf_op | source)
XLA Modules:
  0.0 152.1 jit_solution(4966984231100845361)
XLA Ops:
  0.0 0.9 constant_dynamic-slice_fusion.1
  1.5 0.9 collective-permute-done.2
  2.4 2.9 %collective-permute-start.3 = (bf16[96,768]{1,0:T(8,128)(2,1)S(1)}, bf16[96,768]{1,0:T(8,128)(2,1)S(1)}, u32[]{:S(2)}, u32[]{:S(2)}) collective-permute-start(bf16[96,768]{1,0:T(8,128)(2,1)S(1)} %pad_maximum_fusion.refs_0_), channel_id=1, source_target_pairs={{0,16},{16,0},{1,17},{17,1},{2,18},{18,2},{3,19},{19,3},{4,20},{20... | collective-permute-start | bytes 442376 | tf_op jit(solution)/shard_map/ppermute | solution.py:194
  5.3 1.6 %collective-permute-start.4 = (bf16[96,768]{1,0:T(8,128)(2,1)S(1)}, bf16[96,768]{1,0:T(8,128)(2,1)S(1)}, u32[]{:S(2)}, u32[]{:S(2)}) collective-permute-start(bf16[96,768]{1,0:T(8,128)(2,1)S(1)} %pad_maximum_fusion.refs_0_), channel_id=1, source_target_pairs={{0,4},{1,5},{4,8},{5,9},{8,12},{9,13},{12,14},{13,15},{14,10},{15,... | collective-permute-start | bytes 442376 | tf_op jit(solution)/shard_map/ppermute | solution.py:180
  7.3 2.1 %collective-permute-done.3.refs_1_ = bf16[96,768]{1,0:T(8,128)(2,1)S(1)} collective-permute-done((bf16[96,768]{1,0:T(8,128)(2,1)S(1)}, bf16[96,768]{1,0:T(8,128)(2,1)S(1)}, u32[]{:S(2)}, u32[]{:S(2)}) %collective-permute-start.3) | collective-permute-done | bytes 147488 | tf_op jit(solution)/shard_map/ppermute | solution.py:194
  9.5 1.7 %collective-permute-start.5 = (bf16[96,768]{1,0:T(8,128)(2,1)S(1)}, bf16[96,768]{1,0:T(8,128)(2,1)S(1)}, u32[]{:S(2)}, u32[]{:S(2)}) collective-permute-start(bf16[96,768]{1,0:T(8,128)(2,1)S(1)} %collective-permute-done.3.refs_1_), channel_id=1, source_target_pairs={{4,0},{5,1},{8,4},{9,5},{12,8},{13,9},{14,12},{15,13},{10,14},{11,... | collective-permute-start | bytes 442376 | tf_op jit(solution)/shard_map/ppermute | solution.py:183
  11.5 1.8 %collective-permute-start.8 = (bf16[96,768]{1,0:T(8,128)(2,1)S(1)}, bf16[96,768]{1,0:T(8,128)(2,1)S(1)}, u32[]{:S(2)}, u32[]{:S(2)}) collective-permute-start(bf16[96,768]{1,0:T(8,128)(2,1)S(1)} %collective-permute-done.4.refs_2_), channel_id=1, source_target_pairs={{0,4},{1,5},{4,8},{5,9},{8,12},{9,13},{12,14},{13,15},{14,10},{15,... | collective-permute-start | bytes 442376 | tf_op jit(solution)/shard_map/ppermute | solution.py:180
  13.5 1.9 %collective-permute-done.5.refs_3_ = bf16[96,768]{1,0:T(8,128)(2,1)S(1)} collective-permute-done((bf16[96,768]{1,0:T(8,128)(2,1)S(1)}, bf16[96,768]{1,0:T(8,128)(2,1)S(1)}, u32[]{:S(2)}, u32[]{:S(2)}) %collective-permute-start.5) | collective-permute-done | bytes 147488 | tf_op jit(solution)/shard_map/ppermute | solution.py:183
  15.4 1.1 collective-permute-start.9
  16.5 1.4 collective-permute-done.7.refs_5_
  17.8 2.8 %collective-permute-done.8.refs_6_ = bf16[96,768]{1,0:T(8,128)(2,1)S(1)} collective-permute-done((bf16[96,768]{1,0:T(8,128)(2,1)S(1)}, bf16[96,768]{1,0:T(8,128)(2,1)S(1)}, u32[]{:S(2)}, u32[]{:S(2)}) %collective-permute-start.8) | collective-permute-done | bytes 147488 | tf_op jit(solution)/shard_map/ppermute | solution.py:180
  20.9 1.8 %collective-permute-start.12 = (bf16[96,768]{1,0:T(8,128)(2,1)S(1)}, bf16[96,768]{1,0:T(8,128)(2,1)S(1)}, u32[]{:S(2)}, u32[]{:S(2)}) collective-permute-start(bf16[96,768]{1,0:T(8,128)(2,1)S(1)} %collective-permute-done.8.refs_6_), channel_id=1, source_target_pairs={{0,4},{1,5},{4,8},{5,9},{8,12},{9,13},{12,14},{13,15},{14,10},{15,... | collective-permute-start | bytes 442376 | tf_op jit(solution)/shard_map/ppermute | solution.py:180
  23.0 1.7 %collective-permute-start.14 = (bf16[96,768]{1,0:T(8,128)(2,1)S(1)}, bf16[96,768]{1,0:T(8,128)(2,1)S(1)}, u32[]{:S(2)}, u32[]{:S(2)}) collective-permute-start(bf16[96,768]{1,0:T(8,128)(2,1)S(1)} %collective-permute-done.10.refs_8_), channel_id=1, source_target_pairs={{4,0},{5,1},{8,4},{9,5},{12,8},{13,9},{14,12},{15,13},{10,14},{11,... | collective-permute-start | bytes 442376 | tf_op jit(solution)/shard_map/ppermute | solution.py:183
  24.7 2.7 %collective-permute-done.11.refs_9_ = bf16[96,768]{1,0:T(8,128)(2,1)S(1)} collective-permute-done((bf16[96,768]{1,0:T(8,128)(2,1)S(1)}, bf16[96,768]{1,0:T(8,128)(2,1)S(1)}, u32[]{:S(2)}, u32[]{:S(2)}) %collective-permute-start.11) | collective-permute-done | bytes 147488 | tf_op jit(solution)/shard_map/ppermute | solution.py:180
  27.7 2.8 %collective-permute-done.12.refs_10_ = bf16[96,768]{1,0:T(8,128)(2,1)S(1)} collective-permute-done((bf16[96,768]{1,0:T(8,128)(2,1)S(1)}, bf16[96,768]{1,0:T(8,128)(2,1)S(1)}, u32[]{:S(2)}, u32[]{:S(2)}) %collective-permute-start.12) | collective-permute-done | bytes 147488 | tf_op jit(solution)/shard_map/ppermute | solution.py:180
  30.8 1.7 %collective-permute-start.17 = (bf16[96,768]{1,0:T(8,128)(2,1)S(1)}, bf16[96,768]{1,0:T(8,128)(2,1)S(1)}, u32[]{:S(2)}, u32[]{:S(2)}) collective-permute-start(bf16[96,768]{1,0:T(8,128)(2,1)S(1)} %collective-permute-done.13.refs_11_), channel_id=1, source_target_pairs={{4,0},{5,1},{8,4},{9,5},{12,8},{13,9},{14,12},{15,13},{10,14},{11,... | collective-permute-start | bytes 442376 | tf_op jit(solution)/shard_map/ppermute | solution.py:183
  32.6 1.4 collective-permute-done.15.refs_13_
  34.0 1.7 %collective-permute-done.16.refs_14_ = bf16[96,768]{1,0:T(8,128)(2,1)S(1)} collective-permute-done((bf16[96,768]{1,0:T(8,128)(2,1)S(1)}, bf16[96,768]{1,0:T(8,128)(2,1)S(1)}, u32[]{:S(2)}, u32[]{:S(2)}) %collective-permute-start.16) | collective-permute-done | bytes 147488 | tf_op jit(solution)/shard_map/ppermute | solution.py:180
  36.0 1.0 copy-done.3
  37.0 1.0 copy-done.4
  38.0 0.7 copy-done.5
  38.7 0.7 copy-done.6
  39.4 1.6 %stream.1.refs_0_.own = bf16[272,768]{1,0:T(8,128)(2,1)S(1)} custom-call(s32[3]{0:T(128)S(1)} %pad_add_fusion.place, bf16[128,1536]{1,0:T(8,128)(2,1)S(1)} %copy-done.3, bf16[128,1536]{1,0:T(8,128)(2,1)S(1)} %collective-permute-done.att_near, bf16[128,1536]{1,0:T(8,128)(2,1)S(1)} %copy-done.4, bf16[128,1536]{1,0:T(8,128)(2,1)S(1)} %collective-permute-done.1.res_near, ...), custom_call_target="tpu_custom_call" | custom-call | flops 603979776 | bytes 4194304 | tf_op jit(solution)/shard_map/stream/pallas_call | solution.py:23
  41.0 1.8 %collective-permute-start.31 = (bf16[272,768]{1,0:T(8,128)(2,1)S(1)}, bf16[272,768]{1,0:T(8,128)(2,1)S(1)}, u32[]{:S(2)}, u32[]{:S(2)}) collective-permute-start(bf16[272,768]{1,0:T(8,128)(2,1)S(1)} %stream.1.refs_0_.own), channel_id=1, source_target_pairs={{0,4},{1,5},{4,8},{5,9},{8,12},{9,13},{12,14},{13,15},{14,10},{15,... | collective-permute-start | bytes 1253384 | tf_op jit(solution)/shard_map/ppermute | solution.py:180
  43.1 7.8 %collective-permute-done.31.refs_0_ = bf16[272,768]{1,0:T(8,128)(2,1)S(1)} collective-permute-done((bf16[272,768]{1,0:T(8,128)(2,1)S(1)}, bf16[272,768]{1,0:T(8,128)(2,1)S(1)}, u32[]{:S(2)}, u32[]{:S(2)}) %collective-permute-start.31) | collective-permute-done | bytes 417824 | tf_op jit(solution)/shard_map/ppermute | solution.py:180
  50.9 0.9 collective-permute-start.32
  51.8 1.1 collective-permute-start.25
  52.9 1.7 %collective-permute-start.19 = (bf16[768,512]{1,0:T(8,128)(2,1)S(1)}, bf16[768,512]{1,0:T(8,128)(2,1)S(1)}, u32[]{:S(2)}, u32[]{:S(2)}) collective-permute-start(bf16[768,512]{1,0:T(8,128)(2,1)S(1)} %bitcast.16), channel_id=1, source_target_pairs={{0,16},{16,0},{1,17},{17,1},{2,18},{18,2},{3,19},{19,3},{4,20},{20... | collective-permute-start | bytes 2359304 | tf_op jit(solution)/shard_map/ppermute | solution.py:208
  54.9 5.7 %collective-permute-done.32.refs_0_ = bf16[272,768]{1,0:T(8,128)(2,1)S(1)} collective-permute-done((bf16[272,768]{1,0:T(8,128)(2,1)S(1)}, bf16[272,768]{1,0:T(8,128)(2,1)S(1)}, u32[]{:S(2)}, u32[]{:S(2)}) %collective-permute-start.32) | collective-permute-done | bytes 417824 | tf_op jit(solution)/shard_map/ppermute | solution.py:180
  60.7 1.8 %collective-permute-start.33 = (bf16[272,768]{1,0:T(8,128)(2,1)S(1)}, bf16[272,768]{1,0:T(8,128)(2,1)S(1)}, u32[]{:S(2)}, u32[]{:S(2)}) collective-permute-start(bf16[272,768]{1,0:T(8,128)(2,1)S(1)} %collective-permute-done.32.refs_0_), channel_id=1, source_target_pairs={{0,4},{1,5},{4,8},{5,9},{8,12},{9,13},{12,14},{13,15},{14,10},{15,... | collective-permute-start | bytes 1253384 | tf_op jit(solution)/shard_map/ppermute | solution.py:180
  62.7 7.9 %collective-permute-done.33.refs_0_ = bf16[272,768]{1,0:T(8,128)(2,1)S(1)} collective-permute-done((bf16[272,768]{1,0:T(8,128)(2,1)S(1)}, bf16[272,768]{1,0:T(8,128)(2,1)S(1)}, u32[]{:S(2)}, u32[]{:S(2)}) %collective-permute-start.33) | collective-permute-done | bytes 417824 | tf_op jit(solution)/shard_map/ppermute | solution.py:180
  70.6 2.3 %collective-permute-start.34 = (bf16[144,768]{1,0:T(8,128)(2,1)S(1)}, bf16[144,768]{1,0:T(8,128)(2,1)S(1)}, u32[]{:S(2)}, u32[]{:S(2)}) collective-permute-start(bf16[144,768]{1,0:T(8,128)(2,1)S(1)} %slice.123), channel_id=1, source_target_pairs={{0,4},{1,5},{4,8},{5,9},{8,12},{9,13},{12,14},{13,15},{14,10},{15,... | collective-permute-start | bytes 663560 | tf_op jit(solution)/shard_map/ppermute | solution.py:180
  73.5 3.1 %collective-permute-done.34.refs_0_ = bf16[144,768]{1,0:T(8,128)(2,1)S(1)} collective-permute-done((bf16[144,768]{1,0:T(8,128)(2,1)S(1)}, bf16[144,768]{1,0:T(8,128)(2,1)S(1)}, u32[]{:S(2)}, u32[]{:S(2)}) %collective-permute-start.34) | collective-permute-done | bytes 221216 | tf_op jit(solution)/shard_map/ppermute | solution.py:180
  76.6 2.8 %collective-permute-done.35.refs_1_ = bf16[144,768]{1,0:T(8,128)(2,1)S(1)} collective-permute-done((bf16[144,768]{1,0:T(8,128)(2,1)S(1)}, bf16[144,768]{1,0:T(8,128)(2,1)S(1)}, u32[]{:S(2)}, u32[]{:S(2)}) %collective-permute-start.35) | collective-permute-done | bytes 221216 | tf_op jit(solution)/shard_map/ppermute | solution.py:183
  79.4 6.0 %collective-permute-done.20.refs_5_.refs_7_ = bf16[768,512]{1,0:T(8,128)(2,1)S(1)} collective-permute-done((bf16[768,512]{1,0:T(8,128)(2,1)S(1)}, bf16[768,512]{1,0:T(8,128)(2,1)S(1)}, u32[]{:S(2)}, u32[]{:S(2)}) %collective-permute-start.20) | collective-permute-done | bytes 786464 | tf_op jit(solution)/shard_map/ppermute | solution.py:208
  85.9 2.2 %experts.8 = (f32[128,1536]{1,0:T(8,128)S(1)}, bf16[128,1536]{1,0:T(8,128)(2,1)S(1)}) custom-call(s32[3]{0:T(128)S(1)} %pad_add_fusion.place, bf16[272,768]{1,0:T(8,128)(2,1)S(1)} %stream.1.refs_0_.own, bf16[272,768]{1,0:T(8,128)(2,1)S(1)} %collective-permute-done.18.refs_1_.near, bf16[768,512]{1,0:T(8,128)(2,1)S(1)} %bitcast.17, ...), custom_call_target="tpu_custom_call" | custom-call | flops 1207959552 | bytes 4194304 | tf_op jit(solution)/shard_map/experts/pallas_call | solution.py:23
  88.7 2.2 %experts.12 = (f32[128,1536]{1,0:T(8,128)S(1)}, bf16[128,1536]{1,0:T(8,128)(2,1)S(1)}) custom-call(s32[3]{0:T(128)S(1)} %pad_add_fusion.place, bf16[144,768]{1,0:T(8,128)(2,1)S(1)} %collective-permute-done.34.refs_0_, bf16[144,768]{1,0:T(8,128)(2,1)S(1)} %collective-permute-done.35.refs_1_, bf16[144,768]{1,0:T(8,128)(2,1)S(1)} %collective-permute-done.36.refs_2_, ...), custom_call_target="tpu_custom_call" | custom-call | flops 1207959552 | bytes 4194304 | tf_op jit(solution)/shard_map/experts/pallas_call | solution.py:23
  91.1 2.2 %experts.13 = (f32[128,1536]{1,0:T(8,128)S(1)}, bf16[128,1536]{1,0:T(8,128)(2,1)S(1)}) custom-call(s32[3]{0:T(128)S(1)} %pad_add_fusion.place, bf16[272,768]{1,0:T(8,128)(2,1)S(1)} %collective-permute-done.31.refs_0_, bf16[272,768]{1,0:T(8,128)(2,1)S(1)} %collective-permute-done.43.refs_1_, bf16[768,512]{1,0:T(8,128)(2,1)S(1)} %bitcast.19, ...), custom_call_target="tpu_custom_call" | custom-call | flops 1207959552 | bytes 4194304 | tf_op jit(solution)/shard_map/experts/pallas_call | solution.py:23
  93.9 2.2 %experts.9 = (f32[128,1536]{1,0:T(8,128)S(1)}, bf16[128,1536]{1,0:T(8,128)(2,1)S(1)}) custom-call(s32[3]{0:T(128)S(1)} %pad_add_fusion.place, bf16[272,768]{1,0:T(8,128)(2,1)S(1)} %collective-permute-done.22.refs_0_, bf16[272,768]{1,0:T(8,128)(2,1)S(1)} %collective-permute-done.23.refs_1_, bf16[768,512]{1,0:T(8,128)(2,1)S(1)} %bitcast.20, ...), custom_call_target="tpu_custom_call" | custom-call | flops 1207959552 | bytes 4194304 | tf_op jit(solution)/shard_map/experts/pallas_call | solution.py:23
  96.3 2.4 %experts.14 = (f32[128,1536]{1,0:T(8,128)S(1)}, bf16[128,1536]{1,0:T(8,128)(2,1)S(1)}) custom-call(s32[3]{0:T(128)S(1)} %pad_add_fusion.place, bf16[272,768]{1,0:T(8,128)(2,1)S(1)} %collective-permute-done.32.refs_0_, bf16[272,768]{1,0:T(8,128)(2,1)S(1)} %collective-permute-done.45.refs_1_, bf16[768,512]{1,0:T(8,128)(2,1)S(1)} %bitcast.21, ...), custom_call_target="tpu_custom_call" | custom-call | flops 1207959552 | bytes 4194304 | tf_op jit(solution)/shard_map/experts/pallas_call | solution.py:23
  99.2 2.2 %experts.15 = (f32[128,1536]{1,0:T(8,128)S(1)}, bf16[128,1536]{1,0:T(8,128)(2,1)S(1)}) custom-call(s32[3]{0:T(128)S(1)} %pad_add_fusion.place, bf16[272,768]{1,0:T(8,128)(2,1)S(1)} %collective-permute-done.33.refs_0_, bf16[272,768]{1,0:T(8,128)(2,1)S(1)} %collective-permute-done.47.refs_1_, bf16[768,512]{1,0:T(8,128)(2,1)S(1)} %bitcast.22, ...), custom_call_target="tpu_custom_call" | custom-call | flops 1207959552 | bytes 4194304 | tf_op jit(solution)/shard_map/experts/pallas_call | solution.py:23
  101.7 1.5 collective-permute-start.55
  103.2 2.2 %experts.10 = (f32[128,1536]{1,0:T(8,128)S(1)}, bf16[128,1536]{1,0:T(8,128)(2,1)S(1)}) custom-call(s32[3]{0:T(128)S(1)} %pad_add_fusion.place, bf16[272,768]{1,0:T(8,128)(2,1)S(1)} %collective-permute-done.25.refs_0_, bf16[272,768]{1,0:T(8,128)(2,1)S(1)} %collective-permute-done.26.refs_1_, bf16[768,512]{1,0:T(8,128)(2,1)S(1)} %bitcast.23, ...), custom_call_target="tpu_custom_call" | custom-call | flops 1207959552 | bytes 4194304 | tf_op jit(solution)/shard_map/experts/pallas_call | solution.py:23
  105.7 2.2 %experts.11 = (f32[128,1536]{1,0:T(8,128)S(1)}, bf16[128,1536]{1,0:T(8,128)(2,1)S(1)}) custom-call(s32[3]{0:T(128)S(1)} %pad_add_fusion.place, bf16[272,768]{1,0:T(8,128)(2,1)S(1)} %collective-permute-done.28.refs_0_, bf16[272,768]{1,0:T(8,128)(2,1)S(1)} %collective-permute-done.29.refs_1_, bf16[768,512]{1,0:T(8,128)(2,1)S(1)} %bitcast.24, ...), custom_call_target="tpu_custom_call" | custom-call | flops 1207959552 | bytes 4194304 | tf_op jit(solution)/shard_map/experts/pallas_call | solution.py:23
  108.3 0.6 collective-permute-done.55
  109.7 1.6 %collective-permute-start.49 = (bf16[64,1536]{1,0:T(8,128)(2,1)S(1)}, bf16[64,1536]{1,0:T(8,128)(2,1)S(1)}, u32[]{:S(2)}, u32[]{:S(2)}) collective-permute-start(bf16[64,1536]{1,0:T(8,128)(2,1)S(1)} %get-tuple-element.42), channel_id=1, source_target_pairs={{4,0},{5,1},{8,4},{9,5},{12,8},{13,9},{14,12},{15,13},{10,14},{11,... | collective-permute-start | bytes 589832 | tf_op jit(solution)/shard_map/ppermute | solution.py:183
  111.3 4.1 %collective-permute-done.39 = bf16[64,1536]{1,0:T(8,128)(2,1)S(1)} collective-permute-done((bf16[64,1536]{1,0:T(8,128)(2,1)S(1)}, bf16[64,1536]{1,0:T(8,128)(2,1)S(1)}, u32[]{:S(2)}, u32[]{:S(2)}) %collective-permute-start.39) | collective-permute-done | bytes 196640 | tf_op jit(solution)/shard_map/ppermute | solution.py:180
  115.4 1.4 collective-permute-start.56
  117.1 0.6 collective-permute-start.40
  117.7 3.4 %collective-permute-done.56 = bf16[64,1536]{1,0:T(8,128)(2,1)S(1)} collective-permute-done((bf16[64,1536]{1,0:T(8,128)(2,1)S(1)}, bf16[64,1536]{1,0:T(8,128)(2,1)S(1)}, u32[]{:S(2)}, u32[]{:S(2)}) %collective-permute-start.56) | collective-permute-done | bytes 196640 | tf_op jit(solution)/shard_map/ppermute | solution.py:183
  121.9 3.0 %collective-permute-done.40 = bf16[64,1536]{1,0:T(8,128)(2,1)S(1)} collective-permute-done((bf16[64,1536]{1,0:T(8,128)(2,1)S(1)}, bf16[64,1536]{1,0:T(8,128)(2,1)S(1)}, u32[]{:S(2)}, u32[]{:S(2)}) %collective-permute-start.40) | collective-permute-done | bytes 196640 | tf_op jit(solution)/shard_map/ppermute | solution.py:180
  124.8 1.6 %collective-permute-start.50 = (bf16[64,1536]{1,0:T(8,128)(2,1)S(1)}, bf16[64,1536]{1,0:T(8,128)(2,1)S(1)}, u32[]{:S(2)}, u32[]{:S(2)}) collective-permute-start(bf16[64,1536]{1,0:T(8,128)(2,1)S(1)} %get-tuple-element.40), channel_id=1, source_target_pairs={{4,0},{5,1},{8,4},{9,5},{12,8},{13,9},{14,12},{15,13},{10,14},{11,... | collective-permute-start | bytes 589832 | tf_op jit(solution)/shard_map/ppermute | solution.py:183
  126.4 2.2 %collective-permute-done.52 = bf16[64,1536]{1,0:T(8,128)(2,1)S(1)} collective-permute-done((bf16[64,1536]{1,0:T(8,128)(2,1)S(1)}, bf16[64,1536]{1,0:T(8,128)(2,1)S(1)}, u32[]{:S(2)}, u32[]{:S(2)}) %collective-permute-start.52) | collective-permute-done | bytes 196640 | tf_op jit(solution)/shard_map/ppermute | solution.py:180
  128.6 1.6 %collective-permute-start.57 = (bf16[64,1536]{1,0:T(8,128)(2,1)S(1)}, bf16[64,1536]{1,0:T(8,128)(2,1)S(1)}, u32[]{:S(2)}, u32[]{:S(2)}) collective-permute-start(bf16[64,1536]{1,0:T(8,128)(2,1)S(1)} %get-tuple-element.39), channel_id=1, source_target_pairs={{4,0},{5,1},{8,4},{9,5},{12,8},{13,9},{14,12},{15,13},{10,14},{11,... | collective-permute-start | bytes 589832 | tf_op jit(solution)/shard_map/ppermute | solution.py:183
  131.4 3.6 %collective-permute-done.57 = bf16[64,1536]{1,0:T(8,128)(2,1)S(1)} collective-permute-done((bf16[64,1536]{1,0:T(8,128)(2,1)S(1)}, bf16[64,1536]{1,0:T(8,128)(2,1)S(1)}, u32[]{:S(2)}, u32[]{:S(2)}) %collective-permute-start.57) | collective-permute-done | bytes 196640 | tf_op jit(solution)/shard_map/ppermute | solution.py:183
  135.2 1.6 %collective-permute-start.51 = (bf16[64,1536]{1,0:T(8,128)(2,1)S(1)}, bf16[64,1536]{1,0:T(8,128)(2,1)S(1)}, u32[]{:S(2)}, u32[]{:S(2)}) collective-permute-start(bf16[64,1536]{1,0:T(8,128)(2,1)S(1)} %get-tuple-element.38), channel_id=1, source_target_pairs={{4,0},{5,1},{8,4},{9,5},{12,8},{13,9},{14,12},{15,13},{10,14},{11,... | collective-permute-start | bytes 589832 | tf_op jit(solution)/shard_map/ppermute | solution.py:183
  136.8 1.6 %collective-permute-start.58 = (bf16[64,1536]{1,0:T(8,128)(2,1)S(1)}, bf16[64,1536]{1,0:T(8,128)(2,1)S(1)}, u32[]{:S(2)}, u32[]{:S(2)}) collective-permute-start(bf16[64,1536]{1,0:T(8,128)(2,1)S(1)} %get-tuple-element.37), channel_id=1, source_target_pairs={{4,0},{5,1},{8,4},{9,5},{12,8},{13,9},{14,12},{15,13},{10,14},{11,... | collective-permute-start | bytes 589832 | tf_op jit(solution)/shard_map/ppermute | solution.py:183
  138.4 2.4 %collective-permute-done.53 = bf16[64,1536]{1,0:T(8,128)(2,1)S(1)} collective-permute-done((bf16[64,1536]{1,0:T(8,128)(2,1)S(1)}, bf16[64,1536]{1,0:T(8,128)(2,1)S(1)}, u32[]{:S(2)}, u32[]{:S(2)}) %collective-permute-start.53) | collective-permute-done | bytes 196640 | tf_op jit(solution)/shard_map/ppermute | solution.py:180
  141.4 0.6 collective-permute-start.54
  142.0 0.9 collective-permute-done.51.first_b
  142.9 2.1 %collective-permute-done.58.second_b = bf16[64,1536]{1,0:T(8,128)(2,1)S(1)} collective-permute-done((bf16[64,1536]{1,0:T(8,128)(2,1)S(1)}, bf16[64,1536]{1,0:T(8,128)(2,1)S(1)}, u32[]{:S(2)}, u32[]{:S(2)}) %collective-permute-start.58) | collective-permute-done | bytes 196640 | tf_op jit(solution)/shard_map/ppermute | solution.py:183
  145.0 3.3 %collective-permute-done.42.first_a = bf16[64,1536]{1,0:T(8,128)(2,1)S(1)} collective-permute-done((bf16[64,1536]{1,0:T(8,128)(2,1)S(1)}, bf16[64,1536]{1,0:T(8,128)(2,1)S(1)}, u32[]{:S(2)}, u32[]{:S(2)}) %collective-permute-start.42) | collective-permute-done | bytes 196640 | tf_op jit(solution)/shard_map/ppermute | solution.py:180
  148.3 2.1 %collective-permute-done.54.second_a = bf16[64,1536]{1,0:T(8,128)(2,1)S(1)} collective-permute-done((bf16[64,1536]{1,0:T(8,128)(2,1)S(1)}, bf16[64,1536]{1,0:T(8,128)(2,1)S(1)}, u32[]{:S(2)}, u32[]{:S(2)}) %collective-permute-start.54) | collective-permute-done | bytes 196640 | tf_op jit(solution)/shard_map/ppermute | solution.py:180
  150.4 1.7 %final.1 = bf16[128,1536]{1,0:T(8,128)(2,1)} custom-call(s32[3]{0:T(128)S(1)} %pad_add_fusion.place, bf16[272,768]{1,0:T(8,128)(2,1)S(1)} %stream.1.refs_0_.own, bf16[272,768]{1,0:T(8,128)(2,1)S(1)} %collective-permute-done.18.refs_1_.near, f32[128,1536]{1,0:T(8,128)S(1)} %get-tuple-element.21.mine, bf16[128,1536]{1,0:T(8,128)(2,1)S(1)} %collective-permute-done.21.shared, ...), custom_call_target="tpu_custom_call" | custom-call | bytes 4194304 | tf_op jit(solution)/shard_map/final/pallas_call | solution.py:23
  (93 shorter events, 11.5 us)
Async XLA Ops:
  0.9 1.4 collective-permute-start.2
  2.4 7.1 %collective-permute-start.3 = (bf16[96,768]{1,0:T(8,128)(2,1)S(1)}, bf16[96,768]{1,0:T(8,128)(2,1)S(1)}, u32[]{:S(2)}, u32[]{:S(2)}) collective-permute-start(bf16[96,768]{1,0:T(8,128)(2,1)S(1)} %pad_maximum_fusion.refs_0_), channel_id=1, source_target_pairs={{0,16},{16,0},{1,17},{17,1},{2,18},{18,2},{3,19},{19,3},{4,20},{20... | collective-permute-start | bytes 442376 | tf_op jit(solution)/shard_map/ppermute | solution.py:194
  5.3 6.2 %collective-permute-start.4 = (bf16[96,768]{1,0:T(8,128)(2,1)S(1)}, bf16[96,768]{1,0:T(8,128)(2,1)S(1)}, u32[]{:S(2)}, u32[]{:S(2)}) collective-permute-start(bf16[96,768]{1,0:T(8,128)(2,1)S(1)} %pad_maximum_fusion.refs_0_), channel_id=1, source_target_pairs={{0,4},{1,5},{4,8},{5,9},{8,12},{9,13},{12,14},{13,15},{14,10},{15,... | collective-permute-start | bytes 442376 | tf_op jit(solution)/shard_map/ppermute | solution.py:180
  6.9 6.4 %collective-permute-start.6 = (bf16[96,768]{1,0:T(8,128)(2,1)S(1)}, bf16[96,768]{1,0:T(8,128)(2,1)S(1)}, u32[]{:S(2)}, u32[]{:S(2)}) collective-permute-start(bf16[96,768]{1,0:T(8,128)(2,1)S(1)} %pad_maximum_fusion.refs_0_), channel_id=1, source_target_pairs={{4,0},{5,1},{8,4},{9,5},{12,8},{13,9},{14,12},{15,13},{10,14},{11,... | collective-permute-start | bytes 442376 | tf_op jit(solution)/shard_map/ppermute | solution.py:183
  9.5 5.9 %collective-permute-start.5 = (bf16[96,768]{1,0:T(8,128)(2,1)S(1)}, bf16[96,768]{1,0:T(8,128)(2,1)S(1)}, u32[]{:S(2)}, u32[]{:S(2)}) collective-permute-start(bf16[96,768]{1,0:T(8,128)(2,1)S(1)} %collective-permute-done.3.refs_1_), channel_id=1, source_target_pairs={{4,0},{5,1},{8,4},{9,5},{12,8},{13,9},{14,12},{15,13},{10,14},{11,... | collective-permute-start | bytes 442376 | tf_op jit(solution)/shard_map/ppermute | solution.py:183
  11.2 11.8 %collective-permute-start = (bf16[128,1536]{1,0:T(8,128)(2,1)}, bf16[128,1536]{1,0:T(8,128)(2,1)S(1)}, u32[]{:S(2)}, u32[]{:S(2)}) collective-permute-start(bf16[128,1536]{1,0:T(8,128)(2,1)} %att.1), channel_id=1, source_target_pairs={{0,1},{1,0},{2,3},{3,2},{4,5},{5,4},{6,7},{7,6},{8,9},{9,8},{10,11... | collective-permute-start | bytes 1179656 | tf_op jit(solution)/shard_map/ppermute | solution.py:177
  11.2 6.6 %collective-permute-start.7 = (bf16[96,768]{1,0:T(8,128)(2,1)S(1)}, bf16[96,768]{1,0:T(8,128)(2,1)S(1)}, u32[]{:S(2)}, u32[]{:S(2)}) collective-permute-start(bf16[96,768]{1,0:T(8,128)(2,1)S(1)} %collective-permute-done.3.refs_1_), channel_id=1, source_target_pairs={{0,4},{1,5},{4,8},{5,9},{8,12},{9,13},{12,14},{13,15},{14,10},{15,... | collective-permute-start | bytes 442376 | tf_op jit(solution)/shard_map/ppermute | solution.py:180
  11.5 9.1 %collective-permute-start.8 = (bf16[96,768]{1,0:T(8,128)(2,1)S(1)}, bf16[96,768]{1,0:T(8,128)(2,1)S(1)}, u32[]{:S(2)}, u32[]{:S(2)}) collective-permute-start(bf16[96,768]{1,0:T(8,128)(2,1)S(1)} %collective-permute-done.4.refs_2_), channel_id=1, source_target_pairs={{0,4},{1,5},{4,8},{5,9},{8,12},{9,13},{12,14},{13,15},{14,10},{15,... | collective-permute-start | bytes 442376 | tf_op jit(solution)/shard_map/ppermute | solution.py:180
  13.3 7.6 %collective-permute-start.10 = (bf16[96,768]{1,0:T(8,128)(2,1)S(1)}, bf16[96,768]{1,0:T(8,128)(2,1)S(1)}, u32[]{:S(2)}, u32[]{:S(2)}) collective-permute-start(bf16[96,768]{1,0:T(8,128)(2,1)S(1)} %collective-permute-done.6.refs_4_), channel_id=1, source_target_pairs={{4,0},{5,1},{8,4},{9,5},{12,8},{13,9},{14,12},{15,13},{10,14},{11,... | collective-permute-start | bytes 442376 | tf_op jit(solution)/shard_map/ppermute | solution.py:183
  15.4 7.3 %collective-permute-start.9 = (bf16[96,768]{1,0:T(8,128)(2,1)S(1)}, bf16[96,768]{1,0:T(8,128)(2,1)S(1)}, u32[]{:S(2)}, u32[]{:S(2)}) collective-permute-start(bf16[96,768]{1,0:T(8,128)(2,1)S(1)} %collective-permute-done.5.refs_3_), channel_id=1, source_target_pairs={{4,0},{5,1},{8,4},{9,5},{12,8},{13,9},{14,12},{15,13},{10,14},{11,... | collective-permute-start | bytes 442376 | tf_op jit(solution)/shard_map/ppermute | solution.py:183
  17.8 14.8 %collective-permute-start.1 = (bf16[128,1536]{1,0:T(8,128)(2,1)}, bf16[128,1536]{1,0:T(8,128)(2,1)S(1)}, u32[]{:S(2)}, u32[]{:S(2)}) collective-permute-start(bf16[128,1536]{1,0:T(8,128)(2,1)} %res.1), channel_id=1, source_target_pairs={{0,1},{1,0},{2,3},{3,2},{4,5},{5,4},{6,7},{7,6},{8,9},{9,8},{10,11... | collective-permute-start | bytes 1179656 | tf_op jit(solution)/shard_map/ppermute | solution.py:177
  20.6 6.8 %collective-permute-start.11 = (bf16[96,768]{1,0:T(8,128)(2,1)S(1)}, bf16[96,768]{1,0:T(8,128)(2,1)S(1)}, u32[]{:S(2)}, u32[]{:S(2)}) collective-permute-start(bf16[96,768]{1,0:T(8,128)(2,1)S(1)} %collective-permute-done.7.refs_5_), channel_id=1, source_target_pairs={{0,4},{1,5},{4,8},{5,9},{8,12},{9,13},{12,14},{13,15},{14,10},{15,... | collective-permute-start | bytes 442376 | tf_op jit(solution)/shard_map/ppermute | solution.py:180
  20.9 9.6 %collective-permute-start.12 = (bf16[96,768]{1,0:T(8,128)(2,1)S(1)}, bf16[96,768]{1,0:T(8,128)(2,1)S(1)}, u32[]{:S(2)}, u32[]{:S(2)}) collective-permute-start(bf16[96,768]{1,0:T(8,128)(2,1)S(1)} %collective-permute-done.8.refs_6_), channel_id=1, source_target_pairs={{0,4},{1,5},{4,8},{5,9},{8,12},{9,13},{12,14},{13,15},{14,10},{15,... | collective-permute-start | bytes 442376 | tf_op jit(solution)/shard_map/ppermute | solution.py:180
  22.7 8.1 %collective-permute-start.13 = (bf16[96,768]{1,0:T(8,128)(2,1)S(1)}, bf16[96,768]{1,0:T(8,128)(2,1)S(1)}, u32[]{:S(2)}, u32[]{:S(2)}) collective-permute-start(bf16[96,768]{1,0:T(8,128)(2,1)S(1)} %collective-permute-done.9.refs_7_), channel_id=1, source_target_pairs={{4,0},{5,1},{8,4},{9,5},{12,8},{13,9},{14,12},{15,13},{10,14},{11,... | collective-permute-start | bytes 442376 | tf_op jit(solution)/shard_map/ppermute | solution.py:183
  23.0 9.7 %collective-permute-start.14 = (bf16[96,768]{1,0:T(8,128)(2,1)S(1)}, bf16[96,768]{1,0:T(8,128)(2,1)S(1)}, u32[]{:S(2)}, u32[]{:S(2)}) collective-permute-start(bf16[96,768]{1,0:T(8,128)(2,1)S(1)} %collective-permute-done.10.refs_8_), channel_id=1, source_target_pairs={{4,0},{5,1},{8,4},{9,5},{12,8},{13,9},{14,12},{15,13},{10,14},{11,... | collective-permute-start | bytes 442376 | tf_op jit(solution)/shard_map/ppermute | solution.py:183
  27.4 6.6 %collective-permute-start.15 = (bf16[96,768]{1,0:T(8,128)(2,1)S(1)}, bf16[96,768]{1,0:T(8,128)(2,1)S(1)}, u32[]{:S(2)}, u32[]{:S(2)}) collective-permute-start(bf16[96,768]{1,0:T(8,128)(2,1)S(1)} %collective-permute-done.11.refs_9_), channel_id=1, source_target_pairs={{0,4},{1,5},{4,8},{5,9},{8,12},{9,13},{12,14},{13,15},{14,10},{15,... | collective-permute-start | bytes 442376 | tf_op jit(solution)/shard_map/ppermute | solution.py:180
  30.5 5.1 %collective-permute-start.16 = (bf16[96,768]{1,0:T(8,128)(2,1)S(1)}, bf16[96,768]{1,0:T(8,128)(2,1)S(1)}, u32[]{:S(2)}, u32[]{:S(2)}) collective-permute-start(bf16[96,768]{1,0:T(8,128)(2,1)S(1)} %collective-permute-done.12.refs_10_), channel_id=1, source_target_pairs={{0,4},{1,5},{4,8},{5,9},{8,12},{9,13},{12,14},{13,15},{14,10},{15,... | collective-permute-start | bytes 442376 | tf_op jit(solution)/shard_map/ppermute | solution.py:180
  30.8 5.1 %collective-permute-start.17 = (bf16[96,768]{1,0:T(8,128)(2,1)S(1)}, bf16[96,768]{1,0:T(8,128)(2,1)S(1)}, u32[]{:S(2)}, u32[]{:S(2)}) collective-permute-start(bf16[96,768]{1,0:T(8,128)(2,1)S(1)} %collective-permute-done.13.refs_11_), channel_id=1, source_target_pairs={{4,0},{5,1},{8,4},{9,5},{12,8},{13,9},{14,12},{15,13},{10,14},{11,... | collective-permute-start | bytes 442376 | tf_op jit(solution)/shard_map/ppermute | solution.py:183
  36.0 1.0 copy-start.3
  39.4 13.5 %copy-start.1 = (bf16[1,768,512]{2,1,0:T(8,128)(2,1)S(1)}, bf16[1,768,512]{2,1,0:T(8,128)(2,1)}, u32[]{:S(2)}) copy-start(bf16[1,768,512]{2,1,0:T(8,128)(2,1)} %param.12) | copy-start | bytes 2359300
  39.4 15.3 %copy-start.2 = (bf16[1,768,512]{2,1,0:T(8,128)(2,1)S(1)}, bf16[1,768,512]{2,1,0:T(8,128)(2,1)}, u32[]{:S(2)}) copy-start(bf16[1,768,512]{2,1,0:T(8,128)(2,1)} %param.13) | copy-start | bytes 2359300
  39.4 46.5 %copy-start = (bf16[1,512,1536]{2,1,0:T(8,128)(2,1)S(1)}, bf16[1,512,1536]{2,1,0:T(8,128)(2,1)}, u32[]{:S(2)}) copy-start(bf16[1,512,1536]{2,1,0:T(8,128)(2,1)} %param.14) | copy-start | bytes 4718596
  41.0 9.9 %collective-permute-start.31 = (bf16[272,768]{1,0:T(8,128)(2,1)S(1)}, bf16[272,768]{1,0:T(8,128)(2,1)S(1)}, u32[]{:S(2)}, u32[]{:S(2)}) collective-permute-start(bf16[272,768]{1,0:T(8,128)(2,1)S(1)} %stream.1.refs_0_.own), channel_id=1, source_target_pairs={{0,4},{1,5},{4,8},{5,9},{8,12},{9,13},{12,14},{13,15},{14,10},{15,... | collective-permute-start | bytes 1253384 | tf_op jit(solution)/shard_map/ppermute | solution.py:180
  42.9 8.9 %collective-permute-start.22 = (bf16[272,768]{1,0:T(8,128)(2,1)S(1)}, bf16[272,768]{1,0:T(8,128)(2,1)S(1)}, u32[]{:S(2)}, u32[]{:S(2)}) collective-permute-start(bf16[272,768]{1,0:T(8,128)(2,1)S(1)} %stream.1.refs_0_.own), channel_id=1, source_target_pairs={{4,0},{5,1},{8,4},{9,5},{12,8},{13,9},{14,12},{15,13},{10,14},{11,... | collective-permute-start | bytes 1253384 | tf_op jit(solution)/shard_map/ppermute | solution.py:183
  50.9 9.8 %collective-permute-start.32 = (bf16[272,768]{1,0:T(8,128)(2,1)S(1)}, bf16[272,768]{1,0:T(8,128)(2,1)S(1)}, u32[]{:S(2)}, u32[]{:S(2)}) collective-permute-start(bf16[272,768]{1,0:T(8,128)(2,1)S(1)} %collective-permute-done.31.refs_0_), channel_id=1, source_target_pairs={{0,4},{1,5},{4,8},{5,9},{8,12},{9,13},{12,14},{13,15},{14,10},{15,... | collective-permute-start | bytes 1253384 | tf_op jit(solution)/shard_map/ppermute | solution.py:180
  51.8 10.7 %collective-permute-start.25 = (bf16[272,768]{1,0:T(8,128)(2,1)S(1)}, bf16[272,768]{1,0:T(8,128)(2,1)S(1)}, u32[]{:S(2)}, u32[]{:S(2)}) collective-permute-start(bf16[272,768]{1,0:T(8,128)(2,1)S(1)} %collective-permute-done.22.refs_0_), channel_id=1, source_target_pairs={{4,0},{5,1},{8,4},{9,5},{12,8},{13,9},{14,12},{15,13},{10,14},{11,... | collective-permute-start | bytes 1253384 | tf_op jit(solution)/shard_map/ppermute | solution.py:183
  52.9 20.5 %collective-permute-start.19 = (bf16[768,512]{1,0:T(8,128)(2,1)S(1)}, bf16[768,512]{1,0:T(8,128)(2,1)S(1)}, u32[]{:S(2)}, u32[]{:S(2)}) collective-permute-start(bf16[768,512]{1,0:T(8,128)(2,1)S(1)} %bitcast.16), channel_id=1, source_target_pairs={{0,16},{16,0},{1,17},{17,1},{2,18},{18,2},{3,19},{19,3},{4,20},{20... | collective-permute-start | bytes 2359304 | tf_op jit(solution)/shard_map/ppermute | solution.py:208
  54.7 30.7 %collective-permute-start.20 = (bf16[768,512]{1,0:T(8,128)(2,1)S(1)}, bf16[768,512]{1,0:T(8,128)(2,1)S(1)}, u32[]{:S(2)}, u32[]{:S(2)}) collective-permute-start(bf16[768,512]{1,0:T(8,128)(2,1)S(1)} %bitcast.25), channel_id=1, source_target_pairs={{0,16},{16,0},{1,17},{17,1},{2,18},{18,2},{3,19},{19,3},{4,20},{20... | collective-permute-start | bytes 2359304 | tf_op jit(solution)/shard_map/ppermute | solution.py:208
  60.7 9.9 %collective-permute-start.33 = (bf16[272,768]{1,0:T(8,128)(2,1)S(1)}, bf16[272,768]{1,0:T(8,128)(2,1)S(1)}, u32[]{:S(2)}, u32[]{:S(2)}) collective-permute-start(bf16[272,768]{1,0:T(8,128)(2,1)S(1)} %collective-permute-done.32.refs_0_), channel_id=1, source_target_pairs={{0,4},{1,5},{4,8},{5,9},{8,12},{9,13},{12,14},{13,15},{14,10},{15,... | collective-permute-start | bytes 1253384 | tf_op jit(solution)/shard_map/ppermute | solution.py:180
  62.5 10.9 %collective-permute-start.28 = (bf16[272,768]{1,0:T(8,128)(2,1)S(1)}, bf16[272,768]{1,0:T(8,128)(2,1)S(1)}, u32[]{:S(2)}, u32[]{:S(2)}) collective-permute-start(bf16[272,768]{1,0:T(8,128)(2,1)S(1)} %collective-permute-done.25.refs_0_), channel_id=1, source_target_pairs={{4,0},{5,1},{8,4},{9,5},{12,8},{13,9},{14,12},{15,13},{10,14},{11,... | collective-permute-start | bytes 1253384 | tf_op jit(solution)/shard_map/ppermute | solution.py:183
  62.7 22.7 %collective-permute-start.18 = (bf16[272,768]{1,0:T(8,128)(2,1)S(1)}, bf16[272,768]{1,0:T(8,128)(2,1)S(1)}, u32[]{:S(2)}, u32[]{:S(2)}) collective-permute-start(bf16[272,768]{1,0:T(8,128)(2,1)S(1)} %stream.1.refs_0_.own), channel_id=1, source_target_pairs={{0,1},{1,0},{2,3},{3,2},{4,5},{5,4},{6,7},{7,6},{8,9},{9,8},{10,11... | collective-permute-start | bytes 1253384 | tf_op jit(solution)/shard_map/ppermute | solution.py:177
  70.6 6.0 %collective-permute-start.34 = (bf16[144,768]{1,0:T(8,128)(2,1)S(1)}, bf16[144,768]{1,0:T(8,128)(2,1)S(1)}, u32[]{:S(2)}, u32[]{:S(2)}) collective-permute-start(bf16[144,768]{1,0:T(8,128)(2,1)S(1)} %slice.123), channel_id=1, source_target_pairs={{0,4},{1,5},{4,8},{5,9},{8,12},{9,13},{12,14},{13,15},{14,10},{15,... | collective-permute-start | bytes 663560 | tf_op jit(solution)/shard_map/ppermute | solution.py:180
  73.4 6.1 %collective-permute-start.35 = (bf16[144,768]{1,0:T(8,128)(2,1)S(1)}, bf16[144,768]{1,0:T(8,128)(2,1)S(1)}, u32[]{:S(2)}, u32[]{:S(2)}) collective-permute-start(bf16[144,768]{1,0:T(8,128)(2,1)S(1)} %slice.124), channel_id=1, source_target_pairs={{4,0},{5,1},{8,4},{9,5},{12,8},{13,9},{14,12},{15,13},{10,14},{11,... | collective-permute-start | bytes 663560 | tf_op jit(solution)/shard_map/ppermute | solution.py:183
  73.4 17.5 %collective-permute-start.43 = (bf16[272,768]{1,0:T(8,128)(2,1)S(1)}, bf16[272,768]{1,0:T(8,128)(2,1)S(1)}, u32[]{:S(2)}, u32[]{:S(2)}) collective-permute-start(bf16[272,768]{1,0:T(8,128)(2,1)S(1)} %collective-permute-done.31.refs_0_), channel_id=1, source_target_pairs={{0,1},{1,0},{2,3},{3,2},{4,5},{5,4},{6,7},{7,6},{8,9},{9,8},{10,11... | collective-permute-start | bytes 1253384 | tf_op jit(solution)/shard_map/ppermute | solution.py:177
  76.6 11.5 %collective-permute-start.36 = (bf16[144,768]{1,0:T(8,128)(2,1)S(1)}, bf16[144,768]{1,0:T(8,128)(2,1)S(1)}, u32[]{:S(2)}, u32[]{:S(2)}) collective-permute-start(bf16[144,768]{1,0:T(8,128)(2,1)S(1)} %collective-permute-done.34.refs_0_), channel_id=1, source_target_pairs={{0,1},{1,0},{2,3},{3,2},{4,5},{5,4},{6,7},{7,6},{8,9},{9,8},{10,11... | collective-permute-start | bytes 663560 | tf_op jit(solution)/shard_map/ppermute | solution.py:177
  79.4 8.8 %collective-permute-start.37 = (bf16[144,768]{1,0:T(8,128)(2,1)S(1)}, bf16[144,768]{1,0:T(8,128)(2,1)S(1)}, u32[]{:S(2)}, u32[]{:S(2)}) collective-permute-start(bf16[144,768]{1,0:T(8,128)(2,1)S(1)} %collective-permute-done.35.refs_1_), channel_id=1, source_target_pairs={{0,1},{1,0},{2,3},{3,2},{4,5},{5,4},{6,7},{7,6},{8,9},{9,8},{10,11... | collective-permute-start | bytes 663560 | tf_op jit(solution)/shard_map/ppermute | solution.py:177
  85.4 8.0 %collective-permute-start.23 = (bf16[272,768]{1,0:T(8,128)(2,1)S(1)}, bf16[272,768]{1,0:T(8,128)(2,1)S(1)}, u32[]{:S(2)}, u32[]{:S(2)}) collective-permute-start(bf16[272,768]{1,0:T(8,128)(2,1)S(1)} %collective-permute-done.22.refs_0_), channel_id=1, source_target_pairs={{0,1},{1,0},{2,3},{3,2},{4,5},{5,4},{6,7},{7,6},{8,9},{9,8},{10,11... | collective-permute-start | bytes 1253384 | tf_op jit(solution)/shard_map/ppermute | solution.py:177
  85.4 10.7 %collective-permute-start.45 = (bf16[272,768]{1,0:T(8,128)(2,1)S(1)}, bf16[272,768]{1,0:T(8,128)(2,1)S(1)}, u32[]{:S(2)}, u32[]{:S(2)}) collective-permute-start(bf16[272,768]{1,0:T(8,128)(2,1)S(1)} %collective-permute-done.32.refs_0_), channel_id=1, source_target_pairs={{0,1},{1,0},{2,3},{3,2},{4,5},{5,4},{6,7},{7,6},{8,9},{9,8},{10,11... | collective-permute-start | bytes 1253384 | tf_op jit(solution)/shard_map/ppermute | solution.py:177
  88.1 53.9 %collective-permute-start.21 = (bf16[128,1536]{1,0:T(8,128)(2,1)S(1)}, bf16[128,1536]{1,0:T(8,128)(2,1)S(1)}, u32[]{:S(2)}, u32[]{:S(2)}) collective-permute-start(bf16[128,1536]{1,0:T(8,128)(2,1)S(1)} %get-tuple-element.22), channel_id=1, source_target_pairs={{0,1},{1,0},{2,3},{3,2},{4,5},{5,4},{6,7},{7,6},{8,9},{9,8},{10,11... | collective-permute-start | bytes 1179656 | tf_op jit(solution)/shard_map/ppermute | solution.py:177
  88.2 10.5 %collective-permute-start.47 = (bf16[272,768]{1,0:T(8,128)(2,1)S(1)}, bf16[272,768]{1,0:T(8,128)(2,1)S(1)}, u32[]{:S(2)}, u32[]{:S(2)}) collective-permute-start(bf16[272,768]{1,0:T(8,128)(2,1)S(1)} %collective-permute-done.33.refs_0_), channel_id=1, source_target_pairs={{0,1},{1,0},{2,3},{3,2},{4,5},{5,4},{6,7},{7,6},{8,9},{9,8},{10,11... | collective-permute-start | bytes 1253384 | tf_op jit(solution)/shard_map/ppermute | solution.py:177
  91.0 10.5 %collective-permute-start.38 = (bf16[128,1536]{1,0:T(8,128)(2,1)S(1)}, bf16[128,1536]{1,0:T(8,128)(2,1)S(1)}, u32[]{:S(2)}, u32[]{:S(2)}) collective-permute-start(bf16[128,1536]{1,0:T(8,128)(2,1)S(1)} %get-tuple-element.30), channel_id=1, source_target_pairs={{0,1},{1,0},{2,3},{3,2},{4,5},{5,4},{6,7},{7,6},{8,9},{9,8},{10,11... | collective-permute-start | bytes 1179656 | tf_op jit(solution)/shard_map/ppermute | solution.py:177
  93.4 36.9 %collective-permute-start.44 = (bf16[128,1536]{1,0:T(8,128)(2,1)S(1)}, bf16[128,1536]{1,0:T(8,128)(2,1)S(1)}, u32[]{:S(2)}, u32[]{:S(2)}) collective-permute-start(bf16[128,1536]{1,0:T(8,128)(2,1)S(1)} %get-tuple-element.32), channel_id=1, source_target_pairs={{0,1},{1,0},{2,3},{3,2},{4,5},{5,4},{6,7},{7,6},{8,9},{9,8},{10,11... | collective-permute-start | bytes 1179656 | tf_op jit(solution)/shard_map/ppermute | solution.py:177
  96.1 5.6 %collective-permute-start.26 = (bf16[272,768]{1,0:T(8,128)(2,1)S(1)}, bf16[272,768]{1,0:T(8,128)(2,1)S(1)}, u32[]{:S(2)}, u32[]{:S(2)}) collective-permute-start(bf16[272,768]{1,0:T(8,128)(2,1)S(1)} %collective-permute-done.25.refs_0_), channel_id=1, source_target_pairs={{0,1},{1,0},{2,3},{3,2},{4,5},{5,4},{6,7},{7,6},{8,9},{9,8},{10,11... | collective-permute-start | bytes 1253384 | tf_op jit(solution)/shard_map/ppermute | solution.py:177
  98.7 6.7 %collective-permute-start.29 = (bf16[272,768]{1,0:T(8,128)(2,1)S(1)}, bf16[272,768]{1,0:T(8,128)(2,1)S(1)}, u32[]{:S(2)}, u32[]{:S(2)}) collective-permute-start(bf16[272,768]{1,0:T(8,128)(2,1)S(1)} %collective-permute-done.28.refs_0_), channel_id=1, source_target_pairs={{0,1},{1,0},{2,3},{3,2},{4,5},{5,4},{6,7},{7,6},{8,9},{9,8},{10,11... | collective-permute-start | bytes 1253384 | tf_op jit(solution)/shard_map/ppermute | solution.py:177
  101.4 6.5 %collective-permute-start.48 = (bf16[128,1536]{1,0:T(8,128)(2,1)S(1)}, bf16[128,1536]{1,0:T(8,128)(2,1)S(1)}, u32[]{:S(2)}, u32[]{:S(2)}) collective-permute-start(bf16[128,1536]{1,0:T(8,128)(2,1)S(1)} %get-tuple-element.36), channel_id=1, source_target_pairs={{0,1},{1,0},{2,3},{3,2},{4,5},{5,4},{6,7},{7,6},{8,9},{9,8},{10,11... | collective-permute-start | bytes 1179656 | tf_op jit(solution)/shard_map/ppermute | solution.py:177
  101.7 7.3 %collective-permute-start.55 = (bf16[64,1536]{1,0:T(8,128)(2,1)S(1)}, bf16[64,1536]{1,0:T(8,128)(2,1)S(1)}, u32[]{:S(2)}, u32[]{:S(2)}) collective-permute-start(bf16[64,1536]{1,0:T(8,128)(2,1)S(1)} %get-tuple-element.43), channel_id=1, source_target_pairs={{4,0},{5,1},{8,4},{9,5},{12,8},{13,9},{14,12},{15,13},{10,14},{11,... | collective-permute-start | bytes 589832 | tf_op jit(solution)/shard_map/ppermute | solution.py:183
  105.4 11.5 %collective-permute-start.46 = (bf16[128,1536]{1,0:T(8,128)(2,1)S(1)}, bf16[128,1536]{1,0:T(8,128)(2,1)S(1)}, u32[]{:S(2)}, u32[]{:S(2)}) collective-permute-start(bf16[128,1536]{1,0:T(8,128)(2,1)S(1)} %get-tuple-element.34), channel_id=1, source_target_pairs={{0,1},{1,0},{2,3},{3,2},{4,5},{5,4},{6,7},{7,6},{8,9},{9,8},{10,11... | collective-permute-start | bytes 1179656 | tf_op jit(solution)/shard_map/ppermute | solution.py:177
  107.9 1.8 %collective-permute-start.30 = (bf16[128,1536]{1,0:T(8,128)(2,1)S(1)}, bf16[128,1536]{1,0:T(8,128)(2,1)S(1)}, u32[]{:S(2)}, u32[]{:S(2)}) collective-permute-start(bf16[128,1536]{1,0:T(8,128)(2,1)S(1)} %get-tuple-element.28), channel_id=1, source_target_pairs={{0,1},{1,0},{2,3},{3,2},{4,5},{5,4},{6,7},{7,6},{8,9},{9,8},{10,11... | collective-permute-start | bytes 1179656 | tf_op jit(solution)/shard_map/ppermute | solution.py:177
  109.0 6.4 %collective-permute-start.39 = (bf16[64,1536]{1,0:T(8,128)(2,1)S(1)}, bf16[64,1536]{1,0:T(8,128)(2,1)S(1)}, u32[]{:S(2)}, u32[]{:S(2)}) collective-permute-start(bf16[64,1536]{1,0:T(8,128)(2,1)S(1)} %get-tuple-element.44), channel_id=1, source_target_pairs={{0,4},{1,5},{4,8},{5,9},{8,12},{9,13},{12,14},{13,15},{14,10},{15,... | collective-permute-start | bytes 589832 | tf_op jit(solution)/shard_map/ppermute | solution.py:180
  109.7 7.4 %collective-permute-start.49 = (bf16[64,1536]{1,0:T(8,128)(2,1)S(1)}, bf16[64,1536]{1,0:T(8,128)(2,1)S(1)}, u32[]{:S(2)}, u32[]{:S(2)}) collective-permute-start(bf16[64,1536]{1,0:T(8,128)(2,1)S(1)} %get-tuple-element.42), channel_id=1, source_target_pairs={{4,0},{5,1},{8,4},{9,5},{12,8},{13,9},{14,12},{15,13},{10,14},{11,... | collective-permute-start | bytes 589832 | tf_op jit(solution)/shard_map/ppermute | solution.py:183
  115.4 5.7 %collective-permute-start.56 = (bf16[64,1536]{1,0:T(8,128)(2,1)S(1)}, bf16[64,1536]{1,0:T(8,128)(2,1)S(1)}, u32[]{:S(2)}, u32[]{:S(2)}) collective-permute-start(bf16[64,1536]{1,0:T(8,128)(2,1)S(1)} %get-tuple-element.41), channel_id=1, source_target_pairs={{4,0},{5,1},{8,4},{9,5},{12,8},{13,9},{14,12},{15,13},{10,14},{11,... | collective-permute-start | bytes 589832 | tf_op jit(solution)/shard_map/ppermute | solution.py:183
  117.0 4.8 %collective-permute-start.27 = (bf16[128,1536]{1,0:T(8,128)(2,1)S(1)}, bf16[128,1536]{1,0:T(8,128)(2,1)S(1)}, u32[]{:S(2)}, u32[]{:S(2)}) collective-permute-start(bf16[128,1536]{1,0:T(8,128)(2,1)S(1)} %get-tuple-element.26), channel_id=1, source_target_pairs={{0,1},{1,0},{2,3},{3,2},{4,5},{5,4},{6,7},{7,6},{8,9},{9,8},{10,11... | collective-permute-start | bytes 1179656 | tf_op jit(solution)/shard_map/ppermute | solution.py:177
  117.1 7.8 %collective-permute-start.40 = (bf16[64,1536]{1,0:T(8,128)(2,1)S(1)}, bf16[64,1536]{1,0:T(8,128)(2,1)S(1)}, u32[]{:S(2)}, u32[]{:S(2)}) collective-permute-start(bf16[64,1536]{1,0:T(8,128)(2,1)S(1)} %get-tuple-element.50), channel_id=1, source_target_pairs={{0,4},{1,5},{4,8},{5,9},{8,12},{9,13},{12,14},{13,15},{14,10},{15,... | collective-permute-start | bytes 589832 | tf_op jit(solution)/shard_map/ppermute | solution.py:180
  121.1 7.5 %collective-permute-start.52 = (bf16[64,1536]{1,0:T(8,128)(2,1)S(1)}, bf16[64,1536]{1,0:T(8,128)(2,1)S(1)}, u32[]{:S(2)}, u32[]{:S(2)}) collective-permute-start(bf16[64,1536]{1,0:T(8,128)(2,1)S(1)} %get-tuple-element.49), channel_id=1, source_target_pairs={{0,4},{1,5},{4,8},{5,9},{8,12},{9,13},{12,14},{13,15},{14,10},{15,... | collective-permute-start | bytes 589832 | tf_op jit(solution)/shard_map/ppermute | solution.py:180
  121.8 15.0 %collective-permute-start.24 = (bf16[128,1536]{1,0:T(8,128)(2,1)S(1)}, bf16[128,1536]{1,0:T(8,128)(2,1)S(1)}, u32[]{:S(2)}, u32[]{:S(2)}) collective-permute-start(bf16[128,1536]{1,0:T(8,128)(2,1)S(1)} %get-tuple-element.24), channel_id=1, source_target_pairs={{0,1},{1,0},{2,3},{3,2},{4,5},{5,4},{6,7},{7,6},{8,9},{9,8},{10,11... | collective-permute-start | bytes 1179656 | tf_op jit(solution)/shard_map/ppermute | solution.py:177
  124.8 6.0 %collective-permute-start.50 = (bf16[64,1536]{1,0:T(8,128)(2,1)S(1)}, bf16[64,1536]{1,0:T(8,128)(2,1)S(1)}, u32[]{:S(2)}, u32[]{:S(2)}) collective-permute-start(bf16[64,1536]{1,0:T(8,128)(2,1)S(1)} %get-tuple-element.40), channel_id=1, source_target_pairs={{4,0},{5,1},{8,4},{9,5},{12,8},{13,9},{14,12},{15,13},{10,14},{11,... | collective-permute-start | bytes 589832 | tf_op jit(solution)/shard_map/ppermute | solution.py:183
  128.6 6.5 %collective-permute-start.57 = (bf16[64,1536]{1,0:T(8,128)(2,1)S(1)}, bf16[64,1536]{1,0:T(8,128)(2,1)S(1)}, u32[]{:S(2)}, u32[]{:S(2)}) collective-permute-start(bf16[64,1536]{1,0:T(8,128)(2,1)S(1)} %get-tuple-element.39), channel_id=1, source_target_pairs={{4,0},{5,1},{8,4},{9,5},{12,8},{13,9},{14,12},{15,13},{10,14},{11,... | collective-permute-start | bytes 589832 | tf_op jit(solution)/shard_map/ppermute | solution.py:183
  130.3 8.1 %collective-permute-start.41 = (bf16[64,1536]{1,0:T(8,128)(2,1)S(1)}, bf16[64,1536]{1,0:T(8,128)(2,1)S(1)}, u32[]{:S(2)}, u32[]{:S(2)}) collective-permute-start(bf16[64,1536]{1,0:T(8,128)(2,1)S(1)} %get-tuple-element.48), channel_id=1, source_target_pairs={{0,4},{1,5},{4,8},{5,9},{8,12},{9,13},{12,14},{13,15},{14,10},{15,... | collective-permute-start | bytes 589832 | tf_op jit(solution)/shard_map/ppermute | solution.py:180
  130.8 9.9 %collective-permute-start.53 = (bf16[64,1536]{1,0:T(8,128)(2,1)S(1)}, bf16[64,1536]{1,0:T(8,128)(2,1)S(1)}, u32[]{:S(2)}, u32[]{:S(2)}) collective-permute-start(bf16[64,1536]{1,0:T(8,128)(2,1)S(1)} %get-tuple-element.47), channel_id=1, source_target_pairs={{0,4},{1,5},{4,8},{5,9},{8,12},{9,13},{12,14},{13,15},{14,10},{15,... | collective-permute-start | bytes 589832 | tf_op jit(solution)/shard_map/ppermute | solution.py:180
  135.0 7.0 %copy-start.7 = (f32[1536]{0:T(1024)S(1)}, f32[1536]{0:T(1024)}, u32[]{:S(2)}) copy-start(f32[1536]{0:T(1024)} %param.17) | copy-start | bytes 18436
  135.2 7.7 %collective-permute-start.51 = (bf16[64,1536]{1,0:T(8,128)(2,1)S(1)}, bf16[64,1536]{1,0:T(8,128)(2,1)S(1)}, u32[]{:S(2)}, u32[]{:S(2)}) collective-permute-start(bf16[64,1536]{1,0:T(8,128)(2,1)S(1)} %get-tuple-element.38), channel_id=1, source_target_pairs={{4,0},{5,1},{8,4},{9,5},{12,8},{13,9},{14,12},{15,13},{10,14},{11,... | collective-permute-start | bytes 589832 | tf_op jit(solution)/shard_map/ppermute | solution.py:183
  136.8 8.2 %collective-permute-start.58 = (bf16[64,1536]{1,0:T(8,128)(2,1)S(1)}, bf16[64,1536]{1,0:T(8,128)(2,1)S(1)}, u32[]{:S(2)}, u32[]{:S(2)}) collective-permute-start(bf16[64,1536]{1,0:T(8,128)(2,1)S(1)} %get-tuple-element.37), channel_id=1, source_target_pairs={{4,0},{5,1},{8,4},{9,5},{12,8},{13,9},{14,12},{15,13},{10,14},{11,... | collective-permute-start | bytes 589832 | tf_op jit(solution)/shard_map/ppermute | solution.py:183
  140.9 7.4 %collective-permute-start.42 = (bf16[64,1536]{1,0:T(8,128)(2,1)S(1)}, bf16[64,1536]{1,0:T(8,128)(2,1)S(1)}, u32[]{:S(2)}, u32[]{:S(2)}) collective-permute-start(bf16[64,1536]{1,0:T(8,128)(2,1)S(1)} %get-tuple-element.46), channel_id=1, source_target_pairs={{0,4},{1,5},{4,8},{5,9},{8,12},{9,13},{12,14},{13,15},{14,10},{15,... | collective-permute-start | bytes 589832 | tf_op jit(solution)/shard_map/ppermute | solution.py:180
  141.4 9.0 %collective-permute-start.54 = (bf16[64,1536]{1,0:T(8,128)(2,1)S(1)}, bf16[64,1536]{1,0:T(8,128)(2,1)S(1)}, u32[]{:S(2)}, u32[]{:S(2)}) collective-permute-start(bf16[64,1536]{1,0:T(8,128)(2,1)S(1)} %get-tuple-element.45), channel_id=1, source_target_pairs={{0,4},{1,5},{4,8},{5,9},{8,12},{9,13},{12,14},{13,15},{14,10},{15,... | collective-permute-start | bytes 589832 | tf_op jit(solution)/shard_map/ppermute | solution.py:180
  (3 other events, 2.4 us)

commit v3 on v2

--- a/solution.py
+++ b/solution.py
@@ -17,6 +17,10 @@
 
 def ring_order(chips):
     return list(range(0, chips, 2)) + list(range(chips - 1, 0, -2))
+
+
+def together(*arrays):
+    return lax.optimization_barrier(arrays)
 
 
 def call(kernel, out_shape, *args, scratch=(), flops=0, name=None):
@@ -32,21 +36,48 @@
     )(*args)
 
 
-def stream_kernel(layout, place, att, att_near, res, res_near, routes, scores, *refs):
-    *blocks, out, full, tokens = refs
-    core, expert, group = place[0], place[1], place[2]
+def prepare_kernel(place, att, att_near, res, res_near, routes, scores, tokens, base):
+    core = place[0]
     rows, width = att.shape
     half = width // 2
+    extra = base.shape[0] - 2 * rows
+    mine = pl.ds(pl.multiple_of(core * half, 128), half)
+    for c in range(2):
+        at_rows = slice(c * (rows + extra), c * (rows + extra) + rows)
+
+        @pl.when(core == c)
+        def _(c=c, at_rows=at_rows):
+            tokens[c * rows : (c + 1) * rows, :] = att[...]
+            base[at_rows, :] = res[:, mine]
+
+        @pl.when(core != c)
+        def _(c=c, at_rows=at_rows):
+            tokens[c * rows : (c + 1) * rows, :] = att_near[...]
+            base[at_rows, :] = res_near[:, mine]
+
+    combine = scores[...] / jnp.sum(scores[...], axis=0, keepdims=True)
+    named = lax.broadcasted_iota(jnp.int32, (extra, rows), 0)
+    left = jnp.zeros((extra, rows), F32)
+    for k in range(routes.shape[0]):
+        left = left + jnp.where(routes[k : k + 1, :] == named, combine[k : k + 1, :], 0.0)
+    base[rows : rows + extra, :] = jnp.zeros((extra, half), BF16)
+    for piece in range(PIECES):
+        value = left.astype(BF16)
+        base[rows : rows + extra, piece * rows : (piece + 1) * rows] = value
+        left = left - value.astype(F32)
+
+
+def stream_kernel(layout, place, tokens, base, *refs):
+    *blocks, out, full = refs
+    core, expert, group = place[0], place[1], place[2]
+    rows, width = tokens.shape[0] // 2, tokens.shape[1]
+    half = width // 2
     extra = out.shape[0] - 2 * rows
-    mine = pl.ds(pl.multiple_of(core * half, 128), half)
-    own_rows = pl.ds(pl.multiple_of(core * rows, 16), rows)
-    near_rows = pl.ds(pl.multiple_of((1 - core) * rows, 16), rows)
-    tokens[own_rows, :] = att[...]
-    tokens[near_rows, :] = att_near[...]
     if layout is None:
-        full[...] = blocks[0][:, mine]
+        full[...] = blocks[0][:, pl.ds(pl.multiple_of(core * half, 128), half)]
     else:
         chips, where = layout
+        depth = blocks[0].shape[0] // 2
         pair = lax.shift_right_logical(expert, 1)
         down = (pair & 1) == 1
         at = jnp.where(down, chips - lax.shift_right_logical(pair + 1, 1), lax.shift_right_logical(pair, 1))
@@ -54,32 +85,17 @@
             spot = lax.rem(at + (offset + chips), chips)
             source = jnp.where(spot < chips // 2, 2 * spot, 2 * (chips - spot) - 1)
             of_group = group if other == 0 else 1 - group
-            depth = block.shape[0] // 2
-            for index, c in enumerate((core, 1 - core)):
+            sides = (core, 1 - core)
+            if block.shape[0] == depth:
+                sides = sides[:1] if offset < 0 else sides[1:]
+            for index, c in enumerate(sides):
                 start = ((of_group * chips + source) * 2 + c) * depth
                 full[pl.ds(pl.multiple_of(start, 16), depth), :] = block[index * depth : (index + 1) * depth, :]
     projected = dot(tokens[...], full[...])
+    out[rows : rows + extra, :] = base[rows : rows + extra, :]
     for c in range(2):
         at_rows = slice(c * (rows + extra), c * (rows + extra) + rows)
-        part = projected[c * rows : (c + 1) * rows]
-
-        @pl.when(core == c)
-        def _(at_rows=at_rows, part=part):
-            out[at_rows, :] = (res[:, mine].astype(F32) + part).astype(BF16)
-
-        @pl.when(core != c)
-        def _(at_rows=at_rows, part=part):
-            out[at_rows, :] = (res_near[:, mine].astype(F32) + part).astype(BF16)
-
-    combine = scores[...] / jnp.sum(scores[...], axis=0, keepdims=True)
-    named = lax.broadcasted_iota(jnp.int32, (extra, rows), 0)
-    left = jnp.zeros((extra, rows), F32)
-    for k in range(routes.shape[0]):
-        left = left + jnp.where(routes[k : k + 1, :] == named, combine[k : k + 1, :], 0.0)
-    for piece in range(PIECES):
-        value = left.astype(BF16)
-        out[rows : rows + extra, piece * rows : (piece + 1) * rows] = value
-        left = left - value.astype(F32)
+        out[at_rows, :] = (base[at_rows, :].astype(F32) + projected[c * rows : (c + 1) * rows]).astype(BF16)
 
 
 def expert_kernel(parts, place, *refs):
@@ -182,41 +198,14 @@
     def come(x):
         return lax.ppermute(x, "expert", back)
 
-    if groups == 2:
-        flip = [(0, 1), (1, 0)]
-
-        def columns(which):
-            return lax.dynamic_slice(
-                out_weight, (0, which * half), (out_weight.shape[0], half), allow_negative_indices=False
-            )
-
-        mine = jnp.concatenate([columns(core), swap(columns(1 - core))], axis=0)
-        other = lax.ppermute(mine, "dp", flip)
-        blocks, layout = [mine, other], [(0, 0), (0, 1)]
-        mine_f = mine_b = mine
-        other_f = other_b = other
-        for step in range(1, far + 1):
-            mine_f, other_b = go(mine_f), come(other_b)
-            blocks += [mine_f, other_b]
-            layout += [(-step, 0), (step, 1)]
-            if step < far:
-                mine_b, other_f = come(mine_b), go(other_f)
-                blocks += [mine_b, other_f]
-                layout += [(step, 0), (-step, 1)]
-        layout = (chips, layout)
-        gate, up = gate_weight[0], up_weight[0]
-        weights = (gate, lax.ppermute(gate, "dp", flip), up, lax.ppermute(up, "dp", flip), down_weight[0])
-    else:
-        blocks, layout = [lax.all_gather(out_weight, ("dp", "expert"), axis=0, tiled=True)], None
-        gate = lax.all_gather(gate_weight, "dp", axis=1, tiled=True)[0]
-        up = lax.all_gather(up_weight, "dp", axis=1, tiled=True)[0]
-        weights = (gate[:half], gate[half:], up[:half], up[half:], down_weight[0])
-
     extra = -(-peers // 16) * 16
     block_rows = 2 * token_count + extra
-    stream = call(
-        functools.partial(stream_kernel, layout),
-        jax.ShapeDtypeStruct((block_rows, half), BF16),
+    tokens, base = call(
+        prepare_kernel,
+        [
+            jax.ShapeDtypeStruct((2 * token_count, width), BF16),
+            jax.ShapeDtypeStruct((block_rows, half), BF16),
+        ],
         place,
         attention,
         swap(attention),
@@ -224,39 +213,105 @@
         swap(residual),
         routes.T,
         router_scores.T,
+        name="prepare",
+    )
+
+    if groups == 2:
+        flip = [(0, 1), (1, 0)]
+
+        def columns(which):
+            return lax.dynamic_slice(
+                out_weight, (0, which * half), (out_weight.shape[0], half), allow_negative_indices=False
+            )
+
+        mine = jnp.concatenate([columns(core), swap(columns(1 - core))], axis=0)
+        other = lax.ppermute(mine, "dp", flip)
+        depth = out_weight.shape[0]
+        blocks, layout = [mine, other], [(0, 0), (0, 1)]
+        mine_f, mine_b = go(mine), come(mine)
+        mine_f, mine_b, other, tokens, base = together(mine_f, mine_b, other, tokens, base)
+        blocks += [mine_f, mine_b]
+        layout += [(-1, 0), (1, 0)]
+        other_f = other_b = other
+        for step in range(1, far + 1):
+            if step < far:
+                mine_f = go(mine_f)
+                blocks += [mine_f]
+                layout += [(-step - 1, 0)]
+                other_f = go(other_f)
+                blocks += [other_f]
+                layout += [(-step, 1)]
+            if step < far - 1:
+                mine_b = come(mine_b)
+                blocks += [mine_b]
+                layout += [(step + 1, 0)]
+            other_b = come(other_b)
+            blocks += [other_b]
+            layout += [(step, 1)]
+        layout = (chips, layout)
+        gate, up = gate_weight[0], up_weight[0]
+        other, gate_later, up_later = together(other, gate, up)
+        gate_near, up_near = lax.ppermute(gate_later, "dp", flip), lax.ppermute(up_later, "dp", flip)
+        *blocks, gate_near = together(*blocks, gate_near)
+    else:
+        blocks, layout = [lax.all_gather(out_weight, ("dp", "expert"), axis=0, tiled=True)], None
+        gate_full = lax.all_gather(gate_weight, "dp", axis=1, tiled=True)[0]
+        up_full = lax.all_gather(up_weight, "dp", axis=1, tiled=True)[0]
+        gate, gate_near, up, up_near = gate_full[:half], gate_full[half:], up_full[:half], up_full[half:]
+
+    stream = call(
+        functools.partial(stream_kernel, layout),
+        jax.ShapeDtypeStruct((block_rows, half), BF16),
+        place,
+        tokens,
+        base,
         *blocks,
-        scratch=[pltpu.VMEM((width, half), BF16), pltpu.VMEM((2 * token_count, width), BF16)],
+        scratch=[pltpu.VMEM((width, half), BF16)],
         flops=4 * token_count * width * half,
         name="stream",
     )
 
-    def experts(*tokens):
-        hidden = weights[0].shape[1]
+    def experts(*arrays):
+        hidden = down_weight.shape[1]
         return call(
-            functools.partial(expert_kernel, len(tokens) // 2),
+            functools.partial(expert_kernel, len(arrays) // 2),
             [
                 jax.ShapeDtypeStruct((token_count, width), F32),
                 jax.ShapeDtypeStruct((token_count, width), BF16),
             ],
             place,
-            *tokens,
-            *weights,
+            *arrays,
+            gate,
+            gate_near,
+            up,
+            up_near,
+            down_weight[0],
             flops=4 * token_count * 3 * width * hidden,
             name="experts",
         )
 
-    out = {}
+    shared = {}
     stream_near = swap(stream)
-    out[0] = experts(stream, stream_near)
     f = b = stream
-    for step in range(1, far):
-        f, b = go(f), come(b)
-        out[-step] = experts(f, swap(f))
-        out[step] = experts(b, swap(b))
-    f, b = go(f[: token_count + extra]), come(b[token_count:])
-    out[far] = experts(f, b, swap(f), swap(b))
-
-    shared = {offset: (own, swap(near)) for offset, (own, near) in out.items()}
+    waiting = [(0, stream, stream_near)]
+    results = {}
+    for step in range(1, far + 1):
+        if step < far:
+            f, b = go(f), come(b)
+        else:
+            f, b = go(f[: token_count + extra]), come(b[token_count:])
+        shared.update({offset: (own, swap(near)) for offset, (own, near) in results.items()})
+        if step == 1:
+            f, b, up_near = together(f, b, up_near)
+            results = {}
+        else:
+            results = {offset: experts(*arrays) for offset, *arrays in waiting}
+            waiting = []
+            f, b, results, shared = together(f, b, results, shared)
+        if step < far:
+            waiting += [(-step, f, swap(f)), (step, b, swap(b))]
+    shared.update({offset: (own, swap(near)) for offset, (own, near) in results.items()})
+
     cut = token_count // 2
 
     def term(offset, part):
@@ -264,11 +319,37 @@
         rows = slice(part * cut, (part + 1) * cut)
         return own[rows] + near[rows].astype(F32)
 
-    def chain(move, sign, part, distance):
-        total = move(term(distance if distance == far else sign * distance, part).astype(BF16))
-        for left in range(distance - 1, 0, -1):
-            total = move((term(sign * left, part) + total.astype(F32)).astype(BF16))
-        return total
+    ways = ((go, 1, 0), (come, -1, 1))
+
+    def onward(received, left, flipped):
+        return together(
+            *(
+                (term(sign * left, 1 - part if flipped else part) + x.astype(F32)).astype(BF16)
+                for (_, sign, part), x in zip(ways, received)
+            )
+        )
+
+    def send(pair):
+        return [move(x) for (move, _, _), x in zip(ways, pair)]
+
+    nearer = send(together(*(term(sign * (far - 1), 1 - part).astype(BF16) for _, sign, part in ways)))
+    own, near = experts(f, b, swap(f), swap(b))
+    pieces = 4
+    near = [swap(near[i * token_count // pieces : (i + 1) * token_count // pieces]) for i in range(pieces)]
+    shared[far] = (own, jnp.concatenate(near, axis=0))
+    *farther, n0, n1 = together(*(term(far, part).astype(BF16) for _, _, part in ways), *nearer)
+    nearer = [n0, n1]
+    farther = send(farther)
+    for left in range(far - 1, 0, -1):
+        if left > 1:
+            nearer = onward(nearer, left - 1, True)
+            nearer_sent = send(nearer)
+            farther = onward(farther, left, False)
+            farther = together(*farther, *nearer)[:2]
+            nearer = nearer_sent
+        else:
+            farther = onward(farther, left, False)
+        farther = send(farther)
 
     return call(
         final_kernel,
@@ -277,10 +358,10 @@
         stream,
         stream_near,
         *shared[0],
-        chain(go, 1, 0, far),
-        chain(come, -1, 0, far - 1),
-        chain(go, 1, 1, far - 1),
-        chain(come, -1, 1, far),
+        farther[0],
+        nearer[1],
+        nearer[0],
+        farther[1],
         norm_gain[None, :],
         name="final",
     )

time: 152 us -> 133 us (0.88)
  waiting for transfers between devices: 79.7 us -> 54.9 us
  starting transfers between devices: 45.5 us -> 50.3 us
    ppermute x18, waiting for transfers between devices: 54.2 us -> 32.8 us  [go(): return lax.ppermute(x, 'expert', forth)]
    ppermute x18, starting transfers between devices: 16.9 us -> 24.1 us  [go(): return lax.ppermute(x, 'expert', forth)]
    ppermute x18, starting transfers between devices: 19.7 us -> 16 us  [come(): return lax.ppermute(x, 'expert', back)]
    ppermute x1, waiting for transfers between devices: 2.14 us -> 0.01 us  [body(): other = lax.ppermute(mine, 'dp', flip)]
    ppermute x20 -> x23, starting transfers between devices: 3.97 us -> 5.75 us  [swap(): return lax.ppermute(x, 'expert', across)]
    pallas_call x10 -> x11, Pallas kernels: 21.3 us -> 21.8 us  [call(): pl.pallas_call(kernel, in_specs=[SMEM] + [VMEM] * (len(args) - 1), out_sp...]
  transfers between devices with their start and end apart: 59 -> 62, of which waited for: 29 -> 32; matrix products, arithmetic and copies ran while one was open for 1% -> 1% of each run, Pallas kernels for 12% -> 15%
where the time goes in v3:
time: 133 us
  waiting for transfers between devices  54.9 us (41%)
  starting transfers between devices  50.3 us (38%)
  Pallas kernels  21.8 us (16%)
  local copies, waits for them, and re-layouts  4.38 us (3%)
    ppermute x18, waiting for transfers between devices, go(): return lax.ppermute(x, 'expert', forth)  32.8 us
    ppermute x18, starting transfers between devices, go(): return lax.ppermute(x, 'expert', forth)  24.1 us
    pallas_call x11, Pallas kernels, call(): pl.pallas_call(kernel, in_specs=[SMEM] + [VMEM] * (len(args) - 1), out_sp...  21.8 us
    ppermute x18, starting transfers between devices, come(): return lax.ppermute(x, 'expert', back)  16 us
    ppermute x18, waiting for transfers between devices, come(): return lax.ppermute(x, 'expert', back)  15.2 us
    ppermute x23, starting transfers between devices, swap(): return lax.ppermute(x, 'expert', across)  5.75 us
    ppermute x1, waiting for transfers between devices, body(): lax.ppermute(up_later, 'dp', flip)  5.13 us
    unnamed x16, local copies, waits for them, and re-layouts  3.38 us
  transfers between devices with their start and end apart: 62, of which 32 were waited for; matrix products, arithmetic and copies ran while one was open for 1% of the time, Pallas kernels for 15%

profile of v3, /device:TPU:0, one launch (start us, length us, event | category | flops | bytes accessed | tf_op | source)
XLA Modules:
  0.0 132.7 jit_solution(16611621123359658379)
XLA Ops:
  0.5 0.9 constant_dynamic-slice_fusion.1
  2.0 0.9 collective-permute-done
  2.9 3.0 %collective-permute-start.1 = (bf16[96,768]{1,0:T(8,128)(2,1)S(1)}, bf16[96,768]{1,0:T(8,128)(2,1)S(1)}, u32[]{:S(2)}, u32[]{:S(2)}) collective-permute-start(bf16[96,768]{1,0:T(8,128)(2,1)S(1)} %pad_maximum_fusion.refs_0_), channel_id=1, source_target_pairs={{0,4},{1,5},{4,8},{5,9},{8,12},{9,13},{12,14},{13,15},{14,10},{15,... | collective-permute-start | bytes 442376 | tf_op jit(solution)/shard_map/ppermute | solution.py:196
  5.9 2.0 %collective-permute-start.3 = (bf16[96,768]{1,0:T(8,128)(2,1)S(1)}, bf16[96,768]{1,0:T(8,128)(2,1)S(1)}, u32[]{:S(2)}, u32[]{:S(2)}) collective-permute-start(bf16[96,768]{1,0:T(8,128)(2,1)S(1)} %pad_maximum_fusion.refs_0_), channel_id=1, source_target_pairs={{0,16},{16,0},{1,17},{17,1},{2,18},{18,2},{3,19},{19,3},{4,20},{20... | collective-permute-start | bytes 442376 | tf_op jit(solution)/shard_map/ppermute | solution.py:228
  7.9 1.0 copy-done.3
  8.9 1.0 copy-done.4
  12.0 1.2 collective-permute-start.18
  13.2 1.6 %collective-permute-start.6 = (bf16[96,768]{1,0:T(8,128)(2,1)S(1)}, bf16[96,768]{1,0:T(8,128)(2,1)S(1)}, u32[]{:S(2)}, u32[]{:S(2)}) collective-permute-start(bf16[96,768]{1,0:T(8,128)(2,1)S(1)} %collective-permute-done.1.refs_2_), channel_id=1, source_target_pairs={{0,4},{1,5},{4,8},{5,9},{8,12},{9,13},{12,14},{13,15},{14,10},{15,... | collective-permute-start | bytes 442376 | tf_op jit(solution)/shard_map/ppermute | solution.py:196
  15.2 1.6 %collective-permute-start.7 = (bf16[96,768]{1,0:T(8,128)(2,1)S(1)}, bf16[96,768]{1,0:T(8,128)(2,1)S(1)}, u32[]{:S(2)}, u32[]{:S(2)}) collective-permute-start(bf16[96,768]{1,0:T(8,128)(2,1)S(1)} %collective-permute-done.3.refs_1_), channel_id=1, source_target_pairs={{0,4},{1,5},{4,8},{5,9},{8,12},{9,13},{12,14},{13,15},{14,10},{15,... | collective-permute-start | bytes 442376 | tf_op jit(solution)/shard_map/ppermute | solution.py:196
  17.3 2.3 %collective-permute-done.6.refs_4_ = bf16[96,768]{1,0:T(8,128)(2,1)S(1)} collective-permute-done((bf16[96,768]{1,0:T(8,128)(2,1)S(1)}, bf16[96,768]{1,0:T(8,128)(2,1)S(1)}, u32[]{:S(2)}, u32[]{:S(2)}) %collective-permute-start.6) | collective-permute-done | bytes 147488 | tf_op jit(solution)/shard_map/ppermute | solution.py:196
  19.5 1.6 %collective-permute-start.10 = (bf16[96,768]{1,0:T(8,128)(2,1)S(1)}, bf16[96,768]{1,0:T(8,128)(2,1)S(1)}, u32[]{:S(2)}, u32[]{:S(2)}) collective-permute-start(bf16[96,768]{1,0:T(8,128)(2,1)S(1)} %collective-permute-done.6.refs_4_), channel_id=1, source_target_pairs={{0,4},{1,5},{4,8},{5,9},{8,12},{9,13},{12,14},{13,15},{14,10},{15,... | collective-permute-start | bytes 442376 | tf_op jit(solution)/shard_map/ppermute | solution.py:196
  21.6 0.7 collective-permute-done.7.refs_5_
  22.3 1.3 collective-permute-start.22
  23.6 1.6 %collective-permute-start.11 = (bf16[96,768]{1,0:T(8,128)(2,1)S(1)}, bf16[96,768]{1,0:T(8,128)(2,1)S(1)}, u32[]{:S(2)}, u32[]{:S(2)}) collective-permute-start(bf16[96,768]{1,0:T(8,128)(2,1)S(1)} %collective-permute-done.7.refs_5_), channel_id=1, source_target_pairs={{0,4},{1,5},{4,8},{5,9},{8,12},{9,13},{12,14},{13,15},{14,10},{15,... | collective-permute-start | bytes 442376 | tf_op jit(solution)/shard_map/ppermute | solution.py:196
  25.6 1.5 %collective-permute-start.12 = (bf16[96,768]{1,0:T(8,128)(2,1)S(1)}, bf16[96,768]{1,0:T(8,128)(2,1)S(1)}, u32[]{:S(2)}, u32[]{:S(2)}) collective-permute-start(bf16[96,768]{1,0:T(8,128)(2,1)S(1)} %collective-permute-done.8.refs_6_), channel_id=1, source_target_pairs={{4,0},{5,1},{8,4},{9,5},{12,8},{13,9},{14,12},{15,13},{10,14},{11,... | collective-permute-start | bytes 442376 | tf_op jit(solution)/shard_map/ppermute | solution.py:199
  27.8 0.9 collective-permute-start.16
  28.7 1.1 collective-permute-done.11.refs_9_
  29.8 1.6 %collective-permute-start.14 = (bf16[96,768]{1,0:T(8,128)(2,1)S(1)}, bf16[96,768]{1,0:T(8,128)(2,1)S(1)}, u32[]{:S(2)}, u32[]{:S(2)}) collective-permute-start(bf16[96,768]{1,0:T(8,128)(2,1)S(1)} %collective-permute-done.10.refs_8_), channel_id=1, source_target_pairs={{0,4},{1,5},{4,8},{5,9},{8,12},{9,13},{12,14},{13,15},{14,10},{15,... | collective-permute-start | bytes 442376 | tf_op jit(solution)/shard_map/ppermute | solution.py:196
  31.4 1.6 %collective-permute-start.15 = (bf16[96,768]{1,0:T(8,128)(2,1)S(1)}, bf16[96,768]{1,0:T(8,128)(2,1)S(1)}, u32[]{:S(2)}, u32[]{:S(2)}) collective-permute-start(bf16[96,768]{1,0:T(8,128)(2,1)S(1)} %collective-permute-done.11.refs_9_), channel_id=1, source_target_pairs={{0,4},{1,5},{4,8},{5,9},{8,12},{9,13},{12,14},{13,15},{14,10},{15,... | collective-permute-start | bytes 442376 | tf_op jit(solution)/shard_map/ppermute | solution.py:196
  33.0 0.8 collective-permute-done.16.refs_14_
  33.8 1.3 collective-permute-start.17
  35.1 1.5 %collective-permute-done.15.refs_13_ = bf16[96,768]{1,0:T(8,128)(2,1)S(1)} collective-permute-done((bf16[96,768]{1,0:T(8,128)(2,1)S(1)}, bf16[96,768]{1,0:T(8,128)(2,1)S(1)}, u32[]{:S(2)}, u32[]{:S(2)}) %collective-permute-start.15) | collective-permute-done | bytes 147488 | tf_op jit(solution)/shard_map/ppermute | solution.py:196
  36.7 2.3 %collective-permute-done.17.refs_15_ = bf16[96,768]{1,0:T(8,128)(2,1)S(1)} collective-permute-done((bf16[96,768]{1,0:T(8,128)(2,1)S(1)}, bf16[96,768]{1,0:T(8,128)(2,1)S(1)}, u32[]{:S(2)}, u32[]{:S(2)}) %collective-permute-start.17) | collective-permute-done | bytes 147488 | tf_op jit(solution)/shard_map/ppermute | solution.py:199
  39.0 1.5 %stream.1.refs_0_.own = bf16[272,768]{1,0:T(8,128)(2,1)S(1)} custom-call(s32[3]{0:T(128)S(1)} %pad_add_fusion.place, bf16[256,1536]{1,0:T(8,128)(2,1)S(1)} %get-tuple-element.108.tokens, bf16[272,768]{1,0:T(8,128)(2,1)S(1)} %get-tuple-element.109.base, bf16[96,768]{1,0:T(8,128)(2,1)S(1)} %pad_maximum_fusion.refs_0_, ...), custom_call_target="tpu_custom_call" | custom-call | flops 603979776 | bytes 4194304 | tf_op jit(solution)/shard_map/stream/pallas_call | solution.py:27
  40.5 1.6 %collective-permute-start.20 = (bf16[272,768]{1,0:T(8,128)(2,1)S(1)}, bf16[272,768]{1,0:T(8,128)(2,1)S(1)}, u32[]{:S(2)}, u32[]{:S(2)}) collective-permute-start(bf16[272,768]{1,0:T(8,128)(2,1)S(1)} %stream.1.refs_0_.own), channel_id=1, source_target_pairs={{0,4},{1,5},{4,8},{5,9},{8,12},{9,13},{12,14},{13,15},{14,10},{15,... | collective-permute-start | bytes 1253384 | tf_op jit(solution)/shard_map/ppermute | solution.py:196
  42.6 5.1 %collective-permute-done.22.refs_5_.refs_7_ = bf16[768,512]{1,0:T(8,128)(2,1)S(1)} collective-permute-done((bf16[768,512]{1,0:T(8,128)(2,1)S(1)}, bf16[768,512]{1,0:T(8,128)(2,1)S(1)}, u32[]{:S(2)}, u32[]{:S(2)}) %collective-permute-start.22) | collective-permute-done | bytes 786464 | tf_op jit(solution)/shard_map/ppermute | solution.py:254
  47.7 0.9 collective-permute-done.20.refs_0_
  48.6 1.6 %collective-permute-done.21.refs_0_ = bf16[272,768]{1,0:T(8,128)(2,1)S(1)} collective-permute-done((bf16[272,768]{1,0:T(8,128)(2,1)S(1)}, bf16[272,768]{1,0:T(8,128)(2,1)S(1)}, u32[]{:S(2)}, u32[]{:S(2)}) %collective-permute-start.21) | collective-permute-done | bytes 417824 | tf_op jit(solution)/shard_map/ppermute | solution.py:199
  50.7 1.4 %collective-permute-start.23 = (bf16[272,768]{1,0:T(8,128)(2,1)S(1)}, bf16[272,768]{1,0:T(8,128)(2,1)S(1)}, u32[]{:S(2)}, u32[]{:S(2)}) collective-permute-start(bf16[272,768]{1,0:T(8,128)(2,1)S(1)} %collective-permute-done.20.refs_0_), channel_id=1, source_target_pairs={{0,4},{1,5},{4,8},{5,9},{8,12},{9,13},{12,14},{13,15},{14,10},{15,... | collective-permute-start | bytes 1253384 | tf_op jit(solution)/shard_map/ppermute | solution.py:196
  52.7 2.2 %experts.9 = (f32[128,1536]{1,0:T(8,128)S(1)}, bf16[128,1536]{1,0:T(8,128)(2,1)S(1)}) custom-call(s32[3]{0:T(128)S(1)} %pad_add_fusion.place, bf16[272,768]{1,0:T(8,128)(2,1)S(1)} %stream.1.refs_0_.own, bf16[272,768]{1,0:T(8,128)(2,1)S(1)} %collective-permute-done.19.refs_1_.near, bf16[768,512]{1,0:T(8,128)(2,1)S(1)} %bitcast.17, ...), custom_call_target="tpu_custom_call" | custom-call | flops 1207959552 | bytes 4194304 | tf_op jit(solution)/shard_map/experts/pallas_call | solution.py:27
  54.9 2.2 %experts.8 = (f32[128,1536]{1,0:T(8,128)S(1)}, bf16[128,1536]{1,0:T(8,128)(2,1)S(1)}) custom-call(s32[3]{0:T(128)S(1)} %pad_add_fusion.place, bf16[272,768]{1,0:T(8,128)(2,1)S(1)} %collective-permute-done.20.refs_0_, bf16[272,768]{1,0:T(8,128)(2,1)S(1)} %collective-permute-done.25.refs_1_, bf16[768,512]{1,0:T(8,128)(2,1)S(1)} %bitcast.18, ...), custom_call_target="tpu_custom_call" | custom-call | flops 1207959552 | bytes 4194304 | tf_op jit(solution)/shard_map/experts/pallas_call | solution.py:27
  57.2 2.3 %experts.10 = (f32[128,1536]{1,0:T(8,128)S(1)}, bf16[128,1536]{1,0:T(8,128)(2,1)S(1)}) custom-call(s32[3]{0:T(128)S(1)} %pad_add_fusion.place, bf16[272,768]{1,0:T(8,128)(2,1)S(1)} %collective-permute-done.21.refs_0_, bf16[272,768]{1,0:T(8,128)(2,1)S(1)} %collective-permute-done.26.refs_1_, bf16[768,512]{1,0:T(8,128)(2,1)S(1)} %bitcast.19, ...), custom_call_target="tpu_custom_call" | custom-call | flops 1207959552 | bytes 4194304 | tf_op jit(solution)/shard_map/experts/pallas_call | solution.py:27
  59.5 2.7 %collective-permute-done.23.refs_0_ = bf16[272,768]{1,0:T(8,128)(2,1)S(1)} collective-permute-done((bf16[272,768]{1,0:T(8,128)(2,1)S(1)}, bf16[272,768]{1,0:T(8,128)(2,1)S(1)}, u32[]{:S(2)}, u32[]{:S(2)}) %collective-permute-start.23) | collective-permute-done | bytes 417824 | tf_op jit(solution)/shard_map/ppermute | solution.py:196
  62.2 1.3 collective-permute-done.24.refs_0_
  64.0 2.0 %collective-permute-start.27 = (bf16[272,768]{1,0:T(8,128)(2,1)S(1)}, bf16[272,768]{1,0:T(8,128)(2,1)S(1)}, u32[]{:S(2)}, u32[]{:S(2)}) collective-permute-start(bf16[272,768]{1,0:T(8,128)(2,1)S(1)} %collective-permute-done.23.refs_0_), channel_id=1, source_target_pairs={{0,4},{1,5},{4,8},{5,9},{8,12},{9,13},{12,14},{13,15},{14,10},{15,... | collective-permute-start | bytes 1253384 | tf_op jit(solution)/shard_map/ppermute | solution.py:196
  66.6 2.2 %experts.11 = (f32[128,1536]{1,0:T(8,128)S(1)}, bf16[128,1536]{1,0:T(8,128)(2,1)S(1)}) custom-call(s32[3]{0:T(128)S(1)} %pad_add_fusion.place, bf16[272,768]{1,0:T(8,128)(2,1)S(1)} %collective-permute-done.23.refs_0_, bf16[272,768]{1,0:T(8,128)(2,1)S(1)} %collective-permute-done.29.refs_1_, bf16[768,512]{1,0:T(8,128)(2,1)S(1)} %bitcast.20, ...), custom_call_target="tpu_custom_call" | custom-call | flops 1207959552 | bytes 4194304 | tf_op jit(solution)/shard_map/experts/pallas_call | solution.py:27
  68.9 2.2 %experts.12 = (f32[128,1536]{1,0:T(8,128)S(1)}, bf16[128,1536]{1,0:T(8,128)(2,1)S(1)}) custom-call(s32[3]{0:T(128)S(1)} %pad_add_fusion.place, bf16[272,768]{1,0:T(8,128)(2,1)S(1)} %collective-permute-done.24.refs_0_, bf16[272,768]{1,0:T(8,128)(2,1)S(1)} %collective-permute-done.30.refs_1_, bf16[768,512]{1,0:T(8,128)(2,1)S(1)} %bitcast.21, ...), custom_call_target="tpu_custom_call" | custom-call | flops 1207959552 | bytes 4194304 | tf_op jit(solution)/shard_map/experts/pallas_call | solution.py:27
  71.1 4.4 %collective-permute-done.27.refs_0_ = bf16[272,768]{1,0:T(8,128)(2,1)S(1)} collective-permute-done((bf16[272,768]{1,0:T(8,128)(2,1)S(1)}, bf16[272,768]{1,0:T(8,128)(2,1)S(1)}, u32[]{:S(2)}, u32[]{:S(2)}) %collective-permute-start.27) | collective-permute-done | bytes 417824 | tf_op jit(solution)/shard_map/ppermute | solution.py:196
  75.5 1.7 %collective-permute-done.28.refs_0_ = bf16[272,768]{1,0:T(8,128)(2,1)S(1)} collective-permute-done((bf16[272,768]{1,0:T(8,128)(2,1)S(1)}, bf16[272,768]{1,0:T(8,128)(2,1)S(1)}, u32[]{:S(2)}, u32[]{:S(2)}) %collective-permute-start.28) | collective-permute-done | bytes 417824 | tf_op jit(solution)/shard_map/ppermute | solution.py:199
  78.3 1.8 %collective-permute-start.34 = (bf16[144,768]{1,0:T(8,128)(2,1)S(1)}, bf16[144,768]{1,0:T(8,128)(2,1)S(1)}, u32[]{:S(2)}, u32[]{:S(2)}) collective-permute-start(bf16[144,768]{1,0:T(8,128)(2,1)S(1)} %slice.100), channel_id=1, source_target_pairs={{0,4},{1,5},{4,8},{5,9},{8,12},{9,13},{12,14},{13,15},{14,10},{15,... | collective-permute-start | bytes 663560 | tf_op jit(solution)/shard_map/ppermute | solution.py:196
  80.4 2.2 %experts.13 = (f32[128,1536]{1,0:T(8,128)S(1)}, bf16[128,1536]{1,0:T(8,128)(2,1)S(1)}) custom-call(s32[3]{0:T(128)S(1)} %pad_add_fusion.place, bf16[272,768]{1,0:T(8,128)(2,1)S(1)} %collective-permute-done.27.refs_0_, bf16[272,768]{1,0:T(8,128)(2,1)S(1)} %collective-permute-done.36.refs_1_, bf16[768,512]{1,0:T(8,128)(2,1)S(1)} %bitcast.22, ...), custom_call_target="tpu_custom_call" | custom-call | flops 1207959552 | bytes 4194304 | tf_op jit(solution)/shard_map/experts/pallas_call | solution.py:27
  82.7 2.2 %experts.14 = (f32[128,1536]{1,0:T(8,128)S(1)}, bf16[128,1536]{1,0:T(8,128)(2,1)S(1)}) custom-call(s32[3]{0:T(128)S(1)} %pad_add_fusion.place, bf16[272,768]{1,0:T(8,128)(2,1)S(1)} %collective-permute-done.28.refs_0_, bf16[272,768]{1,0:T(8,128)(2,1)S(1)} %collective-permute-done.37.refs_1_, bf16[768,512]{1,0:T(8,128)(2,1)S(1)} %bitcast.23, ...), custom_call_target="tpu_custom_call" | custom-call | flops 1207959552 | bytes 4194304 | tf_op jit(solution)/shard_map/experts/pallas_call | solution.py:27
  84.9 0.8 collective-permute-done.34.refs_0_
  85.7 1.5 %collective-permute-done.35.refs_1_ = bf16[144,768]{1,0:T(8,128)(2,1)S(1)} collective-permute-done((bf16[144,768]{1,0:T(8,128)(2,1)S(1)}, bf16[144,768]{1,0:T(8,128)(2,1)S(1)}, u32[]{:S(2)}, u32[]{:S(2)}) %collective-permute-start.35) | collective-permute-done | bytes 221216 | tf_op jit(solution)/shard_map/ppermute | solution.py:199
  89.0 2.2 %experts.15 = (f32[128,1536]{1,0:T(8,128)S(1)}, bf16[128,1536]{1,0:T(8,128)(2,1)S(1)}) custom-call(s32[3]{0:T(128)S(1)} %pad_add_fusion.place, bf16[144,768]{1,0:T(8,128)(2,1)S(1)} %collective-permute-done.34.refs_0_, bf16[144,768]{1,0:T(8,128)(2,1)S(1)} %collective-permute-done.35.refs_1_, bf16[144,768]{1,0:T(8,128)(2,1)S(1)} %collective-permute-done.41.refs_2_, ...), custom_call_target="tpu_custom_call" | custom-call | flops 1207959552 | bytes 4194304 | tf_op jit(solution)/shard_map/experts/pallas_call | solution.py:27
  92.5 1.1 collective-permute-start.48
  93.6 1.0 collective-permute-start.49
  94.7 4.9 %collective-permute-done.48 = bf16[64,1536]{1,0:T(8,128)(2,1)S(1)} collective-permute-done((bf16[64,1536]{1,0:T(8,128)(2,1)S(1)}, bf16[64,1536]{1,0:T(8,128)(2,1)S(1)}, u32[]{:S(2)}, u32[]{:S(2)}) %collective-permute-start.48) | collective-permute-done | bytes 196640 | tf_op jit(solution)/shard_map/ppermute | solution.py:196
  99.6 0.8 collective-permute-done.49
  100.9 1.4 %collective-permute-start.51 = (bf16[64,1536]{1,0:T(8,128)(2,1)S(1)}, bf16[64,1536]{1,0:T(8,128)(2,1)S(1)}, u32[]{:S(2)}, u32[]{:S(2)}) collective-permute-start(bf16[64,1536]{1,0:T(8,128)(2,1)S(1)} %get-tuple-element.186), channel_id=1, source_target_pairs={{4,0},{5,1},{8,4},{9,5},{12,8},{13,9},{14,12},{15,13},{10,14},{11,... | collective-permute-start | bytes 589832 | tf_op jit(solution)/shard_map/ppermute | solution.py:199
  103.2 1.4 %collective-permute-start.55 = (bf16[64,1536]{1,0:T(8,128)(2,1)S(1)}, bf16[64,1536]{1,0:T(8,128)(2,1)S(1)}, u32[]{:S(2)}, u32[]{:S(2)}) collective-permute-start(bf16[64,1536]{1,0:T(8,128)(2,1)S(1)} %get-tuple-element.194), channel_id=1, source_target_pairs={{4,0},{5,1},{8,4},{9,5},{12,8},{13,9},{14,12},{15,13},{10,14},{11,... | collective-permute-start | bytes 589832 | tf_op jit(solution)/shard_map/ppermute | solution.py:199
  104.6 3.6 %collective-permute-done.50 = bf16[64,1536]{1,0:T(8,128)(2,1)S(1)} collective-permute-done((bf16[64,1536]{1,0:T(8,128)(2,1)S(1)}, bf16[64,1536]{1,0:T(8,128)(2,1)S(1)}, u32[]{:S(2)}, u32[]{:S(2)}) %collective-permute-start.50) | collective-permute-done | bytes 196640 | tf_op jit(solution)/shard_map/ppermute | solution.py:196
  109.3 1.6 %collective-permute-start.53 = (bf16[64,1536]{1,0:T(8,128)(2,1)S(1)}, bf16[64,1536]{1,0:T(8,128)(2,1)S(1)}, u32[]{:S(2)}, u32[]{:S(2)}) collective-permute-start(bf16[64,1536]{1,0:T(8,128)(2,1)S(1)} %add_convert_fusion.8), channel_id=1, source_target_pairs={{4,0},{5,1},{8,4},{9,5},{12,8},{13,9},{14,12},{15,13},{10,14},{11,... | collective-permute-start | bytes 589832 | tf_op jit(solution)/shard_map/ppermute | solution.py:199
  110.9 1.5 %collective-permute-done.54 = bf16[64,1536]{1,0:T(8,128)(2,1)S(1)} collective-permute-done((bf16[64,1536]{1,0:T(8,128)(2,1)S(1)}, bf16[64,1536]{1,0:T(8,128)(2,1)S(1)}, u32[]{:S(2)}, u32[]{:S(2)}) %collective-permute-start.54) | collective-permute-done | bytes 196640 | tf_op jit(solution)/shard_map/ppermute | solution.py:196
  112.9 1.7 %collective-permute-done.52 = bf16[64,1536]{1,0:T(8,128)(2,1)S(1)} collective-permute-done((bf16[64,1536]{1,0:T(8,128)(2,1)S(1)}, bf16[64,1536]{1,0:T(8,128)(2,1)S(1)}, u32[]{:S(2)}, u32[]{:S(2)}) %collective-permute-start.52) | collective-permute-done | bytes 196640 | tf_op jit(solution)/shard_map/ppermute | solution.py:196
  115.7 1.5 %collective-permute-start.59 = (bf16[64,1536]{1,0:T(8,128)(2,1)S(1)}, bf16[64,1536]{1,0:T(8,128)(2,1)S(1)}, u32[]{:S(2)}, u32[]{:S(2)}) collective-permute-start(bf16[64,1536]{1,0:T(8,128)(2,1)S(1)} %add_convert_fusion.2), channel_id=1, source_target_pairs={{4,0},{5,1},{8,4},{9,5},{12,8},{13,9},{14,12},{15,13},{10,14},{11,... | collective-permute-start | bytes 589832 | tf_op jit(solution)/shard_map/ppermute | solution.py:199
  117.7 1.5 %collective-permute-start.57 = (bf16[64,1536]{1,0:T(8,128)(2,1)S(1)}, bf16[64,1536]{1,0:T(8,128)(2,1)S(1)}, u32[]{:S(2)}, u32[]{:S(2)}) collective-permute-start(bf16[64,1536]{1,0:T(8,128)(2,1)S(1)} %add_convert_fusion.4), channel_id=1, source_target_pairs={{4,0},{5,1},{8,4},{9,5},{12,8},{13,9},{14,12},{15,13},{10,14},{11,... | collective-permute-start | bytes 589832 | tf_op jit(solution)/shard_map/ppermute | solution.py:199
  119.2 2.7 %collective-permute-done.56 = bf16[64,1536]{1,0:T(8,128)(2,1)S(1)} collective-permute-done((bf16[64,1536]{1,0:T(8,128)(2,1)S(1)}, bf16[64,1536]{1,0:T(8,128)(2,1)S(1)}, u32[]{:S(2)}, u32[]{:S(2)}) %collective-permute-start.56) | collective-permute-done | bytes 196640 | tf_op jit(solution)/shard_map/ppermute | solution.py:196
  121.9 2.5 %collective-permute-done.57 = bf16[64,1536]{1,0:T(8,128)(2,1)S(1)} collective-permute-done((bf16[64,1536]{1,0:T(8,128)(2,1)S(1)}, bf16[64,1536]{1,0:T(8,128)(2,1)S(1)}, u32[]{:S(2)}, u32[]{:S(2)}) %collective-permute-start.57) | collective-permute-done | bytes 196640 | tf_op jit(solution)/shard_map/ppermute | solution.py:199
  124.5 0.8 collective-permute-start.58
  125.3 1.3 collective-permute-start.61
  126.6 3.6 %collective-permute-done.58.first_a = bf16[64,1536]{1,0:T(8,128)(2,1)S(1)} collective-permute-done((bf16[64,1536]{1,0:T(8,128)(2,1)S(1)}, bf16[64,1536]{1,0:T(8,128)(2,1)S(1)}, u32[]{:S(2)}, u32[]{:S(2)}) %collective-permute-start.58) | collective-permute-done | bytes 196640 | tf_op jit(solution)/shard_map/ppermute | solution.py:196
  130.2 0.8 collective-permute-done.61.second_b
  131.0 1.7 %final.1 = bf16[128,1536]{1,0:T(8,128)(2,1)} custom-call(s32[3]{0:T(128)S(1)} %pad_add_fusion.place, bf16[272,768]{1,0:T(8,128)(2,1)S(1)} %stream.1.refs_0_.own, bf16[272,768]{1,0:T(8,128)(2,1)S(1)} %collective-permute-done.19.refs_1_.near, f32[128,1536]{1,0:T(8,128)S(1)} %get-tuple-element.169.mine, bf16[128,1536]{1,0:T(8,128)(2,1)S(1)} %collective-permute-done.32.shared, ...), custom_call_target="tpu_custom_call" | custom-call | bytes 4194304 | tf_op jit(solution)/shard_map/final/pallas_call | solution.py:27
  (106 shorter events, 17.6 us)
Async XLA Ops:
  0.0 22.3 %copy-start.2 = (bf16[1,768,512]{2,1,0:T(8,128)(2,1)S(1)}, bf16[1,768,512]{2,1,0:T(8,128)(2,1)}, u32[]{:S(2)}) copy-start(bf16[1,768,512]{2,1,0:T(8,128)(2,1)} %param.13) | copy-start | bytes 2359300
  0.0 7.9 %collective-permute-start.4 = (bf16[128,1536]{1,0:T(8,128)(2,1)}, bf16[128,1536]{1,0:T(8,128)(2,1)S(1)}, u32[]{:S(2)}, u32[]{:S(2)}) collective-permute-start(bf16[128,1536]{1,0:T(8,128)(2,1)} %att.1), channel_id=1, source_target_pairs={{0,1},{1,0},{2,3},{3,2},{4,5},{5,4},{6,7},{7,6},{8,9},{9,8},{10,11... | collective-permute-start | bytes 1179656 | tf_op jit(solution)/shard_map/ppermute | solution.py:193
  0.5 7.5 %collective-permute-start.5 = (bf16[128,1536]{1,0:T(8,128)(2,1)}, bf16[128,1536]{1,0:T(8,128)(2,1)S(1)}, u32[]{:S(2)}, u32[]{:S(2)}) collective-permute-start(bf16[128,1536]{1,0:T(8,128)(2,1)} %res.1), channel_id=1, source_target_pairs={{0,1},{1,0},{2,3},{3,2},{4,5},{5,4},{6,7},{7,6},{8,9},{9,8},{10,11... | collective-permute-start | bytes 1179656 | tf_op jit(solution)/shard_map/ppermute | solution.py:193
  1.5 1.4 %collective-permute-start = (bf16[48,768]{1,0:T(8,128)(2,1)S(1)}, bf16[48,768]{1,0:T(8,128)(2,1)S(1)}, u32[]{:S(2)}, u32[]{:S(2)}) collective-permute-start(bf16[48,768]{1,0:T(8,128)(2,1)S(1)} %get-tuple-element.214), channel_id=1, source_target_pairs={{0,1},{1,0},{2,3},{3,2},{4,5},{5,4},{6,7},{7,6},{8,9},{9,8},{10,11... | collective-permute-start | bytes 221192 | tf_op jit(solution)/shard_map/ppermute | solution.py:193
  2.9 9.1 %collective-permute-start.1 = (bf16[96,768]{1,0:T(8,128)(2,1)S(1)}, bf16[96,768]{1,0:T(8,128)(2,1)S(1)}, u32[]{:S(2)}, u32[]{:S(2)}) collective-permute-start(bf16[96,768]{1,0:T(8,128)(2,1)S(1)} %pad_maximum_fusion.refs_0_), channel_id=1, source_target_pairs={{0,4},{1,5},{4,8},{5,9},{8,12},{9,13},{12,14},{13,15},{14,10},{15,... | collective-permute-start | bytes 442376 | tf_op jit(solution)/shard_map/ppermute | solution.py:196
  5.9 6.1 %collective-permute-start.2 = (bf16[96,768]{1,0:T(8,128)(2,1)S(1)}, bf16[96,768]{1,0:T(8,128)(2,1)S(1)}, u32[]{:S(2)}, u32[]{:S(2)}) collective-permute-start(bf16[96,768]{1,0:T(8,128)(2,1)S(1)} %pad_maximum_fusion.refs_0_), channel_id=1, source_target_pairs={{4,0},{5,1},{8,4},{9,5},{12,8},{13,9},{14,12},{15,13},{10,14},{11,... | collective-permute-start | bytes 442376 | tf_op jit(solution)/shard_map/ppermute | solution.py:199
  5.9 6.1 %collective-permute-start.3 = (bf16[96,768]{1,0:T(8,128)(2,1)S(1)}, bf16[96,768]{1,0:T(8,128)(2,1)S(1)}, u32[]{:S(2)}, u32[]{:S(2)}) collective-permute-start(bf16[96,768]{1,0:T(8,128)(2,1)S(1)} %pad_maximum_fusion.refs_0_), channel_id=1, source_target_pairs={{0,16},{16,0},{1,17},{17,1},{2,18},{18,2},{3,19},{19,3},{4,20},{20... | collective-permute-start | bytes 442376 | tf_op jit(solution)/shard_map/ppermute | solution.py:228
  12.0 40.7 %copy-start = (bf16[1,512,1536]{2,1,0:T(8,128)(2,1)S(1)}, bf16[1,512,1536]{2,1,0:T(8,128)(2,1)}, u32[]{:S(2)}) copy-start(bf16[1,512,1536]{2,1,0:T(8,128)(2,1)} %param.14) | copy-start | bytes 4718596
  12.0 27.0 %collective-permute-start.18 = (bf16[768,512]{1,0:T(8,128)(2,1)S(1)}, bf16[768,512]{1,0:T(8,128)(2,1)S(1)}, u32[]{:S(2)}, u32[]{:S(2)}) collective-permute-start(bf16[768,512]{1,0:T(8,128)(2,1)S(1)} %bitcast.16), channel_id=1, source_target_pairs={{0,16},{16,0},{1,17},{17,1},{2,18},{18,2},{3,19},{19,3},{4,20},{20... | collective-permute-start | bytes 2359304 | tf_op jit(solution)/shard_map/ppermute | solution.py:254
  13.2 6.3 %collective-permute-start.6 = (bf16[96,768]{1,0:T(8,128)(2,1)S(1)}, bf16[96,768]{1,0:T(8,128)(2,1)S(1)}, u32[]{:S(2)}, u32[]{:S(2)}) collective-permute-start(bf16[96,768]{1,0:T(8,128)(2,1)S(1)} %collective-permute-done.1.refs_2_), channel_id=1, source_target_pairs={{0,4},{1,5},{4,8},{5,9},{8,12},{9,13},{12,14},{13,15},{14,10},{15,... | collective-permute-start | bytes 442376 | tf_op jit(solution)/shard_map/ppermute | solution.py:196
  14.8 6.3 %collective-permute-start.9 = (bf16[96,768]{1,0:T(8,128)(2,1)S(1)}, bf16[96,768]{1,0:T(8,128)(2,1)S(1)}, u32[]{:S(2)}, u32[]{:S(2)}) collective-permute-start(bf16[96,768]{1,0:T(8,128)(2,1)S(1)} %collective-permute-done.3.refs_1_), channel_id=1, source_target_pairs={{4,0},{5,1},{8,4},{9,5},{12,8},{13,9},{14,12},{15,13},{10,14},{11,... | collective-permute-start | bytes 442376 | tf_op jit(solution)/shard_map/ppermute | solution.py:199
  15.2 7.1 %collective-permute-start.7 = (bf16[96,768]{1,0:T(8,128)(2,1)S(1)}, bf16[96,768]{1,0:T(8,128)(2,1)S(1)}, u32[]{:S(2)}, u32[]{:S(2)}) collective-permute-start(bf16[96,768]{1,0:T(8,128)(2,1)S(1)} %collective-permute-done.3.refs_1_), channel_id=1, source_target_pairs={{0,4},{1,5},{4,8},{5,9},{8,12},{9,13},{12,14},{13,15},{14,10},{15,... | collective-permute-start | bytes 442376 | tf_op jit(solution)/shard_map/ppermute | solution.py:196
  16.8 6.8 %collective-permute-start.8 = (bf16[96,768]{1,0:T(8,128)(2,1)S(1)}, bf16[96,768]{1,0:T(8,128)(2,1)S(1)}, u32[]{:S(2)}, u32[]{:S(2)}) collective-permute-start(bf16[96,768]{1,0:T(8,128)(2,1)S(1)} %collective-permute-done.2.refs_3_), channel_id=1, source_target_pairs={{4,0},{5,1},{8,4},{9,5},{12,8},{13,9},{14,12},{15,13},{10,14},{11,... | collective-permute-start | bytes 442376 | tf_op jit(solution)/shard_map/ppermute | solution.py:199
  19.5 6.1 %collective-permute-start.10 = (bf16[96,768]{1,0:T(8,128)(2,1)S(1)}, bf16[96,768]{1,0:T(8,128)(2,1)S(1)}, u32[]{:S(2)}, u32[]{:S(2)}) collective-permute-start(bf16[96,768]{1,0:T(8,128)(2,1)S(1)} %collective-permute-done.6.refs_4_), channel_id=1, source_target_pairs={{0,4},{1,5},{4,8},{5,9},{8,12},{9,13},{12,14},{13,15},{14,10},{15,... | collective-permute-start | bytes 442376 | tf_op jit(solution)/shard_map/ppermute | solution.py:196
  21.1 6.7 %collective-permute-start.13 = (bf16[96,768]{1,0:T(8,128)(2,1)S(1)}, bf16[96,768]{1,0:T(8,128)(2,1)S(1)}, u32[]{:S(2)}, u32[]{:S(2)}) collective-permute-start(bf16[96,768]{1,0:T(8,128)(2,1)S(1)} %collective-permute-done.9.refs_7_), channel_id=1, source_target_pairs={{4,0},{5,1},{8,4},{9,5},{12,8},{13,9},{14,12},{15,13},{10,14},{11,... | collective-permute-start | bytes 442376 | tf_op jit(solution)/shard_map/ppermute | solution.py:199
  22.3 25.4 %collective-permute-start.22 = (bf16[768,512]{1,0:T(8,128)(2,1)S(1)}, bf16[768,512]{1,0:T(8,128)(2,1)S(1)}, u32[]{:S(2)}, u32[]{:S(2)}) collective-permute-start(bf16[768,512]{1,0:T(8,128)(2,1)S(1)} %bitcast.25), channel_id=1, source_target_pairs={{0,16},{16,0},{1,17},{17,1},{2,18},{18,2},{3,19},{19,3},{4,20},{20... | collective-permute-start | bytes 2359304 | tf_op jit(solution)/shard_map/ppermute | solution.py:254
  23.6 6.2 %collective-permute-start.11 = (bf16[96,768]{1,0:T(8,128)(2,1)S(1)}, bf16[96,768]{1,0:T(8,128)(2,1)S(1)}, u32[]{:S(2)}, u32[]{:S(2)}) collective-permute-start(bf16[96,768]{1,0:T(8,128)(2,1)S(1)} %collective-permute-done.7.refs_5_), channel_id=1, source_target_pairs={{0,4},{1,5},{4,8},{5,9},{8,12},{9,13},{12,14},{13,15},{14,10},{15,... | collective-permute-start | bytes 442376 | tf_op jit(solution)/shard_map/ppermute | solution.py:196
  25.6 5.8 %collective-permute-start.12 = (bf16[96,768]{1,0:T(8,128)(2,1)S(1)}, bf16[96,768]{1,0:T(8,128)(2,1)S(1)}, u32[]{:S(2)}, u32[]{:S(2)}) collective-permute-start(bf16[96,768]{1,0:T(8,128)(2,1)S(1)} %collective-permute-done.8.refs_6_), channel_id=1, source_target_pairs={{4,0},{5,1},{8,4},{9,5},{12,8},{13,9},{14,12},{15,13},{10,14},{11,... | collective-permute-start | bytes 442376 | tf_op jit(solution)/shard_map/ppermute | solution.py:199
  27.8 6.0 %collective-permute-start.16 = (bf16[96,768]{1,0:T(8,128)(2,1)S(1)}, bf16[96,768]{1,0:T(8,128)(2,1)S(1)}, u32[]{:S(2)}, u32[]{:S(2)}) collective-permute-start(bf16[96,768]{1,0:T(8,128)(2,1)S(1)} %collective-permute-done.13.refs_11_), channel_id=1, source_target_pairs={{4,0},{5,1},{8,4},{9,5},{12,8},{13,9},{14,12},{15,13},{10,14},{11,... | collective-permute-start | bytes 442376 | tf_op jit(solution)/shard_map/ppermute | solution.py:199
  29.8 5.3 %collective-permute-start.14 = (bf16[96,768]{1,0:T(8,128)(2,1)S(1)}, bf16[96,768]{1,0:T(8,128)(2,1)S(1)}, u32[]{:S(2)}, u32[]{:S(2)}) collective-permute-start(bf16[96,768]{1,0:T(8,128)(2,1)S(1)} %collective-permute-done.10.refs_8_), channel_id=1, source_target_pairs={{0,4},{1,5},{4,8},{5,9},{8,12},{9,13},{12,14},{13,15},{14,10},{15,... | collective-permute-start | bytes 442376 | tf_op jit(solution)/shard_map/ppermute | solution.py:196
  31.4 5.2 %collective-permute-start.15 = (bf16[96,768]{1,0:T(8,128)(2,1)S(1)}, bf16[96,768]{1,0:T(8,128)(2,1)S(1)}, u32[]{:S(2)}, u32[]{:S(2)}) collective-permute-start(bf16[96,768]{1,0:T(8,128)(2,1)S(1)} %collective-permute-done.11.refs_9_), channel_id=1, source_target_pairs={{0,4},{1,5},{4,8},{5,9},{8,12},{9,13},{12,14},{13,15},{14,10},{15,... | collective-permute-start | bytes 442376 | tf_op jit(solution)/shard_map/ppermute | solution.py:196
  33.8 5.1 %collective-permute-start.17 = (bf16[96,768]{1,0:T(8,128)(2,1)S(1)}, bf16[96,768]{1,0:T(8,128)(2,1)S(1)}, u32[]{:S(2)}, u32[]{:S(2)}) collective-permute-start(bf16[96,768]{1,0:T(8,128)(2,1)S(1)} %collective-permute-done.16.refs_14_), channel_id=1, source_target_pairs={{4,0},{5,1},{8,4},{9,5},{12,8},{13,9},{14,12},{15,13},{10,14},{11,... | collective-permute-start | bytes 442376 | tf_op jit(solution)/shard_map/ppermute | solution.py:199
  40.5 8.1 %collective-permute-start.20 = (bf16[272,768]{1,0:T(8,128)(2,1)S(1)}, bf16[272,768]{1,0:T(8,128)(2,1)S(1)}, u32[]{:S(2)}, u32[]{:S(2)}) collective-permute-start(bf16[272,768]{1,0:T(8,128)(2,1)S(1)} %stream.1.refs_0_.own), channel_id=1, source_target_pairs={{0,4},{1,5},{4,8},{5,9},{8,12},{9,13},{12,14},{13,15},{14,10},{15,... | collective-permute-start | bytes 1253384 | tf_op jit(solution)/shard_map/ppermute | solution.py:196
  42.1 8.0 %collective-permute-start.21 = (bf16[272,768]{1,0:T(8,128)(2,1)S(1)}, bf16[272,768]{1,0:T(8,128)(2,1)S(1)}, u32[]{:S(2)}, u32[]{:S(2)}) collective-permute-start(bf16[272,768]{1,0:T(8,128)(2,1)S(1)} %stream.1.refs_0_.own), channel_id=1, source_target_pairs={{4,0},{5,1},{8,4},{9,5},{12,8},{13,9},{14,12},{15,13},{10,14},{11,... | collective-permute-start | bytes 1253384 | tf_op jit(solution)/shard_map/ppermute | solution.py:199
  42.6 10.1 %collective-permute-start.19 = (bf16[272,768]{1,0:T(8,128)(2,1)S(1)}, bf16[272,768]{1,0:T(8,128)(2,1)S(1)}, u32[]{:S(2)}, u32[]{:S(2)}) collective-permute-start(bf16[272,768]{1,0:T(8,128)(2,1)S(1)} %stream.1.refs_0_.own), channel_id=1, source_target_pairs={{0,1},{1,0},{2,3},{3,2},{4,5},{5,4},{6,7},{7,6},{8,9},{9,8},{10,11... | collective-permute-start | bytes 1253384 | tf_op jit(solution)/shard_map/ppermute | solution.py:193
  50.1 4.8 %collective-permute-start.25 = (bf16[272,768]{1,0:T(8,128)(2,1)S(1)}, bf16[272,768]{1,0:T(8,128)(2,1)S(1)}, u32[]{:S(2)}, u32[]{:S(2)}) collective-permute-start(bf16[272,768]{1,0:T(8,128)(2,1)S(1)} %collective-permute-done.20.refs_0_), channel_id=1, source_target_pairs={{0,1},{1,0},{2,3},{3,2},{4,5},{5,4},{6,7},{7,6},{8,9},{9,8},{10,11... | collective-permute-start | bytes 1253384 | tf_op jit(solution)/shard_map/ppermute | solution.py:193
  50.1 7.1 %collective-permute-start.26 = (bf16[272,768]{1,0:T(8,128)(2,1)S(1)}, bf16[272,768]{1,0:T(8,128)(2,1)S(1)}, u32[]{:S(2)}, u32[]{:S(2)}) collective-permute-start(bf16[272,768]{1,0:T(8,128)(2,1)S(1)} %collective-permute-done.21.refs_0_), channel_id=1, source_target_pairs={{0,1},{1,0},{2,3},{3,2},{4,5},{5,4},{6,7},{7,6},{8,9},{9,8},{10,11... | collective-permute-start | bytes 1253384 | tf_op jit(solution)/shard_map/ppermute | solution.py:193
  50.7 11.6 %collective-permute-start.23 = (bf16[272,768]{1,0:T(8,128)(2,1)S(1)}, bf16[272,768]{1,0:T(8,128)(2,1)S(1)}, u32[]{:S(2)}, u32[]{:S(2)}) collective-permute-start(bf16[272,768]{1,0:T(8,128)(2,1)S(1)} %collective-permute-done.20.refs_0_), channel_id=1, source_target_pairs={{0,4},{1,5},{4,8},{5,9},{8,12},{9,13},{12,14},{13,15},{14,10},{15,... | collective-permute-start | bytes 1253384 | tf_op jit(solution)/shard_map/ppermute | solution.py:196
  52.1 11.4 %collective-permute-start.24 = (bf16[272,768]{1,0:T(8,128)(2,1)S(1)}, bf16[272,768]{1,0:T(8,128)(2,1)S(1)}, u32[]{:S(2)}, u32[]{:S(2)}) collective-permute-start(bf16[272,768]{1,0:T(8,128)(2,1)S(1)} %collective-permute-done.21.refs_0_), channel_id=1, source_target_pairs={{4,0},{5,1},{8,4},{9,5},{12,8},{13,9},{14,12},{15,13},{10,14},{11,... | collective-permute-start | bytes 1253384 | tf_op jit(solution)/shard_map/ppermute | solution.py:199
  63.5 2.5 %collective-permute-start.29 = (bf16[272,768]{1,0:T(8,128)(2,1)S(1)}, bf16[272,768]{1,0:T(8,128)(2,1)S(1)}, u32[]{:S(2)}, u32[]{:S(2)}) collective-permute-start(bf16[272,768]{1,0:T(8,128)(2,1)S(1)} %collective-permute-done.23.refs_0_), channel_id=1, source_target_pairs={{0,1},{1,0},{2,3},{3,2},{4,5},{5,4},{6,7},{7,6},{8,9},{9,8},{10,11... | collective-permute-start | bytes 1253384 | tf_op jit(solution)/shard_map/ppermute | solution.py:193
  63.5 3.1 %collective-permute-start.30 = (bf16[272,768]{1,0:T(8,128)(2,1)S(1)}, bf16[272,768]{1,0:T(8,128)(2,1)S(1)}, u32[]{:S(2)}, u32[]{:S(2)}) collective-permute-start(bf16[272,768]{1,0:T(8,128)(2,1)S(1)} %collective-permute-done.24.refs_0_), channel_id=1, source_target_pairs={{0,1},{1,0},{2,3},{3,2},{4,5},{5,4},{6,7},{7,6},{8,9},{9,8},{10,11... | collective-permute-start | bytes 1253384 | tf_op jit(solution)/shard_map/ppermute | solution.py:193
  64.0 11.6 %collective-permute-start.27 = (bf16[272,768]{1,0:T(8,128)(2,1)S(1)}, bf16[272,768]{1,0:T(8,128)(2,1)S(1)}, u32[]{:S(2)}, u32[]{:S(2)}) collective-permute-start(bf16[272,768]{1,0:T(8,128)(2,1)S(1)} %collective-permute-done.23.refs_0_), channel_id=1, source_target_pairs={{0,4},{1,5},{4,8},{5,9},{8,12},{9,13},{12,14},{13,15},{14,10},{15,... | collective-permute-start | bytes 1253384 | tf_op jit(solution)/shard_map/ppermute | solution.py:196
  66.0 11.3 %collective-permute-start.28 = (bf16[272,768]{1,0:T(8,128)(2,1)S(1)}, bf16[272,768]{1,0:T(8,128)(2,1)S(1)}, u32[]{:S(2)}, u32[]{:S(2)}) collective-permute-start(bf16[272,768]{1,0:T(8,128)(2,1)S(1)} %collective-permute-done.24.refs_0_), channel_id=1, source_target_pairs={{4,0},{5,1},{8,4},{9,5},{12,8},{13,9},{14,12},{15,13},{10,14},{11,... | collective-permute-start | bytes 1253384 | tf_op jit(solution)/shard_map/ppermute | solution.py:199
  66.0 5.1 %collective-permute-start.31 = (bf16[128,1536]{1,0:T(8,128)(2,1)S(1)}, bf16[128,1536]{1,0:T(8,128)(2,1)S(1)}, u32[]{:S(2)}, u32[]{:S(2)}) collective-permute-start(bf16[128,1536]{1,0:T(8,128)(2,1)S(1)} %get-tuple-element.148), channel_id=1, source_target_pairs={{0,1},{1,0},{2,3},{3,2},{4,5},{5,4},{6,7},{7,6},{8,9},{9,8},{10,11... | collective-permute-start | bytes 1179656 | tf_op jit(solution)/shard_map/ppermute | solution.py:193
  66.0 5.1 %collective-permute-start.32 = (bf16[128,1536]{1,0:T(8,128)(2,1)S(1)}, bf16[128,1536]{1,0:T(8,128)(2,1)S(1)}, u32[]{:S(2)}, u32[]{:S(2)}) collective-permute-start(bf16[128,1536]{1,0:T(8,128)(2,1)S(1)} %get-tuple-element.150), channel_id=1, source_target_pairs={{0,1},{1,0},{2,3},{3,2},{4,5},{5,4},{6,7},{7,6},{8,9},{9,8},{10,11... | collective-permute-start | bytes 1179656 | tf_op jit(solution)/shard_map/ppermute | solution.py:193
  66.5 4.6 %collective-permute-start.33 = (bf16[128,1536]{1,0:T(8,128)(2,1)S(1)}, bf16[128,1536]{1,0:T(8,128)(2,1)S(1)}, u32[]{:S(2)}, u32[]{:S(2)}) collective-permute-start(bf16[128,1536]{1,0:T(8,128)(2,1)S(1)} %get-tuple-element.152), channel_id=1, source_target_pairs={{0,1},{1,0},{2,3},{3,2},{4,5},{5,4},{6,7},{7,6},{8,9},{9,8},{10,11... | collective-permute-start | bytes 1179656 | tf_op jit(solution)/shard_map/ppermute | solution.py:193
  77.3 2.9 %collective-permute-start.36 = (bf16[272,768]{1,0:T(8,128)(2,1)S(1)}, bf16[272,768]{1,0:T(8,128)(2,1)S(1)}, u32[]{:S(2)}, u32[]{:S(2)}) collective-permute-start(bf16[272,768]{1,0:T(8,128)(2,1)S(1)} %collective-permute-done.27.refs_0_), channel_id=1, source_target_pairs={{0,1},{1,0},{2,3},{3,2},{4,5},{5,4},{6,7},{7,6},{8,9},{9,8},{10,11... | collective-permute-start | bytes 1253384 | tf_op jit(solution)/shard_map/ppermute | solution.py:193
  77.3 5.4 %collective-permute-start.37 = (bf16[272,768]{1,0:T(8,128)(2,1)S(1)}, bf16[272,768]{1,0:T(8,128)(2,1)S(1)}, u32[]{:S(2)}, u32[]{:S(2)}) collective-permute-start(bf16[272,768]{1,0:T(8,128)(2,1)S(1)} %collective-permute-done.28.refs_0_), channel_id=1, source_target_pairs={{0,1},{1,0},{2,3},{3,2},{4,5},{5,4},{6,7},{7,6},{8,9},{9,8},{10,11... | collective-permute-start | bytes 1253384 | tf_op jit(solution)/shard_map/ppermute | solution.py:193
  77.8 9.4 %collective-permute-start.38 = (bf16[128,1536]{1,0:T(8,128)(2,1)S(1)}, bf16[128,1536]{1,0:T(8,128)(2,1)S(1)}, u32[]{:S(2)}, u32[]{:S(2)}) collective-permute-start(bf16[128,1536]{1,0:T(8,128)(2,1)S(1)} %get-tuple-element.160), channel_id=1, source_target_pairs={{0,1},{1,0},{2,3},{3,2},{4,5},{5,4},{6,7},{7,6},{8,9},{9,8},{10,11... | collective-permute-start | bytes 1179656 | tf_op jit(solution)/shard_map/ppermute | solution.py:193
  77.8 9.4 %collective-permute-start.39 = (bf16[128,1536]{1,0:T(8,128)(2,1)S(1)}, bf16[128,1536]{1,0:T(8,128)(2,1)S(1)}, u32[]{:S(2)}, u32[]{:S(2)}) collective-permute-start(bf16[128,1536]{1,0:T(8,128)(2,1)S(1)} %get-tuple-element.168), channel_id=1, source_target_pairs={{0,1},{1,0},{2,3},{3,2},{4,5},{5,4},{6,7},{7,6},{8,9},{9,8},{10,11... | collective-permute-start | bytes 1179656 | tf_op jit(solution)/shard_map/ppermute | solution.py:193
  78.3 7.4 %collective-permute-start.34 = (bf16[144,768]{1,0:T(8,128)(2,1)S(1)}, bf16[144,768]{1,0:T(8,128)(2,1)S(1)}, u32[]{:S(2)}, u32[]{:S(2)}) collective-permute-start(bf16[144,768]{1,0:T(8,128)(2,1)S(1)} %slice.100), channel_id=1, source_target_pairs={{0,4},{1,5},{4,8},{5,9},{8,12},{9,13},{12,14},{13,15},{14,10},{15,... | collective-permute-start | bytes 663560 | tf_op jit(solution)/shard_map/ppermute | solution.py:196
  80.1 7.1 %collective-permute-start.35 = (bf16[144,768]{1,0:T(8,128)(2,1)S(1)}, bf16[144,768]{1,0:T(8,128)(2,1)S(1)}, u32[]{:S(2)}, u32[]{:S(2)}) collective-permute-start(bf16[144,768]{1,0:T(8,128)(2,1)S(1)} %slice.101), channel_id=1, source_target_pairs={{4,0},{5,1},{8,4},{9,5},{12,8},{13,9},{14,12},{15,13},{10,14},{11,... | collective-permute-start | bytes 663560 | tf_op jit(solution)/shard_map/ppermute | solution.py:199
  87.2 1.5 %collective-permute-start.41 = (bf16[144,768]{1,0:T(8,128)(2,1)S(1)}, bf16[144,768]{1,0:T(8,128)(2,1)S(1)}, u32[]{:S(2)}, u32[]{:S(2)}) collective-permute-start(bf16[144,768]{1,0:T(8,128)(2,1)S(1)} %collective-permute-done.34.refs_0_), channel_id=1, source_target_pairs={{0,1},{1,0},{2,3},{3,2},{4,5},{5,4},{6,7},{7,6},{8,9},{9,8},{10,11... | collective-permute-start | bytes 663560 | tf_op jit(solution)/shard_map/ppermute | solution.py:193
  87.2 1.8 %collective-permute-start.42 = (bf16[144,768]{1,0:T(8,128)(2,1)S(1)}, bf16[144,768]{1,0:T(8,128)(2,1)S(1)}, u32[]{:S(2)}, u32[]{:S(2)}) collective-permute-start(bf16[144,768]{1,0:T(8,128)(2,1)S(1)} %collective-permute-done.35.refs_1_), channel_id=1, source_target_pairs={{0,1},{1,0},{2,3},{3,2},{4,5},{5,4},{6,7},{7,6},{8,9},{9,8},{10,11... | collective-permute-start | bytes 663560 | tf_op jit(solution)/shard_map/ppermute | solution.py:193
  87.7 4.4 %collective-permute-start.40 = (bf16[128,1536]{1,0:T(8,128)(2,1)S(1)}, bf16[128,1536]{1,0:T(8,128)(2,1)S(1)}, u32[]{:S(2)}, u32[]{:S(2)}) collective-permute-start(bf16[128,1536]{1,0:T(8,128)(2,1)S(1)} %get-tuple-element.176), channel_id=1, source_target_pairs={{0,1},{1,0},{2,3},{3,2},{4,5},{5,4},{6,7},{7,6},{8,9},{9,8},{10,11... | collective-permute-start | bytes 1179656 | tf_op jit(solution)/shard_map/ppermute | solution.py:193
  87.8 4.6 %collective-permute-start.47 = (bf16[128,1536]{1,0:T(8,128)(2,1)S(1)}, bf16[128,1536]{1,0:T(8,128)(2,1)S(1)}, u32[]{:S(2)}, u32[]{:S(2)}) collective-permute-start(bf16[128,1536]{1,0:T(8,128)(2,1)S(1)} %get-tuple-element.182), channel_id=1, source_target_pairs={{0,1},{1,0},{2,3},{3,2},{4,5},{5,4},{6,7},{7,6},{8,9},{9,8},{10,11... | collective-permute-start | bytes 1179656 | tf_op jit(solution)/shard_map/ppermute | solution.py:193
  91.3 2.3 %collective-permute-start.46 = (bf16[32,1536]{1,0:T(8,128)(2,1)S(1)}, bf16[32,1536]{1,0:T(8,128)(2,1)S(1)}, u32[]{:S(2)}, u32[]{:S(2)}) collective-permute-start(bf16[32,1536]{1,0:T(8,128)(2,1)S(1)} %get-tuple-element.210), channel_id=1, source_target_pairs={{0,1},{1,0},{2,3},{3,2},{4,5},{5,4},{6,7},{7,6},{8,9},{9,8},{10,11... | collective-permute-start | bytes 294920 | tf_op jit(solution)/shard_map/ppermute | solution.py:193
  91.6 3.0 %collective-permute-start.45 = (bf16[32,1536]{1,0:T(8,128)(2,1)S(1)}, bf16[32,1536]{1,0:T(8,128)(2,1)S(1)}, u32[]{:S(2)}, u32[]{:S(2)}) collective-permute-start(bf16[32,1536]{1,0:T(8,128)(2,1)S(1)} %get-tuple-element.209), channel_id=1, source_target_pairs={{0,1},{1,0},{2,3},{3,2},{4,5},{5,4},{6,7},{7,6},{8,9},{9,8},{10,11... | collective-permute-start | bytes 294920 | tf_op jit(solution)/shard_map/ppermute | solution.py:193
  91.9 2.7 %collective-permute-start.44 = (bf16[32,1536]{1,0:T(8,128)(2,1)S(1)}, bf16[32,1536]{1,0:T(8,128)(2,1)S(1)}, u32[]{:S(2)}, u32[]{:S(2)}) collective-permute-start(bf16[32,1536]{1,0:T(8,128)(2,1)S(1)} %get-tuple-element.211), channel_id=1, source_target_pairs={{0,1},{1,0},{2,3},{3,2},{4,5},{5,4},{6,7},{7,6},{8,9},{9,8},{10,11... | collective-permute-start | bytes 294920 | tf_op jit(solution)/shard_map/ppermute | solution.py:193
  92.1 2.5 %collective-permute-start.43 = (bf16[32,1536]{1,0:T(8,128)(2,1)S(1)}, bf16[32,1536]{1,0:T(8,128)(2,1)S(1)}, u32[]{:S(2)}, u32[]{:S(2)}) collective-permute-start(bf16[32,1536]{1,0:T(8,128)(2,1)S(1)} %get-tuple-element.212), channel_id=1, source_target_pairs={{0,1},{1,0},{2,3},{3,2},{4,5},{5,4},{6,7},{7,6},{8,9},{9,8},{10,11... | collective-permute-start | bytes 294920 | tf_op jit(solution)/shard_map/ppermute | solution.py:193
  92.5 7.1 %collective-permute-start.48 = (bf16[64,1536]{1,0:T(8,128)(2,1)S(1)}, bf16[64,1536]{1,0:T(8,128)(2,1)S(1)}, u32[]{:S(2)}, u32[]{:S(2)}) collective-permute-start(bf16[64,1536]{1,0:T(8,128)(2,1)S(1)} %add_convert_fusion.11), channel_id=1, source_target_pairs={{0,4},{1,5},{4,8},{5,9},{8,12},{9,13},{12,14},{13,15},{14,10},{15,... | collective-permute-start | bytes 589832 | tf_op jit(solution)/shard_map/ppermute | solution.py:196
  93.6 6.7 %collective-permute-start.49 = (bf16[64,1536]{1,0:T(8,128)(2,1)S(1)}, bf16[64,1536]{1,0:T(8,128)(2,1)S(1)}, u32[]{:S(2)}, u32[]{:S(2)}) collective-permute-start(bf16[64,1536]{1,0:T(8,128)(2,1)S(1)} %add_convert_fusion.10), channel_id=1, source_target_pairs={{4,0},{5,1},{8,4},{9,5},{12,8},{13,9},{14,12},{15,13},{10,14},{11,... | collective-permute-start | bytes 589832 | tf_op jit(solution)/shard_map/ppermute | solution.py:199
  100.3 7.8 %collective-permute-start.50 = (bf16[64,1536]{1,0:T(8,128)(2,1)S(1)}, bf16[64,1536]{1,0:T(8,128)(2,1)S(1)}, u32[]{:S(2)}, u32[]{:S(2)}) collective-permute-start(bf16[64,1536]{1,0:T(8,128)(2,1)S(1)} %get-tuple-element.185), channel_id=1, source_target_pairs={{0,4},{1,5},{4,8},{5,9},{8,12},{9,13},{12,14},{13,15},{14,10},{15,... | collective-permute-start | bytes 589832 | tf_op jit(solution)/shard_map/ppermute | solution.py:196
  100.9 7.8 %collective-permute-start.51 = (bf16[64,1536]{1,0:T(8,128)(2,1)S(1)}, bf16[64,1536]{1,0:T(8,128)(2,1)S(1)}, u32[]{:S(2)}, u32[]{:S(2)}) collective-permute-start(bf16[64,1536]{1,0:T(8,128)(2,1)S(1)} %get-tuple-element.186), channel_id=1, source_target_pairs={{4,0},{5,1},{8,4},{9,5},{12,8},{13,9},{14,12},{15,13},{10,14},{11,... | collective-permute-start | bytes 589832 | tf_op jit(solution)/shard_map/ppermute | solution.py:199
  102.5 9.9 %collective-permute-start.54 = (bf16[64,1536]{1,0:T(8,128)(2,1)S(1)}, bf16[64,1536]{1,0:T(8,128)(2,1)S(1)}, u32[]{:S(2)}, u32[]{:S(2)}) collective-permute-start(bf16[64,1536]{1,0:T(8,128)(2,1)S(1)} %get-tuple-element.193), channel_id=1, source_target_pairs={{0,4},{1,5},{4,8},{5,9},{8,12},{9,13},{12,14},{13,15},{14,10},{15,... | collective-permute-start | bytes 589832 | tf_op jit(solution)/shard_map/ppermute | solution.py:196
  103.2 9.7 %collective-permute-start.55 = (bf16[64,1536]{1,0:T(8,128)(2,1)S(1)}, bf16[64,1536]{1,0:T(8,128)(2,1)S(1)}, u32[]{:S(2)}, u32[]{:S(2)}) collective-permute-start(bf16[64,1536]{1,0:T(8,128)(2,1)S(1)} %get-tuple-element.194), channel_id=1, source_target_pairs={{4,0},{5,1},{8,4},{9,5},{12,8},{13,9},{14,12},{15,13},{10,14},{11,... | collective-permute-start | bytes 589832 | tf_op jit(solution)/shard_map/ppermute | solution.py:199
  108.8 5.8 %collective-permute-start.52 = (bf16[64,1536]{1,0:T(8,128)(2,1)S(1)}, bf16[64,1536]{1,0:T(8,128)(2,1)S(1)}, u32[]{:S(2)}, u32[]{:S(2)}) collective-permute-start(bf16[64,1536]{1,0:T(8,128)(2,1)S(1)} %add_convert_fusion.9), channel_id=1, source_target_pairs={{0,4},{1,5},{4,8},{5,9},{8,12},{9,13},{12,14},{13,15},{14,10},{15,... | collective-permute-start | bytes 589832 | tf_op jit(solution)/shard_map/ppermute | solution.py:196
  109.3 5.7 %collective-permute-start.53 = (bf16[64,1536]{1,0:T(8,128)(2,1)S(1)}, bf16[64,1536]{1,0:T(8,128)(2,1)S(1)}, u32[]{:S(2)}, u32[]{:S(2)}) collective-permute-start(bf16[64,1536]{1,0:T(8,128)(2,1)S(1)} %add_convert_fusion.8), channel_id=1, source_target_pairs={{4,0},{5,1},{8,4},{9,5},{12,8},{13,9},{14,12},{15,13},{10,14},{11,... | collective-permute-start | bytes 589832 | tf_op jit(solution)/shard_map/ppermute | solution.py:199
  115.1 6.8 %collective-permute-start.56 = (bf16[64,1536]{1,0:T(8,128)(2,1)S(1)}, bf16[64,1536]{1,0:T(8,128)(2,1)S(1)}, u32[]{:S(2)}, u32[]{:S(2)}) collective-permute-start(bf16[64,1536]{1,0:T(8,128)(2,1)S(1)} %add_convert_fusion.5), channel_id=1, source_target_pairs={{0,4},{1,5},{4,8},{5,9},{8,12},{9,13},{12,14},{13,15},{14,10},{15,... | collective-permute-start | bytes 589832 | tf_op jit(solution)/shard_map/ppermute | solution.py:196
  115.7 10.9 %collective-permute-start.59 = (bf16[64,1536]{1,0:T(8,128)(2,1)S(1)}, bf16[64,1536]{1,0:T(8,128)(2,1)S(1)}, u32[]{:S(2)}, u32[]{:S(2)}) collective-permute-start(bf16[64,1536]{1,0:T(8,128)(2,1)S(1)} %add_convert_fusion.2), channel_id=1, source_target_pairs={{4,0},{5,1},{8,4},{9,5},{12,8},{13,9},{14,12},{15,13},{10,14},{11,... | collective-permute-start | bytes 589832 | tf_op jit(solution)/shard_map/ppermute | solution.py:199
  117.2 9.4 %collective-permute-start.60 = (bf16[64,1536]{1,0:T(8,128)(2,1)S(1)}, bf16[64,1536]{1,0:T(8,128)(2,1)S(1)}, u32[]{:S(2)}, u32[]{:S(2)}) collective-permute-start(bf16[64,1536]{1,0:T(8,128)(2,1)S(1)} %add_convert_fusion.3), channel_id=1, source_target_pairs={{0,4},{1,5},{4,8},{5,9},{8,12},{9,13},{12,14},{13,15},{14,10},{15,... | collective-permute-start | bytes 589832 | tf_op jit(solution)/shard_map/ppermute | solution.py:196
  117.7 6.7 %collective-permute-start.57 = (bf16[64,1536]{1,0:T(8,128)(2,1)S(1)}, bf16[64,1536]{1,0:T(8,128)(2,1)S(1)}, u32[]{:S(2)}, u32[]{:S(2)}) collective-permute-start(bf16[64,1536]{1,0:T(8,128)(2,1)S(1)} %add_convert_fusion.4), channel_id=1, source_target_pairs={{4,0},{5,1},{8,4},{9,5},{12,8},{13,9},{14,12},{15,13},{10,14},{11,... | collective-permute-start | bytes 589832 | tf_op jit(solution)/shard_map/ppermute | solution.py:199
  124.5 5.7 %collective-permute-start.58 = (bf16[64,1536]{1,0:T(8,128)(2,1)S(1)}, bf16[64,1536]{1,0:T(8,128)(2,1)S(1)}, u32[]{:S(2)}, u32[]{:S(2)}) collective-permute-start(bf16[64,1536]{1,0:T(8,128)(2,1)S(1)} %add_convert_fusion.1), channel_id=1, source_target_pairs={{0,4},{1,5},{4,8},{5,9},{8,12},{9,13},{12,14},{13,15},{14,10},{15,... | collective-permute-start | bytes 589832 | tf_op jit(solution)/shard_map/ppermute | solution.py:196
  125.3 5.7 %collective-permute-start.61 = (bf16[64,1536]{1,0:T(8,128)(2,1)S(1)}, bf16[64,1536]{1,0:T(8,128)(2,1)S(1)}, u32[]{:S(2)}, u32[]{:S(2)}) collective-permute-start(bf16[64,1536]{1,0:T(8,128)(2,1)S(1)} %add_convert_fusion), channel_id=1, source_target_pairs={{4,0},{5,1},{8,4},{9,5},{12,8},{13,9},{14,12},{15,13},{10,14},{11,... | collective-permute-start | bytes 589832 | tf_op jit(solution)/shard_map/ppermute | solution.py:199
  (6 other events, 27.3 us)

commit v4 on v3

v4 whole, which is shorter than its diff:
```python
import functools

import jax
import jax.numpy as jnp
from jax import lax
from jax.experimental import pallas as pl
from jax.experimental.pallas import tpu as pltpu
from jax.sharding import PartitionSpec as P

BF16 = jnp.bfloat16
F32 = jnp.float32
VMEM = pl.BlockSpec(memory_space=pltpu.VMEM)
SMEM = pl.BlockSpec(memory_space=pltpu.SMEM)
PIECES = 3
dot = functools.partial(jnp.dot, preferred_element_type=F32)


def ring_order(chips):
    return list(range(0, chips, 2)) + list(range(chips - 1, 0, -2))


def together(*arrays):
    return lax.optimization_barrier(arrays)


def call(kernel, out_shape, *args, scratch=(), flops=0, name=None):
    return pl.pallas_call(
        kernel,
        in_specs=[SMEM] + [VMEM] * (len(args) - 1),
        out_specs=jax.tree.map(lambda _: VMEM, out_shape),
        out_shape=out_shape,
        scratch_shapes=list(scratch),
        compiler_params=pltpu.CompilerParams(vmem_limit_bytes=32 * 1024 * 1024),
        cost_estimate=pl.CostEstimate(flops=flops, bytes_accessed=4 * 1024 * 1024, transcendentals=0),
        name=name,
    )(*args)


def prepare_kernel(peers, place, att, att_near, res, res_near, routes, scores, tokens, base, marks):
    core = place[0]
    rows, width = att.shape
    half = width // 2
    mine = pl.ds(pl.multiple_of(core * half, 128), half)
    tokens[:rows, :] = att[...]
    tokens[rows:, :] = att_near[...]
    base[:rows, :] = res[:, mine]
    base[rows:, :] = res_near[:, mine]
    combine = scores[...] / jnp.sum(scores[...], axis=0, keepdims=True)
    lanes = marks.shape[1]
    number = lax.broadcasted_iota(jnp.int32, (lanes, rows), 0)
    spread = jnp.zeros((lanes, rows), F32)
    for k in range(routes.shape[0]):
        left = combine[k : k + 1, :]
        for piece in range(PIECES):
            value = left.astype(BF16).astype(F32)
            spread = spread + jnp.where(routes[k : k + 1, :] + piece * peers == number, value, 0.0)
            left = left - value
    marks[...] = spread.T.astype(BF16)


def pack_kernel(place, gate, up, both):
    both[: gate.shape[0], :] = gate[...]
    both[gate.shape[0] :, :] = up[...]


def stream_kernel(layout, place, tokens, base, *refs):
    *blocks, own_out, near_out, full = refs
    core, expert, group = place[0], place[1], place[2]
    rows, width = tokens.shape[0] // 2, tokens.shape[1]
    half = width // 2
    if layout is None:
        full[...] = blocks[0][:, pl.ds(pl.multiple_of(core * half, 128), half)]
    else:
        chips, where = layout
        depth = blocks[0].shape[0] // 2
        pair = lax.shift_right_logical(expert, 1)
        down = (pair & 1) == 1
        at = jnp.where(down, chips - lax.shift_right_logical(pair + 1, 1), lax.shift_right_logical(pair, 1))
        for block, (offset, other) in zip(blocks, where, strict=True):
            spot = lax.rem(at + (offset + chips), chips)
            source = jnp.where(spot < chips // 2, 2 * spot, 2 * (chips - spot) - 1)
            of_group = group if other == 0 else 1 - group
            sides = (core, 1 - core)
            if block.shape[0] == depth:
                sides = sides[:1] if offset < 0 else sides[1:]
            for index, c in enumerate(sides):
                start = ((of_group * chips + source) * 2 + c) * depth
                full[pl.ds(pl.multiple_of(start, 16), depth), :] = block[index * depth : (index + 1) * depth, :]
    projected = dot(tokens[...], full[...])
    own_out[...] = (base[:rows, :].astype(F32) + projected[:rows]).astype(BF16)
    near_out[...] = (base[rows:, :].astype(F32) + projected[rows:]).astype(BF16)


def join_kernel(place, own, near, marks, *outs):
    core = place[0]
    half = own.shape[1]
    cut = outs[0].shape[0]
    for index, out in enumerate(outs):
        at = slice(index * cut, (index + 1) * cut)
        out[:, pl.ds(pl.multiple_of(core * half, 128), half)] = own[at, :]
        out[:, pl.ds(pl.multiple_of((1 - core) * half, 128), half)] = near[at, :]
        out[:, 2 * half :] = marks[at, :]


def expert_kernel(count, peers, place, *refs):
    blocks, refs = refs[:count], refs[count:]
    weights, outs = (refs[:3], refs[3:6]), refs[6:]
    expert, group = place[1], place[2]
    width = outs[0].shape[1]
    half = width // 2

    def columns(which):
        at = pl.ds(pl.multiple_of(which * half, 128), half)
        return jnp.concatenate([block[:, at] for block in blocks], axis=0)

    first, second = columns(group), columns(1 - group)
    marks = jnp.concatenate([block[:, width:] for block in blocks], axis=0).astype(F32)
    lane = lax.broadcasted_iota(jnp.int32, marks.shape, 1)
    total = None
    for index, (both_a, both_b, down) in enumerate(weights):
        gate_act = dot(first, both_a[:half, :]) + dot(second, both_b[:half, :])
        up_act = dot(first, both_a[half:, :]) + dot(second, both_b[half:, :])
        hidden = (jax.nn.silu(gate_act) * up_act).astype(BF16)
        number = expert if index == 0 else expert ^ 1
        named = lane == number
        for piece in range(1, PIECES):
            named = named | (lane == number + piece * peers)
        weighted = dot(hidden, down[...]) * jnp.sum(jnp.where(named, marks, 0.0), axis=1, keepdims=True)
        total = weighted if total is None else total + weighted
    start = 0
    for out in outs:
        out[...] = total[start : start + out.shape[0]]
        start += out.shape[0]


def final_kernel(place, *refs):
    *parts, gain, out = refs
    rows, width = out.shape
    cut = rows // 2
    for index in range(2):
        stream, mine, a, b = parts[index::2]
        total = stream[:, :width].astype(F32) + mine[...] + (a[...].astype(F32) + b[...].astype(F32))
        scale = lax.rsqrt(jnp.sum(total * total, axis=1, keepdims=True) / width + 1e-06)
        out[index * cut : (index + 1) * cut, :] = (total * scale * gain[...]).astype(BF16)


def body(
    attention,
    residual,
    out_weight,
    gate_weight,
    up_weight,
    down_weight,
    routes,
    router_scores,
    norm_gain,
):
    token_count, width = attention.shape
    half = width // 2
    groups = lax.axis_size("dp")
    peers = lax.axis_size("expert")
    chips = peers // 2
    far = chips // 2
    ring = ring_order(chips)
    forth = [(2 * ring[k] + c, 2 * ring[(k + 1) % chips] + c) for k in range(chips) for c in range(2)]
    back = [(b, a) for a, b in forth]
    across = [(e, e ^ 1) for e in range(peers)]
    group = lax.axis_index("dp")
    expert = lax.axis_index("expert")
    core = expert & 1
    place = jnp.stack([core, expert, group if groups == 2 else jnp.zeros_like(group)]).astype(jnp.int32)

    def swap(x):
        return lax.ppermute(x, "expert", across)

    def go(x):
        return lax.ppermute(x, "expert", forth)

    def come(x):
        return lax.ppermute(x, "expert", back)

    gate, up, down = gate_weight[0], up_weight[0], down_weight[0]
    hidden = gate.shape[1]
    lanes = -(-PIECES * peers // 128) * 128
    tokens, base, marks = call(
        functools.partial(prepare_kernel, peers),
        [
            jax.ShapeDtypeStruct((2 * token_count, width), BF16),
            jax.ShapeDtypeStruct((2 * token_count, half), BF16),
            jax.ShapeDtypeStruct((token_count, lanes), BF16),
        ],
        place,
        attention,
        swap(attention),
        residual,
        swap(residual),
        routes.T,
        router_scores.T,
        name="prepare",
    )
    down_near = swap(down)

    if groups == 2:
        flip = [(0, 1), (1, 0)]

        def columns(which):
            return lax.dynamic_slice(
                out_weight, (0, which * half), (out_weight.shape[0], half), allow_negative_indices=False
            )

        mine = jnp.concatenate([columns(core), swap(columns(1 - core))], axis=0)
        other = lax.ppermute(mine, "dp", flip)
        depth = out_weight.shape[0]
        blocks, layout = [mine, other], [(0, 0), (0, 1)]
        mine_f, mine_b = go(mine), come(mine)
        mine_f, mine_b, other, tokens, base, marks, down_near = together(
            mine_f, mine_b, other, tokens, base, marks, down_near
        )
        other, gate, up = together(other, gate, up)
        both = call(
            pack_kernel, jax.ShapeDtypeStruct((2 * gate.shape[0], hidden), BF16), place, gate, up, name="pack"
        )
        both_far = lax.ppermute(both, "dp", flip)
        both_near = swap(both)
        blocks += [mine_f, mine_b]
        layout += [(-1, 0), (1, 0)]
        other_f = other_b = other
        for step in range(1, far + 1):
            if step < far:
                mine_f = go(mine_f)
                if step == 1:
                    mine_f, both_near = together(mine_f, both_near)
                blocks += [mine_f]
                layout += [(-step - 1, 0)]
                other_f = go(other_f)
                blocks += [other_f]
                layout += [(-step, 1)]
            if step < far - 1:
                mine_b = come(mine_b)
                blocks += [mine_b]
                layout += [(step + 1, 0)]
            other_b = come(other_b)
            blocks += [other_b]
            layout += [(step, 1)]
        layout = (chips, layout)
    else:
        both = call(
            pack_kernel, jax.ShapeDtypeStruct((2 * gate.shape[0], hidden), BF16), place, gate, up, name="pack"
        )
        blocks, layout = [lax.all_gather(out_weight, ("dp", "expert"), axis=0, tiled=True)], None
        both = lax.all_gather(both, "dp", axis=0).reshape(groups, 2, -1, hidden).swapaxes(0, 1)
        both = both.reshape(2, 2, half, hidden).swapaxes(0, 1).reshape(2, 2 * half, hidden)
        both, both_far = both[0], both[1]
        both_near = swap(both)

    own_half, near_half = call(
        functools.partial(stream_kernel, layout),
        [jax.ShapeDtypeStruct((token_count, half), BF16)] * 2,
        place,
        tokens,
        base,
        *blocks,
        scratch=[pltpu.VMEM((width, half), BF16)],
        flops=4 * token_count * width * half,
        name="stream",
    )
    cut = token_count // 2
    stream = call(
        join_kernel,
        [jax.ShapeDtypeStruct((cut, width + lanes), BF16)] * 2,
        place,
        own_half,
        swap(near_half),
        marks,
        name="join",
    )

    def experts(*arrays):
        return call(
            functools.partial(expert_kernel, len(arrays), peers),
            [jax.ShapeDtypeStruct((array.shape[0], width), F32) for array in arrays],
            place,
            *arrays,
            *weights,
            flops=4 * sum(array.shape[0] for array in arrays) * 3 * width * hidden,
            name="experts",
        )

    terms = {}
    rows_at = {(0, 0): stream[0], (0, 1): stream[1]}

    def work(distance):
        offsets = [(offset, part) for offset in (-distance, distance) for part in range(2)]
        if distance == 1:
            offsets += [(0, 0), (0, 1)]
        return dict(zip(offsets, experts(*(rows_at[at] for at in offsets))))

    lead, rest = list(stream), list(stream[::-1])
    for step in range(1, far + 1):
        if step == far:
            lead, done = together(lead, work(far - 2))
            terms.update(done)
        lead = [go(lead[0]), come(lead[1])]
        if step == 1:
            _, both_far = together(lead, both_far)
            weights = (both, both_far, down, both_near, swap(both_far), down_near)
        if step == far:
            lead, done = together(lead, work(far - 1))
            terms.update(done)
            break
        rows_at[-step, 0], rows_at[step, 1] = lead
        if step > 2:
            rest, done = together(rest, work(step - 2))
            terms.update(done)
        rest = [go(rest[0]), come(rest[1])]
        rows_at[-step, 1], rows_at[step, 0] = rest

    def term(offset, part):
        return terms[offset, part]

    ways = ((go, 1, 0), (come, -1, 1))

    def onward(received, left, flipped):
        return together(
            *(
                (term(sign * left, 1 - part if flipped else part) + x.astype(F32)).astype(BF16)
                for (_, sign, part), x in zip(ways, received)
            )
        )

    def send(pair):
        return [move(x) for (move, _, _), x in zip(ways, pair)]

    nearer = send(together(*(term(sign * (far - 1), 1 - part).astype(BF16) for _, sign, part in ways)))
    farther = send(together(*(result.astype(BF16) for result in experts(*lead))))
    for left in range(far - 1, 0, -1):
        if left > 1:
            ready = onward(nearer, left - 1, True)
            farther = together(*onward(farther, left, False), *ready)[:2]
            if left == 2:
                ready = together(*ready, *farther)[:2]
            nearer = send(ready)
        else:
            farther = onward(farther, left, False)
        farther = send(farther)

    return call(
        final_kernel,
        jax.ShapeDtypeStruct((token_count, width), BF16),
        place,
        *stream,
        terms[0, 0],
        terms[0, 1],
        farther[0],
        nearer[0],
        nearer[1],
        farther[1],
        norm_gain[None, :],
        name="final",
    )


def solution(mesh):
    in_specs = (
        P(("dp", "expert"), None),
        P(("dp", "expert"), None),
        P(("dp", "expert"), None),
        P("expert", "dp", None),
        P("expert", "dp", None),
        P("expert", None, None),
        P(("dp", "expert"), None),
        P(("dp", "expert"), None),
        P(),
    )
    out_specs = P(("dp", "expert"), None)
    return jax.shard_map(body, mesh=mesh, in_specs=in_specs, out_specs=out_specs, check_vma=False)
```

time: 133 us -> 122 us (0.917)
  waiting for transfers between devices: 54.9 us -> 48 us
  Pallas kernels: 21.8 us -> 19.6 us
  starting transfers between devices: 50.3 us -> 48.7 us
    ppermute x18 -> x21, waiting for transfers between devices: 32.8 us -> 18.9 us  [go(): return lax.ppermute(x, 'expert', forth)]
    ppermute x18 -> x21, waiting for transfers between devices: 15.2 us -> 21.9 us  [come(): return lax.ppermute(x, 'expert', back)]
    ppermute x18 -> x21, starting transfers between devices: 16 us -> 20.7 us  [come(): return lax.ppermute(x, 'expert', back)]
    ppermute x23 -> x7, starting transfers between devices: 5.75 us -> 1.25 us  [swap(): return lax.ppermute(x, 'expert', across)]
    pallas_call x11 -> x9, Pallas kernels: 21.8 us -> 19.6 us  [call(): pl.pallas_call(kernel, in_specs=[SMEM] + [VMEM] * (len(args) - 1), out_sp...]
    ppermute x2 -> x1, starting transfers between devices: 2.5 us -> 0.57 us  [body(): both_far = lax.ppermute(both, 'dp', flip)]
    ppermute x23 -> x7, waiting for transfers between devices: 1.74 us -> 3.02 us  [swap(): return lax.ppermute(x, 'expert', across)]
    ppermute x2 -> x1, waiting for transfers between devices: 5.13 us -> 4.18 us  [body(): both_far = lax.ppermute(both, 'dp', flip)]
  transfers between devices with their start and end apart: 62 -> 51, of which waited for: 32 -> 32; matrix products, arithmetic and copies ran while one was open for 1% -> 1% of each run, Pallas kernels for 15% -> 14%
where the time goes in v4:
time: 122 us
  starting transfers between devices  48.7 us (40%)
  waiting for transfers between devices  48 us (39%)
  Pallas kernels  19.6 us (16%)
  local copies, waits for them, and re-layouts  4.32 us (4%)
    ppermute x21, starting transfers between devices, go(): return lax.ppermute(x, 'expert', forth)  23.5 us
    ppermute x21, waiting for transfers between devices, come(): return lax.ppermute(x, 'expert', back)  21.9 us
    ppermute x21, starting transfers between devices, come(): return lax.ppermute(x, 'expert', back)  20.7 us
    pallas_call x9, Pallas kernels, call(): pl.pallas_call(kernel, in_specs=[SMEM] + [VMEM] * (len(args) - 1), out_sp...  19.6 us
    ppermute x21, waiting for transfers between devices, go(): return lax.ppermute(x, 'expert', forth)  18.9 us
    ppermute x1, waiting for transfers between devices, body(): both_far = lax.ppermute(both, 'dp', flip)  4.18 us
    unnamed x16, local copies, waits for them, and re-layouts  3.39 us
    ppermute x7, waiting for transfers between devices, swap(): return lax.ppermute(x, 'expert', across)  3.02 us
  transfers between devices with their start and end apart: 51, of which 32 were waited for; matrix products, arithmetic and copies ran while one was open for 1% of the time, Pallas kernels for 14%

profile of v4, /device:TPU:0, one launch (start us, length us, event | category | flops | bytes accessed | tf_op | source)
XLA Modules:
  0.0 121.5 jit_solution(3512668835962354476)
XLA Ops:
  1.0 0.9 constant_dynamic-slice_fusion.1
  2.0 1.6 %collective-permute-done = bf16[48,768]{1,0:T(8,128)(2,1)S(1)} collective-permute-done((bf16[48,768]{1,0:T(8,128)(2,1)S(1)}, bf16[48,768]{1,0:T(8,128)(2,1)S(1)}, u32[]{:S(2)}, u32[]{:S(2)}) %collective-permute-start) | collective-permute-done | bytes 73760 | tf_op jit(solution)/shard_map/ppermute | solution.py:174
  3.6 2.8 %collective-permute-start.3 = (bf16[96,768]{1,0:T(8,128)(2,1)S(1)}, bf16[96,768]{1,0:T(8,128)(2,1)S(1)}, u32[]{:S(2)}, u32[]{:S(2)}) collective-permute-start(bf16[96,768]{1,0:T(8,128)(2,1)S(1)} %pad_maximum_fusion.refs_0_), channel_id=1, source_target_pairs={{0,16},{16,0},{1,17},{17,1},{2,18},{18,2},{3,19},{19,3},{4,20},{20... | collective-permute-start | bytes 442376 | tf_op jit(solution)/shard_map/ppermute | solution.py:212
  6.4 1.6 %collective-permute-start.1 = (bf16[96,768]{1,0:T(8,128)(2,1)S(1)}, bf16[96,768]{1,0:T(8,128)(2,1)}, u32[]{:S(2)}, u32[]{:S(2)}) collective-permute-start(bf16[96,768]{1,0:T(8,128)(2,1)S(1)} %pad_maximum_fusion.refs_0_), channel_id=1, source_target_pairs={{0,4},{1,5},{4,8},{5,9},{8,12},{9,13},{12,14},{13,15},{14,10},{15,... | collective-permute-start | bytes 442376 | tf_op jit(solution)/shard_map/ppermute | solution.py:177
  8.5 1.0 copy-done.3
  9.5 1.0 copy-done.4
  10.5 0.7 copy-done.5
  11.2 0.7 copy-done.6
  11.9 1.5 %prepare.1 = (bf16[256,1536]{1,0:T(8,128)(2,1)S(1)}, bf16[256,768]{1,0:T(8,128)(2,1)S(1)}, bf16[128,128]{1,0:T(8,128)(2,1)S(1)}) custom-call(s32[3]{0:T(128)S(1)} %pad_add_fusion.place, bf16[128,1536]{1,0:T(8,128)(2,1)S(1)} %copy-done.3, bf16[128,1536]{1,0:T(8,128)(2,1)} %collective-permute-done.4.att_near, bf16[128,1536]{1,0:T(8,128)(2,1)S(1)} %copy-done.4, ...), custom_call_target="tpu_custom_call" | custom-call | bytes 4194304 | tf_op jit(solution)/shard_map/prepare/pallas_call | solution.py:27
  14.9 1.4 %collective-permute-start.11 = (bf16[96,768]{1,0:T(8,128)(2,1)S(1)}, bf16[96,768]{1,0:T(8,128)(2,1)S(1)}, u32[]{:S(2)}, u32[]{:S(2)}) collective-permute-start(bf16[96,768]{1,0:T(8,128)(2,1)S(1)} %collective-permute-done.3.refs_1_), channel_id=1, source_target_pairs={{4,0},{5,1},{8,4},{9,5},{12,8},{13,9},{14,12},{15,13},{10,14},{11,... | collective-permute-start | bytes 442376 | tf_op jit(solution)/shard_map/ppermute | solution.py:180
  16.9 1.6 %collective-permute-start.9 = (bf16[96,768]{1,0:T(8,128)(2,1)S(1)}, bf16[96,768]{1,0:T(8,128)(2,1)S(1)}, u32[]{:S(2)}, u32[]{:S(2)}) collective-permute-start(bf16[96,768]{1,0:T(8,128)(2,1)S(1)} %collective-permute-done.3.refs_1_), channel_id=1, source_target_pairs={{0,4},{1,5},{4,8},{5,9},{8,12},{9,13},{12,14},{13,15},{14,10},{15,... | collective-permute-start | bytes 442376 | tf_op jit(solution)/shard_map/ppermute | solution.py:177
  18.5 2.3 %collective-permute-done.11.refs_7_ = bf16[96,768]{1,0:T(8,128)(2,1)S(1)} collective-permute-done((bf16[96,768]{1,0:T(8,128)(2,1)S(1)}, bf16[96,768]{1,0:T(8,128)(2,1)S(1)}, u32[]{:S(2)}, u32[]{:S(2)}) %collective-permute-start.11) | collective-permute-done | bytes 147488 | tf_op jit(solution)/shard_map/ppermute | solution.py:180
  20.8 1.4 %collective-permute-start.15 = (bf16[96,768]{1,0:T(8,128)(2,1)S(1)}, bf16[96,768]{1,0:T(8,128)(2,1)S(1)}, u32[]{:S(2)}, u32[]{:S(2)}) collective-permute-start(bf16[96,768]{1,0:T(8,128)(2,1)S(1)} %collective-permute-done.11.refs_7_), channel_id=1, source_target_pairs={{4,0},{5,1},{8,4},{9,5},{12,8},{13,9},{14,12},{15,13},{10,14},{11,... | collective-permute-start | bytes 442376 | tf_op jit(solution)/shard_map/ppermute | solution.py:180
  22.2 1.0 collective-permute-done.7.refs_4_
  23.2 1.6 %collective-permute-start.10 = (bf16[96,768]{1,0:T(8,128)(2,1)}, bf16[96,768]{1,0:T(8,128)(2,1)S(1)}, u32[]{:S(2)}, u32[]{:S(2)}) collective-permute-start(bf16[96,768]{1,0:T(8,128)(2,1)} %collective-permute-done.2.refs_3_), channel_id=1, source_target_pairs={{4,0},{5,1},{8,4},{9,5},{12,8},{13,9},{14,12},{15,13},{10,14},{11,... | collective-permute-start | bytes 442376 | tf_op jit(solution)/shard_map/ppermute | solution.py:180
  25.9 1.7 %collective-permute-done.15.refs_11_ = bf16[96,768]{1,0:T(8,128)(2,1)S(1)} collective-permute-done((bf16[96,768]{1,0:T(8,128)(2,1)S(1)}, bf16[96,768]{1,0:T(8,128)(2,1)S(1)}, u32[]{:S(2)}, u32[]{:S(2)}) %collective-permute-start.15) | collective-permute-done | bytes 147488 | tf_op jit(solution)/shard_map/ppermute | solution.py:180
  27.6 1.4 %collective-permute-start.18 = (bf16[96,768]{1,0:T(8,128)(2,1)S(1)}, bf16[96,768]{1,0:T(8,128)(2,1)S(1)}, u32[]{:S(2)}, u32[]{:S(2)}) collective-permute-start(bf16[96,768]{1,0:T(8,128)(2,1)S(1)} %collective-permute-done.15.refs_11_), channel_id=1, source_target_pairs={{4,0},{5,1},{8,4},{9,5},{12,8},{13,9},{14,12},{15,13},{10,14},{11,... | collective-permute-start | bytes 442376 | tf_op jit(solution)/shard_map/ppermute | solution.py:180
  29.6 1.1 collective-permute-done.10.refs_6_
  30.7 1.4 %collective-permute-start.14 = (bf16[96,768]{1,0:T(8,128)(2,1)S(1)}, bf16[96,768]{1,0:T(8,128)(2,1)S(1)}, u32[]{:S(2)}, u32[]{:S(2)}) collective-permute-start(bf16[96,768]{1,0:T(8,128)(2,1)S(1)} %collective-permute-done.10.refs_6_), channel_id=1, source_target_pairs={{4,0},{5,1},{8,4},{9,5},{12,8},{13,9},{14,12},{15,13},{10,14},{11,... | collective-permute-start | bytes 442376 | tf_op jit(solution)/shard_map/ppermute | solution.py:180
  32.8 1.5 %collective-permute-done.18.refs_14_ = bf16[96,768]{1,0:T(8,128)(2,1)S(1)} collective-permute-done((bf16[96,768]{1,0:T(8,128)(2,1)S(1)}, bf16[96,768]{1,0:T(8,128)(2,1)S(1)}, u32[]{:S(2)}, u32[]{:S(2)}) %collective-permute-start.18) | collective-permute-done | bytes 147488 | tf_op jit(solution)/shard_map/ppermute | solution.py:180
  34.3 1.4 %collective-permute-start.19 = (bf16[96,768]{1,0:T(8,128)(2,1)S(1)}, bf16[96,768]{1,0:T(8,128)(2,1)S(1)}, u32[]{:S(2)}, u32[]{:S(2)}) collective-permute-start(bf16[96,768]{1,0:T(8,128)(2,1)S(1)} %collective-permute-done.18.refs_14_), channel_id=1, source_target_pairs={{4,0},{5,1},{8,4},{9,5},{12,8},{13,9},{14,12},{15,13},{10,14},{11,... | collective-permute-start | bytes 442376 | tf_op jit(solution)/shard_map/ppermute | solution.py:180
  37.0 1.0 collective-permute-done.17.refs_13_
  37.9 1.5 %collective-permute-done.19.refs_15_ = bf16[96,768]{1,0:T(8,128)(2,1)S(1)} collective-permute-done((bf16[96,768]{1,0:T(8,128)(2,1)S(1)}, bf16[96,768]{1,0:T(8,128)(2,1)S(1)}, u32[]{:S(2)}, u32[]{:S(2)}) %collective-permute-start.19) | collective-permute-done | bytes 147488 | tf_op jit(solution)/shard_map/ppermute | solution.py:180
  39.4 1.4 %collective-permute-done.16.refs_12_ = bf16[96,768]{1,0:T(8,128)(2,1)S(1)} collective-permute-done((bf16[96,768]{1,0:T(8,128)(2,1)S(1)}, bf16[96,768]{1,0:T(8,128)(2,1)S(1)}, u32[]{:S(2)}, u32[]{:S(2)}) %collective-permute-start.16) | collective-permute-done | bytes 147488 | tf_op jit(solution)/shard_map/ppermute | solution.py:177
  40.8 2.0 %stream.1 = (bf16[128,768]{1,0:T(8,128)(2,1)S(1)}, bf16[128,768]{1,0:T(8,128)(2,1)S(1)}) custom-call(s32[3]{0:T(128)S(1)} %pad_add_fusion.place, bf16[256,1536]{1,0:T(8,128)(2,1)S(1)} %get-tuple-element.84.tokens, bf16[256,768]{1,0:T(8,128)(2,1)S(1)} %get-tuple-element.85.base, bf16[96,768]{1,0:T(8,128)(2,1)S(1)} %pad_maximum_fusion.refs_0_, ...), custom_call_target="tpu_custom_call" | custom-call | flops 603979776 | bytes 4194304 | tf_op jit(solution)/shard_map/stream/pallas_call | solution.py:27
  42.8 1.4 %collective-permute-done.20.near = bf16[128,768]{1,0:T(8,128)(2,1)S(1)} collective-permute-done((bf16[128,768]{1,0:T(8,128)(2,1)S(1)}, bf16[128,768]{1,0:T(8,128)(2,1)S(1)}, u32[]{:S(2)}, u32[]{:S(2)}) %collective-permute-start.20) | collective-permute-done | bytes 196640 | tf_op jit(solution)/shard_map/ppermute | solution.py:174
  44.9 0.7 collective-permute-start.25
  45.6 1.4 %collective-permute-start.26 = (bf16[64,1664]{1,0:T(8,128)(2,1)S(1)}, bf16[64,1664]{1,0:T(8,128)(2,1)S(1)}, u32[]{:S(2)}, u32[]{:S(2)}) collective-permute-start(bf16[64,1664]{1,0:T(8,128)(2,1)S(1)} %get-tuple-element.97.refs_5_.refs_1_), channel_id=1, source_target_pairs={{4,0},{5,1},{8,4},{9,5},{12,8},{13,9},{14,12},{15,13},{10,14},{11,... | collective-permute-start | bytes 638984 | tf_op jit(solution)/shard_map/ppermute | solution.py:180
  46.9 4.2 %collective-permute-done.27.refs_7_.refs_5_.refs_3_ = bf16[1536,512]{1,0:T(8,128)(2,1)S(1)} collective-permute-done((bf16[1536,512]{1,0:T(8,128)(2,1)S(1)}, bf16[1536,512]{1,0:T(8,128)(2,1)S(1)}, u32[]{:S(2)}, u32[]{:S(2)}) %collective-permute-start.27) | collective-permute-done | bytes 1572896 | tf_op jit(solution)/shard_map/ppermute | solution.py:223
  51.1 1.1 collective-permute-done.25.refs_0_
  52.6 1.6 %collective-permute-start.21 = (bf16[64,1664]{1,0:T(8,128)(2,1)S(1)}, bf16[64,1664]{1,0:T(8,128)(2,1)S(1)}, u32[]{:S(2)}, u32[]{:S(2)}) collective-permute-start(bf16[64,1664]{1,0:T(8,128)(2,1)S(1)} %get-tuple-element.97.refs_5_.refs_1_), channel_id=1, source_target_pairs={{0,4},{1,5},{4,8},{5,9},{8,12},{9,13},{12,14},{13,15},{14,10},{15,... | collective-permute-start | bytes 638984 | tf_op jit(solution)/shard_map/ppermute | solution.py:177
  54.6 1.6 %collective-permute-start.29 = (bf16[64,1664]{1,0:T(8,128)(2,1)S(1)}, bf16[64,1664]{1,0:T(8,128)(2,1)S(1)}, u32[]{:S(2)}, u32[]{:S(2)}) collective-permute-start(bf16[64,1664]{1,0:T(8,128)(2,1)S(1)} %collective-permute-done.25.refs_0_), channel_id=1, source_target_pairs={{0,4},{1,5},{4,8},{5,9},{8,12},{9,13},{12,14},{13,15},{14,10},{15,... | collective-permute-start | bytes 638984 | tf_op jit(solution)/shard_map/ppermute | solution.py:177
  56.6 4.0 %collective-permute-done.21.refs_1_ = bf16[64,1664]{1,0:T(8,128)(2,1)S(1)} collective-permute-done((bf16[64,1664]{1,0:T(8,128)(2,1)S(1)}, bf16[64,1664]{1,0:T(8,128)(2,1)S(1)}, u32[]{:S(2)}, u32[]{:S(2)}) %collective-permute-start.21) | collective-permute-done | bytes 213024 | tf_op jit(solution)/shard_map/ppermute | solution.py:177
  60.6 1.6 %collective-permute-start.22 = (bf16[64,1664]{1,0:T(8,128)(2,1)S(1)}, bf16[64,1664]{1,0:T(8,128)(2,1)S(1)}, u32[]{:S(2)}, u32[]{:S(2)}) collective-permute-start(bf16[64,1664]{1,0:T(8,128)(2,1)S(1)} %collective-permute-done.21.refs_1_), channel_id=1, source_target_pairs={{0,4},{1,5},{4,8},{5,9},{8,12},{9,13},{12,14},{13,15},{14,10},{15,... | collective-permute-start | bytes 638984 | tf_op jit(solution)/shard_map/ppermute | solution.py:177
  62.7 2.5 %collective-permute-done.29.refs_0_ = bf16[64,1664]{1,0:T(8,128)(2,1)S(1)} collective-permute-done((bf16[64,1664]{1,0:T(8,128)(2,1)S(1)}, bf16[64,1664]{1,0:T(8,128)(2,1)S(1)}, u32[]{:S(2)}, u32[]{:S(2)}) %collective-permute-start.29) | collective-permute-done | bytes 213024 | tf_op jit(solution)/shard_map/ppermute | solution.py:177
  65.2 1.6 %collective-permute-start.30 = (bf16[64,1664]{1,0:T(8,128)(2,1)S(1)}, bf16[64,1664]{1,0:T(8,128)(2,1)S(1)}, u32[]{:S(2)}, u32[]{:S(2)}) collective-permute-start(bf16[64,1664]{1,0:T(8,128)(2,1)S(1)} %collective-permute-done.29.refs_0_), channel_id=1, source_target_pairs={{0,4},{1,5},{4,8},{5,9},{8,12},{9,13},{12,14},{13,15},{14,10},{15,... | collective-permute-start | bytes 638984 | tf_op jit(solution)/shard_map/ppermute | solution.py:177
  67.3 4.5 %experts.4 = (f32[64,1536]{1,0:T(8,128)S(1)}, f32[64,1536]{1,0:T(8,128)S(1)}, f32[64,1536]{1,0:T(8,128)S(1)}, f32[64,1536]{1,0:T(8,128)S(1)}, f32[64,1536]{1,0:T(8,128)S(1)}, /*index=5*/f32[64,1536]{1,0:T(8,128)S(1)}) custom-call(s32[3]{0:T(128)S(1)} %pad_add_fusion.place, bf16[64,1664]{1,0:T(8,128)(2,1)S(1)} %collective-permute-done.25.refs_0_, ...), custom_call_target="tpu_custom_call" | custom-call | flops 3623878656 | bytes 4194304 | tf_op jit(solution)/shard_map/experts/pallas_call | solution.py:27
  71.8 1.6 %collective-permute-start.35 = (bf16[64,1664]{1,0:T(8,128)(2,1)S(1)}, bf16[64,1664]{1,0:T(8,128)(2,1)S(1)}, u32[]{:S(2)}, u32[]{:S(2)}) collective-permute-start(bf16[64,1664]{1,0:T(8,128)(2,1)S(1)} %collective-permute-done.22.refs_1_), channel_id=1, source_target_pairs={{0,4},{1,5},{4,8},{5,9},{8,12},{9,13},{12,14},{13,15},{14,10},{15,... | collective-permute-start | bytes 638984 | tf_op jit(solution)/shard_map/ppermute | solution.py:177
  73.9 3.3 %experts.5 = (f32[64,1536]{1,0:T(8,128)S(1)}, f32[64,1536]{1,0:T(8,128)S(1)}, f32[64,1536]{1,0:T(8,128)S(1)}, f32[64,1536]{1,0:T(8,128)S(1)}) custom-call(s32[3]{0:T(128)S(1)} %pad_add_fusion.place, bf16[64,1664]{1,0:T(8,128)(2,1)S(1)} %collective-permute-done.29.refs_0_, bf16[64,1664]{1,0:T(8,128)(2,1)S(1)} %collective-permute-done.22.refs_1_, ...), custom_call_target="tpu_custom_call" | custom-call | flops 2415919104 | bytes 4194304 | tf_op jit(solution)/shard_map/experts/pallas_call | solution.py:27
  77.2 1.6 %collective-permute-start.33 = (bf16[64,1664]{1,0:T(8,128)(2,1)S(1)}, bf16[64,1664]{1,0:T(8,128)(2,1)S(1)}, u32[]{:S(2)}, u32[]{:S(2)}) collective-permute-start(bf16[64,1664]{1,0:T(8,128)(2,1)S(1)} %collective-permute-done.30.refs_0_), channel_id=1, source_target_pairs={{0,4},{1,5},{4,8},{5,9},{8,12},{9,13},{12,14},{13,15},{14,10},{15,... | collective-permute-start | bytes 638984 | tf_op jit(solution)/shard_map/ppermute | solution.py:177
  79.3 0.8 collective-permute-done.36.refs_2_
  80.2 3.3 %experts.6 = (f32[64,1536]{1,0:T(8,128)S(1)}, f32[64,1536]{1,0:T(8,128)S(1)}, f32[64,1536]{1,0:T(8,128)S(1)}, f32[64,1536]{1,0:T(8,128)S(1)}) custom-call(s32[3]{0:T(128)S(1)} %pad_add_fusion.place, bf16[64,1664]{1,0:T(8,128)(2,1)S(1)} %collective-permute-done.30.refs_0_, bf16[64,1664]{1,0:T(8,128)(2,1)S(1)} %collective-permute-done.35.refs_1_, ...), custom_call_target="tpu_custom_call" | custom-call | flops 2415919104 | bytes 4194304 | tf_op jit(solution)/shard_map/experts/pallas_call | solution.py:27
  83.5 1.2 collective-permute-done.34.refs_1_
  85.3 1.6 %collective-permute-start.39 = (bf16[64,1536]{1,0:T(8,128)(2,1)S(1)}, bf16[64,1536]{1,0:T(8,128)(2,1)S(1)}, u32[]{:S(2)}, u32[]{:S(2)}) collective-permute-start(bf16[64,1536]{1,0:T(8,128)(2,1)S(1)} %convert_element_type.78), channel_id=1, source_target_pairs={{0,4},{1,5},{4,8},{5,9},{8,12},{9,13},{12,14},{13,15},{14,10},{15,... | collective-permute-start | bytes 589832 | tf_op jit(solution)/shard_map/ppermute | solution.py:177
  86.9 2.2 %experts.7 = (f32[64,1536]{1,0:T(8,128)S(1)}, f32[64,1536]{1,0:T(8,128)S(1)}) custom-call(s32[3]{0:T(128)S(1)} %pad_add_fusion.place, bf16[64,1664]{1,0:T(8,128)(2,1)S(1)} %collective-permute-done.33.refs_0_, bf16[64,1664]{1,0:T(8,128)(2,1)S(1)} %collective-permute-done.34.refs_1_, bf16[1536,512]{1,0:T(8,128)(2,1)S(1)} %pack.1.refs_6_.refs_4_.refs_2_, ...), custom_call_target="tpu_custom_call" | custom-call | flops 1207959552 | bytes 4194304 | tf_op jit(solution)/shard_map/experts/pallas_call | solution.py:27
  89.6 1.6 %collective-permute-start.37 = (bf16[64,1536]{1,0:T(8,128)(2,1)S(1)}, bf16[64,1536]{1,0:T(8,128)(2,1)S(1)}, u32[]{:S(2)}, u32[]{:S(2)}) collective-permute-start(bf16[64,1536]{1,0:T(8,128)(2,1)S(1)} %convert_element_type.72), channel_id=1, source_target_pairs={{0,4},{1,5},{4,8},{5,9},{8,12},{9,13},{12,14},{13,15},{14,10},{15,... | collective-permute-start | bytes 589832 | tf_op jit(solution)/shard_map/ppermute | solution.py:177
  91.2 1.1 collective-permute-done.40
  93.0 1.5 %collective-permute-start.44 = (bf16[64,1536]{1,0:T(8,128)(2,1)S(1)}, bf16[64,1536]{1,0:T(8,128)(2,1)S(1)}, u32[]{:S(2)}, u32[]{:S(2)}) collective-permute-start(bf16[64,1536]{1,0:T(8,128)(2,1)S(1)} %add_convert_fusion.6), channel_id=1, source_target_pairs={{4,0},{5,1},{8,4},{9,5},{12,8},{13,9},{14,12},{15,13},{10,14},{11,... | collective-permute-start | bytes 589832 | tf_op jit(solution)/shard_map/ppermute | solution.py:180
  95.1 1.9 %collective-permute-done.38 = bf16[64,1536]{1,0:T(8,128)(2,1)S(1)} collective-permute-done((bf16[64,1536]{1,0:T(8,128)(2,1)S(1)}, bf16[64,1536]{1,0:T(8,128)(2,1)S(1)}, u32[]{:S(2)}, u32[]{:S(2)}) %collective-permute-start.38) | collective-permute-done | bytes 196640 | tf_op jit(solution)/shard_map/ppermute | solution.py:180
  97.5 1.3 %collective-permute-start.42 = (bf16[64,1536]{1,0:T(8,128)(2,1)S(1)}, bf16[64,1536]{1,0:T(8,128)(2,1)S(1)}, u32[]{:S(2)}, u32[]{:S(2)}) collective-permute-start(bf16[64,1536]{1,0:T(8,128)(2,1)S(1)} %add_convert_fusion.8), channel_id=1, source_target_pairs={{4,0},{5,1},{8,4},{9,5},{12,8},{13,9},{14,12},{15,13},{10,14},{11,... | collective-permute-start | bytes 589832 | tf_op jit(solution)/shard_map/ppermute | solution.py:180
  98.8 0.8 collective-permute-start.41
  99.6 1.5 %collective-permute-done.44 = bf16[64,1536]{1,0:T(8,128)(2,1)S(1)} collective-permute-done((bf16[64,1536]{1,0:T(8,128)(2,1)S(1)}, bf16[64,1536]{1,0:T(8,128)(2,1)S(1)}, u32[]{:S(2)}, u32[]{:S(2)}) %collective-permute-start.44) | collective-permute-done | bytes 196640 | tf_op jit(solution)/shard_map/ppermute | solution.py:180
  101.5 1.7 %collective-permute-done.42 = bf16[64,1536]{1,0:T(8,128)(2,1)S(1)} collective-permute-done((bf16[64,1536]{1,0:T(8,128)(2,1)S(1)}, bf16[64,1536]{1,0:T(8,128)(2,1)S(1)}, u32[]{:S(2)}, u32[]{:S(2)}) %collective-permute-start.42) | collective-permute-done | bytes 196640 | tf_op jit(solution)/shard_map/ppermute | solution.py:180
  103.3 1.2 collective-permute-done.41
  104.5 1.6 %collective-permute-start.46 = (bf16[64,1536]{1,0:T(8,128)(2,1)S(1)}, bf16[64,1536]{1,0:T(8,128)(2,1)S(1)}, u32[]{:S(2)}, u32[]{:S(2)}) collective-permute-start(bf16[64,1536]{1,0:T(8,128)(2,1)S(1)} %add_convert_fusion.4), channel_id=1, source_target_pairs={{4,0},{5,1},{8,4},{9,5},{12,8},{13,9},{14,12},{15,13},{10,14},{11,... | collective-permute-start | bytes 589832 | tf_op jit(solution)/shard_map/ppermute | solution.py:180
  106.6 0.8 collective-permute-start.48
  107.4 1.2 %collective-permute-start.49 = (bf16[64,1536]{1,0:T(8,128)(2,1)S(1)}, bf16[64,1536]{1,0:T(8,128)(2,1)S(1)}, u32[]{:S(2)}, u32[]{:S(2)}) collective-permute-start(bf16[64,1536]{1,0:T(8,128)(2,1)S(1)} %add_convert_fusion.2), channel_id=1, source_target_pairs={{4,0},{5,1},{8,4},{9,5},{12,8},{13,9},{14,12},{15,13},{10,14},{11,... | collective-permute-start | bytes 589832 | tf_op jit(solution)/shard_map/ppermute | solution.py:180
  108.6 3.4 %collective-permute-done.46 = bf16[64,1536]{1,0:T(8,128)(2,1)S(1)} collective-permute-done((bf16[64,1536]{1,0:T(8,128)(2,1)S(1)}, bf16[64,1536]{1,0:T(8,128)(2,1)S(1)}, u32[]{:S(2)}, u32[]{:S(2)}) %collective-permute-start.46) | collective-permute-done | bytes 196640 | tf_op jit(solution)/shard_map/ppermute | solution.py:180
  112.0 1.2 %collective-permute-done.45 = bf16[64,1536]{1,0:T(8,128)(2,1)S(1)} collective-permute-done((bf16[64,1536]{1,0:T(8,128)(2,1)S(1)}, bf16[64,1536]{1,0:T(8,128)(2,1)S(1)}, u32[]{:S(2)}, u32[]{:S(2)}) %collective-permute-start.45) | collective-permute-done | bytes 196640 | tf_op jit(solution)/shard_map/ppermute | solution.py:177
  113.3 0.9 collective-permute-start.47
  114.2 1.2 collective-permute-start.50
  115.4 3.6 %collective-permute-done.47.refs_4_ = bf16[64,1536]{1,0:T(8,128)(2,1)S(1)} collective-permute-done((bf16[64,1536]{1,0:T(8,128)(2,1)S(1)}, bf16[64,1536]{1,0:T(8,128)(2,1)S(1)}, u32[]{:S(2)}, u32[]{:S(2)}) %collective-permute-start.47) | collective-permute-done | bytes 196640 | tf_op jit(solution)/shard_map/ppermute | solution.py:177
  119.0 0.9 collective-permute-done.50.refs_7_
  119.9 1.6 %final.1 = bf16[128,1536]{1,0:T(8,128)(2,1)} custom-call(s32[3]{0:T(128)S(1)} %pad_add_fusion.place, bf16[64,1664]{1,0:T(8,128)(2,1)S(1)} %get-tuple-element.96.refs_4_.refs_0_, bf16[64,1664]{1,0:T(8,128)(2,1)S(1)} %get-tuple-element.97.refs_5_.refs_1_, f32[64,1536]{1,0:T(8,128)S(1)} %get-tuple-element.107.refs_2_, ...), custom_call_target="tpu_custom_call" | custom-call | bytes 4194304 | tf_op jit(solution)/shard_map/final/pallas_call | solution.py:27
  (81 shorter events, 15.4 us)
Async XLA Ops:
  0.0 13.6 %copy-start.1 = (bf16[1,768,512]{2,1,0:T(8,128)(2,1)S(1)}, bf16[1,768,512]{2,1,0:T(8,128)(2,1)}, u32[]{:S(2)}) copy-start(bf16[1,768,512]{2,1,0:T(8,128)(2,1)} %param.12) | copy-start | bytes 2359300
  0.0 13.6 %copy-start.2 = (bf16[1,768,512]{2,1,0:T(8,128)(2,1)S(1)}, bf16[1,768,512]{2,1,0:T(8,128)(2,1)}, u32[]{:S(2)}) copy-start(bf16[1,768,512]{2,1,0:T(8,128)(2,1)} %param.13) | copy-start | bytes 2359300
  0.0 13.6 %collective-permute-start.6 = (bf16[512,1536]{1,0:T(8,128)(2,1)}, bf16[512,1536]{1,0:T(8,128)(2,1)S(1)}, u32[]{:S(2)}, u32[]{:S(2)}) collective-permute-start(bf16[512,1536]{1,0:T(8,128)(2,1)} %bitcast.8), channel_id=1, source_target_pairs={{0,1},{1,0},{2,3},{3,2},{4,5},{5,4},{6,7},{7,6},{8,9},{9,8},{10,11... | collective-permute-start | bytes 4718600 | tf_op jit(solution)/shard_map/ppermute | solution.py:174
  0.5 7.5 %collective-permute-start.4 = (bf16[128,1536]{1,0:T(8,128)(2,1)}, bf16[128,1536]{1,0:T(8,128)(2,1)}, u32[]{:S(2)}, u32[]{:S(2)}) collective-permute-start(bf16[128,1536]{1,0:T(8,128)(2,1)} %att.1), channel_id=1, source_target_pairs={{0,1},{1,0},{2,3},{3,2},{4,5},{5,4},{6,7},{7,6},{8,9},{9,8},{10,11... | collective-permute-start | bytes 1179656 | tf_op jit(solution)/shard_map/ppermute | solution.py:174
  0.5 8.0 %collective-permute-start.5 = (bf16[128,1536]{1,0:T(8,128)(2,1)}, bf16[128,1536]{1,0:T(8,128)(2,1)}, u32[]{:S(2)}, u32[]{:S(2)}) collective-permute-start(bf16[128,1536]{1,0:T(8,128)(2,1)} %res.1), channel_id=1, source_target_pairs={{0,1},{1,0},{2,3},{3,2},{4,5},{5,4},{6,7},{7,6},{8,9},{9,8},{10,11... | collective-permute-start | bytes 1179656 | tf_op jit(solution)/shard_map/ppermute | solution.py:174
  1.9 1.7 %collective-permute-start = (bf16[48,768]{1,0:T(8,128)(2,1)S(1)}, bf16[48,768]{1,0:T(8,128)(2,1)S(1)}, u32[]{:S(2)}, u32[]{:S(2)}) collective-permute-start(bf16[48,768]{1,0:T(8,128)(2,1)S(1)} %get-tuple-element.158), channel_id=1, source_target_pairs={{0,1},{1,0},{2,3},{3,2},{4,5},{5,4},{6,7},{7,6},{8,9},{9,8},{10,11... | collective-permute-start | bytes 221192 | tf_op jit(solution)/shard_map/ppermute | solution.py:174
  3.6 9.7 %collective-permute-start.3 = (bf16[96,768]{1,0:T(8,128)(2,1)S(1)}, bf16[96,768]{1,0:T(8,128)(2,1)S(1)}, u32[]{:S(2)}, u32[]{:S(2)}) collective-permute-start(bf16[96,768]{1,0:T(8,128)(2,1)S(1)} %pad_maximum_fusion.refs_0_), channel_id=1, source_target_pairs={{0,16},{16,0},{1,17},{17,1},{2,18},{18,2},{3,19},{19,3},{4,20},{20... | collective-permute-start | bytes 442376 | tf_op jit(solution)/shard_map/ppermute | solution.py:212
  6.4 7.0 %collective-permute-start.1 = (bf16[96,768]{1,0:T(8,128)(2,1)S(1)}, bf16[96,768]{1,0:T(8,128)(2,1)}, u32[]{:S(2)}, u32[]{:S(2)}) collective-permute-start(bf16[96,768]{1,0:T(8,128)(2,1)S(1)} %pad_maximum_fusion.refs_0_), channel_id=1, source_target_pairs={{0,4},{1,5},{4,8},{5,9},{8,12},{9,13},{12,14},{13,15},{14,10},{15,... | collective-permute-start | bytes 442376 | tf_op jit(solution)/shard_map/ppermute | solution.py:177
  8.0 5.6 %collective-permute-start.2 = (bf16[96,768]{1,0:T(8,128)(2,1)S(1)}, bf16[96,768]{1,0:T(8,128)(2,1)}, u32[]{:S(2)}, u32[]{:S(2)}) collective-permute-start(bf16[96,768]{1,0:T(8,128)(2,1)S(1)} %pad_maximum_fusion.refs_0_), channel_id=1, source_target_pairs={{4,0},{5,1},{8,4},{9,5},{12,8},{13,9},{14,12},{15,13},{10,14},{11,... | collective-permute-start | bytes 442376 | tf_op jit(solution)/shard_map/ppermute | solution.py:180
  8.5 1.0 copy-start.3
  9.5 1.0 copy-start.4
  10.5 0.7 copy-start.5
  11.2 0.7 copy-start.6
  14.2 53.1 %copy-start = (bf16[1,512,1536]{2,1,0:T(8,128)(2,1)S(1)}, bf16[1,512,1536]{2,1,0:T(8,128)(2,1)}, u32[]{:S(2)}) copy-start(bf16[1,512,1536]{2,1,0:T(8,128)(2,1)} %param.14) | copy-start | bytes 4718596
  14.2 14.7 %collective-permute-start.8 = (bf16[1536,512]{1,0:T(8,128)(2,1)S(1)}, bf16[1536,512]{1,0:T(8,128)(2,1)S(1)}, u32[]{:S(2)}, u32[]{:S(2)}) collective-permute-start(bf16[1536,512]{1,0:T(8,128)(2,1)S(1)} %pack.1.refs_6_.refs_4_.refs_2_), channel_id=1, source_target_pairs={{0,1},{1,0},{2,3},{3,2},{4,5},{5,4},{6,7},{7,6},{8,9},{9,8},{10,11... | collective-permute-start | bytes 4718600 | tf_op jit(solution)/shard_map/ppermute | solution.py:174
  14.3 36.8 %collective-permute-start.27 = (bf16[1536,512]{1,0:T(8,128)(2,1)S(1)}, bf16[1536,512]{1,0:T(8,128)(2,1)S(1)}, u32[]{:S(2)}, u32[]{:S(2)}) collective-permute-start(bf16[1536,512]{1,0:T(8,128)(2,1)S(1)} %pack.1.refs_6_.refs_4_.refs_2_), channel_id=1, source_target_pairs={{0,16},{16,0},{1,17},{17,1},{2,18},{18,2},{3,19},{19,3},{4,20},{20... | collective-permute-start | bytes 4718600 | tf_op jit(solution)/shard_map/ppermute | solution.py:223
  14.9 5.9 %collective-permute-start.11 = (bf16[96,768]{1,0:T(8,128)(2,1)S(1)}, bf16[96,768]{1,0:T(8,128)(2,1)S(1)}, u32[]{:S(2)}, u32[]{:S(2)}) collective-permute-start(bf16[96,768]{1,0:T(8,128)(2,1)S(1)} %collective-permute-done.3.refs_1_), channel_id=1, source_target_pairs={{4,0},{5,1},{8,4},{9,5},{12,8},{13,9},{14,12},{15,13},{10,14},{11,... | collective-permute-start | bytes 442376 | tf_op jit(solution)/shard_map/ppermute | solution.py:180
  16.2 6.9 %collective-permute-start.7 = (bf16[96,768]{1,0:T(8,128)(2,1)}, bf16[96,768]{1,0:T(8,128)(2,1)S(1)}, u32[]{:S(2)}, u32[]{:S(2)}) collective-permute-start(bf16[96,768]{1,0:T(8,128)(2,1)} %collective-permute-done.1.refs_2_), channel_id=1, source_target_pairs={{0,4},{1,5},{4,8},{5,9},{8,12},{9,13},{12,14},{13,15},{14,10},{15,... | collective-permute-start | bytes 442376 | tf_op jit(solution)/shard_map/ppermute | solution.py:177
  16.9 8.3 %collective-permute-start.9 = (bf16[96,768]{1,0:T(8,128)(2,1)S(1)}, bf16[96,768]{1,0:T(8,128)(2,1)S(1)}, u32[]{:S(2)}, u32[]{:S(2)}) collective-permute-start(bf16[96,768]{1,0:T(8,128)(2,1)S(1)} %collective-permute-done.3.refs_1_), channel_id=1, source_target_pairs={{0,4},{1,5},{4,8},{5,9},{8,12},{9,13},{12,14},{13,15},{14,10},{15,... | collective-permute-start | bytes 442376 | tf_op jit(solution)/shard_map/ppermute | solution.py:177
  20.8 6.8 %collective-permute-start.15 = (bf16[96,768]{1,0:T(8,128)(2,1)S(1)}, bf16[96,768]{1,0:T(8,128)(2,1)S(1)}, u32[]{:S(2)}, u32[]{:S(2)}) collective-permute-start(bf16[96,768]{1,0:T(8,128)(2,1)S(1)} %collective-permute-done.11.refs_7_), channel_id=1, source_target_pairs={{4,0},{5,1},{8,4},{9,5},{12,8},{13,9},{14,12},{15,13},{10,14},{11,... | collective-permute-start | bytes 442376 | tf_op jit(solution)/shard_map/ppermute | solution.py:180
  23.2 7.6 %collective-permute-start.10 = (bf16[96,768]{1,0:T(8,128)(2,1)}, bf16[96,768]{1,0:T(8,128)(2,1)S(1)}, u32[]{:S(2)}, u32[]{:S(2)}) collective-permute-start(bf16[96,768]{1,0:T(8,128)(2,1)} %collective-permute-done.2.refs_3_), channel_id=1, source_target_pairs={{4,0},{5,1},{8,4},{9,5},{12,8},{13,9},{14,12},{15,13},{10,14},{11,... | collective-permute-start | bytes 442376 | tf_op jit(solution)/shard_map/ppermute | solution.py:180
  25.3 6.9 %collective-permute-start.13 = (bf16[96,768]{1,0:T(8,128)(2,1)S(1)}, bf16[96,768]{1,0:T(8,128)(2,1)S(1)}, u32[]{:S(2)}, u32[]{:S(2)}) collective-permute-start(bf16[96,768]{1,0:T(8,128)(2,1)S(1)} %collective-permute-done.9.refs_5_), channel_id=1, source_target_pairs={{0,4},{1,5},{4,8},{5,9},{8,12},{9,13},{12,14},{13,15},{14,10},{15,... | collective-permute-start | bytes 442376 | tf_op jit(solution)/shard_map/ppermute | solution.py:177
  27.6 6.7 %collective-permute-start.18 = (bf16[96,768]{1,0:T(8,128)(2,1)S(1)}, bf16[96,768]{1,0:T(8,128)(2,1)S(1)}, u32[]{:S(2)}, u32[]{:S(2)}) collective-permute-start(bf16[96,768]{1,0:T(8,128)(2,1)S(1)} %collective-permute-done.15.refs_11_), channel_id=1, source_target_pairs={{4,0},{5,1},{8,4},{9,5},{12,8},{13,9},{14,12},{15,13},{10,14},{11,... | collective-permute-start | bytes 442376 | tf_op jit(solution)/shard_map/ppermute | solution.py:180
  29.0 6.7 %collective-permute-start.12 = (bf16[96,768]{1,0:T(8,128)(2,1)S(1)}, bf16[96,768]{1,0:T(8,128)(2,1)S(1)}, u32[]{:S(2)}, u32[]{:S(2)}) collective-permute-start(bf16[96,768]{1,0:T(8,128)(2,1)S(1)} %collective-permute-done.7.refs_4_), channel_id=1, source_target_pairs={{0,4},{1,5},{4,8},{5,9},{8,12},{9,13},{12,14},{13,15},{14,10},{15,... | collective-permute-start | bytes 442376 | tf_op jit(solution)/shard_map/ppermute | solution.py:177
  30.7 6.2 %collective-permute-start.14 = (bf16[96,768]{1,0:T(8,128)(2,1)S(1)}, bf16[96,768]{1,0:T(8,128)(2,1)S(1)}, u32[]{:S(2)}, u32[]{:S(2)}) collective-permute-start(bf16[96,768]{1,0:T(8,128)(2,1)S(1)} %collective-permute-done.10.refs_6_), channel_id=1, source_target_pairs={{4,0},{5,1},{8,4},{9,5},{12,8},{13,9},{14,12},{15,13},{10,14},{11,... | collective-permute-start | bytes 442376 | tf_op jit(solution)/shard_map/ppermute | solution.py:180
  32.1 5.8 %collective-permute-start.17 = (bf16[96,768]{1,0:T(8,128)(2,1)S(1)}, bf16[96,768]{1,0:T(8,128)(2,1)S(1)}, u32[]{:S(2)}, u32[]{:S(2)}) collective-permute-start(bf16[96,768]{1,0:T(8,128)(2,1)S(1)} %collective-permute-done.13.refs_9_), channel_id=1, source_target_pairs={{0,4},{1,5},{4,8},{5,9},{8,12},{9,13},{12,14},{13,15},{14,10},{15,... | collective-permute-start | bytes 442376 | tf_op jit(solution)/shard_map/ppermute | solution.py:177
  34.3 5.1 %collective-permute-start.19 = (bf16[96,768]{1,0:T(8,128)(2,1)S(1)}, bf16[96,768]{1,0:T(8,128)(2,1)S(1)}, u32[]{:S(2)}, u32[]{:S(2)}) collective-permute-start(bf16[96,768]{1,0:T(8,128)(2,1)S(1)} %collective-permute-done.18.refs_14_), channel_id=1, source_target_pairs={{4,0},{5,1},{8,4},{9,5},{12,8},{13,9},{14,12},{15,13},{10,14},{11,... | collective-permute-start | bytes 442376 | tf_op jit(solution)/shard_map/ppermute | solution.py:180
  35.7 5.1 %collective-permute-start.16 = (bf16[96,768]{1,0:T(8,128)(2,1)S(1)}, bf16[96,768]{1,0:T(8,128)(2,1)S(1)}, u32[]{:S(2)}, u32[]{:S(2)}) collective-permute-start(bf16[96,768]{1,0:T(8,128)(2,1)S(1)} %collective-permute-done.12.refs_8_), channel_id=1, source_target_pairs={{0,4},{1,5},{4,8},{5,9},{8,12},{9,13},{12,14},{13,15},{14,10},{15,... | collective-permute-start | bytes 442376 | tf_op jit(solution)/shard_map/ppermute | solution.py:177
  42.8 1.5 %collective-permute-start.20 = (bf16[128,768]{1,0:T(8,128)(2,1)S(1)}, bf16[128,768]{1,0:T(8,128)(2,1)S(1)}, u32[]{:S(2)}, u32[]{:S(2)}) collective-permute-start(bf16[128,768]{1,0:T(8,128)(2,1)S(1)} %get-tuple-element.94), channel_id=1, source_target_pairs={{0,1},{1,0},{2,3},{3,2},{4,5},{5,4},{6,7},{7,6},{8,9},{9,8},{10,11... | collective-permute-start | bytes 589832 | tf_op jit(solution)/shard_map/ppermute | solution.py:174
  44.9 7.3 %collective-permute-start.25 = (bf16[64,1664]{1,0:T(8,128)(2,1)S(1)}, bf16[64,1664]{1,0:T(8,128)(2,1)S(1)}, u32[]{:S(2)}, u32[]{:S(2)}) collective-permute-start(bf16[64,1664]{1,0:T(8,128)(2,1)S(1)} %get-tuple-element.96.refs_4_.refs_0_), channel_id=1, source_target_pairs={{0,4},{1,5},{4,8},{5,9},{8,12},{9,13},{12,14},{13,15},{14,10},{15,... | collective-permute-start | bytes 638984 | tf_op jit(solution)/shard_map/ppermute | solution.py:177
  45.6 7.0 %collective-permute-start.26 = (bf16[64,1664]{1,0:T(8,128)(2,1)S(1)}, bf16[64,1664]{1,0:T(8,128)(2,1)S(1)}, u32[]{:S(2)}, u32[]{:S(2)}) collective-permute-start(bf16[64,1664]{1,0:T(8,128)(2,1)S(1)} %get-tuple-element.97.refs_5_.refs_1_), channel_id=1, source_target_pairs={{4,0},{5,1},{8,4},{9,5},{12,8},{13,9},{14,12},{15,13},{10,14},{11,... | collective-permute-start | bytes 638984 | tf_op jit(solution)/shard_map/ppermute | solution.py:180
  52.6 14.7 %collective-permute-start.28 = (bf16[1536,512]{1,0:T(8,128)(2,1)S(1)}, bf16[1536,512]{1,0:T(8,128)(2,1)S(1)}, u32[]{:S(2)}, u32[]{:S(2)}) collective-permute-start(bf16[1536,512]{1,0:T(8,128)(2,1)S(1)} %collective-permute-done.27.refs_7_.refs_5_.refs_3_), channel_id=1, source_target_pairs={{0,1},{1,0},{2,3},{3,2},{4,5},{5,4},{6,7},{7,6},{8,9},{9,8},{10,11... | collective-permute-start | bytes 4718600 | tf_op jit(solution)/shard_map/ppermute | solution.py:174
  52.6 8.0 %collective-permute-start.21 = (bf16[64,1664]{1,0:T(8,128)(2,1)S(1)}, bf16[64,1664]{1,0:T(8,128)(2,1)S(1)}, u32[]{:S(2)}, u32[]{:S(2)}) collective-permute-start(bf16[64,1664]{1,0:T(8,128)(2,1)S(1)} %get-tuple-element.97.refs_5_.refs_1_), channel_id=1, source_target_pairs={{0,4},{1,5},{4,8},{5,9},{8,12},{9,13},{12,14},{13,15},{14,10},{15,... | collective-permute-start | bytes 638984 | tf_op jit(solution)/shard_map/ppermute | solution.py:177
  54.2 8.1 %collective-permute-start.23 = (bf16[64,1664]{1,0:T(8,128)(2,1)S(1)}, bf16[64,1664]{1,0:T(8,128)(2,1)S(1)}, u32[]{:S(2)}, u32[]{:S(2)}) collective-permute-start(bf16[64,1664]{1,0:T(8,128)(2,1)S(1)} %get-tuple-element.96.refs_4_.refs_0_), channel_id=1, source_target_pairs={{4,0},{5,1},{8,4},{9,5},{12,8},{13,9},{14,12},{15,13},{10,14},{11,... | collective-permute-start | bytes 638984 | tf_op jit(solution)/shard_map/ppermute | solution.py:180
  54.6 10.6 %collective-permute-start.29 = (bf16[64,1664]{1,0:T(8,128)(2,1)S(1)}, bf16[64,1664]{1,0:T(8,128)(2,1)S(1)}, u32[]{:S(2)}, u32[]{:S(2)}) collective-permute-start(bf16[64,1664]{1,0:T(8,128)(2,1)S(1)} %collective-permute-done.25.refs_0_), channel_id=1, source_target_pairs={{0,4},{1,5},{4,8},{5,9},{8,12},{9,13},{12,14},{13,15},{14,10},{15,... | collective-permute-start | bytes 638984 | tf_op jit(solution)/shard_map/ppermute | solution.py:177
  56.2 10.6 %collective-permute-start.31 = (bf16[64,1664]{1,0:T(8,128)(2,1)S(1)}, bf16[64,1664]{1,0:T(8,128)(2,1)S(1)}, u32[]{:S(2)}, u32[]{:S(2)}) collective-permute-start(bf16[64,1664]{1,0:T(8,128)(2,1)S(1)} %collective-permute-done.26.refs_3_), channel_id=1, source_target_pairs={{4,0},{5,1},{8,4},{9,5},{12,8},{13,9},{14,12},{15,13},{10,14},{11,... | collective-permute-start | bytes 638984 | tf_op jit(solution)/shard_map/ppermute | solution.py:180
  60.6 11.1 %collective-permute-start.22 = (bf16[64,1664]{1,0:T(8,128)(2,1)S(1)}, bf16[64,1664]{1,0:T(8,128)(2,1)S(1)}, u32[]{:S(2)}, u32[]{:S(2)}) collective-permute-start(bf16[64,1664]{1,0:T(8,128)(2,1)S(1)} %collective-permute-done.21.refs_1_), channel_id=1, source_target_pairs={{0,4},{1,5},{4,8},{5,9},{8,12},{9,13},{12,14},{13,15},{14,10},{15,... | collective-permute-start | bytes 638984 | tf_op jit(solution)/shard_map/ppermute | solution.py:177
  62.3 9.5 %collective-permute-start.24 = (bf16[64,1664]{1,0:T(8,128)(2,1)S(1)}, bf16[64,1664]{1,0:T(8,128)(2,1)S(1)}, u32[]{:S(2)}, u32[]{:S(2)}) collective-permute-start(bf16[64,1664]{1,0:T(8,128)(2,1)S(1)} %collective-permute-done.23.refs_2_), channel_id=1, source_target_pairs={{4,0},{5,1},{8,4},{9,5},{12,8},{13,9},{14,12},{15,13},{10,14},{11,... | collective-permute-start | bytes 638984 | tf_op jit(solution)/shard_map/ppermute | solution.py:180
  65.2 12.0 %collective-permute-start.30 = (bf16[64,1664]{1,0:T(8,128)(2,1)S(1)}, bf16[64,1664]{1,0:T(8,128)(2,1)S(1)}, u32[]{:S(2)}, u32[]{:S(2)}) collective-permute-start(bf16[64,1664]{1,0:T(8,128)(2,1)S(1)} %collective-permute-done.29.refs_0_), channel_id=1, source_target_pairs={{0,4},{1,5},{4,8},{5,9},{8,12},{9,13},{12,14},{13,15},{14,10},{15,... | collective-permute-start | bytes 638984 | tf_op jit(solution)/shard_map/ppermute | solution.py:177
  66.8 10.4 %collective-permute-start.32 = (bf16[64,1664]{1,0:T(8,128)(2,1)S(1)}, bf16[64,1664]{1,0:T(8,128)(2,1)S(1)}, u32[]{:S(2)}, u32[]{:S(2)}) collective-permute-start(bf16[64,1664]{1,0:T(8,128)(2,1)S(1)} %collective-permute-done.31.refs_3_), channel_id=1, source_target_pairs={{4,0},{5,1},{8,4},{9,5},{12,8},{13,9},{14,12},{15,13},{10,14},{11,... | collective-permute-start | bytes 638984 | tf_op jit(solution)/shard_map/ppermute | solution.py:180
  71.8 7.5 %collective-permute-start.35 = (bf16[64,1664]{1,0:T(8,128)(2,1)S(1)}, bf16[64,1664]{1,0:T(8,128)(2,1)S(1)}, u32[]{:S(2)}, u32[]{:S(2)}) collective-permute-start(bf16[64,1664]{1,0:T(8,128)(2,1)S(1)} %collective-permute-done.22.refs_1_), channel_id=1, source_target_pairs={{0,4},{1,5},{4,8},{5,9},{8,12},{9,13},{12,14},{13,15},{14,10},{15,... | collective-permute-start | bytes 638984 | tf_op jit(solution)/shard_map/ppermute | solution.py:177
  73.4 6.7 %collective-permute-start.36 = (bf16[64,1664]{1,0:T(8,128)(2,1)S(1)}, bf16[64,1664]{1,0:T(8,128)(2,1)S(1)}, u32[]{:S(2)}, u32[]{:S(2)}) collective-permute-start(bf16[64,1664]{1,0:T(8,128)(2,1)S(1)} %collective-permute-done.24.refs_2_), channel_id=1, source_target_pairs={{4,0},{5,1},{8,4},{9,5},{12,8},{13,9},{14,12},{15,13},{10,14},{11,... | collective-permute-start | bytes 638984 | tf_op jit(solution)/shard_map/ppermute | solution.py:180
  77.2 6.3 %collective-permute-start.33 = (bf16[64,1664]{1,0:T(8,128)(2,1)S(1)}, bf16[64,1664]{1,0:T(8,128)(2,1)S(1)}, u32[]{:S(2)}, u32[]{:S(2)}) collective-permute-start(bf16[64,1664]{1,0:T(8,128)(2,1)S(1)} %collective-permute-done.30.refs_0_), channel_id=1, source_target_pairs={{0,4},{1,5},{4,8},{5,9},{8,12},{9,13},{12,14},{13,15},{14,10},{15,... | collective-permute-start | bytes 638984 | tf_op jit(solution)/shard_map/ppermute | solution.py:177
  78.9 5.8 %collective-permute-start.34 = (bf16[64,1664]{1,0:T(8,128)(2,1)S(1)}, bf16[64,1664]{1,0:T(8,128)(2,1)S(1)}, u32[]{:S(2)}, u32[]{:S(2)}) collective-permute-start(bf16[64,1664]{1,0:T(8,128)(2,1)S(1)} %collective-permute-done.32.refs_3_), channel_id=1, source_target_pairs={{4,0},{5,1},{8,4},{9,5},{12,8},{13,9},{14,12},{15,13},{10,14},{11,... | collective-permute-start | bytes 638984 | tf_op jit(solution)/shard_map/ppermute | solution.py:180
  84.8 7.5 %collective-permute-start.40 = (bf16[64,1536]{1,0:T(8,128)(2,1)S(1)}, bf16[64,1536]{1,0:T(8,128)(2,1)S(1)}, u32[]{:S(2)}, u32[]{:S(2)}) collective-permute-start(bf16[64,1536]{1,0:T(8,128)(2,1)S(1)} %convert_element_type.79), channel_id=1, source_target_pairs={{4,0},{5,1},{8,4},{9,5},{12,8},{13,9},{14,12},{15,13},{10,14},{11,... | collective-permute-start | bytes 589832 | tf_op jit(solution)/shard_map/ppermute | solution.py:180
  85.3 7.7 %collective-permute-start.39 = (bf16[64,1536]{1,0:T(8,128)(2,1)S(1)}, bf16[64,1536]{1,0:T(8,128)(2,1)S(1)}, u32[]{:S(2)}, u32[]{:S(2)}) collective-permute-start(bf16[64,1536]{1,0:T(8,128)(2,1)S(1)} %convert_element_type.78), channel_id=1, source_target_pairs={{0,4},{1,5},{4,8},{5,9},{8,12},{9,13},{12,14},{13,15},{14,10},{15,... | collective-permute-start | bytes 589832 | tf_op jit(solution)/shard_map/ppermute | solution.py:177
  89.1 7.9 %collective-permute-start.38 = (bf16[64,1536]{1,0:T(8,128)(2,1)S(1)}, bf16[64,1536]{1,0:T(8,128)(2,1)S(1)}, u32[]{:S(2)}, u32[]{:S(2)}) collective-permute-start(bf16[64,1536]{1,0:T(8,128)(2,1)S(1)} %convert_element_type.73), channel_id=1, source_target_pairs={{4,0},{5,1},{8,4},{9,5},{12,8},{13,9},{14,12},{15,13},{10,14},{11,... | collective-permute-start | bytes 589832 | tf_op jit(solution)/shard_map/ppermute | solution.py:180
  89.6 7.8 %collective-permute-start.37 = (bf16[64,1536]{1,0:T(8,128)(2,1)S(1)}, bf16[64,1536]{1,0:T(8,128)(2,1)S(1)}, u32[]{:S(2)}, u32[]{:S(2)}) collective-permute-start(bf16[64,1536]{1,0:T(8,128)(2,1)S(1)} %convert_element_type.72), channel_id=1, source_target_pairs={{0,4},{1,5},{4,8},{5,9},{8,12},{9,13},{12,14},{13,15},{14,10},{15,... | collective-permute-start | bytes 589832 | tf_op jit(solution)/shard_map/ppermute | solution.py:177
  93.0 8.0 %collective-permute-start.44 = (bf16[64,1536]{1,0:T(8,128)(2,1)S(1)}, bf16[64,1536]{1,0:T(8,128)(2,1)S(1)}, u32[]{:S(2)}, u32[]{:S(2)}) collective-permute-start(bf16[64,1536]{1,0:T(8,128)(2,1)S(1)} %add_convert_fusion.6), channel_id=1, source_target_pairs={{4,0},{5,1},{8,4},{9,5},{12,8},{13,9},{14,12},{15,13},{10,14},{11,... | collective-permute-start | bytes 589832 | tf_op jit(solution)/shard_map/ppermute | solution.py:180
  94.5 7.0 %collective-permute-start.43 = (bf16[64,1536]{1,0:T(8,128)(2,1)S(1)}, bf16[64,1536]{1,0:T(8,128)(2,1)S(1)}, u32[]{:S(2)}, u32[]{:S(2)}) collective-permute-start(bf16[64,1536]{1,0:T(8,128)(2,1)S(1)} %add_convert_fusion.7), channel_id=1, source_target_pairs={{0,4},{1,5},{4,8},{5,9},{8,12},{9,13},{12,14},{13,15},{14,10},{15,... | collective-permute-start | bytes 589832 | tf_op jit(solution)/shard_map/ppermute | solution.py:177
  97.5 5.7 %collective-permute-start.42 = (bf16[64,1536]{1,0:T(8,128)(2,1)S(1)}, bf16[64,1536]{1,0:T(8,128)(2,1)S(1)}, u32[]{:S(2)}, u32[]{:S(2)}) collective-permute-start(bf16[64,1536]{1,0:T(8,128)(2,1)S(1)} %add_convert_fusion.8), channel_id=1, source_target_pairs={{4,0},{5,1},{8,4},{9,5},{12,8},{13,9},{14,12},{15,13},{10,14},{11,... | collective-permute-start | bytes 589832 | tf_op jit(solution)/shard_map/ppermute | solution.py:180
  98.8 5.7 %collective-permute-start.41 = (bf16[64,1536]{1,0:T(8,128)(2,1)S(1)}, bf16[64,1536]{1,0:T(8,128)(2,1)S(1)}, u32[]{:S(2)}, u32[]{:S(2)}) collective-permute-start(bf16[64,1536]{1,0:T(8,128)(2,1)S(1)} %add_convert_fusion.9), channel_id=1, source_target_pairs={{0,4},{1,5},{4,8},{5,9},{8,12},{9,13},{12,14},{13,15},{14,10},{15,... | collective-permute-start | bytes 589832 | tf_op jit(solution)/shard_map/ppermute | solution.py:177
  101.5 13.9 %copy-start.7 = (f32[1536]{0:T(1024)S(1)}, f32[1536]{0:T(1024)}, u32[]{:S(2)}) copy-start(f32[1536]{0:T(1024)} %param.17) | copy-start | bytes 18436
  104.5 7.5 %collective-permute-start.46 = (bf16[64,1536]{1,0:T(8,128)(2,1)S(1)}, bf16[64,1536]{1,0:T(8,128)(2,1)S(1)}, u32[]{:S(2)}, u32[]{:S(2)}) collective-permute-start(bf16[64,1536]{1,0:T(8,128)(2,1)S(1)} %add_convert_fusion.4), channel_id=1, source_target_pairs={{4,0},{5,1},{8,4},{9,5},{12,8},{13,9},{14,12},{15,13},{10,14},{11,... | collective-permute-start | bytes 589832 | tf_op jit(solution)/shard_map/ppermute | solution.py:180
  106.1 7.2 %collective-permute-start.45 = (bf16[64,1536]{1,0:T(8,128)(2,1)S(1)}, bf16[64,1536]{1,0:T(8,128)(2,1)S(1)}, u32[]{:S(2)}, u32[]{:S(2)}) collective-permute-start(bf16[64,1536]{1,0:T(8,128)(2,1)S(1)} %add_convert_fusion.5), channel_id=1, source_target_pairs={{0,4},{1,5},{4,8},{5,9},{8,12},{9,13},{12,14},{13,15},{14,10},{15,... | collective-permute-start | bytes 589832 | tf_op jit(solution)/shard_map/ppermute | solution.py:177
  106.6 8.8 %collective-permute-start.48 = (bf16[64,1536]{1,0:T(8,128)(2,1)S(1)}, bf16[64,1536]{1,0:T(8,128)(2,1)S(1)}, u32[]{:S(2)}, u32[]{:S(2)}) collective-permute-start(bf16[64,1536]{1,0:T(8,128)(2,1)S(1)} %add_convert_fusion.3), channel_id=1, source_target_pairs={{0,4},{1,5},{4,8},{5,9},{8,12},{9,13},{12,14},{13,15},{14,10},{15,... | collective-permute-start | bytes 589832 | tf_op jit(solution)/shard_map/ppermute | solution.py:177
  107.4 8.0 %collective-permute-start.49 = (bf16[64,1536]{1,0:T(8,128)(2,1)S(1)}, bf16[64,1536]{1,0:T(8,128)(2,1)S(1)}, u32[]{:S(2)}, u32[]{:S(2)}) collective-permute-start(bf16[64,1536]{1,0:T(8,128)(2,1)S(1)} %add_convert_fusion.2), channel_id=1, source_target_pairs={{4,0},{5,1},{8,4},{9,5},{12,8},{13,9},{14,12},{15,13},{10,14},{11,... | collective-permute-start | bytes 589832 | tf_op jit(solution)/shard_map/ppermute | solution.py:180
  113.3 5.7 %collective-permute-start.47 = (bf16[64,1536]{1,0:T(8,128)(2,1)S(1)}, bf16[64,1536]{1,0:T(8,128)(2,1)S(1)}, u32[]{:S(2)}, u32[]{:S(2)}) collective-permute-start(bf16[64,1536]{1,0:T(8,128)(2,1)S(1)} %add_convert_fusion.1), channel_id=1, source_target_pairs={{0,4},{1,5},{4,8},{5,9},{8,12},{9,13},{12,14},{13,15},{14,10},{15,... | collective-permute-start | bytes 589832 | tf_op jit(solution)/shard_map/ppermute | solution.py:177
  114.2 5.7 %collective-permute-start.50 = (bf16[64,1536]{1,0:T(8,128)(2,1)S(1)}, bf16[64,1536]{1,0:T(8,128)(2,1)S(1)}, u32[]{:S(2)}, u32[]{:S(2)}) collective-permute-start(bf16[64,1536]{1,0:T(8,128)(2,1)S(1)} %add_convert_fusion), channel_id=1, source_target_pairs={{4,0},{5,1},{8,4},{9,5},{12,8},{13,9},{14,12},{15,13},{10,14},{11,... | collective-permute-start | bytes 589832 | tf_op jit(solution)/shard_map/ppermute | solution.py:180

commit v5 on v4

--- a/solution.py
+++ b/solution.py
@@ -36,70 +36,55 @@
     )(*args)
 
 
-def prepare_kernel(peers, place, att, att_near, res, res_near, routes, scores, tokens, base, marks):
+def prepare_kernel(depth, peers, place, att, att_near, table, tokens, marks):
     core = place[0]
     rows, width = att.shape
-    half = width // 2
-    mine = pl.ds(pl.multiple_of(core * half, 128), half)
-    tokens[:rows, :] = att[...]
-    tokens[rows:, :] = att_near[...]
-    base[:rows, :] = res[:, mine]
-    base[rows:, :] = res_near[:, mine]
-    combine = scores[...] / jnp.sum(scores[...], axis=0, keepdims=True)
+    if depth:
+        feature = lax.broadcasted_iota(jnp.int32, (width, tokens.shape[1]), 0)
+        lane = lax.broadcasted_iota(jnp.int32, (width, tokens.shape[1]), 1)
+        pick = (feature == 2 * lane - lax.rem(lane, depth) + core * depth).astype(BF16)
+        tokens[:rows, :] = dot(att[...], pick).astype(BF16)
+        tokens[rows:, :] = dot(att_near[...], pick).astype(BF16)
+    chosen = table.shape[0] // 2
+    scores = table[chosen:, :]
+    combine = scores / jnp.sum(scores, axis=0, keepdims=True)
     lanes = marks.shape[1]
-    number = lax.broadcasted_iota(jnp.int32, (lanes, rows), 0)
+    number = lax.broadcasted_iota(jnp.int32, (lanes, rows), 0).astype(F32)
     spread = jnp.zeros((lanes, rows), F32)
-    for k in range(routes.shape[0]):
+    for k in range(chosen):
         left = combine[k : k + 1, :]
         for piece in range(PIECES):
             value = left.astype(BF16).astype(F32)
-            spread = spread + jnp.where(routes[k : k + 1, :] + piece * peers == number, value, 0.0)
+            spread = spread + jnp.where(table[k : k + 1, :] + float(piece * peers) == number, value, 0.0)
             left = left - value
     marks[...] = spread.T.astype(BF16)
 
 
-def pack_kernel(place, gate, up, both):
-    both[: gate.shape[0], :] = gate[...]
-    both[gate.shape[0] :, :] = up[...]
-
-
-def stream_kernel(layout, place, tokens, base, *refs):
+def project_kernel(layout, place, tokens, *refs):
     *blocks, own_out, near_out, full = refs
     core, expert, group = place[0], place[1], place[2]
-    rows, width = tokens.shape[0] // 2, tokens.shape[1]
-    half = width // 2
-    if layout is None:
-        full[...] = blocks[0][:, pl.ds(pl.multiple_of(core * half, 128), half)]
-    else:
-        chips, where = layout
-        depth = blocks[0].shape[0] // 2
-        pair = lax.shift_right_logical(expert, 1)
-        down = (pair & 1) == 1
-        at = jnp.where(down, chips - lax.shift_right_logical(pair + 1, 1), lax.shift_right_logical(pair, 1))
-        for block, (offset, other) in zip(blocks, where, strict=True):
-            spot = lax.rem(at + (offset + chips), chips)
-            source = jnp.where(spot < chips // 2, 2 * spot, 2 * (chips - spot) - 1)
-            of_group = group if other == 0 else 1 - group
-            sides = (core, 1 - core)
-            if block.shape[0] == depth:
-                sides = sides[:1] if offset < 0 else sides[1:]
-            for index, c in enumerate(sides):
-                start = ((of_group * chips + source) * 2 + c) * depth
-                full[pl.ds(pl.multiple_of(start, 16), depth), :] = block[index * depth : (index + 1) * depth, :]
-    projected = dot(tokens[...], full[...])
-    own_out[...] = (base[:rows, :].astype(F32) + projected[:rows]).astype(BF16)
-    near_out[...] = (base[rows:, :].astype(F32) + projected[rows:]).astype(BF16)
-
-
-def join_kernel(place, own, near, marks, *outs):
-    core = place[0]
-    half = own.shape[1]
+    rows = own_out.shape[0]
+    chips, where = layout
+    pair = lax.shift_right_logical(expert, 1)
+    down = (pair & 1) == 1
+    at = jnp.where(down, chips - lax.shift_right_logical(pair + 1, 1), lax.shift_right_logical(pair, 1))
+    depth = blocks[0].shape[0]
+    for block, (offset, other) in zip(blocks, where, strict=True):
+        spot = lax.rem(at + (offset + chips), chips)
+        source = jnp.where(spot < chips // 2, 2 * spot, 2 * (chips - spot) - 1)
+        of_group = group if other == 0 else 1 - group
+        full[pl.ds(pl.multiple_of((of_group * chips + source) * depth, 16), depth), :] = block[...]
+    own_out[...] = dot(tokens[:rows, :], full[...])
+    near_out[...] = dot(tokens[rows:, :], full[...])
+
+
+def join_kernel(place, res, own, near, marks, *outs):
+    width = res.shape[1]
     cut = outs[0].shape[0]
     for index, out in enumerate(outs):
         at = slice(index * cut, (index + 1) * cut)
-        out[:, pl.ds(pl.multiple_of(core * half, 128), half)] = own[at, :]
-        out[:, pl.ds(pl.multiple_of((1 - core) * half, 128), half)] = near[at, :]
-        out[:, 2 * half :] = marks[at, :]
+        out[:, :width] = (res[at, :].astype(F32) + (own[at, :] + near[at, :])).astype(BF16)
+        out[:, width:] = marks[at, :]
 
 
 def expert_kernel(count, peers, place, *refs):
@@ -182,44 +167,31 @@
     gate, up, down = gate_weight[0], up_weight[0], down_weight[0]
     hidden = gate.shape[1]
     lanes = -(-PIECES * peers // 128) * 128
-    tokens, base, marks = call(
-        functools.partial(prepare_kernel, peers),
+    depth = out_weight.shape[0] if groups == 2 else 0
+    tokens, marks = call(
+        functools.partial(prepare_kernel, depth, peers),
         [
-            jax.ShapeDtypeStruct((2 * token_count, width), BF16),
             jax.ShapeDtypeStruct((2 * token_count, half), BF16),
             jax.ShapeDtypeStruct((token_count, lanes), BF16),
         ],
         place,
         attention,
         swap(attention),
-        residual,
-        swap(residual),
-        routes.T,
-        router_scores.T,
+        jnp.concatenate([routes.T.astype(F32), router_scores.T], axis=0),
         name="prepare",
     )
     down_near = swap(down)
 
     if groups == 2:
         flip = [(0, 1), (1, 0)]
-
-        def columns(which):
-            return lax.dynamic_slice(
-                out_weight, (0, which * half), (out_weight.shape[0], half), allow_negative_indices=False
-            )
-
-        mine = jnp.concatenate([columns(core), swap(columns(1 - core))], axis=0)
-        other = lax.ppermute(mine, "dp", flip)
-        depth = out_weight.shape[0]
+        mine, other = out_weight, lax.ppermute(out_weight, "dp", flip)
         blocks, layout = [mine, other], [(0, 0), (0, 1)]
         mine_f, mine_b = go(mine), come(mine)
-        mine_f, mine_b, other, tokens, base, marks, down_near = together(
-            mine_f, mine_b, other, tokens, base, marks, down_near
+        mine_f, mine_b, other, tokens, marks, down_near = together(
+            mine_f, mine_b, other, tokens, marks, down_near
         )
-        other, gate, up = together(other, gate, up)
-        both = call(
-            pack_kernel, jax.ShapeDtypeStruct((2 * gate.shape[0], hidden), BF16), place, gate, up, name="pack"
-        )
+        both = jnp.concatenate([gate, up], axis=0)
+        other, both = together(other, both)
         both_far = lax.ppermute(both, "dp", flip)
         both_near = swap(both)
         blocks += [mine_f, mine_b]
@@ -243,36 +215,37 @@
             blocks += [other_b]
             layout += [(step, 1)]
         layout = (chips, layout)
+        own, near = call(
+            functools.partial(project_kernel, layout),
+            [jax.ShapeDtypeStruct((token_count, width), F32)] * 2,
+            place,
+            tokens,
+            *blocks,
+            scratch=[pltpu.VMEM((half, width), BF16)],
+            flops=4 * token_count * width * half,
+            name="project",
+        )
+        near = swap(near)
     else:
-        both = call(
-            pack_kernel, jax.ShapeDtypeStruct((2 * gate.shape[0], hidden), BF16), place, gate, up, name="pack"
-        )
-        blocks, layout = [lax.all_gather(out_weight, ("dp", "expert"), axis=0, tiled=True)], None
+        both = jnp.concatenate([gate, up], axis=0)
         both = lax.all_gather(both, "dp", axis=0).reshape(groups, 2, -1, hidden).swapaxes(0, 1)
         both = both.reshape(2, 2, half, hidden).swapaxes(0, 1).reshape(2, 2 * half, hidden)
         both, both_far = both[0], both[1]
         both_near = swap(both)
-
-    own_half, near_half = call(
-        functools.partial(stream_kernel, layout),
-        [jax.ShapeDtypeStruct((token_count, half), BF16)] * 2,
-        place,
-        tokens,
-        base,
-        *blocks,
-        scratch=[pltpu.VMEM((width, half), BF16)],
-        flops=4 * token_count * width * half,
-        name="stream",
-    )
+        full_weight = lax.all_gather(out_weight, ("dp", "expert"), axis=0, tiled=True)
+        own = jnp.dot(attention, full_weight, preferred_element_type=F32)
+        near = jnp.zeros_like(own)
+
     cut = token_count // 2
     stream = call(
         join_kernel,
         [jax.ShapeDtypeStruct((cut, width + lanes), BF16)] * 2,
         place,
-        own_half,
-        swap(near_half),
+        residual,
+        own,
+        near,
         marks,
-        name="join",
+        name="stream",
     )
 
     def experts(*arrays):

time: 122 us -> 118 us (0.967)
  local copies, waits for them, and re-layouts: 4.32 us -> 0.04 us
  other arithmetic: 0.54 us -> 2.07 us
    ppermute x21, starting transfers between devices: 23.5 us -> 31.8 us  [go(): return lax.ppermute(x, 'expert', forth)]
    ppermute x21, starting transfers between devices: 20.7 us -> 12.6 us  [come(): return lax.ppermute(x, 'expert', back)]
    unnamed x16 -> x14, local copies, waits for them, and re-layouts: 3.39 us -> 0.03 us
    ppermute x21, waiting for transfers between devices: 21.9 us -> 24.9 us  [come(): return lax.ppermute(x, 'expert', back)]
    ppermute x21, waiting for transfers between devices: 18.9 us -> 15.9 us  [go(): return lax.ppermute(x, 'expert', forth)]
    concatenate x1 -> x2, other arithmetic: 0.01 us -> 1.54 us  [the longest x1 1.53 us: body(): both = jnp.concatenate([gate, up], axis=0)]
    pallas_call x9 -> x8, Pallas kernels: 19.6 us -> 18.8 us  [call(): pl.pallas_call(kernel, in_specs=[SMEM] + [VMEM] * (len(args) - 1), out_sp...]
    ppermute x7 -> x5, waiting for transfers between devices: 3.02 us -> 2.55 us  [swap(): return lax.ppermute(x, 'expert', across)]
  transfers between devices with their start and end apart: 51 -> 49, of which waited for: 32 -> 33; matrix products, arithmetic and copies ran while one was open for 1% -> 2% of each run, Pallas kernels for 14% -> 15%
where the time goes in v5:
time: 118 us; the launch traced here: 117 us
  waiting for transfers between devices  48.3 us (41%)
  starting transfers between devices  47.9 us (41%)
  Pallas kernels  18.8 us (16%)
  other arithmetic  2.07 us (2%)
    ppermute x21, starting transfers between devices, go(): return lax.ppermute(x, 'expert', forth)  31.8 us
    ppermute x21, waiting for transfers between devices, come(): return lax.ppermute(x, 'expert', back)  24.9 us
    pallas_call x8, Pallas kernels, call(): pl.pallas_call(kernel, in_specs=[SMEM] + [VMEM] * (len(args) - 1), out_sp...  18.8 us
    ppermute x21, waiting for transfers between devices, go(): return lax.ppermute(x, 'expert', forth)  15.9 us
    ppermute x21, starting transfers between devices, come(): return lax.ppermute(x, 'expert', back)  12.6 us
    ppermute x1, waiting for transfers between devices, body(): both_far = lax.ppermute(both, 'dp', flip)  4.99 us
    ppermute x5, waiting for transfers between devices, swap(): return lax.ppermute(x, 'expert', across)  2.55 us
    ppermute x1, starting transfers between devices, body(): mine, other = (out_weight, lax.ppermute(out_weight, 'dp', flip))  2.52 us
  transfers between devices with their start and end apart: 49, of which 33 were waited for; matrix products, arithmetic and copies ran while one was open for 2% of the time, Pallas kernels for 15%

profile of v5, /device:TPU:0, one launch (start us, length us, event | category | flops | bytes accessed | tf_op | source)
XLA Modules:
  0.0 117.4 jit_solution(13878995947020829638)
XLA Ops:
  0.5 2.5 %collective-permute-start.2 = (bf16[48,1536]{1,0:T(8,128)(2,1)}, bf16[48,1536]{1,0:T(8,128)(2,1)S(1)}, u32[]{:S(2)}, u32[]{:S(2)}) collective-permute-start(bf16[48,1536]{1,0:T(8,128)(2,1)} %refs_0_.1), channel_id=1, source_target_pairs={{0,16},{16,0},{1,17},{17,1},{2,18},{18,2},{3,19},{19,3},{4,20},{20... | collective-permute-start | bytes 442376 | tf_op jit(solution)/shard_map/ppermute | solution.py:187
  3.0 1.6 %collective-permute-start = (bf16[48,1536]{1,0:T(8,128)(2,1)}, bf16[48,1536]{1,0:T(8,128)(2,1)S(1)}, u32[]{:S(2)}, u32[]{:S(2)}) collective-permute-start(bf16[48,1536]{1,0:T(8,128)(2,1)} %refs_0_.1), channel_id=1, source_target_pairs={{0,4},{1,5},{4,8},{5,9},{8,12},{9,13},{12,14},{13,15},{14,10},{15,... | collective-permute-start | bytes 442376 | tf_op jit(solution)/shard_map/ppermute | solution.py:162
  5.0 1.5 %pad_maximum_fusion.refs_6_.refs_4_.refs_2_ = bf16[1536,512]{1,0:T(8,128)(2,1)S(1)} fusion(bf16[768,512]{1,0:T(8,128)(2,1)} %bitcast.14, bf16[768,512]{1,0:T(8,128)(2,1)} %bitcast.15), kind=kLoop, calls=%fused_computation | loop fusion | flops 3145728 | bytes 3145728 | tf_op jit(solution)/shard_map/concatenate | solution.py:193
  6.9 1.7 %prepare.1 = (bf16[256,768]{1,0:T(8,128)(2,1)S(1)}, bf16[128,128]{1,0:T(8,128)(2,1)S(1)}) custom-call(s32[3]{0:T(128)S(1)} %pad_add_fusion.place, bf16[128,1536]{1,0:T(8,128)(2,1)S(1)} %copy-done.1, bf16[128,1536]{1,0:T(8,128)(2,1)S(1)} %collective-permute-done.3.att_near, f32[16,128]{1,0:T(8,128)S(1)} %pad_maximum_fusion.1.table), custom_call_target="tpu_custom_call" | custom-call | bytes 4194304 | tf_op jit(solution)/shard_map/prepare/pallas_call | solution.py:27
  8.6 0.6 collective-permute-done.refs_2_
  9.2 1.3 %collective-permute-done.1.refs_3_ = bf16[48,1536]{1,0:T(8,128)(2,1)S(1)} collective-permute-done((bf16[48,1536]{1,0:T(8,128)(2,1)}, bf16[48,1536]{1,0:T(8,128)(2,1)S(1)}, u32[]{:S(2)}, u32[]{:S(2)}) %collective-permute-start.1) | collective-permute-done | bytes 147488 | tf_op jit(solution)/shard_map/ppermute | solution.py:165
  11.3 1.7 %collective-permute-start.5 = (bf16[48,1536]{1,0:T(8,128)(2,1)S(1)}, bf16[48,1536]{1,0:T(8,128)(2,1)S(1)}, u32[]{:S(2)}, u32[]{:S(2)}) collective-permute-start(bf16[48,1536]{1,0:T(8,128)(2,1)S(1)} %collective-permute-done.refs_2_), channel_id=1, source_target_pairs={{0,4},{1,5},{4,8},{5,9},{8,12},{9,13},{12,14},{13,15},{14,10},{15,... | collective-permute-start | bytes 442376 | tf_op jit(solution)/shard_map/ppermute | solution.py:162
  13.0 1.6 %collective-permute-start.7 = (bf16[48,1536]{1,0:T(8,128)(2,1)S(1)}, bf16[48,1536]{1,0:T(8,128)(2,1)S(1)}, u32[]{:S(2)}, u32[]{:S(2)}) collective-permute-start(bf16[48,1536]{1,0:T(8,128)(2,1)S(1)} %collective-permute-done.2.refs_1_), channel_id=1, source_target_pairs={{0,4},{1,5},{4,8},{5,9},{8,12},{9,13},{12,14},{13,15},{14,10},{15,... | collective-permute-start | bytes 442376 | tf_op jit(solution)/shard_map/ppermute | solution.py:162
  14.6 2.1 %collective-permute-done.9.refs_7_ = bf16[48,1536]{1,0:T(8,128)(2,1)S(1)} collective-permute-done((bf16[48,1536]{1,0:T(8,128)(2,1)S(1)}, bf16[48,1536]{1,0:T(8,128)(2,1)S(1)}, u32[]{:S(2)}, u32[]{:S(2)}) %collective-permute-start.9) | collective-permute-done | bytes 147488 | tf_op jit(solution)/shard_map/ppermute | solution.py:165
  17.2 0.8 collective-permute-done.5.refs_4_
  18.0 1.6 %collective-permute-start.8 = (bf16[48,1536]{1,0:T(8,128)(2,1)S(1)}, bf16[48,1536]{1,0:T(8,128)(2,1)S(1)}, u32[]{:S(2)}, u32[]{:S(2)}) collective-permute-start(bf16[48,1536]{1,0:T(8,128)(2,1)S(1)} %collective-permute-done.1.refs_3_), channel_id=1, source_target_pairs={{4,0},{5,1},{8,4},{9,5},{12,8},{13,9},{14,12},{15,13},{10,14},{11,... | collective-permute-start | bytes 442376 | tf_op jit(solution)/shard_map/ppermute | solution.py:165
  19.6 0.5 collective-permute-done.7.refs_5_
  20.2 1.7 %collective-permute-start.11 = (bf16[48,1536]{1,0:T(8,128)(2,1)S(1)}, bf16[48,1536]{1,0:T(8,128)(2,1)S(1)}, u32[]{:S(2)}, u32[]{:S(2)}) collective-permute-start(bf16[48,1536]{1,0:T(8,128)(2,1)S(1)} %collective-permute-done.7.refs_5_), channel_id=1, source_target_pairs={{0,4},{1,5},{4,8},{5,9},{8,12},{9,13},{12,14},{13,15},{14,10},{15,... | collective-permute-start | bytes 442376 | tf_op jit(solution)/shard_map/ppermute | solution.py:162
  21.9 1.6 %collective-permute-done.13.refs_11_ = bf16[48,1536]{1,0:T(8,128)(2,1)S(1)} collective-permute-done((bf16[48,1536]{1,0:T(8,128)(2,1)S(1)}, bf16[48,1536]{1,0:T(8,128)(2,1)S(1)}, u32[]{:S(2)}, u32[]{:S(2)}) %collective-permute-start.13) | collective-permute-done | bytes 147488 | tf_op jit(solution)/shard_map/ppermute | solution.py:165
  23.9 1.6 %collective-permute-start.10 = (bf16[48,1536]{1,0:T(8,128)(2,1)S(1)}, bf16[48,1536]{1,0:T(8,128)(2,1)S(1)}, u32[]{:S(2)}, u32[]{:S(2)}) collective-permute-start(bf16[48,1536]{1,0:T(8,128)(2,1)S(1)} %collective-permute-done.5.refs_4_), channel_id=1, source_target_pairs={{0,4},{1,5},{4,8},{5,9},{8,12},{9,13},{12,14},{13,15},{14,10},{15,... | collective-permute-start | bytes 442376 | tf_op jit(solution)/shard_map/ppermute | solution.py:162
  25.5 1.1 collective-permute-done.8.refs_6_
  27.1 1.6 %collective-permute-start.15 = (bf16[48,1536]{1,0:T(8,128)(2,1)S(1)}, bf16[48,1536]{1,0:T(8,128)(2,1)S(1)}, u32[]{:S(2)}, u32[]{:S(2)}) collective-permute-start(bf16[48,1536]{1,0:T(8,128)(2,1)S(1)} %collective-permute-done.11.refs_9_), channel_id=1, source_target_pairs={{0,4},{1,5},{4,8},{5,9},{8,12},{9,13},{12,14},{13,15},{14,10},{15,... | collective-permute-start | bytes 442376 | tf_op jit(solution)/shard_map/ppermute | solution.py:162
  28.7 1.6 %collective-permute-done.16.refs_14_ = bf16[48,1536]{1,0:T(8,128)(2,1)S(1)} collective-permute-done((bf16[48,1536]{1,0:T(8,128)(2,1)S(1)}, bf16[48,1536]{1,0:T(8,128)(2,1)S(1)}, u32[]{:S(2)}, u32[]{:S(2)}) %collective-permute-start.16) | collective-permute-done | bytes 147488 | tf_op jit(solution)/shard_map/ppermute | solution.py:165
  30.7 1.6 %collective-permute-start.14 = (bf16[48,1536]{1,0:T(8,128)(2,1)S(1)}, bf16[48,1536]{1,0:T(8,128)(2,1)S(1)}, u32[]{:S(2)}, u32[]{:S(2)}) collective-permute-start(bf16[48,1536]{1,0:T(8,128)(2,1)S(1)} %collective-permute-done.10.refs_8_), channel_id=1, source_target_pairs={{0,4},{1,5},{4,8},{5,9},{8,12},{9,13},{12,14},{13,15},{14,10},{15,... | collective-permute-start | bytes 442376 | tf_op jit(solution)/shard_map/ppermute | solution.py:162
  32.3 1.0 collective-permute-done.12.refs_10_
  33.3 2.1 %collective-permute-done.17.refs_15_ = bf16[48,1536]{1,0:T(8,128)(2,1)S(1)} collective-permute-done((bf16[48,1536]{1,0:T(8,128)(2,1)S(1)}, bf16[48,1536]{1,0:T(8,128)(2,1)S(1)}, u32[]{:S(2)}, u32[]{:S(2)}) %collective-permute-start.17) | collective-permute-done | bytes 147488 | tf_op jit(solution)/shard_map/ppermute | solution.py:165
  35.9 1.5 %project.1 = (f32[128,1536]{1,0:T(8,128)S(1)}, f32[128,1536]{1,0:T(8,128)S(1)}) custom-call(s32[3]{0:T(128)S(1)} %pad_add_fusion.place, bf16[256,768]{1,0:T(8,128)(2,1)S(1)} %get-tuple-element.80.tokens, bf16[48,1536]{1,0:T(8,128)(2,1)S(1)} %copy-done.3, bf16[48,1536]{1,0:T(8,128)(2,1)S(1)} %collective-permute-done.2.refs_1_, ...), custom_call_target="tpu_custom_call" | custom-call | flops 603979776 | bytes 4194304 | tf_op jit(solution)/shard_map/project/pallas_call | solution.py:27
  37.5 2.3 %collective-permute-done.18.near = f32[128,1536]{1,0:T(8,128)S(1)} collective-permute-done((f32[128,1536]{1,0:T(8,128)S(1)}, f32[128,1536]{1,0:T(8,128)S(1)}, u32[]{:S(2)}, u32[]{:S(2)}) %collective-permute-start.18) | collective-permute-done | bytes 786464 | tf_op jit(solution)/shard_map/ppermute | solution.py:159
  39.7 0.6 stream.1
  40.4 1.6 %collective-permute-start.23 = (bf16[64,1664]{1,0:T(8,128)(2,1)S(1)}, bf16[64,1664]{1,0:T(8,128)(2,1)S(1)}, u32[]{:S(2)}, u32[]{:S(2)}) collective-permute-start(bf16[64,1664]{1,0:T(8,128)(2,1)S(1)} %get-tuple-element.90.refs_4_.refs_0_), channel_id=1, source_target_pairs={{0,4},{1,5},{4,8},{5,9},{8,12},{9,13},{12,14},{13,15},{14,10},{15,... | collective-permute-start | bytes 638984 | tf_op jit(solution)/shard_map/ppermute | solution.py:162
  42.5 5.0 %collective-permute-done.25.refs_7_.refs_5_.refs_3_ = bf16[1536,512]{1,0:T(8,128)(2,1)S(1)} collective-permute-done((bf16[1536,512]{1,0:T(8,128)(2,1)S(1)}, bf16[1536,512]{1,0:T(8,128)(2,1)S(1)}, u32[]{:S(2)}, u32[]{:S(2)}) %collective-permute-start.25) | collective-permute-done | bytes 1572896 | tf_op jit(solution)/shard_map/ppermute | solution.py:195
  47.7 1.3 %collective-permute-done.24.refs_3_ = bf16[64,1664]{1,0:T(8,128)(2,1)S(1)} collective-permute-done((bf16[64,1664]{1,0:T(8,128)(2,1)S(1)}, bf16[64,1664]{1,0:T(8,128)(2,1)S(1)}, u32[]{:S(2)}, u32[]{:S(2)}) %collective-permute-start.24) | collective-permute-done | bytes 213024 | tf_op jit(solution)/shard_map/ppermute | solution.py:165
  49.0 1.6 %collective-permute-start.19 = (bf16[64,1664]{1,0:T(8,128)(2,1)S(1)}, bf16[64,1664]{1,0:T(8,128)(2,1)S(1)}, u32[]{:S(2)}, u32[]{:S(2)}) collective-permute-start(bf16[64,1664]{1,0:T(8,128)(2,1)S(1)} %get-tuple-element.91.refs_5_.refs_1_), channel_id=1, source_target_pairs={{0,4},{1,5},{4,8},{5,9},{8,12},{9,13},{12,14},{13,15},{14,10},{15,... | collective-permute-start | bytes 638984 | tf_op jit(solution)/shard_map/ppermute | solution.py:162
  51.0 1.6 %collective-permute-start.27 = (bf16[64,1664]{1,0:T(8,128)(2,1)S(1)}, bf16[64,1664]{1,0:T(8,128)(2,1)S(1)}, u32[]{:S(2)}, u32[]{:S(2)}) collective-permute-start(bf16[64,1664]{1,0:T(8,128)(2,1)S(1)} %collective-permute-done.23.refs_0_), channel_id=1, source_target_pairs={{0,4},{1,5},{4,8},{5,9},{8,12},{9,13},{12,14},{13,15},{14,10},{15,... | collective-permute-start | bytes 638984 | tf_op jit(solution)/shard_map/ppermute | solution.py:162
  53.1 4.0 %collective-permute-done.19.refs_1_ = bf16[64,1664]{1,0:T(8,128)(2,1)S(1)} collective-permute-done((bf16[64,1664]{1,0:T(8,128)(2,1)S(1)}, bf16[64,1664]{1,0:T(8,128)(2,1)S(1)}, u32[]{:S(2)}, u32[]{:S(2)}) %collective-permute-start.19) | collective-permute-done | bytes 213024 | tf_op jit(solution)/shard_map/ppermute | solution.py:162
  57.1 1.6 %collective-permute-start.20 = (bf16[64,1664]{1,0:T(8,128)(2,1)S(1)}, bf16[64,1664]{1,0:T(8,128)(2,1)S(1)}, u32[]{:S(2)}, u32[]{:S(2)}) collective-permute-start(bf16[64,1664]{1,0:T(8,128)(2,1)S(1)} %collective-permute-done.19.refs_1_), channel_id=1, source_target_pairs={{0,4},{1,5},{4,8},{5,9},{8,12},{9,13},{12,14},{13,15},{14,10},{15,... | collective-permute-start | bytes 638984 | tf_op jit(solution)/shard_map/ppermute | solution.py:162
  59.1 2.5 %collective-permute-done.27.refs_0_ = bf16[64,1664]{1,0:T(8,128)(2,1)S(1)} collective-permute-done((bf16[64,1664]{1,0:T(8,128)(2,1)S(1)}, bf16[64,1664]{1,0:T(8,128)(2,1)S(1)}, u32[]{:S(2)}, u32[]{:S(2)}) %collective-permute-start.27) | collective-permute-done | bytes 213024 | tf_op jit(solution)/shard_map/ppermute | solution.py:162
  61.6 1.6 %collective-permute-start.28 = (bf16[64,1664]{1,0:T(8,128)(2,1)S(1)}, bf16[64,1664]{1,0:T(8,128)(2,1)S(1)}, u32[]{:S(2)}, u32[]{:S(2)}) collective-permute-start(bf16[64,1664]{1,0:T(8,128)(2,1)S(1)} %collective-permute-done.27.refs_0_), channel_id=1, source_target_pairs={{0,4},{1,5},{4,8},{5,9},{8,12},{9,13},{12,14},{13,15},{14,10},{15,... | collective-permute-start | bytes 638984 | tf_op jit(solution)/shard_map/ppermute | solution.py:162
  63.7 4.5 %experts.4 = (f32[64,1536]{1,0:T(8,128)S(1)}, f32[64,1536]{1,0:T(8,128)S(1)}, f32[64,1536]{1,0:T(8,128)S(1)}, f32[64,1536]{1,0:T(8,128)S(1)}, f32[64,1536]{1,0:T(8,128)S(1)}, /*index=5*/f32[64,1536]{1,0:T(8,128)S(1)}) custom-call(s32[3]{0:T(128)S(1)} %pad_add_fusion.place, bf16[64,1664]{1,0:T(8,128)(2,1)S(1)} %collective-permute-done.23.refs_0_, ...), custom_call_target="tpu_custom_call" | custom-call | flops 3623878656 | bytes 4194304 | tf_op jit(solution)/shard_map/experts/pallas_call | solution.py:27
  68.2 1.6 %collective-permute-start.33 = (bf16[64,1664]{1,0:T(8,128)(2,1)S(1)}, bf16[64,1664]{1,0:T(8,128)(2,1)S(1)}, u32[]{:S(2)}, u32[]{:S(2)}) collective-permute-start(bf16[64,1664]{1,0:T(8,128)(2,1)S(1)} %collective-permute-done.20.refs_1_), channel_id=1, source_target_pairs={{0,4},{1,5},{4,8},{5,9},{8,12},{9,13},{12,14},{13,15},{14,10},{15,... | collective-permute-start | bytes 638984 | tf_op jit(solution)/shard_map/ppermute | solution.py:162
  69.9 0.5 collective-permute-start.34
  70.3 3.3 %experts.5 = (f32[64,1536]{1,0:T(8,128)S(1)}, f32[64,1536]{1,0:T(8,128)S(1)}, f32[64,1536]{1,0:T(8,128)S(1)}, f32[64,1536]{1,0:T(8,128)S(1)}) custom-call(s32[3]{0:T(128)S(1)} %pad_add_fusion.place, bf16[64,1664]{1,0:T(8,128)(2,1)S(1)} %collective-permute-done.27.refs_0_, bf16[64,1664]{1,0:T(8,128)(2,1)S(1)} %collective-permute-done.20.refs_1_, ...), custom_call_target="tpu_custom_call" | custom-call | flops 2415919104 | bytes 4194304 | tf_op jit(solution)/shard_map/experts/pallas_call | solution.py:27
  73.7 1.6 %collective-permute-start.31 = (bf16[64,1664]{1,0:T(8,128)(2,1)S(1)}, bf16[64,1664]{1,0:T(8,128)(2,1)S(1)}, u32[]{:S(2)}, u32[]{:S(2)}) collective-permute-start(bf16[64,1664]{1,0:T(8,128)(2,1)S(1)} %collective-permute-done.28.refs_0_), channel_id=1, source_target_pairs={{0,4},{1,5},{4,8},{5,9},{8,12},{9,13},{12,14},{13,15},{14,10},{15,... | collective-permute-start | bytes 638984 | tf_op jit(solution)/shard_map/ppermute | solution.py:162
  75.8 0.9 collective-permute-done.34.refs_2_
  76.6 3.3 %experts.6 = (f32[64,1536]{1,0:T(8,128)S(1)}, f32[64,1536]{1,0:T(8,128)S(1)}, f32[64,1536]{1,0:T(8,128)S(1)}, f32[64,1536]{1,0:T(8,128)S(1)}) custom-call(s32[3]{0:T(128)S(1)} %pad_add_fusion.place, bf16[64,1664]{1,0:T(8,128)(2,1)S(1)} %collective-permute-done.28.refs_0_, bf16[64,1664]{1,0:T(8,128)(2,1)S(1)} %collective-permute-done.33.refs_1_, ...), custom_call_target="tpu_custom_call" | custom-call | flops 2415919104 | bytes 4194304 | tf_op jit(solution)/shard_map/experts/pallas_call | solution.py:27
  80.0 1.2 collective-permute-done.32.refs_1_
  81.2 0.5 collective-permute-start.38
  81.7 1.6 %collective-permute-start.37 = (bf16[64,1536]{1,0:T(8,128)(2,1)S(1)}, bf16[64,1536]{1,0:T(8,128)(2,1)S(1)}, u32[]{:S(2)}, u32[]{:S(2)}) collective-permute-start(bf16[64,1536]{1,0:T(8,128)(2,1)S(1)} %convert_element_type.86), channel_id=1, source_target_pairs={{0,4},{1,5},{4,8},{5,9},{8,12},{9,13},{12,14},{13,15},{14,10},{15,... | collective-permute-start | bytes 589832 | tf_op jit(solution)/shard_map/ppermute | solution.py:162
  83.3 2.2 %experts.7 = (f32[64,1536]{1,0:T(8,128)S(1)}, f32[64,1536]{1,0:T(8,128)S(1)}) custom-call(s32[3]{0:T(128)S(1)} %pad_add_fusion.place, bf16[64,1664]{1,0:T(8,128)(2,1)S(1)} %collective-permute-done.31.refs_0_, bf16[64,1664]{1,0:T(8,128)(2,1)S(1)} %collective-permute-done.32.refs_1_, bf16[1536,512]{1,0:T(8,128)(2,1)S(1)} %pad_maximum_fusion.refs_6_.refs_4_.refs_2_, ...), custom_call_target="tpu_custom_call" | custom-call | flops 1207959552 | bytes 4194304 | tf_op jit(solution)/shard_map/experts/pallas_call | solution.py:27
  85.6 0.5 collective-permute-start.36
  86.1 1.6 %collective-permute-start.35 = (bf16[64,1536]{1,0:T(8,128)(2,1)S(1)}, bf16[64,1536]{1,0:T(8,128)(2,1)S(1)}, u32[]{:S(2)}, u32[]{:S(2)}) collective-permute-start(bf16[64,1536]{1,0:T(8,128)(2,1)S(1)} %convert_element_type.80), channel_id=1, source_target_pairs={{0,4},{1,5},{4,8},{5,9},{8,12},{9,13},{12,14},{13,15},{14,10},{15,... | collective-permute-start | bytes 589832 | tf_op jit(solution)/shard_map/ppermute | solution.py:162
  87.6 1.1 collective-permute-done.38
  88.8 0.7 collective-permute-done.37
  89.5 0.5 collective-permute-start.42
  90.0 1.6 %collective-permute-start.41 = (bf16[64,1536]{1,0:T(8,128)(2,1)S(1)}, bf16[64,1536]{1,0:T(8,128)(2,1)S(1)}, u32[]{:S(2)}, u32[]{:S(2)}) collective-permute-start(bf16[64,1536]{1,0:T(8,128)(2,1)S(1)} %add_convert_fusion.7), channel_id=1, source_target_pairs={{0,4},{1,5},{4,8},{5,9},{8,12},{9,13},{12,14},{13,15},{14,10},{15,... | collective-permute-start | bytes 589832 | tf_op jit(solution)/shard_map/ppermute | solution.py:162
  91.6 1.9 %collective-permute-done.36 = bf16[64,1536]{1,0:T(8,128)(2,1)S(1)} collective-permute-done((bf16[64,1536]{1,0:T(8,128)(2,1)S(1)}, bf16[64,1536]{1,0:T(8,128)(2,1)S(1)}, u32[]{:S(2)}, u32[]{:S(2)}) %collective-permute-start.36) | collective-permute-done | bytes 196640 | tf_op jit(solution)/shard_map/ppermute | solution.py:165
  94.4 1.7 %collective-permute-start.39 = (bf16[64,1536]{1,0:T(8,128)(2,1)S(1)}, bf16[64,1536]{1,0:T(8,128)(2,1)S(1)}, u32[]{:S(2)}, u32[]{:S(2)}) collective-permute-start(bf16[64,1536]{1,0:T(8,128)(2,1)S(1)} %add_convert_fusion.9), channel_id=1, source_target_pairs={{0,4},{1,5},{4,8},{5,9},{8,12},{9,13},{12,14},{13,15},{14,10},{15,... | collective-permute-start | bytes 589832 | tf_op jit(solution)/shard_map/ppermute | solution.py:162
  96.0 1.4 %collective-permute-done.42 = bf16[64,1536]{1,0:T(8,128)(2,1)S(1)} collective-permute-done((bf16[64,1536]{1,0:T(8,128)(2,1)S(1)}, bf16[64,1536]{1,0:T(8,128)(2,1)S(1)}, u32[]{:S(2)}, u32[]{:S(2)}) %collective-permute-start.42) | collective-permute-done | bytes 196640 | tf_op jit(solution)/shard_map/ppermute | solution.py:165
  98.0 1.7 %collective-permute-done.40 = bf16[64,1536]{1,0:T(8,128)(2,1)S(1)} collective-permute-done((bf16[64,1536]{1,0:T(8,128)(2,1)S(1)}, bf16[64,1536]{1,0:T(8,128)(2,1)S(1)}, u32[]{:S(2)}, u32[]{:S(2)}) %collective-permute-start.40) | collective-permute-done | bytes 196640 | tf_op jit(solution)/shard_map/ppermute | solution.py:165
  100.1 1.5 %collective-permute-start.44 = (bf16[64,1536]{1,0:T(8,128)(2,1)S(1)}, bf16[64,1536]{1,0:T(8,128)(2,1)S(1)}, u32[]{:S(2)}, u32[]{:S(2)}) collective-permute-start(bf16[64,1536]{1,0:T(8,128)(2,1)S(1)} %add_convert_fusion.4), channel_id=1, source_target_pairs={{4,0},{5,1},{8,4},{9,5},{12,8},{13,9},{14,12},{15,13},{10,14},{11,... | collective-permute-start | bytes 589832 | tf_op jit(solution)/shard_map/ppermute | solution.py:165
  101.6 0.6 collective-permute-start.43
  102.2 1.7 %collective-permute-start.46 = (bf16[64,1536]{1,0:T(8,128)(2,1)S(1)}, bf16[64,1536]{1,0:T(8,128)(2,1)S(1)}, u32[]{:S(2)}, u32[]{:S(2)}) collective-permute-start(bf16[64,1536]{1,0:T(8,128)(2,1)S(1)} %add_convert_fusion.3), channel_id=1, source_target_pairs={{0,4},{1,5},{4,8},{5,9},{8,12},{9,13},{12,14},{13,15},{14,10},{15,... | collective-permute-start | bytes 589832 | tf_op jit(solution)/shard_map/ppermute | solution.py:162
  104.2 3.6 %collective-permute-done.44 = bf16[64,1536]{1,0:T(8,128)(2,1)S(1)} collective-permute-done((bf16[64,1536]{1,0:T(8,128)(2,1)S(1)}, bf16[64,1536]{1,0:T(8,128)(2,1)S(1)}, u32[]{:S(2)}, u32[]{:S(2)}) %collective-permute-start.44) | collective-permute-done | bytes 196640 | tf_op jit(solution)/shard_map/ppermute | solution.py:165
  107.9 1.4 %collective-permute-done.43 = bf16[64,1536]{1,0:T(8,128)(2,1)S(1)} collective-permute-done((bf16[64,1536]{1,0:T(8,128)(2,1)S(1)}, bf16[64,1536]{1,0:T(8,128)(2,1)S(1)}, u32[]{:S(2)}, u32[]{:S(2)}) %collective-permute-start.43) | collective-permute-done | bytes 196640 | tf_op jit(solution)/shard_map/ppermute | solution.py:162
  109.4 0.7 collective-permute-start.45
  110.1 1.3 %collective-permute-start.48 = (bf16[64,1536]{1,0:T(8,128)(2,1)S(1)}, bf16[64,1536]{1,0:T(8,128)(2,1)S(1)}, u32[]{:S(2)}, u32[]{:S(2)}) collective-permute-start(bf16[64,1536]{1,0:T(8,128)(2,1)S(1)} %add_convert_fusion), channel_id=1, source_target_pairs={{4,0},{5,1},{8,4},{9,5},{12,8},{13,9},{14,12},{15,13},{10,14},{11,... | collective-permute-start | bytes 589832 | tf_op jit(solution)/shard_map/ppermute | solution.py:165
  111.7 3.4 %collective-permute-done.45.refs_4_ = bf16[64,1536]{1,0:T(8,128)(2,1)S(1)} collective-permute-done((bf16[64,1536]{1,0:T(8,128)(2,1)S(1)}, bf16[64,1536]{1,0:T(8,128)(2,1)S(1)}, u32[]{:S(2)}, u32[]{:S(2)}) %collective-permute-start.45) | collective-permute-done | bytes 196640 | tf_op jit(solution)/shard_map/ppermute | solution.py:162
  115.1 0.7 collective-permute-done.48.refs_7_
  115.8 1.6 %final.1 = bf16[128,1536]{1,0:T(8,128)(2,1)} custom-call(s32[3]{0:T(128)S(1)} %pad_add_fusion.place, bf16[64,1664]{1,0:T(8,128)(2,1)S(1)} %get-tuple-element.90.refs_4_.refs_0_, bf16[64,1664]{1,0:T(8,128)(2,1)S(1)} %get-tuple-element.91.refs_5_.refs_1_, f32[64,1536]{1,0:T(8,128)S(1)} %get-tuple-element.101.refs_2_, ...), custom_call_target="tpu_custom_call" | custom-call | bytes 4194304 | tf_op jit(solution)/shard_map/final/pallas_call | solution.py:27
  (75 shorter events, 10.2 us)
Async XLA Ops:
  0.0 10.5 %collective-permute-start.4 = (bf16[512,1536]{1,0:T(8,128)(2,1)}, bf16[512,1536]{1,0:T(8,128)(2,1)S(1)}, u32[]{:S(2)}, u32[]{:S(2)}) collective-permute-start(bf16[512,1536]{1,0:T(8,128)(2,1)} %bitcast.9), channel_id=1, source_target_pairs={{0,1},{1,0},{2,3},{3,2},{4,5},{5,4},{6,7},{7,6},{8,9},{9,8},{10,11... | collective-permute-start | bytes 4718600 | tf_op jit(solution)/shard_map/ppermute | solution.py:159
  0.5 8.2 %collective-permute-start.2 = (bf16[48,1536]{1,0:T(8,128)(2,1)}, bf16[48,1536]{1,0:T(8,128)(2,1)S(1)}, u32[]{:S(2)}, u32[]{:S(2)}) collective-permute-start(bf16[48,1536]{1,0:T(8,128)(2,1)} %refs_0_.1), channel_id=1, source_target_pairs={{0,16},{16,0},{1,17},{17,1},{2,18},{18,2},{3,19},{19,3},{4,20},{20... | collective-permute-start | bytes 442376 | tf_op jit(solution)/shard_map/ppermute | solution.py:187
  3.0 6.2 %collective-permute-start = (bf16[48,1536]{1,0:T(8,128)(2,1)}, bf16[48,1536]{1,0:T(8,128)(2,1)S(1)}, u32[]{:S(2)}, u32[]{:S(2)}) collective-permute-start(bf16[48,1536]{1,0:T(8,128)(2,1)} %refs_0_.1), channel_id=1, source_target_pairs={{0,4},{1,5},{4,8},{5,9},{8,12},{9,13},{12,14},{13,15},{14,10},{15,... | collective-permute-start | bytes 442376 | tf_op jit(solution)/shard_map/ppermute | solution.py:162
  4.5 5.9 %collective-permute-start.1 = (bf16[48,1536]{1,0:T(8,128)(2,1)}, bf16[48,1536]{1,0:T(8,128)(2,1)S(1)}, u32[]{:S(2)}, u32[]{:S(2)}) collective-permute-start(bf16[48,1536]{1,0:T(8,128)(2,1)} %refs_0_.1), channel_id=1, source_target_pairs={{4,0},{5,1},{8,4},{9,5},{12,8},{13,9},{14,12},{15,13},{10,14},{11,... | collective-permute-start | bytes 442376 | tf_op jit(solution)/shard_map/ppermute | solution.py:165
  5.0 1.9 %collective-permute-start.3 = (bf16[128,1536]{1,0:T(8,128)(2,1)}, bf16[128,1536]{1,0:T(8,128)(2,1)S(1)}, u32[]{:S(2)}, u32[]{:S(2)}) collective-permute-start(bf16[128,1536]{1,0:T(8,128)(2,1)} %att.1), channel_id=1, source_target_pairs={{0,1},{1,0},{2,3},{3,2},{4,5},{5,4},{6,7},{7,6},{8,9},{9,8},{10,11... | collective-permute-start | bytes 1179656 | tf_op jit(solution)/shard_map/ppermute | solution.py:159
  5.0 1.6 %copy-start.5 = (s32[128,8]{0,1:T(8,128)S(1)}, s32[128,8]{0,1:T(8,128)}, u32[]{:S(2)}) copy-start(s32[128,8]{0,1:T(8,128)} %param.15) | copy-start | bytes 12292
  5.0 1.7 %copy-start.6 = (f32[128,8]{0,1:T(8,128)S(1)}, f32[128,8]{0,1:T(8,128)}, u32[]{:S(2)}) copy-start(f32[128,8]{0,1:T(8,128)} %param.16) | copy-start | bytes 12292
  5.0 1.9 %copy-start.1 = (bf16[128,1536]{1,0:T(8,128)(2,1)S(1)}, bf16[128,1536]{1,0:T(8,128)(2,1)}, u32[]{:S(2)}) copy-start(bf16[128,1536]{1,0:T(8,128)(2,1)} %att.1) | copy-start | bytes 1179652
  5.0 30.9 %copy-start.3 = (bf16[48,1536]{1,0:T(8,128)(2,1)S(1)}, bf16[48,1536]{1,0:T(8,128)(2,1)}, u32[]{:S(2)}) copy-start(bf16[48,1536]{1,0:T(8,128)(2,1)} %refs_0_.1) | copy-start | bytes 442372
  8.6 31.1 %copy-start.2 = (bf16[128,1536]{1,0:T(8,128)(2,1)S(1)}, bf16[128,1536]{1,0:T(8,128)(2,1)}, u32[]{:S(2)}) copy-start(bf16[128,1536]{1,0:T(8,128)(2,1)} %res.1) | copy-start | bytes 1179652
  10.5 13.5 %collective-permute-start.6 = (bf16[1536,512]{1,0:T(8,128)(2,1)S(1)}, bf16[1536,512]{1,0:T(8,128)(2,1)S(1)}, u32[]{:S(2)}, u32[]{:S(2)}) collective-permute-start(bf16[1536,512]{1,0:T(8,128)(2,1)S(1)} %pad_maximum_fusion.refs_6_.refs_4_.refs_2_), channel_id=1, source_target_pairs={{0,1},{1,0},{2,3},{3,2},{4,5},{5,4},{6,7},{7,6},{8,9},{9,8},{10,11... | collective-permute-start | bytes 4718600 | tf_op jit(solution)/shard_map/ppermute | solution.py:159
  10.5 6.3 %collective-permute-start.9 = (bf16[48,1536]{1,0:T(8,128)(2,1)S(1)}, bf16[48,1536]{1,0:T(8,128)(2,1)S(1)}, u32[]{:S(2)}, u32[]{:S(2)}) collective-permute-start(bf16[48,1536]{1,0:T(8,128)(2,1)S(1)} %collective-permute-done.2.refs_1_), channel_id=1, source_target_pairs={{4,0},{5,1},{8,4},{9,5},{12,8},{13,9},{14,12},{15,13},{10,14},{11,... | collective-permute-start | bytes 442376 | tf_op jit(solution)/shard_map/ppermute | solution.py:165
  10.9 36.5 %collective-permute-start.25 = (bf16[1536,512]{1,0:T(8,128)(2,1)S(1)}, bf16[1536,512]{1,0:T(8,128)(2,1)S(1)}, u32[]{:S(2)}, u32[]{:S(2)}) collective-permute-start(bf16[1536,512]{1,0:T(8,128)(2,1)S(1)} %pad_maximum_fusion.refs_6_.refs_4_.refs_2_), channel_id=1, source_target_pairs={{0,16},{16,0},{1,17},{17,1},{2,18},{18,2},{3,19},{19,3},{4,20},{20... | collective-permute-start | bytes 4718600 | tf_op jit(solution)/shard_map/ppermute | solution.py:195
  11.3 6.7 %collective-permute-start.5 = (bf16[48,1536]{1,0:T(8,128)(2,1)S(1)}, bf16[48,1536]{1,0:T(8,128)(2,1)S(1)}, u32[]{:S(2)}, u32[]{:S(2)}) collective-permute-start(bf16[48,1536]{1,0:T(8,128)(2,1)S(1)} %collective-permute-done.refs_2_), channel_id=1, source_target_pairs={{0,4},{1,5},{4,8},{5,9},{8,12},{9,13},{12,14},{13,15},{14,10},{15,... | collective-permute-start | bytes 442376 | tf_op jit(solution)/shard_map/ppermute | solution.py:162
  13.0 7.1 %collective-permute-start.7 = (bf16[48,1536]{1,0:T(8,128)(2,1)S(1)}, bf16[48,1536]{1,0:T(8,128)(2,1)S(1)}, u32[]{:S(2)}, u32[]{:S(2)}) collective-permute-start(bf16[48,1536]{1,0:T(8,128)(2,1)S(1)} %collective-permute-done.2.refs_1_), channel_id=1, source_target_pairs={{0,4},{1,5},{4,8},{5,9},{8,12},{9,13},{12,14},{13,15},{14,10},{15,... | collective-permute-start | bytes 442376 | tf_op jit(solution)/shard_map/ppermute | solution.py:162
  16.7 6.8 %collective-permute-start.13 = (bf16[48,1536]{1,0:T(8,128)(2,1)S(1)}, bf16[48,1536]{1,0:T(8,128)(2,1)S(1)}, u32[]{:S(2)}, u32[]{:S(2)}) collective-permute-start(bf16[48,1536]{1,0:T(8,128)(2,1)S(1)} %collective-permute-done.9.refs_7_), channel_id=1, source_target_pairs={{4,0},{5,1},{8,4},{9,5},{12,8},{13,9},{14,12},{15,13},{10,14},{11,... | collective-permute-start | bytes 442376 | tf_op jit(solution)/shard_map/ppermute | solution.py:165
  18.0 8.6 %collective-permute-start.8 = (bf16[48,1536]{1,0:T(8,128)(2,1)S(1)}, bf16[48,1536]{1,0:T(8,128)(2,1)S(1)}, u32[]{:S(2)}, u32[]{:S(2)}) collective-permute-start(bf16[48,1536]{1,0:T(8,128)(2,1)S(1)} %collective-permute-done.1.refs_3_), channel_id=1, source_target_pairs={{4,0},{5,1},{8,4},{9,5},{12,8},{13,9},{14,12},{15,13},{10,14},{11,... | collective-permute-start | bytes 442376 | tf_op jit(solution)/shard_map/ppermute | solution.py:165
  20.2 6.9 %collective-permute-start.11 = (bf16[48,1536]{1,0:T(8,128)(2,1)S(1)}, bf16[48,1536]{1,0:T(8,128)(2,1)S(1)}, u32[]{:S(2)}, u32[]{:S(2)}) collective-permute-start(bf16[48,1536]{1,0:T(8,128)(2,1)S(1)} %collective-permute-done.7.refs_5_), channel_id=1, source_target_pairs={{0,4},{1,5},{4,8},{5,9},{8,12},{9,13},{12,14},{13,15},{14,10},{15,... | collective-permute-start | bytes 442376 | tf_op jit(solution)/shard_map/ppermute | solution.py:162
  23.5 6.8 %collective-permute-start.16 = (bf16[48,1536]{1,0:T(8,128)(2,1)S(1)}, bf16[48,1536]{1,0:T(8,128)(2,1)S(1)}, u32[]{:S(2)}, u32[]{:S(2)}) collective-permute-start(bf16[48,1536]{1,0:T(8,128)(2,1)S(1)} %collective-permute-done.13.refs_11_), channel_id=1, source_target_pairs={{4,0},{5,1},{8,4},{9,5},{12,8},{13,9},{14,12},{15,13},{10,14},{11,... | collective-permute-start | bytes 442376 | tf_op jit(solution)/shard_map/ppermute | solution.py:165
  23.9 6.8 %collective-permute-start.10 = (bf16[48,1536]{1,0:T(8,128)(2,1)S(1)}, bf16[48,1536]{1,0:T(8,128)(2,1)S(1)}, u32[]{:S(2)}, u32[]{:S(2)}) collective-permute-start(bf16[48,1536]{1,0:T(8,128)(2,1)S(1)} %collective-permute-done.5.refs_4_), channel_id=1, source_target_pairs={{0,4},{1,5},{4,8},{5,9},{8,12},{9,13},{12,14},{13,15},{14,10},{15,... | collective-permute-start | bytes 442376 | tf_op jit(solution)/shard_map/ppermute | solution.py:162
  26.6 6.6 %collective-permute-start.12 = (bf16[48,1536]{1,0:T(8,128)(2,1)S(1)}, bf16[48,1536]{1,0:T(8,128)(2,1)S(1)}, u32[]{:S(2)}, u32[]{:S(2)}) collective-permute-start(bf16[48,1536]{1,0:T(8,128)(2,1)S(1)} %collective-permute-done.8.refs_6_), channel_id=1, source_target_pairs={{4,0},{5,1},{8,4},{9,5},{12,8},{13,9},{14,12},{15,13},{10,14},{11,... | collective-permute-start | bytes 442376 | tf_op jit(solution)/shard_map/ppermute | solution.py:165
  27.1 6.2 %collective-permute-start.15 = (bf16[48,1536]{1,0:T(8,128)(2,1)S(1)}, bf16[48,1536]{1,0:T(8,128)(2,1)S(1)}, u32[]{:S(2)}, u32[]{:S(2)}) collective-permute-start(bf16[48,1536]{1,0:T(8,128)(2,1)S(1)} %collective-permute-done.11.refs_9_), channel_id=1, source_target_pairs={{0,4},{1,5},{4,8},{5,9},{8,12},{9,13},{12,14},{13,15},{14,10},{15,... | collective-permute-start | bytes 442376 | tf_op jit(solution)/shard_map/ppermute | solution.py:162
  30.3 5.1 %collective-permute-start.17 = (bf16[48,1536]{1,0:T(8,128)(2,1)S(1)}, bf16[48,1536]{1,0:T(8,128)(2,1)S(1)}, u32[]{:S(2)}, u32[]{:S(2)}) collective-permute-start(bf16[48,1536]{1,0:T(8,128)(2,1)S(1)} %collective-permute-done.16.refs_14_), channel_id=1, source_target_pairs={{4,0},{5,1},{8,4},{9,5},{12,8},{13,9},{14,12},{15,13},{10,14},{11,... | collective-permute-start | bytes 442376 | tf_op jit(solution)/shard_map/ppermute | solution.py:165
  30.7 5.1 %collective-permute-start.14 = (bf16[48,1536]{1,0:T(8,128)(2,1)S(1)}, bf16[48,1536]{1,0:T(8,128)(2,1)S(1)}, u32[]{:S(2)}, u32[]{:S(2)}) collective-permute-start(bf16[48,1536]{1,0:T(8,128)(2,1)S(1)} %collective-permute-done.10.refs_8_), channel_id=1, source_target_pairs={{0,4},{1,5},{4,8},{5,9},{8,12},{9,13},{12,14},{13,15},{14,10},{15,... | collective-permute-start | bytes 442376 | tf_op jit(solution)/shard_map/ppermute | solution.py:162
  37.4 26.3 %copy-start = (bf16[1,512,1536]{2,1,0:T(8,128)(2,1)S(1)}, bf16[1,512,1536]{2,1,0:T(8,128)(2,1)}, u32[]{:S(2)}) copy-start(bf16[1,512,1536]{2,1,0:T(8,128)(2,1)} %param.14) | copy-start | bytes 4718596
  37.4 2.4 %collective-permute-start.18 = (f32[128,1536]{1,0:T(8,128)S(1)}, f32[128,1536]{1,0:T(8,128)S(1)}, u32[]{:S(2)}, u32[]{:S(2)}) collective-permute-start(f32[128,1536]{1,0:T(8,128)S(1)} %get-tuple-element.88), channel_id=1, source_target_pairs={{0,1},{1,0},{2,3},{3,2},{4,5},{5,4},{6,7},{7,6},{8,9},{9,8},{10,11... | collective-permute-start | bytes 2359304 | tf_op jit(solution)/shard_map/ppermute | solution.py:159
  40.4 7.3 %collective-permute-start.23 = (bf16[64,1664]{1,0:T(8,128)(2,1)S(1)}, bf16[64,1664]{1,0:T(8,128)(2,1)S(1)}, u32[]{:S(2)}, u32[]{:S(2)}) collective-permute-start(bf16[64,1664]{1,0:T(8,128)(2,1)S(1)} %get-tuple-element.90.refs_4_.refs_0_), channel_id=1, source_target_pairs={{0,4},{1,5},{4,8},{5,9},{8,12},{9,13},{12,14},{13,15},{14,10},{15,... | collective-permute-start | bytes 638984 | tf_op jit(solution)/shard_map/ppermute | solution.py:162
  42.0 7.0 %collective-permute-start.24 = (bf16[64,1664]{1,0:T(8,128)(2,1)S(1)}, bf16[64,1664]{1,0:T(8,128)(2,1)S(1)}, u32[]{:S(2)}, u32[]{:S(2)}) collective-permute-start(bf16[64,1664]{1,0:T(8,128)(2,1)S(1)} %get-tuple-element.91.refs_5_.refs_1_), channel_id=1, source_target_pairs={{4,0},{5,1},{8,4},{9,5},{12,8},{13,9},{14,12},{15,13},{10,14},{11,... | collective-permute-start | bytes 638984 | tf_op jit(solution)/shard_map/ppermute | solution.py:165
  49.0 14.7 %collective-permute-start.26 = (bf16[1536,512]{1,0:T(8,128)(2,1)S(1)}, bf16[1536,512]{1,0:T(8,128)(2,1)S(1)}, u32[]{:S(2)}, u32[]{:S(2)}) collective-permute-start(bf16[1536,512]{1,0:T(8,128)(2,1)S(1)} %collective-permute-done.25.refs_7_.refs_5_.refs_3_), channel_id=1, source_target_pairs={{0,1},{1,0},{2,3},{3,2},{4,5},{5,4},{6,7},{7,6},{8,9},{9,8},{10,11... | collective-permute-start | bytes 4718600 | tf_op jit(solution)/shard_map/ppermute | solution.py:159
  49.0 8.0 %collective-permute-start.19 = (bf16[64,1664]{1,0:T(8,128)(2,1)S(1)}, bf16[64,1664]{1,0:T(8,128)(2,1)S(1)}, u32[]{:S(2)}, u32[]{:S(2)}) collective-permute-start(bf16[64,1664]{1,0:T(8,128)(2,1)S(1)} %get-tuple-element.91.refs_5_.refs_1_), channel_id=1, source_target_pairs={{0,4},{1,5},{4,8},{5,9},{8,12},{9,13},{12,14},{13,15},{14,10},{15,... | collective-permute-start | bytes 638984 | tf_op jit(solution)/shard_map/ppermute | solution.py:162
  50.6 8.1 %collective-permute-start.21 = (bf16[64,1664]{1,0:T(8,128)(2,1)S(1)}, bf16[64,1664]{1,0:T(8,128)(2,1)S(1)}, u32[]{:S(2)}, u32[]{:S(2)}) collective-permute-start(bf16[64,1664]{1,0:T(8,128)(2,1)S(1)} %get-tuple-element.90.refs_4_.refs_0_), channel_id=1, source_target_pairs={{4,0},{5,1},{8,4},{9,5},{12,8},{13,9},{14,12},{15,13},{10,14},{11,... | collective-permute-start | bytes 638984 | tf_op jit(solution)/shard_map/ppermute | solution.py:165
  51.0 10.6 %collective-permute-start.27 = (bf16[64,1664]{1,0:T(8,128)(2,1)S(1)}, bf16[64,1664]{1,0:T(8,128)(2,1)S(1)}, u32[]{:S(2)}, u32[]{:S(2)}) collective-permute-start(bf16[64,1664]{1,0:T(8,128)(2,1)S(1)} %collective-permute-done.23.refs_0_), channel_id=1, source_target_pairs={{0,4},{1,5},{4,8},{5,9},{8,12},{9,13},{12,14},{13,15},{14,10},{15,... | collective-permute-start | bytes 638984 | tf_op jit(solution)/shard_map/ppermute | solution.py:162
  52.6 10.6 %collective-permute-start.29 = (bf16[64,1664]{1,0:T(8,128)(2,1)S(1)}, bf16[64,1664]{1,0:T(8,128)(2,1)S(1)}, u32[]{:S(2)}, u32[]{:S(2)}) collective-permute-start(bf16[64,1664]{1,0:T(8,128)(2,1)S(1)} %collective-permute-done.24.refs_3_), channel_id=1, source_target_pairs={{4,0},{5,1},{8,4},{9,5},{12,8},{13,9},{14,12},{15,13},{10,14},{11,... | collective-permute-start | bytes 638984 | tf_op jit(solution)/shard_map/ppermute | solution.py:165
  57.1 11.1 %collective-permute-start.20 = (bf16[64,1664]{1,0:T(8,128)(2,1)S(1)}, bf16[64,1664]{1,0:T(8,128)(2,1)S(1)}, u32[]{:S(2)}, u32[]{:S(2)}) collective-permute-start(bf16[64,1664]{1,0:T(8,128)(2,1)S(1)} %collective-permute-done.19.refs_1_), channel_id=1, source_target_pairs={{0,4},{1,5},{4,8},{5,9},{8,12},{9,13},{12,14},{13,15},{14,10},{15,... | collective-permute-start | bytes 638984 | tf_op jit(solution)/shard_map/ppermute | solution.py:162
  58.7 9.5 %collective-permute-start.22 = (bf16[64,1664]{1,0:T(8,128)(2,1)S(1)}, bf16[64,1664]{1,0:T(8,128)(2,1)S(1)}, u32[]{:S(2)}, u32[]{:S(2)}) collective-permute-start(bf16[64,1664]{1,0:T(8,128)(2,1)S(1)} %collective-permute-done.21.refs_2_), channel_id=1, source_target_pairs={{4,0},{5,1},{8,4},{9,5},{12,8},{13,9},{14,12},{15,13},{10,14},{11,... | collective-permute-start | bytes 638984 | tf_op jit(solution)/shard_map/ppermute | solution.py:165
  61.6 12.0 %collective-permute-start.28 = (bf16[64,1664]{1,0:T(8,128)(2,1)S(1)}, bf16[64,1664]{1,0:T(8,128)(2,1)S(1)}, u32[]{:S(2)}, u32[]{:S(2)}) collective-permute-start(bf16[64,1664]{1,0:T(8,128)(2,1)S(1)} %collective-permute-done.27.refs_0_), channel_id=1, source_target_pairs={{0,4},{1,5},{4,8},{5,9},{8,12},{9,13},{12,14},{13,15},{14,10},{15,... | collective-permute-start | bytes 638984 | tf_op jit(solution)/shard_map/ppermute | solution.py:162
  63.3 10.4 %collective-permute-start.30 = (bf16[64,1664]{1,0:T(8,128)(2,1)S(1)}, bf16[64,1664]{1,0:T(8,128)(2,1)S(1)}, u32[]{:S(2)}, u32[]{:S(2)}) collective-permute-start(bf16[64,1664]{1,0:T(8,128)(2,1)S(1)} %collective-permute-done.29.refs_3_), channel_id=1, source_target_pairs={{4,0},{5,1},{8,4},{9,5},{12,8},{13,9},{14,12},{15,13},{10,14},{11,... | collective-permute-start | bytes 638984 | tf_op jit(solution)/shard_map/ppermute | solution.py:165
  68.2 7.5 %collective-permute-start.33 = (bf16[64,1664]{1,0:T(8,128)(2,1)S(1)}, bf16[64,1664]{1,0:T(8,128)(2,1)S(1)}, u32[]{:S(2)}, u32[]{:S(2)}) collective-permute-start(bf16[64,1664]{1,0:T(8,128)(2,1)S(1)} %collective-permute-done.20.refs_1_), channel_id=1, source_target_pairs={{0,4},{1,5},{4,8},{5,9},{8,12},{9,13},{12,14},{13,15},{14,10},{15,... | collective-permute-start | bytes 638984 | tf_op jit(solution)/shard_map/ppermute | solution.py:162
  69.9 6.8 %collective-permute-start.34 = (bf16[64,1664]{1,0:T(8,128)(2,1)S(1)}, bf16[64,1664]{1,0:T(8,128)(2,1)S(1)}, u32[]{:S(2)}, u32[]{:S(2)}) collective-permute-start(bf16[64,1664]{1,0:T(8,128)(2,1)S(1)} %collective-permute-done.22.refs_2_), channel_id=1, source_target_pairs={{4,0},{5,1},{8,4},{9,5},{12,8},{13,9},{14,12},{15,13},{10,14},{11,... | collective-permute-start | bytes 638984 | tf_op jit(solution)/shard_map/ppermute | solution.py:165
  73.7 6.3 %collective-permute-start.31 = (bf16[64,1664]{1,0:T(8,128)(2,1)S(1)}, bf16[64,1664]{1,0:T(8,128)(2,1)S(1)}, u32[]{:S(2)}, u32[]{:S(2)}) collective-permute-start(bf16[64,1664]{1,0:T(8,128)(2,1)S(1)} %collective-permute-done.28.refs_0_), channel_id=1, source_target_pairs={{0,4},{1,5},{4,8},{5,9},{8,12},{9,13},{12,14},{13,15},{14,10},{15,... | collective-permute-start | bytes 638984 | tf_op jit(solution)/shard_map/ppermute | solution.py:162
  75.3 5.8 %collective-permute-start.32 = (bf16[64,1664]{1,0:T(8,128)(2,1)S(1)}, bf16[64,1664]{1,0:T(8,128)(2,1)S(1)}, u32[]{:S(2)}, u32[]{:S(2)}) collective-permute-start(bf16[64,1664]{1,0:T(8,128)(2,1)S(1)} %collective-permute-done.30.refs_3_), channel_id=1, source_target_pairs={{4,0},{5,1},{8,4},{9,5},{12,8},{13,9},{14,12},{15,13},{10,14},{11,... | collective-permute-start | bytes 638984 | tf_op jit(solution)/shard_map/ppermute | solution.py:165
  81.2 7.5 %collective-permute-start.38 = (bf16[64,1536]{1,0:T(8,128)(2,1)S(1)}, bf16[64,1536]{1,0:T(8,128)(2,1)S(1)}, u32[]{:S(2)}, u32[]{:S(2)}) collective-permute-start(bf16[64,1536]{1,0:T(8,128)(2,1)S(1)} %convert_element_type.87), channel_id=1, source_target_pairs={{4,0},{5,1},{8,4},{9,5},{12,8},{13,9},{14,12},{15,13},{10,14},{11,... | collective-permute-start | bytes 589832 | tf_op jit(solution)/shard_map/ppermute | solution.py:165
  81.7 7.8 %collective-permute-start.37 = (bf16[64,1536]{1,0:T(8,128)(2,1)S(1)}, bf16[64,1536]{1,0:T(8,128)(2,1)S(1)}, u32[]{:S(2)}, u32[]{:S(2)}) collective-permute-start(bf16[64,1536]{1,0:T(8,128)(2,1)S(1)} %convert_element_type.86), channel_id=1, source_target_pairs={{0,4},{1,5},{4,8},{5,9},{8,12},{9,13},{12,14},{13,15},{14,10},{15,... | collective-permute-start | bytes 589832 | tf_op jit(solution)/shard_map/ppermute | solution.py:162
  85.6 7.9 %collective-permute-start.36 = (bf16[64,1536]{1,0:T(8,128)(2,1)S(1)}, bf16[64,1536]{1,0:T(8,128)(2,1)S(1)}, u32[]{:S(2)}, u32[]{:S(2)}) collective-permute-start(bf16[64,1536]{1,0:T(8,128)(2,1)S(1)} %convert_element_type.81), channel_id=1, source_target_pairs={{4,0},{5,1},{8,4},{9,5},{12,8},{13,9},{14,12},{15,13},{10,14},{11,... | collective-permute-start | bytes 589832 | tf_op jit(solution)/shard_map/ppermute | solution.py:165
  86.1 7.8 %collective-permute-start.35 = (bf16[64,1536]{1,0:T(8,128)(2,1)S(1)}, bf16[64,1536]{1,0:T(8,128)(2,1)S(1)}, u32[]{:S(2)}, u32[]{:S(2)}) collective-permute-start(bf16[64,1536]{1,0:T(8,128)(2,1)S(1)} %convert_element_type.80), channel_id=1, source_target_pairs={{0,4},{1,5},{4,8},{5,9},{8,12},{9,13},{12,14},{13,15},{14,10},{15,... | collective-permute-start | bytes 589832 | tf_op jit(solution)/shard_map/ppermute | solution.py:162
  89.5 8.0 %collective-permute-start.42 = (bf16[64,1536]{1,0:T(8,128)(2,1)S(1)}, bf16[64,1536]{1,0:T(8,128)(2,1)S(1)}, u32[]{:S(2)}, u32[]{:S(2)}) collective-permute-start(bf16[64,1536]{1,0:T(8,128)(2,1)S(1)} %add_convert_fusion.6), channel_id=1, source_target_pairs={{4,0},{5,1},{8,4},{9,5},{12,8},{13,9},{14,12},{15,13},{10,14},{11,... | collective-permute-start | bytes 589832 | tf_op jit(solution)/shard_map/ppermute | solution.py:165
  90.0 7.9 %collective-permute-start.41 = (bf16[64,1536]{1,0:T(8,128)(2,1)S(1)}, bf16[64,1536]{1,0:T(8,128)(2,1)S(1)}, u32[]{:S(2)}, u32[]{:S(2)}) collective-permute-start(bf16[64,1536]{1,0:T(8,128)(2,1)S(1)} %add_convert_fusion.7), channel_id=1, source_target_pairs={{0,4},{1,5},{4,8},{5,9},{8,12},{9,13},{12,14},{13,15},{14,10},{15,... | collective-permute-start | bytes 589832 | tf_op jit(solution)/shard_map/ppermute | solution.py:162
  93.9 5.7 %collective-permute-start.40 = (bf16[64,1536]{1,0:T(8,128)(2,1)S(1)}, bf16[64,1536]{1,0:T(8,128)(2,1)S(1)}, u32[]{:S(2)}, u32[]{:S(2)}) collective-permute-start(bf16[64,1536]{1,0:T(8,128)(2,1)S(1)} %add_convert_fusion.8), channel_id=1, source_target_pairs={{4,0},{5,1},{8,4},{9,5},{12,8},{13,9},{14,12},{15,13},{10,14},{11,... | collective-permute-start | bytes 589832 | tf_op jit(solution)/shard_map/ppermute | solution.py:165
  94.4 5.7 %collective-permute-start.39 = (bf16[64,1536]{1,0:T(8,128)(2,1)S(1)}, bf16[64,1536]{1,0:T(8,128)(2,1)S(1)}, u32[]{:S(2)}, u32[]{:S(2)}) collective-permute-start(bf16[64,1536]{1,0:T(8,128)(2,1)S(1)} %add_convert_fusion.9), channel_id=1, source_target_pairs={{0,4},{1,5},{4,8},{5,9},{8,12},{9,13},{12,14},{13,15},{14,10},{15,... | collective-permute-start | bytes 589832 | tf_op jit(solution)/shard_map/ppermute | solution.py:162
  98.0 13.5 %copy-start.4 = (f32[1536]{0:T(1024)S(1)}, f32[1536]{0:T(1024)}, u32[]{:S(2)}) copy-start(f32[1536]{0:T(1024)} %param.17) | copy-start | bytes 18436
  100.1 7.7 %collective-permute-start.44 = (bf16[64,1536]{1,0:T(8,128)(2,1)S(1)}, bf16[64,1536]{1,0:T(8,128)(2,1)S(1)}, u32[]{:S(2)}, u32[]{:S(2)}) collective-permute-start(bf16[64,1536]{1,0:T(8,128)(2,1)S(1)} %add_convert_fusion.4), channel_id=1, source_target_pairs={{4,0},{5,1},{8,4},{9,5},{12,8},{13,9},{14,12},{15,13},{10,14},{11,... | collective-permute-start | bytes 589832 | tf_op jit(solution)/shard_map/ppermute | solution.py:165
  101.6 7.7 %collective-permute-start.43 = (bf16[64,1536]{1,0:T(8,128)(2,1)S(1)}, bf16[64,1536]{1,0:T(8,128)(2,1)S(1)}, u32[]{:S(2)}, u32[]{:S(2)}) collective-permute-start(bf16[64,1536]{1,0:T(8,128)(2,1)S(1)} %add_convert_fusion.5), channel_id=1, source_target_pairs={{0,4},{1,5},{4,8},{5,9},{8,12},{9,13},{12,14},{13,15},{14,10},{15,... | collective-permute-start | bytes 589832 | tf_op jit(solution)/shard_map/ppermute | solution.py:162
  102.2 9.3 %collective-permute-start.46 = (bf16[64,1536]{1,0:T(8,128)(2,1)S(1)}, bf16[64,1536]{1,0:T(8,128)(2,1)S(1)}, u32[]{:S(2)}, u32[]{:S(2)}) collective-permute-start(bf16[64,1536]{1,0:T(8,128)(2,1)S(1)} %add_convert_fusion.3), channel_id=1, source_target_pairs={{0,4},{1,5},{4,8},{5,9},{8,12},{9,13},{12,14},{13,15},{14,10},{15,... | collective-permute-start | bytes 589832 | tf_op jit(solution)/shard_map/ppermute | solution.py:162
  103.8 7.9 %collective-permute-start.47 = (bf16[64,1536]{1,0:T(8,128)(2,1)S(1)}, bf16[64,1536]{1,0:T(8,128)(2,1)S(1)}, u32[]{:S(2)}, u32[]{:S(2)}) collective-permute-start(bf16[64,1536]{1,0:T(8,128)(2,1)S(1)} %add_convert_fusion.2), channel_id=1, source_target_pairs={{4,0},{5,1},{8,4},{9,5},{12,8},{13,9},{14,12},{15,13},{10,14},{11,... | collective-permute-start | bytes 589832 | tf_op jit(solution)/shard_map/ppermute | solution.py:165
  109.4 5.7 %collective-permute-start.45 = (bf16[64,1536]{1,0:T(8,128)(2,1)S(1)}, bf16[64,1536]{1,0:T(8,128)(2,1)S(1)}, u32[]{:S(2)}, u32[]{:S(2)}) collective-permute-start(bf16[64,1536]{1,0:T(8,128)(2,1)S(1)} %add_convert_fusion.1), channel_id=1, source_target_pairs={{0,4},{1,5},{4,8},{5,9},{8,12},{9,13},{12,14},{13,15},{14,10},{15,... | collective-permute-start | bytes 589832 | tf_op jit(solution)/shard_map/ppermute | solution.py:162
  110.1 5.7 %collective-permute-start.48 = (bf16[64,1536]{1,0:T(8,128)(2,1)S(1)}, bf16[64,1536]{1,0:T(8,128)(2,1)S(1)}, u32[]{:S(2)}, u32[]{:S(2)}) collective-permute-start(bf16[64,1536]{1,0:T(8,128)(2,1)S(1)} %add_convert_fusion), channel_id=1, source_target_pairs={{4,0},{5,1},{8,4},{9,5},{12,8},{13,9},{14,12},{15,13},{10,14},{11,... | collective-permute-start | bytes 589832 | tf_op jit(solution)/shard_map/ppermute | solution.py:165

commit v6 on v5

--- a/solution.py
+++ b/solution.py
@@ -278,8 +278,7 @@
             _, both_far = together(lead, both_far)
             weights = (both, both_far, down, both_near, swap(both_far), down_near)
         if step == far:
-            lead, done = together(lead, work(far - 1))
-            terms.update(done)
+            terms.update(work(far - 1))
             break
         rows_at[-step, 0], rows_at[step, 1] = lead
         if step > 2:

time: 118 us -> 116 us (0.983)
  transfers between devices with their start and end apart: 49 -> 49, of which waited for: 33 -> 32; matrix products, arithmetic and copies ran while one was open for 2% -> 2% of each run, Pallas kernels for 15% -> 15%
where the time goes in v6:
time: 116 us
  starting transfers between devices  47.9 us (41%)
  waiting for transfers between devices  47.3 us (41%)
  Pallas kernels  18.8 us (16%)
  other arithmetic  2.07 us (2%)
    ppermute x21, starting transfers between devices, go(): return lax.ppermute(x, 'expert', forth)  31.3 us
    ppermute x21, waiting for transfers between devices, come(): return lax.ppermute(x, 'expert', back)  23.8 us
    pallas_call x8, Pallas kernels, call(): pl.pallas_call(kernel, in_specs=[SMEM] + [VMEM] * (len(args) - 1), out_sp...  18.8 us
    ppermute x21, waiting for transfers between devices, go(): return lax.ppermute(x, 'expert', forth)  16 us
    ppermute x21, starting transfers between devices, come(): return lax.ppermute(x, 'expert', back)  13.2 us
    ppermute x1, waiting for transfers between devices, body(): both_far = lax.ppermute(both, 'dp', flip)  4.99 us
    ppermute x5, waiting for transfers between devices, swap(): return lax.ppermute(x, 'expert', across)  2.55 us
    ppermute x1, starting transfers between devices, body(): mine, other = (out_weight, lax.ppermute(out_weight, 'dp', flip))  2.52 us
  transfers between devices with their start and end apart: 49, of which 32 were waited for; matrix products, arithmetic and copies ran while one was open for 2% of the time, Pallas kernels for 15%

profile of v6, /device:TPU:0, one launch (start us, length us, event | category | flops | bytes accessed | tf_op | source)
XLA Modules:
  0.0 116.3 jit_solution(470887252940533507)
XLA Ops:
  0.5 2.5 %collective-permute-start.2 = (bf16[48,1536]{1,0:T(8,128)(2,1)}, bf16[48,1536]{1,0:T(8,128)(2,1)S(1)}, u32[]{:S(2)}, u32[]{:S(2)}) collective-permute-start(bf16[48,1536]{1,0:T(8,128)(2,1)} %refs_0_.1), channel_id=1, source_target_pairs={{0,16},{16,0},{1,17},{17,1},{2,18},{18,2},{3,19},{19,3},{4,20},{20... | collective-permute-start | bytes 442376 | tf_op jit(solution)/shard_map/ppermute | solution.py:187
  3.0 1.6 %collective-permute-start = (bf16[48,1536]{1,0:T(8,128)(2,1)}, bf16[48,1536]{1,0:T(8,128)(2,1)S(1)}, u32[]{:S(2)}, u32[]{:S(2)}) collective-permute-start(bf16[48,1536]{1,0:T(8,128)(2,1)} %refs_0_.1), channel_id=1, source_target_pairs={{0,4},{1,5},{4,8},{5,9},{8,12},{9,13},{12,14},{13,15},{14,10},{15,... | collective-permute-start | bytes 442376 | tf_op jit(solution)/shard_map/ppermute | solution.py:162
  5.0 1.5 %pad_maximum_fusion.refs_6_.refs_4_.refs_2_ = bf16[1536,512]{1,0:T(8,128)(2,1)S(1)} fusion(bf16[768,512]{1,0:T(8,128)(2,1)} %bitcast.14, bf16[768,512]{1,0:T(8,128)(2,1)} %bitcast.15), kind=kLoop, calls=%fused_computation | loop fusion | flops 3145728 | bytes 3145728 | tf_op jit(solution)/shard_map/concatenate | solution.py:193
  6.9 1.7 %prepare.1 = (bf16[256,768]{1,0:T(8,128)(2,1)S(1)}, bf16[128,128]{1,0:T(8,128)(2,1)S(1)}) custom-call(s32[3]{0:T(128)S(1)} %pad_add_fusion.place, bf16[128,1536]{1,0:T(8,128)(2,1)S(1)} %copy-done.1, bf16[128,1536]{1,0:T(8,128)(2,1)S(1)} %collective-permute-done.3.att_near, f32[16,128]{1,0:T(8,128)S(1)} %pad_maximum_fusion.1.table), custom_call_target="tpu_custom_call" | custom-call | bytes 4194304 | tf_op jit(solution)/shard_map/prepare/pallas_call | solution.py:27
  8.6 0.6 collective-permute-done.refs_2_
  9.2 1.3 %collective-permute-done.1.refs_3_ = bf16[48,1536]{1,0:T(8,128)(2,1)S(1)} collective-permute-done((bf16[48,1536]{1,0:T(8,128)(2,1)}, bf16[48,1536]{1,0:T(8,128)(2,1)S(1)}, u32[]{:S(2)}, u32[]{:S(2)}) %collective-permute-start.1) | collective-permute-done | bytes 147488 | tf_op jit(solution)/shard_map/ppermute | solution.py:165
  11.3 1.7 %collective-permute-start.5 = (bf16[48,1536]{1,0:T(8,128)(2,1)S(1)}, bf16[48,1536]{1,0:T(8,128)(2,1)S(1)}, u32[]{:S(2)}, u32[]{:S(2)}) collective-permute-start(bf16[48,1536]{1,0:T(8,128)(2,1)S(1)} %collective-permute-done.refs_2_), channel_id=1, source_target_pairs={{0,4},{1,5},{4,8},{5,9},{8,12},{9,13},{12,14},{13,15},{14,10},{15,... | collective-permute-start | bytes 442376 | tf_op jit(solution)/shard_map/ppermute | solution.py:162
  13.0 1.6 %collective-permute-start.7 = (bf16[48,1536]{1,0:T(8,128)(2,1)S(1)}, bf16[48,1536]{1,0:T(8,128)(2,1)S(1)}, u32[]{:S(2)}, u32[]{:S(2)}) collective-permute-start(bf16[48,1536]{1,0:T(8,128)(2,1)S(1)} %collective-permute-done.2.refs_1_), channel_id=1, source_target_pairs={{0,4},{1,5},{4,8},{5,9},{8,12},{9,13},{12,14},{13,15},{14,10},{15,... | collective-permute-start | bytes 442376 | tf_op jit(solution)/shard_map/ppermute | solution.py:162
  14.6 2.1 %collective-permute-done.9.refs_7_ = bf16[48,1536]{1,0:T(8,128)(2,1)S(1)} collective-permute-done((bf16[48,1536]{1,0:T(8,128)(2,1)S(1)}, bf16[48,1536]{1,0:T(8,128)(2,1)S(1)}, u32[]{:S(2)}, u32[]{:S(2)}) %collective-permute-start.9) | collective-permute-done | bytes 147488 | tf_op jit(solution)/shard_map/ppermute | solution.py:165
  17.2 0.8 collective-permute-done.5.refs_4_
  18.0 1.6 %collective-permute-start.8 = (bf16[48,1536]{1,0:T(8,128)(2,1)S(1)}, bf16[48,1536]{1,0:T(8,128)(2,1)S(1)}, u32[]{:S(2)}, u32[]{:S(2)}) collective-permute-start(bf16[48,1536]{1,0:T(8,128)(2,1)S(1)} %collective-permute-done.1.refs_3_), channel_id=1, source_target_pairs={{4,0},{5,1},{8,4},{9,5},{12,8},{13,9},{14,12},{15,13},{10,14},{11,... | collective-permute-start | bytes 442376 | tf_op jit(solution)/shard_map/ppermute | solution.py:165
  19.6 0.5 collective-permute-done.7.refs_5_
  20.2 1.7 %collective-permute-start.11 = (bf16[48,1536]{1,0:T(8,128)(2,1)S(1)}, bf16[48,1536]{1,0:T(8,128)(2,1)S(1)}, u32[]{:S(2)}, u32[]{:S(2)}) collective-permute-start(bf16[48,1536]{1,0:T(8,128)(2,1)S(1)} %collective-permute-done.7.refs_5_), channel_id=1, source_target_pairs={{0,4},{1,5},{4,8},{5,9},{8,12},{9,13},{12,14},{13,15},{14,10},{15,... | collective-permute-start | bytes 442376 | tf_op jit(solution)/shard_map/ppermute | solution.py:162
  21.9 1.6 %collective-permute-done.13.refs_11_ = bf16[48,1536]{1,0:T(8,128)(2,1)S(1)} collective-permute-done((bf16[48,1536]{1,0:T(8,128)(2,1)S(1)}, bf16[48,1536]{1,0:T(8,128)(2,1)S(1)}, u32[]{:S(2)}, u32[]{:S(2)}) %collective-permute-start.13) | collective-permute-done | bytes 147488 | tf_op jit(solution)/shard_map/ppermute | solution.py:165
  23.9 1.6 %collective-permute-start.10 = (bf16[48,1536]{1,0:T(8,128)(2,1)S(1)}, bf16[48,1536]{1,0:T(8,128)(2,1)S(1)}, u32[]{:S(2)}, u32[]{:S(2)}) collective-permute-start(bf16[48,1536]{1,0:T(8,128)(2,1)S(1)} %collective-permute-done.5.refs_4_), channel_id=1, source_target_pairs={{0,4},{1,5},{4,8},{5,9},{8,12},{9,13},{12,14},{13,15},{14,10},{15,... | collective-permute-start | bytes 442376 | tf_op jit(solution)/shard_map/ppermute | solution.py:162
  25.5 1.1 collective-permute-done.8.refs_6_
  27.1 1.6 %collective-permute-start.15 = (bf16[48,1536]{1,0:T(8,128)(2,1)S(1)}, bf16[48,1536]{1,0:T(8,128)(2,1)S(1)}, u32[]{:S(2)}, u32[]{:S(2)}) collective-permute-start(bf16[48,1536]{1,0:T(8,128)(2,1)S(1)} %collective-permute-done.11.refs_9_), channel_id=1, source_target_pairs={{0,4},{1,5},{4,8},{5,9},{8,12},{9,13},{12,14},{13,15},{14,10},{15,... | collective-permute-start | bytes 442376 | tf_op jit(solution)/shard_map/ppermute | solution.py:162
  28.7 1.6 %collective-permute-done.16.refs_14_ = bf16[48,1536]{1,0:T(8,128)(2,1)S(1)} collective-permute-done((bf16[48,1536]{1,0:T(8,128)(2,1)S(1)}, bf16[48,1536]{1,0:T(8,128)(2,1)S(1)}, u32[]{:S(2)}, u32[]{:S(2)}) %collective-permute-start.16) | collective-permute-done | bytes 147488 | tf_op jit(solution)/shard_map/ppermute | solution.py:165
  30.7 1.6 %collective-permute-start.14 = (bf16[48,1536]{1,0:T(8,128)(2,1)S(1)}, bf16[48,1536]{1,0:T(8,128)(2,1)S(1)}, u32[]{:S(2)}, u32[]{:S(2)}) collective-permute-start(bf16[48,1536]{1,0:T(8,128)(2,1)S(1)} %collective-permute-done.10.refs_8_), channel_id=1, source_target_pairs={{0,4},{1,5},{4,8},{5,9},{8,12},{9,13},{12,14},{13,15},{14,10},{15,... | collective-permute-start | bytes 442376 | tf_op jit(solution)/shard_map/ppermute | solution.py:162
  32.3 1.0 collective-permute-done.12.refs_10_
  33.3 2.1 %collective-permute-done.17.refs_15_ = bf16[48,1536]{1,0:T(8,128)(2,1)S(1)} collective-permute-done((bf16[48,1536]{1,0:T(8,128)(2,1)S(1)}, bf16[48,1536]{1,0:T(8,128)(2,1)S(1)}, u32[]{:S(2)}, u32[]{:S(2)}) %collective-permute-start.17) | collective-permute-done | bytes 147488 | tf_op jit(solution)/shard_map/ppermute | solution.py:165
  35.9 1.5 %project.1 = (f32[128,1536]{1,0:T(8,128)S(1)}, f32[128,1536]{1,0:T(8,128)S(1)}) custom-call(s32[3]{0:T(128)S(1)} %pad_add_fusion.place, bf16[256,768]{1,0:T(8,128)(2,1)S(1)} %get-tuple-element.74.tokens, bf16[48,1536]{1,0:T(8,128)(2,1)S(1)} %copy-done.3, bf16[48,1536]{1,0:T(8,128)(2,1)S(1)} %collective-permute-done.2.refs_1_, ...), custom_call_target="tpu_custom_call" | custom-call | flops 603979776 | bytes 4194304 | tf_op jit(solution)/shard_map/project/pallas_call | solution.py:27
  37.5 2.3 %collective-permute-done.18.near = f32[128,1536]{1,0:T(8,128)S(1)} collective-permute-done((f32[128,1536]{1,0:T(8,128)S(1)}, f32[128,1536]{1,0:T(8,128)S(1)}, u32[]{:S(2)}, u32[]{:S(2)}) %collective-permute-start.18) | collective-permute-done | bytes 786464 | tf_op jit(solution)/shard_map/ppermute | solution.py:159
  39.7 0.6 stream.1
  40.4 1.6 %collective-permute-start.23 = (bf16[64,1664]{1,0:T(8,128)(2,1)S(1)}, bf16[64,1664]{1,0:T(8,128)(2,1)S(1)}, u32[]{:S(2)}, u32[]{:S(2)}) collective-permute-start(bf16[64,1664]{1,0:T(8,128)(2,1)S(1)} %get-tuple-element.84.refs_4_.refs_0_), channel_id=1, source_target_pairs={{0,4},{1,5},{4,8},{5,9},{8,12},{9,13},{12,14},{13,15},{14,10},{15,... | collective-permute-start | bytes 638984 | tf_op jit(solution)/shard_map/ppermute | solution.py:162
  42.5 5.0 %collective-permute-done.25.refs_7_.refs_5_.refs_3_ = bf16[1536,512]{1,0:T(8,128)(2,1)S(1)} collective-permute-done((bf16[1536,512]{1,0:T(8,128)(2,1)S(1)}, bf16[1536,512]{1,0:T(8,128)(2,1)S(1)}, u32[]{:S(2)}, u32[]{:S(2)}) %collective-permute-start.25) | collective-permute-done | bytes 1572896 | tf_op jit(solution)/shard_map/ppermute | solution.py:195
  47.7 1.3 %collective-permute-done.24.refs_3_ = bf16[64,1664]{1,0:T(8,128)(2,1)S(1)} collective-permute-done((bf16[64,1664]{1,0:T(8,128)(2,1)S(1)}, bf16[64,1664]{1,0:T(8,128)(2,1)S(1)}, u32[]{:S(2)}, u32[]{:S(2)}) %collective-permute-start.24) | collective-permute-done | bytes 213024 | tf_op jit(solution)/shard_map/ppermute | solution.py:165
  49.0 1.6 %collective-permute-start.19 = (bf16[64,1664]{1,0:T(8,128)(2,1)S(1)}, bf16[64,1664]{1,0:T(8,128)(2,1)S(1)}, u32[]{:S(2)}, u32[]{:S(2)}) collective-permute-start(bf16[64,1664]{1,0:T(8,128)(2,1)S(1)} %get-tuple-element.85.refs_5_.refs_1_), channel_id=1, source_target_pairs={{0,4},{1,5},{4,8},{5,9},{8,12},{9,13},{12,14},{13,15},{14,10},{15,... | collective-permute-start | bytes 638984 | tf_op jit(solution)/shard_map/ppermute | solution.py:162
  51.0 1.6 %collective-permute-start.27 = (bf16[64,1664]{1,0:T(8,128)(2,1)S(1)}, bf16[64,1664]{1,0:T(8,128)(2,1)S(1)}, u32[]{:S(2)}, u32[]{:S(2)}) collective-permute-start(bf16[64,1664]{1,0:T(8,128)(2,1)S(1)} %collective-permute-done.23.refs_0_), channel_id=1, source_target_pairs={{0,4},{1,5},{4,8},{5,9},{8,12},{9,13},{12,14},{13,15},{14,10},{15,... | collective-permute-start | bytes 638984 | tf_op jit(solution)/shard_map/ppermute | solution.py:162
  53.1 4.0 %collective-permute-done.19.refs_1_ = bf16[64,1664]{1,0:T(8,128)(2,1)S(1)} collective-permute-done((bf16[64,1664]{1,0:T(8,128)(2,1)S(1)}, bf16[64,1664]{1,0:T(8,128)(2,1)S(1)}, u32[]{:S(2)}, u32[]{:S(2)}) %collective-permute-start.19) | collective-permute-done | bytes 213024 | tf_op jit(solution)/shard_map/ppermute | solution.py:162
  57.1 1.6 %collective-permute-start.20 = (bf16[64,1664]{1,0:T(8,128)(2,1)S(1)}, bf16[64,1664]{1,0:T(8,128)(2,1)S(1)}, u32[]{:S(2)}, u32[]{:S(2)}) collective-permute-start(bf16[64,1664]{1,0:T(8,128)(2,1)S(1)} %collective-permute-done.19.refs_1_), channel_id=1, source_target_pairs={{0,4},{1,5},{4,8},{5,9},{8,12},{9,13},{12,14},{13,15},{14,10},{15,... | collective-permute-start | bytes 638984 | tf_op jit(solution)/shard_map/ppermute | solution.py:162
  59.1 2.5 %collective-permute-done.27.refs_0_ = bf16[64,1664]{1,0:T(8,128)(2,1)S(1)} collective-permute-done((bf16[64,1664]{1,0:T(8,128)(2,1)S(1)}, bf16[64,1664]{1,0:T(8,128)(2,1)S(1)}, u32[]{:S(2)}, u32[]{:S(2)}) %collective-permute-start.27) | collective-permute-done | bytes 213024 | tf_op jit(solution)/shard_map/ppermute | solution.py:162
  61.6 1.6 %collective-permute-start.28 = (bf16[64,1664]{1,0:T(8,128)(2,1)S(1)}, bf16[64,1664]{1,0:T(8,128)(2,1)S(1)}, u32[]{:S(2)}, u32[]{:S(2)}) collective-permute-start(bf16[64,1664]{1,0:T(8,128)(2,1)S(1)} %collective-permute-done.27.refs_0_), channel_id=1, source_target_pairs={{0,4},{1,5},{4,8},{5,9},{8,12},{9,13},{12,14},{13,15},{14,10},{15,... | collective-permute-start | bytes 638984 | tf_op jit(solution)/shard_map/ppermute | solution.py:162
  63.7 4.5 %experts.4 = (f32[64,1536]{1,0:T(8,128)S(1)}, f32[64,1536]{1,0:T(8,128)S(1)}, f32[64,1536]{1,0:T(8,128)S(1)}, f32[64,1536]{1,0:T(8,128)S(1)}, f32[64,1536]{1,0:T(8,128)S(1)}, /*index=5*/f32[64,1536]{1,0:T(8,128)S(1)}) custom-call(s32[3]{0:T(128)S(1)} %pad_add_fusion.place, bf16[64,1664]{1,0:T(8,128)(2,1)S(1)} %collective-permute-done.23.refs_0_, ...), custom_call_target="tpu_custom_call" | custom-call | flops 3623878656 | bytes 4194304 | tf_op jit(solution)/shard_map/experts/pallas_call | solution.py:27
  68.2 1.6 %collective-permute-start.31 = (bf16[64,1664]{1,0:T(8,128)(2,1)S(1)}, bf16[64,1664]{1,0:T(8,128)(2,1)S(1)}, u32[]{:S(2)}, u32[]{:S(2)}) collective-permute-start(bf16[64,1664]{1,0:T(8,128)(2,1)S(1)} %collective-permute-done.20.refs_1_), channel_id=1, source_target_pairs={{0,4},{1,5},{4,8},{5,9},{8,12},{9,13},{12,14},{13,15},{14,10},{15,... | collective-permute-start | bytes 638984 | tf_op jit(solution)/shard_map/ppermute | solution.py:162
  70.3 3.3 %experts.5 = (f32[64,1536]{1,0:T(8,128)S(1)}, f32[64,1536]{1,0:T(8,128)S(1)}, f32[64,1536]{1,0:T(8,128)S(1)}, f32[64,1536]{1,0:T(8,128)S(1)}) custom-call(s32[3]{0:T(128)S(1)} %pad_add_fusion.place, bf16[64,1664]{1,0:T(8,128)(2,1)S(1)} %collective-permute-done.27.refs_0_, bf16[64,1664]{1,0:T(8,128)(2,1)S(1)} %collective-permute-done.20.refs_1_, ...), custom_call_target="tpu_custom_call" | custom-call | flops 2415919104 | bytes 4194304 | tf_op jit(solution)/shard_map/experts/pallas_call | solution.py:27
  73.7 1.6 %collective-permute-start.33 = (bf16[64,1664]{1,0:T(8,128)(2,1)S(1)}, bf16[64,1664]{1,0:T(8,128)(2,1)S(1)}, u32[]{:S(2)}, u32[]{:S(2)}) collective-permute-start(bf16[64,1664]{1,0:T(8,128)(2,1)S(1)} %collective-permute-done.28.refs_0_), channel_id=1, source_target_pairs={{0,4},{1,5},{4,8},{5,9},{8,12},{9,13},{12,14},{13,15},{14,10},{15,... | collective-permute-start | bytes 638984 | tf_op jit(solution)/shard_map/ppermute | solution.py:162
  75.8 0.9 collective-permute-done.32.refs_2_
  76.6 3.3 %experts.6 = (f32[64,1536]{1,0:T(8,128)S(1)}, f32[64,1536]{1,0:T(8,128)S(1)}, f32[64,1536]{1,0:T(8,128)S(1)}, f32[64,1536]{1,0:T(8,128)S(1)}) custom-call(s32[3]{0:T(128)S(1)} %pad_add_fusion.place, bf16[64,1664]{1,0:T(8,128)(2,1)S(1)} %collective-permute-done.28.refs_0_, bf16[64,1664]{1,0:T(8,128)(2,1)S(1)} %collective-permute-done.31.refs_1_, ...), custom_call_target="tpu_custom_call" | custom-call | flops 2415919104 | bytes 4194304 | tf_op jit(solution)/shard_map/experts/pallas_call | solution.py:27
  80.0 0.5 collective-permute-start.38
  80.5 1.6 %collective-permute-start.37 = (bf16[64,1536]{1,0:T(8,128)(2,1)S(1)}, bf16[64,1536]{1,0:T(8,128)(2,1)S(1)}, u32[]{:S(2)}, u32[]{:S(2)}) collective-permute-start(bf16[64,1536]{1,0:T(8,128)(2,1)S(1)} %convert_element_type.86), channel_id=1, source_target_pairs={{0,4},{1,5},{4,8},{5,9},{8,12},{9,13},{12,14},{13,15},{14,10},{15,... | collective-permute-start | bytes 589832 | tf_op jit(solution)/shard_map/ppermute | solution.py:162
  82.1 2.2 %experts.7 = (f32[64,1536]{1,0:T(8,128)S(1)}, f32[64,1536]{1,0:T(8,128)S(1)}) custom-call(s32[3]{0:T(128)S(1)} %pad_add_fusion.place, bf16[64,1664]{1,0:T(8,128)(2,1)S(1)} %collective-permute-done.33.refs_0_, bf16[64,1664]{1,0:T(8,128)(2,1)S(1)} %collective-permute-done.34.refs_1_, bf16[1536,512]{1,0:T(8,128)(2,1)S(1)} %pad_maximum_fusion.refs_6_.refs_4_.refs_2_, ...), custom_call_target="tpu_custom_call" | custom-call | flops 1207959552 | bytes 4194304 | tf_op jit(solution)/shard_map/experts/pallas_call | solution.py:27
  84.4 0.5 collective-permute-start.36
  84.9 1.6 %collective-permute-start.35 = (bf16[64,1536]{1,0:T(8,128)(2,1)S(1)}, bf16[64,1536]{1,0:T(8,128)(2,1)S(1)}, u32[]{:S(2)}, u32[]{:S(2)}) collective-permute-start(bf16[64,1536]{1,0:T(8,128)(2,1)S(1)} %convert_element_type.80), channel_id=1, source_target_pairs={{0,4},{1,5},{4,8},{5,9},{8,12},{9,13},{12,14},{13,15},{14,10},{15,... | collective-permute-start | bytes 589832 | tf_op jit(solution)/shard_map/ppermute | solution.py:162
  86.5 0.7 collective-permute-done.38
  87.2 0.7 collective-permute-done.37
  87.9 0.8 collective-permute-start.42
  88.7 1.3 %collective-permute-start.41 = (bf16[64,1536]{1,0:T(8,128)(2,1)S(1)}, bf16[64,1536]{1,0:T(8,128)(2,1)S(1)}, u32[]{:S(2)}, u32[]{:S(2)}) collective-permute-start(bf16[64,1536]{1,0:T(8,128)(2,1)S(1)} %add_convert_fusion.7), channel_id=1, source_target_pairs={{0,4},{1,5},{4,8},{5,9},{8,12},{9,13},{12,14},{13,15},{14,10},{15,... | collective-permute-start | bytes 589832 | tf_op jit(solution)/shard_map/ppermute | solution.py:162
  90.0 2.3 %collective-permute-done.36 = bf16[64,1536]{1,0:T(8,128)(2,1)S(1)} collective-permute-done((bf16[64,1536]{1,0:T(8,128)(2,1)S(1)}, bf16[64,1536]{1,0:T(8,128)(2,1)S(1)}, u32[]{:S(2)}, u32[]{:S(2)}) %collective-permute-start.36) | collective-permute-done | bytes 196640 | tf_op jit(solution)/shard_map/ppermute | solution.py:165
  92.8 0.5 collective-permute-start.40
  93.3 1.5 %collective-permute-start.39 = (bf16[64,1536]{1,0:T(8,128)(2,1)S(1)}, bf16[64,1536]{1,0:T(8,128)(2,1)S(1)}, u32[]{:S(2)}, u32[]{:S(2)}) collective-permute-start(bf16[64,1536]{1,0:T(8,128)(2,1)S(1)} %add_convert_fusion.9), channel_id=1, source_target_pairs={{0,4},{1,5},{4,8},{5,9},{8,12},{9,13},{12,14},{13,15},{14,10},{15,... | collective-permute-start | bytes 589832 | tf_op jit(solution)/shard_map/ppermute | solution.py:162
  94.8 1.4 %collective-permute-done.42 = bf16[64,1536]{1,0:T(8,128)(2,1)S(1)} collective-permute-done((bf16[64,1536]{1,0:T(8,128)(2,1)S(1)}, bf16[64,1536]{1,0:T(8,128)(2,1)S(1)}, u32[]{:S(2)}, u32[]{:S(2)}) %collective-permute-start.42) | collective-permute-done | bytes 196640 | tf_op jit(solution)/shard_map/ppermute | solution.py:165
  96.8 1.7 %collective-permute-done.40 = bf16[64,1536]{1,0:T(8,128)(2,1)S(1)} collective-permute-done((bf16[64,1536]{1,0:T(8,128)(2,1)S(1)}, bf16[64,1536]{1,0:T(8,128)(2,1)S(1)}, u32[]{:S(2)}, u32[]{:S(2)}) %collective-permute-start.40) | collective-permute-done | bytes 196640 | tf_op jit(solution)/shard_map/ppermute | solution.py:165
  99.0 1.6 %collective-permute-start.44 = (bf16[64,1536]{1,0:T(8,128)(2,1)S(1)}, bf16[64,1536]{1,0:T(8,128)(2,1)S(1)}, u32[]{:S(2)}, u32[]{:S(2)}) collective-permute-start(bf16[64,1536]{1,0:T(8,128)(2,1)S(1)} %add_convert_fusion.4), channel_id=1, source_target_pairs={{4,0},{5,1},{8,4},{9,5},{12,8},{13,9},{14,12},{15,13},{10,14},{11,... | collective-permute-start | bytes 589832 | tf_op jit(solution)/shard_map/ppermute | solution.py:165
  100.6 0.5 collective-permute-start.43
  101.1 1.5 %collective-permute-start.46 = (bf16[64,1536]{1,0:T(8,128)(2,1)S(1)}, bf16[64,1536]{1,0:T(8,128)(2,1)S(1)}, u32[]{:S(2)}, u32[]{:S(2)}) collective-permute-start(bf16[64,1536]{1,0:T(8,128)(2,1)S(1)} %add_convert_fusion.3), channel_id=1, source_target_pairs={{0,4},{1,5},{4,8},{5,9},{8,12},{9,13},{12,14},{13,15},{14,10},{15,... | collective-permute-start | bytes 589832 | tf_op jit(solution)/shard_map/ppermute | solution.py:162
  102.6 0.5 collective-permute-start.47
  103.1 3.7 %collective-permute-done.44 = bf16[64,1536]{1,0:T(8,128)(2,1)S(1)} collective-permute-done((bf16[64,1536]{1,0:T(8,128)(2,1)S(1)}, bf16[64,1536]{1,0:T(8,128)(2,1)S(1)}, u32[]{:S(2)}, u32[]{:S(2)}) %collective-permute-start.44) | collective-permute-done | bytes 196640 | tf_op jit(solution)/shard_map/ppermute | solution.py:165
  106.8 1.4 %collective-permute-done.43 = bf16[64,1536]{1,0:T(8,128)(2,1)S(1)} collective-permute-done((bf16[64,1536]{1,0:T(8,128)(2,1)S(1)}, bf16[64,1536]{1,0:T(8,128)(2,1)S(1)}, u32[]{:S(2)}, u32[]{:S(2)}) %collective-permute-start.43) | collective-permute-done | bytes 196640 | tf_op jit(solution)/shard_map/ppermute | solution.py:162
  108.3 0.8 collective-permute-start.45
  109.0 1.3 %collective-permute-start.48 = (bf16[64,1536]{1,0:T(8,128)(2,1)S(1)}, bf16[64,1536]{1,0:T(8,128)(2,1)S(1)}, u32[]{:S(2)}, u32[]{:S(2)}) collective-permute-start(bf16[64,1536]{1,0:T(8,128)(2,1)S(1)} %add_convert_fusion), channel_id=1, source_target_pairs={{4,0},{5,1},{8,4},{9,5},{12,8},{13,9},{14,12},{15,13},{10,14},{11,... | collective-permute-start | bytes 589832 | tf_op jit(solution)/shard_map/ppermute | solution.py:165
  110.5 3.4 %collective-permute-done.45.refs_4_ = bf16[64,1536]{1,0:T(8,128)(2,1)S(1)} collective-permute-done((bf16[64,1536]{1,0:T(8,128)(2,1)S(1)}, bf16[64,1536]{1,0:T(8,128)(2,1)S(1)}, u32[]{:S(2)}, u32[]{:S(2)}) %collective-permute-start.45) | collective-permute-done | bytes 196640 | tf_op jit(solution)/shard_map/ppermute | solution.py:162
  114.0 0.7 collective-permute-done.48.refs_7_
  114.7 1.6 %final.1 = bf16[128,1536]{1,0:T(8,128)(2,1)} custom-call(s32[3]{0:T(128)S(1)} %pad_add_fusion.place, bf16[64,1664]{1,0:T(8,128)(2,1)S(1)} %get-tuple-element.84.refs_4_.refs_0_, bf16[64,1664]{1,0:T(8,128)(2,1)S(1)} %get-tuple-element.85.refs_5_.refs_1_, f32[64,1536]{1,0:T(8,128)S(1)} %get-tuple-element.95.refs_2_, f32[64,1536]{1,0:T(8,128)S(1)} %get-tuple-element.96.refs_3_, ...), custom_call_target="tpu_custom_call" | custom-call | bytes 4194304 | tf_op jit(solution)/shard_map/final/pallas_call | solution.py:27
  (75 shorter events, 9.9 us)
Async XLA Ops:
  0.0 10.5 %collective-permute-start.4 = (bf16[512,1536]{1,0:T(8,128)(2,1)}, bf16[512,1536]{1,0:T(8,128)(2,1)S(1)}, u32[]{:S(2)}, u32[]{:S(2)}) collective-permute-start(bf16[512,1536]{1,0:T(8,128)(2,1)} %bitcast.9), channel_id=1, source_target_pairs={{0,1},{1,0},{2,3},{3,2},{4,5},{5,4},{6,7},{7,6},{8,9},{9,8},{10,11... | collective-permute-start | bytes 4718600 | tf_op jit(solution)/shard_map/ppermute | solution.py:159
  0.5 8.2 %collective-permute-start.2 = (bf16[48,1536]{1,0:T(8,128)(2,1)}, bf16[48,1536]{1,0:T(8,128)(2,1)S(1)}, u32[]{:S(2)}, u32[]{:S(2)}) collective-permute-start(bf16[48,1536]{1,0:T(8,128)(2,1)} %refs_0_.1), channel_id=1, source_target_pairs={{0,16},{16,0},{1,17},{17,1},{2,18},{18,2},{3,19},{19,3},{4,20},{20... | collective-permute-start | bytes 442376 | tf_op jit(solution)/shard_map/ppermute | solution.py:187
  3.0 6.2 %collective-permute-start = (bf16[48,1536]{1,0:T(8,128)(2,1)}, bf16[48,1536]{1,0:T(8,128)(2,1)S(1)}, u32[]{:S(2)}, u32[]{:S(2)}) collective-permute-start(bf16[48,1536]{1,0:T(8,128)(2,1)} %refs_0_.1), channel_id=1, source_target_pairs={{0,4},{1,5},{4,8},{5,9},{8,12},{9,13},{12,14},{13,15},{14,10},{15,... | collective-permute-start | bytes 442376 | tf_op jit(solution)/shard_map/ppermute | solution.py:162
  4.5 5.9 %collective-permute-start.1 = (bf16[48,1536]{1,0:T(8,128)(2,1)}, bf16[48,1536]{1,0:T(8,128)(2,1)S(1)}, u32[]{:S(2)}, u32[]{:S(2)}) collective-permute-start(bf16[48,1536]{1,0:T(8,128)(2,1)} %refs_0_.1), channel_id=1, source_target_pairs={{4,0},{5,1},{8,4},{9,5},{12,8},{13,9},{14,12},{15,13},{10,14},{11,... | collective-permute-start | bytes 442376 | tf_op jit(solution)/shard_map/ppermute | solution.py:165
  5.0 1.9 %collective-permute-start.3 = (bf16[128,1536]{1,0:T(8,128)(2,1)}, bf16[128,1536]{1,0:T(8,128)(2,1)S(1)}, u32[]{:S(2)}, u32[]{:S(2)}) collective-permute-start(bf16[128,1536]{1,0:T(8,128)(2,1)} %att.1), channel_id=1, source_target_pairs={{0,1},{1,0},{2,3},{3,2},{4,5},{5,4},{6,7},{7,6},{8,9},{9,8},{10,11... | collective-permute-start | bytes 1179656 | tf_op jit(solution)/shard_map/ppermute | solution.py:159
  5.0 1.6 %copy-start.5 = (s32[128,8]{0,1:T(8,128)S(1)}, s32[128,8]{0,1:T(8,128)}, u32[]{:S(2)}) copy-start(s32[128,8]{0,1:T(8,128)} %param.15) | copy-start | bytes 12292
  5.0 1.7 %copy-start.6 = (f32[128,8]{0,1:T(8,128)S(1)}, f32[128,8]{0,1:T(8,128)}, u32[]{:S(2)}) copy-start(f32[128,8]{0,1:T(8,128)} %param.16) | copy-start | bytes 12292
  5.0 1.9 %copy-start.1 = (bf16[128,1536]{1,0:T(8,128)(2,1)S(1)}, bf16[128,1536]{1,0:T(8,128)(2,1)}, u32[]{:S(2)}) copy-start(bf16[128,1536]{1,0:T(8,128)(2,1)} %att.1) | copy-start | bytes 1179652
  5.0 30.9 %copy-start.3 = (bf16[48,1536]{1,0:T(8,128)(2,1)S(1)}, bf16[48,1536]{1,0:T(8,128)(2,1)}, u32[]{:S(2)}) copy-start(bf16[48,1536]{1,0:T(8,128)(2,1)} %refs_0_.1) | copy-start | bytes 442372
  8.6 31.1 %copy-start.2 = (bf16[128,1536]{1,0:T(8,128)(2,1)S(1)}, bf16[128,1536]{1,0:T(8,128)(2,1)}, u32[]{:S(2)}) copy-start(bf16[128,1536]{1,0:T(8,128)(2,1)} %res.1) | copy-start | bytes 1179652
  10.5 13.5 %collective-permute-start.6 = (bf16[1536,512]{1,0:T(8,128)(2,1)S(1)}, bf16[1536,512]{1,0:T(8,128)(2,1)S(1)}, u32[]{:S(2)}, u32[]{:S(2)}) collective-permute-start(bf16[1536,512]{1,0:T(8,128)(2,1)S(1)} %pad_maximum_fusion.refs_6_.refs_4_.refs_2_), channel_id=1, source_target_pairs={{0,1},{1,0},{2,3},{3,2},{4,5},{5,4},{6,7},{7,6},{8,9},{9,8},{10,11... | collective-permute-start | bytes 4718600 | tf_op jit(solution)/shard_map/ppermute | solution.py:159
  10.5 6.3 %collective-permute-start.9 = (bf16[48,1536]{1,0:T(8,128)(2,1)S(1)}, bf16[48,1536]{1,0:T(8,128)(2,1)S(1)}, u32[]{:S(2)}, u32[]{:S(2)}) collective-permute-start(bf16[48,1536]{1,0:T(8,128)(2,1)S(1)} %collective-permute-done.2.refs_1_), channel_id=1, source_target_pairs={{4,0},{5,1},{8,4},{9,5},{12,8},{13,9},{14,12},{15,13},{10,14},{11,... | collective-permute-start | bytes 442376 | tf_op jit(solution)/shard_map/ppermute | solution.py:165
  10.9 36.5 %collective-permute-start.25 = (bf16[1536,512]{1,0:T(8,128)(2,1)S(1)}, bf16[1536,512]{1,0:T(8,128)(2,1)S(1)}, u32[]{:S(2)}, u32[]{:S(2)}) collective-permute-start(bf16[1536,512]{1,0:T(8,128)(2,1)S(1)} %pad_maximum_fusion.refs_6_.refs_4_.refs_2_), channel_id=1, source_target_pairs={{0,16},{16,0},{1,17},{17,1},{2,18},{18,2},{3,19},{19,3},{4,20},{20... | collective-permute-start | bytes 4718600 | tf_op jit(solution)/shard_map/ppermute | solution.py:195
  11.3 6.7 %collective-permute-start.5 = (bf16[48,1536]{1,0:T(8,128)(2,1)S(1)}, bf16[48,1536]{1,0:T(8,128)(2,1)S(1)}, u32[]{:S(2)}, u32[]{:S(2)}) collective-permute-start(bf16[48,1536]{1,0:T(8,128)(2,1)S(1)} %collective-permute-done.refs_2_), channel_id=1, source_target_pairs={{0,4},{1,5},{4,8},{5,9},{8,12},{9,13},{12,14},{13,15},{14,10},{15,... | collective-permute-start | bytes 442376 | tf_op jit(solution)/shard_map/ppermute | solution.py:162
  13.0 7.1 %collective-permute-start.7 = (bf16[48,1536]{1,0:T(8,128)(2,1)S(1)}, bf16[48,1536]{1,0:T(8,128)(2,1)S(1)}, u32[]{:S(2)}, u32[]{:S(2)}) collective-permute-start(bf16[48,1536]{1,0:T(8,128)(2,1)S(1)} %collective-permute-done.2.refs_1_), channel_id=1, source_target_pairs={{0,4},{1,5},{4,8},{5,9},{8,12},{9,13},{12,14},{13,15},{14,10},{15,... | collective-permute-start | bytes 442376 | tf_op jit(solution)/shard_map/ppermute | solution.py:162
  16.7 6.8 %collective-permute-start.13 = (bf16[48,1536]{1,0:T(8,128)(2,1)S(1)}, bf16[48,1536]{1,0:T(8,128)(2,1)S(1)}, u32[]{:S(2)}, u32[]{:S(2)}) collective-permute-start(bf16[48,1536]{1,0:T(8,128)(2,1)S(1)} %collective-permute-done.9.refs_7_), channel_id=1, source_target_pairs={{4,0},{5,1},{8,4},{9,5},{12,8},{13,9},{14,12},{15,13},{10,14},{11,... | collective-permute-start | bytes 442376 | tf_op jit(solution)/shard_map/ppermute | solution.py:165
  18.0 8.6 %collective-permute-start.8 = (bf16[48,1536]{1,0:T(8,128)(2,1)S(1)}, bf16[48,1536]{1,0:T(8,128)(2,1)S(1)}, u32[]{:S(2)}, u32[]{:S(2)}) collective-permute-start(bf16[48,1536]{1,0:T(8,128)(2,1)S(1)} %collective-permute-done.1.refs_3_), channel_id=1, source_target_pairs={{4,0},{5,1},{8,4},{9,5},{12,8},{13,9},{14,12},{15,13},{10,14},{11,... | collective-permute-start | bytes 442376 | tf_op jit(solution)/shard_map/ppermute | solution.py:165
  20.2 6.9 %collective-permute-start.11 = (bf16[48,1536]{1,0:T(8,128)(2,1)S(1)}, bf16[48,1536]{1,0:T(8,128)(2,1)S(1)}, u32[]{:S(2)}, u32[]{:S(2)}) collective-permute-start(bf16[48,1536]{1,0:T(8,128)(2,1)S(1)} %collective-permute-done.7.refs_5_), channel_id=1, source_target_pairs={{0,4},{1,5},{4,8},{5,9},{8,12},{9,13},{12,14},{13,15},{14,10},{15,... | collective-permute-start | bytes 442376 | tf_op jit(solution)/shard_map/ppermute | solution.py:162
  23.5 6.8 %collective-permute-start.16 = (bf16[48,1536]{1,0:T(8,128)(2,1)S(1)}, bf16[48,1536]{1,0:T(8,128)(2,1)S(1)}, u32[]{:S(2)}, u32[]{:S(2)}) collective-permute-start(bf16[48,1536]{1,0:T(8,128)(2,1)S(1)} %collective-permute-done.13.refs_11_), channel_id=1, source_target_pairs={{4,0},{5,1},{8,4},{9,5},{12,8},{13,9},{14,12},{15,13},{10,14},{11,... | collective-permute-start | bytes 442376 | tf_op jit(solution)/shard_map/ppermute | solution.py:165
  23.9 6.8 %collective-permute-start.10 = (bf16[48,1536]{1,0:T(8,128)(2,1)S(1)}, bf16[48,1536]{1,0:T(8,128)(2,1)S(1)}, u32[]{:S(2)}, u32[]{:S(2)}) collective-permute-start(bf16[48,1536]{1,0:T(8,128)(2,1)S(1)} %collective-permute-done.5.refs_4_), channel_id=1, source_target_pairs={{0,4},{1,5},{4,8},{5,9},{8,12},{9,13},{12,14},{13,15},{14,10},{15,... | collective-permute-start | bytes 442376 | tf_op jit(solution)/shard_map/ppermute | solution.py:162
  26.6 6.6 %collective-permute-start.12 = (bf16[48,1536]{1,0:T(8,128)(2,1)S(1)}, bf16[48,1536]{1,0:T(8,128)(2,1)S(1)}, u32[]{:S(2)}, u32[]{:S(2)}) collective-permute-start(bf16[48,1536]{1,0:T(8,128)(2,1)S(1)} %collective-permute-done.8.refs_6_), channel_id=1, source_target_pairs={{4,0},{5,1},{8,4},{9,5},{12,8},{13,9},{14,12},{15,13},{10,14},{11,... | collective-permute-start | bytes 442376 | tf_op jit(solution)/shard_map/ppermute | solution.py:165
  27.1 6.2 %collective-permute-start.15 = (bf16[48,1536]{1,0:T(8,128)(2,1)S(1)}, bf16[48,1536]{1,0:T(8,128)(2,1)S(1)}, u32[]{:S(2)}, u32[]{:S(2)}) collective-permute-start(bf16[48,1536]{1,0:T(8,128)(2,1)S(1)} %collective-permute-done.11.refs_9_), channel_id=1, source_target_pairs={{0,4},{1,5},{4,8},{5,9},{8,12},{9,13},{12,14},{13,15},{14,10},{15,... | collective-permute-start | bytes 442376 | tf_op jit(solution)/shard_map/ppermute | solution.py:162
  30.3 5.1 %collective-permute-start.17 = (bf16[48,1536]{1,0:T(8,128)(2,1)S(1)}, bf16[48,1536]{1,0:T(8,128)(2,1)S(1)}, u32[]{:S(2)}, u32[]{:S(2)}) collective-permute-start(bf16[48,1536]{1,0:T(8,128)(2,1)S(1)} %collective-permute-done.16.refs_14_), channel_id=1, source_target_pairs={{4,0},{5,1},{8,4},{9,5},{12,8},{13,9},{14,12},{15,13},{10,14},{11,... | collective-permute-start | bytes 442376 | tf_op jit(solution)/shard_map/ppermute | solution.py:165
  30.7 5.1 %collective-permute-start.14 = (bf16[48,1536]{1,0:T(8,128)(2,1)S(1)}, bf16[48,1536]{1,0:T(8,128)(2,1)S(1)}, u32[]{:S(2)}, u32[]{:S(2)}) collective-permute-start(bf16[48,1536]{1,0:T(8,128)(2,1)S(1)} %collective-permute-done.10.refs_8_), channel_id=1, source_target_pairs={{0,4},{1,5},{4,8},{5,9},{8,12},{9,13},{12,14},{13,15},{14,10},{15,... | collective-permute-start | bytes 442376 | tf_op jit(solution)/shard_map/ppermute | solution.py:162
  37.4 26.3 %copy-start = (bf16[1,512,1536]{2,1,0:T(8,128)(2,1)S(1)}, bf16[1,512,1536]{2,1,0:T(8,128)(2,1)}, u32[]{:S(2)}) copy-start(bf16[1,512,1536]{2,1,0:T(8,128)(2,1)} %param.14) | copy-start | bytes 4718596
  37.4 2.4 %collective-permute-start.18 = (f32[128,1536]{1,0:T(8,128)S(1)}, f32[128,1536]{1,0:T(8,128)S(1)}, u32[]{:S(2)}, u32[]{:S(2)}) collective-permute-start(f32[128,1536]{1,0:T(8,128)S(1)} %get-tuple-element.82), channel_id=1, source_target_pairs={{0,1},{1,0},{2,3},{3,2},{4,5},{5,4},{6,7},{7,6},{8,9},{9,8},{10,11... | collective-permute-start | bytes 2359304 | tf_op jit(solution)/shard_map/ppermute | solution.py:159
  40.4 7.3 %collective-permute-start.23 = (bf16[64,1664]{1,0:T(8,128)(2,1)S(1)}, bf16[64,1664]{1,0:T(8,128)(2,1)S(1)}, u32[]{:S(2)}, u32[]{:S(2)}) collective-permute-start(bf16[64,1664]{1,0:T(8,128)(2,1)S(1)} %get-tuple-element.84.refs_4_.refs_0_), channel_id=1, source_target_pairs={{0,4},{1,5},{4,8},{5,9},{8,12},{9,13},{12,14},{13,15},{14,10},{15,... | collective-permute-start | bytes 638984 | tf_op jit(solution)/shard_map/ppermute | solution.py:162
  42.0 7.0 %collective-permute-start.24 = (bf16[64,1664]{1,0:T(8,128)(2,1)S(1)}, bf16[64,1664]{1,0:T(8,128)(2,1)S(1)}, u32[]{:S(2)}, u32[]{:S(2)}) collective-permute-start(bf16[64,1664]{1,0:T(8,128)(2,1)S(1)} %get-tuple-element.85.refs_5_.refs_1_), channel_id=1, source_target_pairs={{4,0},{5,1},{8,4},{9,5},{12,8},{13,9},{14,12},{15,13},{10,14},{11,... | collective-permute-start | bytes 638984 | tf_op jit(solution)/shard_map/ppermute | solution.py:165
  49.0 14.7 %collective-permute-start.26 = (bf16[1536,512]{1,0:T(8,128)(2,1)S(1)}, bf16[1536,512]{1,0:T(8,128)(2,1)S(1)}, u32[]{:S(2)}, u32[]{:S(2)}) collective-permute-start(bf16[1536,512]{1,0:T(8,128)(2,1)S(1)} %collective-permute-done.25.refs_7_.refs_5_.refs_3_), channel_id=1, source_target_pairs={{0,1},{1,0},{2,3},{3,2},{4,5},{5,4},{6,7},{7,6},{8,9},{9,8},{10,11... | collective-permute-start | bytes 4718600 | tf_op jit(solution)/shard_map/ppermute | solution.py:159
  49.0 8.0 %collective-permute-start.19 = (bf16[64,1664]{1,0:T(8,128)(2,1)S(1)}, bf16[64,1664]{1,0:T(8,128)(2,1)S(1)}, u32[]{:S(2)}, u32[]{:S(2)}) collective-permute-start(bf16[64,1664]{1,0:T(8,128)(2,1)S(1)} %get-tuple-element.85.refs_5_.refs_1_), channel_id=1, source_target_pairs={{0,4},{1,5},{4,8},{5,9},{8,12},{9,13},{12,14},{13,15},{14,10},{15,... | collective-permute-start | bytes 638984 | tf_op jit(solution)/shard_map/ppermute | solution.py:162
  50.6 8.1 %collective-permute-start.21 = (bf16[64,1664]{1,0:T(8,128)(2,1)S(1)}, bf16[64,1664]{1,0:T(8,128)(2,1)S(1)}, u32[]{:S(2)}, u32[]{:S(2)}) collective-permute-start(bf16[64,1664]{1,0:T(8,128)(2,1)S(1)} %get-tuple-element.84.refs_4_.refs_0_), channel_id=1, source_target_pairs={{4,0},{5,1},{8,4},{9,5},{12,8},{13,9},{14,12},{15,13},{10,14},{11,... | collective-permute-start | bytes 638984 | tf_op jit(solution)/shard_map/ppermute | solution.py:165
  51.0 10.6 %collective-permute-start.27 = (bf16[64,1664]{1,0:T(8,128)(2,1)S(1)}, bf16[64,1664]{1,0:T(8,128)(2,1)S(1)}, u32[]{:S(2)}, u32[]{:S(2)}) collective-permute-start(bf16[64,1664]{1,0:T(8,128)(2,1)S(1)} %collective-permute-done.23.refs_0_), channel_id=1, source_target_pairs={{0,4},{1,5},{4,8},{5,9},{8,12},{9,13},{12,14},{13,15},{14,10},{15,... | collective-permute-start | bytes 638984 | tf_op jit(solution)/shard_map/ppermute | solution.py:162
  52.6 10.6 %collective-permute-start.29 = (bf16[64,1664]{1,0:T(8,128)(2,1)S(1)}, bf16[64,1664]{1,0:T(8,128)(2,1)S(1)}, u32[]{:S(2)}, u32[]{:S(2)}) collective-permute-start(bf16[64,1664]{1,0:T(8,128)(2,1)S(1)} %collective-permute-done.24.refs_3_), channel_id=1, source_target_pairs={{4,0},{5,1},{8,4},{9,5},{12,8},{13,9},{14,12},{15,13},{10,14},{11,... | collective-permute-start | bytes 638984 | tf_op jit(solution)/shard_map/ppermute | solution.py:165
  57.1 11.1 %collective-permute-start.20 = (bf16[64,1664]{1,0:T(8,128)(2,1)S(1)}, bf16[64,1664]{1,0:T(8,128)(2,1)S(1)}, u32[]{:S(2)}, u32[]{:S(2)}) collective-permute-start(bf16[64,1664]{1,0:T(8,128)(2,1)S(1)} %collective-permute-done.19.refs_1_), channel_id=1, source_target_pairs={{0,4},{1,5},{4,8},{5,9},{8,12},{9,13},{12,14},{13,15},{14,10},{15,... | collective-permute-start | bytes 638984 | tf_op jit(solution)/shard_map/ppermute | solution.py:162
  58.7 9.5 %collective-permute-start.22 = (bf16[64,1664]{1,0:T(8,128)(2,1)S(1)}, bf16[64,1664]{1,0:T(8,128)(2,1)S(1)}, u32[]{:S(2)}, u32[]{:S(2)}) collective-permute-start(bf16[64,1664]{1,0:T(8,128)(2,1)S(1)} %collective-permute-done.21.refs_2_), channel_id=1, source_target_pairs={{4,0},{5,1},{8,4},{9,5},{12,8},{13,9},{14,12},{15,13},{10,14},{11,... | collective-permute-start | bytes 638984 | tf_op jit(solution)/shard_map/ppermute | solution.py:165
  61.6 12.0 %collective-permute-start.28 = (bf16[64,1664]{1,0:T(8,128)(2,1)S(1)}, bf16[64,1664]{1,0:T(8,128)(2,1)S(1)}, u32[]{:S(2)}, u32[]{:S(2)}) collective-permute-start(bf16[64,1664]{1,0:T(8,128)(2,1)S(1)} %collective-permute-done.27.refs_0_), channel_id=1, source_target_pairs={{0,4},{1,5},{4,8},{5,9},{8,12},{9,13},{12,14},{13,15},{14,10},{15,... | collective-permute-start | bytes 638984 | tf_op jit(solution)/shard_map/ppermute | solution.py:162
  63.3 10.4 %collective-permute-start.30 = (bf16[64,1664]{1,0:T(8,128)(2,1)S(1)}, bf16[64,1664]{1,0:T(8,128)(2,1)S(1)}, u32[]{:S(2)}, u32[]{:S(2)}) collective-permute-start(bf16[64,1664]{1,0:T(8,128)(2,1)S(1)} %collective-permute-done.29.refs_3_), channel_id=1, source_target_pairs={{4,0},{5,1},{8,4},{9,5},{12,8},{13,9},{14,12},{15,13},{10,14},{11,... | collective-permute-start | bytes 638984 | tf_op jit(solution)/shard_map/ppermute | solution.py:165
  68.2 7.5 %collective-permute-start.31 = (bf16[64,1664]{1,0:T(8,128)(2,1)S(1)}, bf16[64,1664]{1,0:T(8,128)(2,1)S(1)}, u32[]{:S(2)}, u32[]{:S(2)}) collective-permute-start(bf16[64,1664]{1,0:T(8,128)(2,1)S(1)} %collective-permute-done.20.refs_1_), channel_id=1, source_target_pairs={{0,4},{1,5},{4,8},{5,9},{8,12},{9,13},{12,14},{13,15},{14,10},{15,... | collective-permute-start | bytes 638984 | tf_op jit(solution)/shard_map/ppermute | solution.py:162
  69.9 6.8 %collective-permute-start.32 = (bf16[64,1664]{1,0:T(8,128)(2,1)S(1)}, bf16[64,1664]{1,0:T(8,128)(2,1)S(1)}, u32[]{:S(2)}, u32[]{:S(2)}) collective-permute-start(bf16[64,1664]{1,0:T(8,128)(2,1)S(1)} %collective-permute-done.22.refs_2_), channel_id=1, source_target_pairs={{4,0},{5,1},{8,4},{9,5},{12,8},{13,9},{14,12},{15,13},{10,14},{11,... | collective-permute-start | bytes 638984 | tf_op jit(solution)/shard_map/ppermute | solution.py:165
  73.7 8.4 %collective-permute-start.33 = (bf16[64,1664]{1,0:T(8,128)(2,1)S(1)}, bf16[64,1664]{1,0:T(8,128)(2,1)S(1)}, u32[]{:S(2)}, u32[]{:S(2)}) collective-permute-start(bf16[64,1664]{1,0:T(8,128)(2,1)S(1)} %collective-permute-done.28.refs_0_), channel_id=1, source_target_pairs={{0,4},{1,5},{4,8},{5,9},{8,12},{9,13},{12,14},{13,15},{14,10},{15,... | collective-permute-start | bytes 638984 | tf_op jit(solution)/shard_map/ppermute | solution.py:162
  75.3 6.8 %collective-permute-start.34 = (bf16[64,1664]{1,0:T(8,128)(2,1)S(1)}, bf16[64,1664]{1,0:T(8,128)(2,1)S(1)}, u32[]{:S(2)}, u32[]{:S(2)}) collective-permute-start(bf16[64,1664]{1,0:T(8,128)(2,1)S(1)} %collective-permute-done.30.refs_3_), channel_id=1, source_target_pairs={{4,0},{5,1},{8,4},{9,5},{12,8},{13,9},{14,12},{15,13},{10,14},{11,... | collective-permute-start | bytes 638984 | tf_op jit(solution)/shard_map/ppermute | solution.py:165
  80.0 7.1 %collective-permute-start.38 = (bf16[64,1536]{1,0:T(8,128)(2,1)S(1)}, bf16[64,1536]{1,0:T(8,128)(2,1)S(1)}, u32[]{:S(2)}, u32[]{:S(2)}) collective-permute-start(bf16[64,1536]{1,0:T(8,128)(2,1)S(1)} %convert_element_type.87), channel_id=1, source_target_pairs={{4,0},{5,1},{8,4},{9,5},{12,8},{13,9},{14,12},{15,13},{10,14},{11,... | collective-permute-start | bytes 589832 | tf_op jit(solution)/shard_map/ppermute | solution.py:165
  80.5 7.4 %collective-permute-start.37 = (bf16[64,1536]{1,0:T(8,128)(2,1)S(1)}, bf16[64,1536]{1,0:T(8,128)(2,1)S(1)}, u32[]{:S(2)}, u32[]{:S(2)}) collective-permute-start(bf16[64,1536]{1,0:T(8,128)(2,1)S(1)} %convert_element_type.86), channel_id=1, source_target_pairs={{0,4},{1,5},{4,8},{5,9},{8,12},{9,13},{12,14},{13,15},{14,10},{15,... | collective-permute-start | bytes 589832 | tf_op jit(solution)/shard_map/ppermute | solution.py:162
  84.4 7.9 %collective-permute-start.36 = (bf16[64,1536]{1,0:T(8,128)(2,1)S(1)}, bf16[64,1536]{1,0:T(8,128)(2,1)S(1)}, u32[]{:S(2)}, u32[]{:S(2)}) collective-permute-start(bf16[64,1536]{1,0:T(8,128)(2,1)S(1)} %convert_element_type.81), channel_id=1, source_target_pairs={{4,0},{5,1},{8,4},{9,5},{12,8},{13,9},{14,12},{15,13},{10,14},{11,... | collective-permute-start | bytes 589832 | tf_op jit(solution)/shard_map/ppermute | solution.py:165
  84.9 7.8 %collective-permute-start.35 = (bf16[64,1536]{1,0:T(8,128)(2,1)S(1)}, bf16[64,1536]{1,0:T(8,128)(2,1)S(1)}, u32[]{:S(2)}, u32[]{:S(2)}) collective-permute-start(bf16[64,1536]{1,0:T(8,128)(2,1)S(1)} %convert_element_type.80), channel_id=1, source_target_pairs={{0,4},{1,5},{4,8},{5,9},{8,12},{9,13},{12,14},{13,15},{14,10},{15,... | collective-permute-start | bytes 589832 | tf_op jit(solution)/shard_map/ppermute | solution.py:162
  87.9 8.3 %collective-permute-start.42 = (bf16[64,1536]{1,0:T(8,128)(2,1)S(1)}, bf16[64,1536]{1,0:T(8,128)(2,1)S(1)}, u32[]{:S(2)}, u32[]{:S(2)}) collective-permute-start(bf16[64,1536]{1,0:T(8,128)(2,1)S(1)} %add_convert_fusion.6), channel_id=1, source_target_pairs={{4,0},{5,1},{8,4},{9,5},{12,8},{13,9},{14,12},{15,13},{10,14},{11,... | collective-permute-start | bytes 589832 | tf_op jit(solution)/shard_map/ppermute | solution.py:165
  88.7 8.0 %collective-permute-start.41 = (bf16[64,1536]{1,0:T(8,128)(2,1)S(1)}, bf16[64,1536]{1,0:T(8,128)(2,1)S(1)}, u32[]{:S(2)}, u32[]{:S(2)}) collective-permute-start(bf16[64,1536]{1,0:T(8,128)(2,1)S(1)} %add_convert_fusion.7), channel_id=1, source_target_pairs={{0,4},{1,5},{4,8},{5,9},{8,12},{9,13},{12,14},{13,15},{14,10},{15,... | collective-permute-start | bytes 589832 | tf_op jit(solution)/shard_map/ppermute | solution.py:162
  92.8 5.7 %collective-permute-start.40 = (bf16[64,1536]{1,0:T(8,128)(2,1)S(1)}, bf16[64,1536]{1,0:T(8,128)(2,1)S(1)}, u32[]{:S(2)}, u32[]{:S(2)}) collective-permute-start(bf16[64,1536]{1,0:T(8,128)(2,1)S(1)} %add_convert_fusion.8), channel_id=1, source_target_pairs={{4,0},{5,1},{8,4},{9,5},{12,8},{13,9},{14,12},{15,13},{10,14},{11,... | collective-permute-start | bytes 589832 | tf_op jit(solution)/shard_map/ppermute | solution.py:165
  93.3 5.7 %collective-permute-start.39 = (bf16[64,1536]{1,0:T(8,128)(2,1)S(1)}, bf16[64,1536]{1,0:T(8,128)(2,1)S(1)}, u32[]{:S(2)}, u32[]{:S(2)}) collective-permute-start(bf16[64,1536]{1,0:T(8,128)(2,1)S(1)} %add_convert_fusion.9), channel_id=1, source_target_pairs={{0,4},{1,5},{4,8},{5,9},{8,12},{9,13},{12,14},{13,15},{14,10},{15,... | collective-permute-start | bytes 589832 | tf_op jit(solution)/shard_map/ppermute | solution.py:162
  96.8 13.6 %copy-start.4 = (f32[1536]{0:T(1024)S(1)}, f32[1536]{0:T(1024)}, u32[]{:S(2)}) copy-start(f32[1536]{0:T(1024)} %param.17) | copy-start | bytes 18436
  99.0 7.8 %collective-permute-start.44 = (bf16[64,1536]{1,0:T(8,128)(2,1)S(1)}, bf16[64,1536]{1,0:T(8,128)(2,1)S(1)}, u32[]{:S(2)}, u32[]{:S(2)}) collective-permute-start(bf16[64,1536]{1,0:T(8,128)(2,1)S(1)} %add_convert_fusion.4), channel_id=1, source_target_pairs={{4,0},{5,1},{8,4},{9,5},{12,8},{13,9},{14,12},{15,13},{10,14},{11,... | collective-permute-start | bytes 589832 | tf_op jit(solution)/shard_map/ppermute | solution.py:165
  100.6 7.6 %collective-permute-start.43 = (bf16[64,1536]{1,0:T(8,128)(2,1)S(1)}, bf16[64,1536]{1,0:T(8,128)(2,1)S(1)}, u32[]{:S(2)}, u32[]{:S(2)}) collective-permute-start(bf16[64,1536]{1,0:T(8,128)(2,1)S(1)} %add_convert_fusion.5), channel_id=1, source_target_pairs={{0,4},{1,5},{4,8},{5,9},{8,12},{9,13},{12,14},{13,15},{14,10},{15,... | collective-permute-start | bytes 589832 | tf_op jit(solution)/shard_map/ppermute | solution.py:162
  101.1 9.3 %collective-permute-start.46 = (bf16[64,1536]{1,0:T(8,128)(2,1)S(1)}, bf16[64,1536]{1,0:T(8,128)(2,1)S(1)}, u32[]{:S(2)}, u32[]{:S(2)}) collective-permute-start(bf16[64,1536]{1,0:T(8,128)(2,1)S(1)} %add_convert_fusion.3), channel_id=1, source_target_pairs={{0,4},{1,5},{4,8},{5,9},{8,12},{9,13},{12,14},{13,15},{14,10},{15,... | collective-permute-start | bytes 589832 | tf_op jit(solution)/shard_map/ppermute | solution.py:162
  102.6 7.9 %collective-permute-start.47 = (bf16[64,1536]{1,0:T(8,128)(2,1)S(1)}, bf16[64,1536]{1,0:T(8,128)(2,1)S(1)}, u32[]{:S(2)}, u32[]{:S(2)}) collective-permute-start(bf16[64,1536]{1,0:T(8,128)(2,1)S(1)} %add_convert_fusion.2), channel_id=1, source_target_pairs={{4,0},{5,1},{8,4},{9,5},{12,8},{13,9},{14,12},{15,13},{10,14},{11,... | collective-permute-start | bytes 589832 | tf_op jit(solution)/shard_map/ppermute | solution.py:165
  108.3 5.7 %collective-permute-start.45 = (bf16[64,1536]{1,0:T(8,128)(2,1)S(1)}, bf16[64,1536]{1,0:T(8,128)(2,1)S(1)}, u32[]{:S(2)}, u32[]{:S(2)}) collective-permute-start(bf16[64,1536]{1,0:T(8,128)(2,1)S(1)} %add_convert_fusion.1), channel_id=1, source_target_pairs={{0,4},{1,5},{4,8},{5,9},{8,12},{9,13},{12,14},{13,15},{14,10},{15,... | collective-permute-start | bytes 589832 | tf_op jit(solution)/shard_map/ppermute | solution.py:162
  109.0 5.7 %collective-permute-start.48 = (bf16[64,1536]{1,0:T(8,128)(2,1)S(1)}, bf16[64,1536]{1,0:T(8,128)(2,1)S(1)}, u32[]{:S(2)}, u32[]{:S(2)}) collective-permute-start(bf16[64,1536]{1,0:T(8,128)(2,1)S(1)} %add_convert_fusion), channel_id=1, source_target_pairs={{4,0},{5,1},{8,4},{9,5},{12,8},{13,9},{14,12},{15,13},{10,14},{11,... | collective-permute-start | bytes 589832 | tf_op jit(solution)/shard_map/ppermute | solution.py:165

commit v7 on v6

--- a/solution.py
+++ b/solution.py
@@ -61,9 +61,9 @@
 
 
 def project_kernel(layout, place, tokens, *refs):
-    *blocks, own_out, near_out, full = refs
+    *blocks, near_out, full = refs
     core, expert, group = place[0], place[1], place[2]
-    rows = own_out.shape[0]
+    rows = near_out.shape[0]
     chips, where = layout
     pair = lax.shift_right_logical(expert, 1)
     down = (pair & 1) == 1
@@ -74,8 +74,11 @@
         source = jnp.where(spot < chips // 2, 2 * spot, 2 * (chips - spot) - 1)
         of_group = group if other == 0 else 1 - group
         full[pl.ds(pl.multiple_of((of_group * chips + source) * depth, 16), depth), :] = block[...]
-    own_out[...] = dot(tokens[:rows, :], full[...])
     near_out[...] = dot(tokens[rows:, :], full[...])
+
+
+def own_kernel(place, tokens, full, own):
+    own[...] = dot(tokens[: own.shape[0], :], full[...])
 
 
 def join_kernel(place, res, own, near, marks, *outs):
@@ -215,15 +218,26 @@
             blocks += [other_b]
             layout += [(step, 1)]
         layout = (chips, layout)
-        own, near = call(
+        near, full = call(
             functools.partial(project_kernel, layout),
-            [jax.ShapeDtypeStruct((token_count, width), F32)] * 2,
+            [
+                jax.ShapeDtypeStruct((token_count, width), F32),
+                jax.ShapeDtypeStruct((half, width), BF16),
+            ],
             place,
             tokens,
             *blocks,
-            scratch=[pltpu.VMEM((half, width), BF16)],
-            flops=4 * token_count * width * half,
+            flops=2 * token_count * width * half,
             name="project",
+        )
+        own = call(
+            own_kernel,
+            jax.ShapeDtypeStruct((token_count, width), F32),
+            place,
+            tokens,
+            full,
+            flops=2 * token_count * width * half,
+            name="own",
         )
         near = swap(near)
     else:

time: 116 us -> 116 us (level)
    pallas_call x8 -> x9, Pallas kernels: 18.8 us -> 19.5 us  [call(): pl.pallas_call(kernel, in_specs=[SMEM] + [VMEM] * (len(args) - 1), out_sp...]
  transfers between devices with their start and end apart: 49 -> 49, of which waited for: 32 -> 31; matrix products, arithmetic and copies ran while one was open for 2% -> 2% of each run, Pallas kernels for 15% -> 15%
where the time goes in v7:
time: 116 us
  starting transfers between devices  47.9 us (41%)
  waiting for transfers between devices  46.2 us (40%)
  Pallas kernels  19.5 us (17%)
  other arithmetic  2.06 us (2%)
    ppermute x21, starting transfers between devices, go(): return lax.ppermute(x, 'expert', forth)  31.2 us
    ppermute x21, waiting for transfers between devices, come(): return lax.ppermute(x, 'expert', back)  23.5 us
    pallas_call x9, Pallas kernels, call(): pl.pallas_call(kernel, in_specs=[SMEM] + [VMEM] * (len(args) - 1), out_sp...  19.5 us
    ppermute x21, waiting for transfers between devices, go(): return lax.ppermute(x, 'expert', forth)  15.8 us
    ppermute x21, starting transfers between devices, come(): return lax.ppermute(x, 'expert', back)  13.3 us
    ppermute x1, waiting for transfers between devices, body(): both_far = lax.ppermute(both, 'dp', flip)  5.31 us
    ppermute x1, starting transfers between devices, body(): mine, other = (out_weight, lax.ppermute(out_weight, 'dp', flip))  2.52 us
  transfers between devices with their start and end apart: 49, of which 31 were waited for; matrix products, arithmetic and copies ran while one was open for 2% of the time, Pallas kernels for 15%

profile of v7, /device:TPU:0, one launch (start us, length us, event | category | flops | bytes accessed | tf_op | source)
XLA Modules:
  0.0 115.9 jit_solution(14332392984149034184)
XLA Ops:
  0.5 2.5 %collective-permute-start.2 = (bf16[48,1536]{1,0:T(8,128)(2,1)}, bf16[48,1536]{1,0:T(8,128)(2,1)S(1)}, u32[]{:S(2)}, u32[]{:S(2)}) collective-permute-start(bf16[48,1536]{1,0:T(8,128)(2,1)} %refs_0_.1), channel_id=1, source_target_pairs={{0,16},{16,0},{1,17},{17,1},{2,18},{18,2},{3,19},{19,3},{4,20},{20... | collective-permute-start | bytes 442376 | tf_op jit(solution)/shard_map/ppermute | solution.py:190
  3.0 1.6 %collective-permute-start = (bf16[48,1536]{1,0:T(8,128)(2,1)}, bf16[48,1536]{1,0:T(8,128)(2,1)S(1)}, u32[]{:S(2)}, u32[]{:S(2)}) collective-permute-start(bf16[48,1536]{1,0:T(8,128)(2,1)} %refs_0_.1), channel_id=1, source_target_pairs={{0,4},{1,5},{4,8},{5,9},{8,12},{9,13},{12,14},{13,15},{14,10},{15,... | collective-permute-start | bytes 442376 | tf_op jit(solution)/shard_map/ppermute | solution.py:165
  5.0 1.5 %pad_maximum_fusion.refs_6_.refs_4_.refs_2_ = bf16[1536,512]{1,0:T(8,128)(2,1)S(1)} fusion(bf16[768,512]{1,0:T(8,128)(2,1)} %bitcast.14, bf16[768,512]{1,0:T(8,128)(2,1)} %bitcast.15), kind=kLoop, calls=%fused_computation | loop fusion | flops 3145728 | bytes 3145728 | tf_op jit(solution)/shard_map/concatenate | solution.py:196
  6.9 1.7 %prepare.1 = (bf16[256,768]{1,0:T(8,128)(2,1)S(1)}, bf16[128,128]{1,0:T(8,128)(2,1)S(1)}) custom-call(s32[3]{0:T(128)S(1)} %pad_add_fusion.place, bf16[128,1536]{1,0:T(8,128)(2,1)S(1)} %copy-done.1, bf16[128,1536]{1,0:T(8,128)(2,1)S(1)} %collective-permute-done.3.att_near, f32[16,128]{1,0:T(8,128)S(1)} %pad_maximum_fusion.1.table), custom_call_target="tpu_custom_call" | custom-call | bytes 4194304 | tf_op jit(solution)/shard_map/prepare/pallas_call | solution.py:27
  8.6 0.6 collective-permute-done.refs_2_
  9.2 1.3 %collective-permute-done.1.refs_3_ = bf16[48,1536]{1,0:T(8,128)(2,1)S(1)} collective-permute-done((bf16[48,1536]{1,0:T(8,128)(2,1)}, bf16[48,1536]{1,0:T(8,128)(2,1)S(1)}, u32[]{:S(2)}, u32[]{:S(2)}) %collective-permute-start.1) | collective-permute-done | bytes 147488 | tf_op jit(solution)/shard_map/ppermute | solution.py:168
  11.3 1.7 %collective-permute-start.5 = (bf16[48,1536]{1,0:T(8,128)(2,1)S(1)}, bf16[48,1536]{1,0:T(8,128)(2,1)S(1)}, u32[]{:S(2)}, u32[]{:S(2)}) collective-permute-start(bf16[48,1536]{1,0:T(8,128)(2,1)S(1)} %collective-permute-done.refs_2_), channel_id=1, source_target_pairs={{0,4},{1,5},{4,8},{5,9},{8,12},{9,13},{12,14},{13,15},{14,10},{15,... | collective-permute-start | bytes 442376 | tf_op jit(solution)/shard_map/ppermute | solution.py:165
  13.0 1.6 %collective-permute-start.7 = (bf16[48,1536]{1,0:T(8,128)(2,1)S(1)}, bf16[48,1536]{1,0:T(8,128)(2,1)S(1)}, u32[]{:S(2)}, u32[]{:S(2)}) collective-permute-start(bf16[48,1536]{1,0:T(8,128)(2,1)S(1)} %collective-permute-done.2.refs_1_), channel_id=1, source_target_pairs={{0,4},{1,5},{4,8},{5,9},{8,12},{9,13},{12,14},{13,15},{14,10},{15,... | collective-permute-start | bytes 442376 | tf_op jit(solution)/shard_map/ppermute | solution.py:165
  14.6 2.1 %collective-permute-done.9.refs_7_ = bf16[48,1536]{1,0:T(8,128)(2,1)S(1)} collective-permute-done((bf16[48,1536]{1,0:T(8,128)(2,1)S(1)}, bf16[48,1536]{1,0:T(8,128)(2,1)S(1)}, u32[]{:S(2)}, u32[]{:S(2)}) %collective-permute-start.9) | collective-permute-done | bytes 147488 | tf_op jit(solution)/shard_map/ppermute | solution.py:168
  17.2 0.8 collective-permute-done.5.refs_4_
  18.0 1.6 %collective-permute-start.8 = (bf16[48,1536]{1,0:T(8,128)(2,1)S(1)}, bf16[48,1536]{1,0:T(8,128)(2,1)S(1)}, u32[]{:S(2)}, u32[]{:S(2)}) collective-permute-start(bf16[48,1536]{1,0:T(8,128)(2,1)S(1)} %collective-permute-done.1.refs_3_), channel_id=1, source_target_pairs={{4,0},{5,1},{8,4},{9,5},{12,8},{13,9},{14,12},{15,13},{10,14},{11,... | collective-permute-start | bytes 442376 | tf_op jit(solution)/shard_map/ppermute | solution.py:168
  19.6 0.5 collective-permute-done.7.refs_5_
  20.2 1.7 %collective-permute-start.11 = (bf16[48,1536]{1,0:T(8,128)(2,1)S(1)}, bf16[48,1536]{1,0:T(8,128)(2,1)S(1)}, u32[]{:S(2)}, u32[]{:S(2)}) collective-permute-start(bf16[48,1536]{1,0:T(8,128)(2,1)S(1)} %collective-permute-done.7.refs_5_), channel_id=1, source_target_pairs={{0,4},{1,5},{4,8},{5,9},{8,12},{9,13},{12,14},{13,15},{14,10},{15,... | collective-permute-start | bytes 442376 | tf_op jit(solution)/shard_map/ppermute | solution.py:165
  21.9 1.6 %collective-permute-done.13.refs_11_ = bf16[48,1536]{1,0:T(8,128)(2,1)S(1)} collective-permute-done((bf16[48,1536]{1,0:T(8,128)(2,1)S(1)}, bf16[48,1536]{1,0:T(8,128)(2,1)S(1)}, u32[]{:S(2)}, u32[]{:S(2)}) %collective-permute-start.13) | collective-permute-done | bytes 147488 | tf_op jit(solution)/shard_map/ppermute | solution.py:168
  23.9 1.6 %collective-permute-start.10 = (bf16[48,1536]{1,0:T(8,128)(2,1)S(1)}, bf16[48,1536]{1,0:T(8,128)(2,1)S(1)}, u32[]{:S(2)}, u32[]{:S(2)}) collective-permute-start(bf16[48,1536]{1,0:T(8,128)(2,1)S(1)} %collective-permute-done.5.refs_4_), channel_id=1, source_target_pairs={{0,4},{1,5},{4,8},{5,9},{8,12},{9,13},{12,14},{13,15},{14,10},{15,... | collective-permute-start | bytes 442376 | tf_op jit(solution)/shard_map/ppermute | solution.py:165
  25.5 1.1 collective-permute-done.8.refs_6_
  27.1 1.6 %collective-permute-start.15 = (bf16[48,1536]{1,0:T(8,128)(2,1)S(1)}, bf16[48,1536]{1,0:T(8,128)(2,1)S(1)}, u32[]{:S(2)}, u32[]{:S(2)}) collective-permute-start(bf16[48,1536]{1,0:T(8,128)(2,1)S(1)} %collective-permute-done.11.refs_9_), channel_id=1, source_target_pairs={{0,4},{1,5},{4,8},{5,9},{8,12},{9,13},{12,14},{13,15},{14,10},{15,... | collective-permute-start | bytes 442376 | tf_op jit(solution)/shard_map/ppermute | solution.py:165
  28.7 1.6 %collective-permute-done.16.refs_14_ = bf16[48,1536]{1,0:T(8,128)(2,1)S(1)} collective-permute-done((bf16[48,1536]{1,0:T(8,128)(2,1)S(1)}, bf16[48,1536]{1,0:T(8,128)(2,1)S(1)}, u32[]{:S(2)}, u32[]{:S(2)}) %collective-permute-start.16) | collective-permute-done | bytes 147488 | tf_op jit(solution)/shard_map/ppermute | solution.py:168
  30.7 1.6 %collective-permute-start.14 = (bf16[48,1536]{1,0:T(8,128)(2,1)S(1)}, bf16[48,1536]{1,0:T(8,128)(2,1)S(1)}, u32[]{:S(2)}, u32[]{:S(2)}) collective-permute-start(bf16[48,1536]{1,0:T(8,128)(2,1)S(1)} %collective-permute-done.10.refs_8_), channel_id=1, source_target_pairs={{0,4},{1,5},{4,8},{5,9},{8,12},{9,13},{12,14},{13,15},{14,10},{15,... | collective-permute-start | bytes 442376 | tf_op jit(solution)/shard_map/ppermute | solution.py:165
  32.3 1.0 collective-permute-done.12.refs_10_
  33.3 2.1 %collective-permute-done.17.refs_15_ = bf16[48,1536]{1,0:T(8,128)(2,1)S(1)} collective-permute-done((bf16[48,1536]{1,0:T(8,128)(2,1)S(1)}, bf16[48,1536]{1,0:T(8,128)(2,1)S(1)}, u32[]{:S(2)}, u32[]{:S(2)}) %collective-permute-start.17) | collective-permute-done | bytes 147488 | tf_op jit(solution)/shard_map/ppermute | solution.py:168
  35.4 0.5 collective-permute-done.14.refs_12_
  35.9 1.2 %project.1 = (f32[128,1536]{1,0:T(8,128)S(1)}, bf16[768,1536]{1,0:T(8,128)(2,1)S(1)}) custom-call(s32[3]{0:T(128)S(1)} %pad_add_fusion.place, bf16[256,768]{1,0:T(8,128)(2,1)S(1)} %get-tuple-element.74.tokens, bf16[48,1536]{1,0:T(8,128)(2,1)S(1)} %copy-done.3, bf16[48,1536]{1,0:T(8,128)(2,1)S(1)} %collective-permute-done.2.refs_1_, ...), custom_call_target="tpu_custom_call" | custom-call | flops 301989888 | bytes 4194304 | tf_op jit(solution)/shard_map/project/pallas_call | solution.py:27
  37.2 1.0 own.1
  38.2 1.2 %collective-permute-done.18.near = f32[128,1536]{1,0:T(8,128)S(1)} collective-permute-done((f32[128,1536]{1,0:T(8,128)S(1)}, f32[128,1536]{1,0:T(8,128)S(1)}, u32[]{:S(2)}, u32[]{:S(2)}) %collective-permute-start.18) | collective-permute-done | bytes 786464 | tf_op jit(solution)/shard_map/ppermute | solution.py:162
  39.4 0.6 stream.1
  40.1 1.6 %collective-permute-start.23 = (bf16[64,1664]{1,0:T(8,128)(2,1)S(1)}, bf16[64,1664]{1,0:T(8,128)(2,1)S(1)}, u32[]{:S(2)}, u32[]{:S(2)}) collective-permute-start(bf16[64,1664]{1,0:T(8,128)(2,1)S(1)} %get-tuple-element.84.refs_4_.refs_0_), channel_id=1, source_target_pairs={{0,4},{1,5},{4,8},{5,9},{8,12},{9,13},{12,14},{13,15},{14,10},{15,... | collective-permute-start | bytes 638984 | tf_op jit(solution)/shard_map/ppermute | solution.py:165
  42.1 5.3 %collective-permute-done.25.refs_7_.refs_5_.refs_3_ = bf16[1536,512]{1,0:T(8,128)(2,1)S(1)} collective-permute-done((bf16[1536,512]{1,0:T(8,128)(2,1)S(1)}, bf16[1536,512]{1,0:T(8,128)(2,1)S(1)}, u32[]{:S(2)}, u32[]{:S(2)}) %collective-permute-start.25) | collective-permute-done | bytes 1572896 | tf_op jit(solution)/shard_map/ppermute | solution.py:198
  47.4 1.3 %collective-permute-done.24.refs_3_ = bf16[64,1664]{1,0:T(8,128)(2,1)S(1)} collective-permute-done((bf16[64,1664]{1,0:T(8,128)(2,1)S(1)}, bf16[64,1664]{1,0:T(8,128)(2,1)S(1)}, u32[]{:S(2)}, u32[]{:S(2)}) %collective-permute-start.24) | collective-permute-done | bytes 213024 | tf_op jit(solution)/shard_map/ppermute | solution.py:168
  48.7 1.6 %collective-permute-start.19 = (bf16[64,1664]{1,0:T(8,128)(2,1)S(1)}, bf16[64,1664]{1,0:T(8,128)(2,1)S(1)}, u32[]{:S(2)}, u32[]{:S(2)}) collective-permute-start(bf16[64,1664]{1,0:T(8,128)(2,1)S(1)} %get-tuple-element.85.refs_5_.refs_1_), channel_id=1, source_target_pairs={{0,4},{1,5},{4,8},{5,9},{8,12},{9,13},{12,14},{13,15},{14,10},{15,... | collective-permute-start | bytes 638984 | tf_op jit(solution)/shard_map/ppermute | solution.py:165
  50.7 1.6 %collective-permute-start.27 = (bf16[64,1664]{1,0:T(8,128)(2,1)S(1)}, bf16[64,1664]{1,0:T(8,128)(2,1)S(1)}, u32[]{:S(2)}, u32[]{:S(2)}) collective-permute-start(bf16[64,1664]{1,0:T(8,128)(2,1)S(1)} %collective-permute-done.23.refs_0_), channel_id=1, source_target_pairs={{0,4},{1,5},{4,8},{5,9},{8,12},{9,13},{12,14},{13,15},{14,10},{15,... | collective-permute-start | bytes 638984 | tf_op jit(solution)/shard_map/ppermute | solution.py:165
  52.8 4.0 %collective-permute-done.19.refs_1_ = bf16[64,1664]{1,0:T(8,128)(2,1)S(1)} collective-permute-done((bf16[64,1664]{1,0:T(8,128)(2,1)S(1)}, bf16[64,1664]{1,0:T(8,128)(2,1)S(1)}, u32[]{:S(2)}, u32[]{:S(2)}) %collective-permute-start.19) | collective-permute-done | bytes 213024 | tf_op jit(solution)/shard_map/ppermute | solution.py:165
  56.8 1.6 %collective-permute-start.20 = (bf16[64,1664]{1,0:T(8,128)(2,1)S(1)}, bf16[64,1664]{1,0:T(8,128)(2,1)S(1)}, u32[]{:S(2)}, u32[]{:S(2)}) collective-permute-start(bf16[64,1664]{1,0:T(8,128)(2,1)S(1)} %collective-permute-done.19.refs_1_), channel_id=1, source_target_pairs={{0,4},{1,5},{4,8},{5,9},{8,12},{9,13},{12,14},{13,15},{14,10},{15,... | collective-permute-start | bytes 638984 | tf_op jit(solution)/shard_map/ppermute | solution.py:165
  58.8 2.5 %collective-permute-done.27.refs_0_ = bf16[64,1664]{1,0:T(8,128)(2,1)S(1)} collective-permute-done((bf16[64,1664]{1,0:T(8,128)(2,1)S(1)}, bf16[64,1664]{1,0:T(8,128)(2,1)S(1)}, u32[]{:S(2)}, u32[]{:S(2)}) %collective-permute-start.27) | collective-permute-done | bytes 213024 | tf_op jit(solution)/shard_map/ppermute | solution.py:165
  61.3 1.6 %collective-permute-start.28 = (bf16[64,1664]{1,0:T(8,128)(2,1)S(1)}, bf16[64,1664]{1,0:T(8,128)(2,1)S(1)}, u32[]{:S(2)}, u32[]{:S(2)}) collective-permute-start(bf16[64,1664]{1,0:T(8,128)(2,1)S(1)} %collective-permute-done.27.refs_0_), channel_id=1, source_target_pairs={{0,4},{1,5},{4,8},{5,9},{8,12},{9,13},{12,14},{13,15},{14,10},{15,... | collective-permute-start | bytes 638984 | tf_op jit(solution)/shard_map/ppermute | solution.py:165
  63.4 4.5 %experts.4 = (f32[64,1536]{1,0:T(8,128)S(1)}, f32[64,1536]{1,0:T(8,128)S(1)}, f32[64,1536]{1,0:T(8,128)S(1)}, f32[64,1536]{1,0:T(8,128)S(1)}, f32[64,1536]{1,0:T(8,128)S(1)}, /*index=5*/f32[64,1536]{1,0:T(8,128)S(1)}) custom-call(s32[3]{0:T(128)S(1)} %pad_add_fusion.place, bf16[64,1664]{1,0:T(8,128)(2,1)S(1)} %collective-permute-done.23.refs_0_, ...), custom_call_target="tpu_custom_call" | custom-call | flops 3623878656 | bytes 4194304 | tf_op jit(solution)/shard_map/experts/pallas_call | solution.py:27
  67.9 1.6 %collective-permute-start.31 = (bf16[64,1664]{1,0:T(8,128)(2,1)S(1)}, bf16[64,1664]{1,0:T(8,128)(2,1)S(1)}, u32[]{:S(2)}, u32[]{:S(2)}) collective-permute-start(bf16[64,1664]{1,0:T(8,128)(2,1)S(1)} %collective-permute-done.20.refs_1_), channel_id=1, source_target_pairs={{0,4},{1,5},{4,8},{5,9},{8,12},{9,13},{12,14},{13,15},{14,10},{15,... | collective-permute-start | bytes 638984 | tf_op jit(solution)/shard_map/ppermute | solution.py:165
  70.0 3.3 %experts.5 = (f32[64,1536]{1,0:T(8,128)S(1)}, f32[64,1536]{1,0:T(8,128)S(1)}, f32[64,1536]{1,0:T(8,128)S(1)}, f32[64,1536]{1,0:T(8,128)S(1)}) custom-call(s32[3]{0:T(128)S(1)} %pad_add_fusion.place, bf16[64,1664]{1,0:T(8,128)(2,1)S(1)} %collective-permute-done.27.refs_0_, bf16[64,1664]{1,0:T(8,128)(2,1)S(1)} %collective-permute-done.20.refs_1_, ...), custom_call_target="tpu_custom_call" | custom-call | flops 2415919104 | bytes 4194304 | tf_op jit(solution)/shard_map/experts/pallas_call | solution.py:27
  73.4 1.6 %collective-permute-start.33 = (bf16[64,1664]{1,0:T(8,128)(2,1)S(1)}, bf16[64,1664]{1,0:T(8,128)(2,1)S(1)}, u32[]{:S(2)}, u32[]{:S(2)}) collective-permute-start(bf16[64,1664]{1,0:T(8,128)(2,1)S(1)} %collective-permute-done.28.refs_0_), channel_id=1, source_target_pairs={{0,4},{1,5},{4,8},{5,9},{8,12},{9,13},{12,14},{13,15},{14,10},{15,... | collective-permute-start | bytes 638984 | tf_op jit(solution)/shard_map/ppermute | solution.py:165
  75.4 0.9 collective-permute-done.32.refs_2_
  76.3 3.3 %experts.6 = (f32[64,1536]{1,0:T(8,128)S(1)}, f32[64,1536]{1,0:T(8,128)S(1)}, f32[64,1536]{1,0:T(8,128)S(1)}, f32[64,1536]{1,0:T(8,128)S(1)}) custom-call(s32[3]{0:T(128)S(1)} %pad_add_fusion.place, bf16[64,1664]{1,0:T(8,128)(2,1)S(1)} %collective-permute-done.28.refs_0_, bf16[64,1664]{1,0:T(8,128)(2,1)S(1)} %collective-permute-done.31.refs_1_, ...), custom_call_target="tpu_custom_call" | custom-call | flops 2415919104 | bytes 4194304 | tf_op jit(solution)/shard_map/experts/pallas_call | solution.py:27
  79.7 0.5 collective-permute-start.38
  80.2 1.6 %collective-permute-start.37 = (bf16[64,1536]{1,0:T(8,128)(2,1)S(1)}, bf16[64,1536]{1,0:T(8,128)(2,1)S(1)}, u32[]{:S(2)}, u32[]{:S(2)}) collective-permute-start(bf16[64,1536]{1,0:T(8,128)(2,1)S(1)} %convert_element_type.86), channel_id=1, source_target_pairs={{0,4},{1,5},{4,8},{5,9},{8,12},{9,13},{12,14},{13,15},{14,10},{15,... | collective-permute-start | bytes 589832 | tf_op jit(solution)/shard_map/ppermute | solution.py:165
  81.8 2.2 %experts.7 = (f32[64,1536]{1,0:T(8,128)S(1)}, f32[64,1536]{1,0:T(8,128)S(1)}) custom-call(s32[3]{0:T(128)S(1)} %pad_add_fusion.place, bf16[64,1664]{1,0:T(8,128)(2,1)S(1)} %collective-permute-done.33.refs_0_, bf16[64,1664]{1,0:T(8,128)(2,1)S(1)} %collective-permute-done.34.refs_1_, bf16[1536,512]{1,0:T(8,128)(2,1)S(1)} %pad_maximum_fusion.refs_6_.refs_4_.refs_2_, ...), custom_call_target="tpu_custom_call" | custom-call | flops 1207959552 | bytes 4194304 | tf_op jit(solution)/shard_map/experts/pallas_call | solution.py:27
  84.0 0.5 collective-permute-start.36
  84.6 1.6 %collective-permute-start.35 = (bf16[64,1536]{1,0:T(8,128)(2,1)S(1)}, bf16[64,1536]{1,0:T(8,128)(2,1)S(1)}, u32[]{:S(2)}, u32[]{:S(2)}) collective-permute-start(bf16[64,1536]{1,0:T(8,128)(2,1)S(1)} %convert_element_type.80), channel_id=1, source_target_pairs={{0,4},{1,5},{4,8},{5,9},{8,12},{9,13},{12,14},{13,15},{14,10},{15,... | collective-permute-start | bytes 589832 | tf_op jit(solution)/shard_map/ppermute | solution.py:165
  86.1 0.7 collective-permute-done.38
  86.8 0.7 collective-permute-done.37
  87.6 0.8 collective-permute-start.42
  88.4 1.3 %collective-permute-start.41 = (bf16[64,1536]{1,0:T(8,128)(2,1)S(1)}, bf16[64,1536]{1,0:T(8,128)(2,1)S(1)}, u32[]{:S(2)}, u32[]{:S(2)}) collective-permute-start(bf16[64,1536]{1,0:T(8,128)(2,1)S(1)} %add_convert_fusion.7), channel_id=1, source_target_pairs={{0,4},{1,5},{4,8},{5,9},{8,12},{9,13},{12,14},{13,15},{14,10},{15,... | collective-permute-start | bytes 589832 | tf_op jit(solution)/shard_map/ppermute | solution.py:165
  89.7 2.2 %collective-permute-done.36 = bf16[64,1536]{1,0:T(8,128)(2,1)S(1)} collective-permute-done((bf16[64,1536]{1,0:T(8,128)(2,1)S(1)}, bf16[64,1536]{1,0:T(8,128)(2,1)S(1)}, u32[]{:S(2)}, u32[]{:S(2)}) %collective-permute-start.36) | collective-permute-done | bytes 196640 | tf_op jit(solution)/shard_map/ppermute | solution.py:168
  92.4 0.5 collective-permute-start.40
  92.9 1.6 %collective-permute-start.39 = (bf16[64,1536]{1,0:T(8,128)(2,1)S(1)}, bf16[64,1536]{1,0:T(8,128)(2,1)S(1)}, u32[]{:S(2)}, u32[]{:S(2)}) collective-permute-start(bf16[64,1536]{1,0:T(8,128)(2,1)S(1)} %add_convert_fusion.9), channel_id=1, source_target_pairs={{0,4},{1,5},{4,8},{5,9},{8,12},{9,13},{12,14},{13,15},{14,10},{15,... | collective-permute-start | bytes 589832 | tf_op jit(solution)/shard_map/ppermute | solution.py:165
  94.5 1.4 %collective-permute-done.42 = bf16[64,1536]{1,0:T(8,128)(2,1)S(1)} collective-permute-done((bf16[64,1536]{1,0:T(8,128)(2,1)S(1)}, bf16[64,1536]{1,0:T(8,128)(2,1)S(1)}, u32[]{:S(2)}, u32[]{:S(2)}) %collective-permute-start.42) | collective-permute-done | bytes 196640 | tf_op jit(solution)/shard_map/ppermute | solution.py:168
  96.5 1.7 %collective-permute-done.40 = bf16[64,1536]{1,0:T(8,128)(2,1)S(1)} collective-permute-done((bf16[64,1536]{1,0:T(8,128)(2,1)S(1)}, bf16[64,1536]{1,0:T(8,128)(2,1)S(1)}, u32[]{:S(2)}, u32[]{:S(2)}) %collective-permute-start.40) | collective-permute-done | bytes 196640 | tf_op jit(solution)/shard_map/ppermute | solution.py:168
  98.6 1.7 %collective-permute-start.44 = (bf16[64,1536]{1,0:T(8,128)(2,1)S(1)}, bf16[64,1536]{1,0:T(8,128)(2,1)S(1)}, u32[]{:S(2)}, u32[]{:S(2)}) collective-permute-start(bf16[64,1536]{1,0:T(8,128)(2,1)S(1)} %add_convert_fusion.4), channel_id=1, source_target_pairs={{4,0},{5,1},{8,4},{9,5},{12,8},{13,9},{14,12},{15,13},{10,14},{11,... | collective-permute-start | bytes 589832 | tf_op jit(solution)/shard_map/ppermute | solution.py:168
  100.7 1.6 %collective-permute-start.46 = (bf16[64,1536]{1,0:T(8,128)(2,1)S(1)}, bf16[64,1536]{1,0:T(8,128)(2,1)S(1)}, u32[]{:S(2)}, u32[]{:S(2)}) collective-permute-start(bf16[64,1536]{1,0:T(8,128)(2,1)S(1)} %add_convert_fusion.3), channel_id=1, source_target_pairs={{0,4},{1,5},{4,8},{5,9},{8,12},{9,13},{12,14},{13,15},{14,10},{15,... | collective-permute-start | bytes 589832 | tf_op jit(solution)/shard_map/ppermute | solution.py:165
  102.8 3.6 %collective-permute-done.44 = bf16[64,1536]{1,0:T(8,128)(2,1)S(1)} collective-permute-done((bf16[64,1536]{1,0:T(8,128)(2,1)S(1)}, bf16[64,1536]{1,0:T(8,128)(2,1)S(1)}, u32[]{:S(2)}, u32[]{:S(2)}) %collective-permute-start.44) | collective-permute-done | bytes 196640 | tf_op jit(solution)/shard_map/ppermute | solution.py:168
  106.4 1.5 %collective-permute-done.43 = bf16[64,1536]{1,0:T(8,128)(2,1)S(1)} collective-permute-done((bf16[64,1536]{1,0:T(8,128)(2,1)S(1)}, bf16[64,1536]{1,0:T(8,128)(2,1)S(1)}, u32[]{:S(2)}, u32[]{:S(2)}) %collective-permute-start.43) | collective-permute-done | bytes 196640 | tf_op jit(solution)/shard_map/ppermute | solution.py:165
  107.9 0.7 collective-permute-start.45
  108.6 1.4 %collective-permute-start.48 = (bf16[64,1536]{1,0:T(8,128)(2,1)S(1)}, bf16[64,1536]{1,0:T(8,128)(2,1)S(1)}, u32[]{:S(2)}, u32[]{:S(2)}) collective-permute-start(bf16[64,1536]{1,0:T(8,128)(2,1)S(1)} %add_convert_fusion), channel_id=1, source_target_pairs={{4,0},{5,1},{8,4},{9,5},{12,8},{13,9},{14,12},{15,13},{10,14},{11,... | collective-permute-start | bytes 589832 | tf_op jit(solution)/shard_map/ppermute | solution.py:168
  110.2 3.5 %collective-permute-done.45.refs_4_ = bf16[64,1536]{1,0:T(8,128)(2,1)S(1)} collective-permute-done((bf16[64,1536]{1,0:T(8,128)(2,1)S(1)}, bf16[64,1536]{1,0:T(8,128)(2,1)S(1)}, u32[]{:S(2)}, u32[]{:S(2)}) %collective-permute-start.45) | collective-permute-done | bytes 196640 | tf_op jit(solution)/shard_map/ppermute | solution.py:165
  113.7 0.7 collective-permute-done.48.refs_7_
  114.3 1.6 %final.1 = bf16[128,1536]{1,0:T(8,128)(2,1)} custom-call(s32[3]{0:T(128)S(1)} %pad_add_fusion.place, bf16[64,1664]{1,0:T(8,128)(2,1)S(1)} %get-tuple-element.84.refs_4_.refs_0_, bf16[64,1664]{1,0:T(8,128)(2,1)S(1)} %get-tuple-element.85.refs_5_.refs_1_, f32[64,1536]{1,0:T(8,128)S(1)} %get-tuple-element.95.refs_2_, f32[64,1536]{1,0:T(8,128)S(1)} %get-tuple-element.96.refs_3_, ...), custom_call_target="tpu_custom_call" | custom-call | bytes 4194304 | tf_op jit(solution)/shard_map/final/pallas_call | solution.py:27
  (76 shorter events, 9.9 us)
Async XLA Ops:
  0.0 10.5 %collective-permute-start.4 = (bf16[512,1536]{1,0:T(8,128)(2,1)}, bf16[512,1536]{1,0:T(8,128)(2,1)S(1)}, u32[]{:S(2)}, u32[]{:S(2)}) collective-permute-start(bf16[512,1536]{1,0:T(8,128)(2,1)} %bitcast.9), channel_id=1, source_target_pairs={{0,1},{1,0},{2,3},{3,2},{4,5},{5,4},{6,7},{7,6},{8,9},{9,8},{10,11... | collective-permute-start | bytes 4718600 | tf_op jit(solution)/shard_map/ppermute | solution.py:162
  0.5 8.1 %collective-permute-start.2 = (bf16[48,1536]{1,0:T(8,128)(2,1)}, bf16[48,1536]{1,0:T(8,128)(2,1)S(1)}, u32[]{:S(2)}, u32[]{:S(2)}) collective-permute-start(bf16[48,1536]{1,0:T(8,128)(2,1)} %refs_0_.1), channel_id=1, source_target_pairs={{0,16},{16,0},{1,17},{17,1},{2,18},{18,2},{3,19},{19,3},{4,20},{20... | collective-permute-start | bytes 442376 | tf_op jit(solution)/shard_map/ppermute | solution.py:190
  3.0 6.2 %collective-permute-start = (bf16[48,1536]{1,0:T(8,128)(2,1)}, bf16[48,1536]{1,0:T(8,128)(2,1)S(1)}, u32[]{:S(2)}, u32[]{:S(2)}) collective-permute-start(bf16[48,1536]{1,0:T(8,128)(2,1)} %refs_0_.1), channel_id=1, source_target_pairs={{0,4},{1,5},{4,8},{5,9},{8,12},{9,13},{12,14},{13,15},{14,10},{15,... | collective-permute-start | bytes 442376 | tf_op jit(solution)/shard_map/ppermute | solution.py:165
  4.5 5.9 %collective-permute-start.1 = (bf16[48,1536]{1,0:T(8,128)(2,1)}, bf16[48,1536]{1,0:T(8,128)(2,1)S(1)}, u32[]{:S(2)}, u32[]{:S(2)}) collective-permute-start(bf16[48,1536]{1,0:T(8,128)(2,1)} %refs_0_.1), channel_id=1, source_target_pairs={{4,0},{5,1},{8,4},{9,5},{12,8},{13,9},{14,12},{15,13},{10,14},{11,... | collective-permute-start | bytes 442376 | tf_op jit(solution)/shard_map/ppermute | solution.py:168
  5.0 1.9 %collective-permute-start.3 = (bf16[128,1536]{1,0:T(8,128)(2,1)}, bf16[128,1536]{1,0:T(8,128)(2,1)S(1)}, u32[]{:S(2)}, u32[]{:S(2)}) collective-permute-start(bf16[128,1536]{1,0:T(8,128)(2,1)} %att.1), channel_id=1, source_target_pairs={{0,1},{1,0},{2,3},{3,2},{4,5},{5,4},{6,7},{7,6},{8,9},{9,8},{10,11... | collective-permute-start | bytes 1179656 | tf_op jit(solution)/shard_map/ppermute | solution.py:162
  5.0 1.6 %copy-start.5 = (s32[128,8]{0,1:T(8,128)S(1)}, s32[128,8]{0,1:T(8,128)}, u32[]{:S(2)}) copy-start(s32[128,8]{0,1:T(8,128)} %param.15) | copy-start | bytes 12292
  5.0 1.7 %copy-start.6 = (f32[128,8]{0,1:T(8,128)S(1)}, f32[128,8]{0,1:T(8,128)}, u32[]{:S(2)}) copy-start(f32[128,8]{0,1:T(8,128)} %param.16) | copy-start | bytes 12292
  5.0 1.9 %copy-start.1 = (bf16[128,1536]{1,0:T(8,128)(2,1)S(1)}, bf16[128,1536]{1,0:T(8,128)(2,1)}, u32[]{:S(2)}) copy-start(bf16[128,1536]{1,0:T(8,128)(2,1)} %att.1) | copy-start | bytes 1179652
  5.0 30.9 %copy-start.3 = (bf16[48,1536]{1,0:T(8,128)(2,1)S(1)}, bf16[48,1536]{1,0:T(8,128)(2,1)}, u32[]{:S(2)}) copy-start(bf16[48,1536]{1,0:T(8,128)(2,1)} %refs_0_.1) | copy-start | bytes 442372
  10.5 13.5 %collective-permute-start.6 = (bf16[1536,512]{1,0:T(8,128)(2,1)S(1)}, bf16[1536,512]{1,0:T(8,128)(2,1)S(1)}, u32[]{:S(2)}, u32[]{:S(2)}) collective-permute-start(bf16[1536,512]{1,0:T(8,128)(2,1)S(1)} %pad_maximum_fusion.refs_6_.refs_4_.refs_2_), channel_id=1, source_target_pairs={{0,1},{1,0},{2,3},{3,2},{4,5},{5,4},{6,7},{7,6},{8,9},{9,8},{10,11... | collective-permute-start | bytes 4718600 | tf_op jit(solution)/shard_map/ppermute | solution.py:162
  10.5 6.3 %collective-permute-start.9 = (bf16[48,1536]{1,0:T(8,128)(2,1)S(1)}, bf16[48,1536]{1,0:T(8,128)(2,1)S(1)}, u32[]{:S(2)}, u32[]{:S(2)}) collective-permute-start(bf16[48,1536]{1,0:T(8,128)(2,1)S(1)} %collective-permute-done.2.refs_1_), channel_id=1, source_target_pairs={{4,0},{5,1},{8,4},{9,5},{12,8},{13,9},{14,12},{15,13},{10,14},{11,... | collective-permute-start | bytes 442376 | tf_op jit(solution)/shard_map/ppermute | solution.py:168
  10.9 36.5 %collective-permute-start.25 = (bf16[1536,512]{1,0:T(8,128)(2,1)S(1)}, bf16[1536,512]{1,0:T(8,128)(2,1)S(1)}, u32[]{:S(2)}, u32[]{:S(2)}) collective-permute-start(bf16[1536,512]{1,0:T(8,128)(2,1)S(1)} %pad_maximum_fusion.refs_6_.refs_4_.refs_2_), channel_id=1, source_target_pairs={{0,16},{16,0},{1,17},{17,1},{2,18},{18,2},{3,19},{19,3},{4,20},{20... | collective-permute-start | bytes 4718600 | tf_op jit(solution)/shard_map/ppermute | solution.py:198
  11.3 6.7 %collective-permute-start.5 = (bf16[48,1536]{1,0:T(8,128)(2,1)S(1)}, bf16[48,1536]{1,0:T(8,128)(2,1)S(1)}, u32[]{:S(2)}, u32[]{:S(2)}) collective-permute-start(bf16[48,1536]{1,0:T(8,128)(2,1)S(1)} %collective-permute-done.refs_2_), channel_id=1, source_target_pairs={{0,4},{1,5},{4,8},{5,9},{8,12},{9,13},{12,14},{13,15},{14,10},{15,... | collective-permute-start | bytes 442376 | tf_op jit(solution)/shard_map/ppermute | solution.py:165
  13.0 7.1 %collective-permute-start.7 = (bf16[48,1536]{1,0:T(8,128)(2,1)S(1)}, bf16[48,1536]{1,0:T(8,128)(2,1)S(1)}, u32[]{:S(2)}, u32[]{:S(2)}) collective-permute-start(bf16[48,1536]{1,0:T(8,128)(2,1)S(1)} %collective-permute-done.2.refs_1_), channel_id=1, source_target_pairs={{0,4},{1,5},{4,8},{5,9},{8,12},{9,13},{12,14},{13,15},{14,10},{15,... | collective-permute-start | bytes 442376 | tf_op jit(solution)/shard_map/ppermute | solution.py:165
  16.7 6.8 %collective-permute-start.13 = (bf16[48,1536]{1,0:T(8,128)(2,1)S(1)}, bf16[48,1536]{1,0:T(8,128)(2,1)S(1)}, u32[]{:S(2)}, u32[]{:S(2)}) collective-permute-start(bf16[48,1536]{1,0:T(8,128)(2,1)S(1)} %collective-permute-done.9.refs_7_), channel_id=1, source_target_pairs={{4,0},{5,1},{8,4},{9,5},{12,8},{13,9},{14,12},{15,13},{10,14},{11,... | collective-permute-start | bytes 442376 | tf_op jit(solution)/shard_map/ppermute | solution.py:168
  18.0 8.6 %collective-permute-start.8 = (bf16[48,1536]{1,0:T(8,128)(2,1)S(1)}, bf16[48,1536]{1,0:T(8,128)(2,1)S(1)}, u32[]{:S(2)}, u32[]{:S(2)}) collective-permute-start(bf16[48,1536]{1,0:T(8,128)(2,1)S(1)} %collective-permute-done.1.refs_3_), channel_id=1, source_target_pairs={{4,0},{5,1},{8,4},{9,5},{12,8},{13,9},{14,12},{15,13},{10,14},{11,... | collective-permute-start | bytes 442376 | tf_op jit(solution)/shard_map/ppermute | solution.py:168
  20.2 6.9 %collective-permute-start.11 = (bf16[48,1536]{1,0:T(8,128)(2,1)S(1)}, bf16[48,1536]{1,0:T(8,128)(2,1)S(1)}, u32[]{:S(2)}, u32[]{:S(2)}) collective-permute-start(bf16[48,1536]{1,0:T(8,128)(2,1)S(1)} %collective-permute-done.7.refs_5_), channel_id=1, source_target_pairs={{0,4},{1,5},{4,8},{5,9},{8,12},{9,13},{12,14},{13,15},{14,10},{15,... | collective-permute-start | bytes 442376 | tf_op jit(solution)/shard_map/ppermute | solution.py:165
  23.5 6.8 %collective-permute-start.16 = (bf16[48,1536]{1,0:T(8,128)(2,1)S(1)}, bf16[48,1536]{1,0:T(8,128)(2,1)S(1)}, u32[]{:S(2)}, u32[]{:S(2)}) collective-permute-start(bf16[48,1536]{1,0:T(8,128)(2,1)S(1)} %collective-permute-done.13.refs_11_), channel_id=1, source_target_pairs={{4,0},{5,1},{8,4},{9,5},{12,8},{13,9},{14,12},{15,13},{10,14},{11,... | collective-permute-start | bytes 442376 | tf_op jit(solution)/shard_map/ppermute | solution.py:168
  23.9 6.8 %collective-permute-start.10 = (bf16[48,1536]{1,0:T(8,128)(2,1)S(1)}, bf16[48,1536]{1,0:T(8,128)(2,1)S(1)}, u32[]{:S(2)}, u32[]{:S(2)}) collective-permute-start(bf16[48,1536]{1,0:T(8,128)(2,1)S(1)} %collective-permute-done.5.refs_4_), channel_id=1, source_target_pairs={{0,4},{1,5},{4,8},{5,9},{8,12},{9,13},{12,14},{13,15},{14,10},{15,... | collective-permute-start | bytes 442376 | tf_op jit(solution)/shard_map/ppermute | solution.py:165
  26.6 6.6 %collective-permute-start.12 = (bf16[48,1536]{1,0:T(8,128)(2,1)S(1)}, bf16[48,1536]{1,0:T(8,128)(2,1)S(1)}, u32[]{:S(2)}, u32[]{:S(2)}) collective-permute-start(bf16[48,1536]{1,0:T(8,128)(2,1)S(1)} %collective-permute-done.8.refs_6_), channel_id=1, source_target_pairs={{4,0},{5,1},{8,4},{9,5},{12,8},{13,9},{14,12},{15,13},{10,14},{11,... | collective-permute-start | bytes 442376 | tf_op jit(solution)/shard_map/ppermute | solution.py:168
  27.1 6.2 %collective-permute-start.15 = (bf16[48,1536]{1,0:T(8,128)(2,1)S(1)}, bf16[48,1536]{1,0:T(8,128)(2,1)S(1)}, u32[]{:S(2)}, u32[]{:S(2)}) collective-permute-start(bf16[48,1536]{1,0:T(8,128)(2,1)S(1)} %collective-permute-done.11.refs_9_), channel_id=1, source_target_pairs={{0,4},{1,5},{4,8},{5,9},{8,12},{9,13},{12,14},{13,15},{14,10},{15,... | collective-permute-start | bytes 442376 | tf_op jit(solution)/shard_map/ppermute | solution.py:165
  30.3 5.1 %collective-permute-start.17 = (bf16[48,1536]{1,0:T(8,128)(2,1)S(1)}, bf16[48,1536]{1,0:T(8,128)(2,1)S(1)}, u32[]{:S(2)}, u32[]{:S(2)}) collective-permute-start(bf16[48,1536]{1,0:T(8,128)(2,1)S(1)} %collective-permute-done.16.refs_14_), channel_id=1, source_target_pairs={{4,0},{5,1},{8,4},{9,5},{12,8},{13,9},{14,12},{15,13},{10,14},{11,... | collective-permute-start | bytes 442376 | tf_op jit(solution)/shard_map/ppermute | solution.py:168
  30.7 5.1 %collective-permute-start.14 = (bf16[48,1536]{1,0:T(8,128)(2,1)S(1)}, bf16[48,1536]{1,0:T(8,128)(2,1)S(1)}, u32[]{:S(2)}, u32[]{:S(2)}) collective-permute-start(bf16[48,1536]{1,0:T(8,128)(2,1)S(1)} %collective-permute-done.10.refs_8_), channel_id=1, source_target_pairs={{0,4},{1,5},{4,8},{5,9},{8,12},{9,13},{12,14},{13,15},{14,10},{15,... | collective-permute-start | bytes 442376 | tf_op jit(solution)/shard_map/ppermute | solution.py:165
  37.1 2.4 %collective-permute-start.18 = (f32[128,1536]{1,0:T(8,128)S(1)}, f32[128,1536]{1,0:T(8,128)S(1)}, u32[]{:S(2)}, u32[]{:S(2)}) collective-permute-start(f32[128,1536]{1,0:T(8,128)S(1)} %get-tuple-element.82), channel_id=1, source_target_pairs={{0,1},{1,0},{2,3},{3,2},{4,5},{5,4},{6,7},{7,6},{8,9},{9,8},{10,11... | collective-permute-start | bytes 2359304 | tf_op jit(solution)/shard_map/ppermute | solution.py:162
  37.1 2.3 %copy-start.2 = (bf16[128,1536]{1,0:T(8,128)(2,1)S(1)}, bf16[128,1536]{1,0:T(8,128)(2,1)}, u32[]{:S(2)}) copy-start(bf16[128,1536]{1,0:T(8,128)(2,1)} %res.1) | copy-start | bytes 1179652
  38.2 25.2 %copy-start = (bf16[1,512,1536]{2,1,0:T(8,128)(2,1)S(1)}, bf16[1,512,1536]{2,1,0:T(8,128)(2,1)}, u32[]{:S(2)}) copy-start(bf16[1,512,1536]{2,1,0:T(8,128)(2,1)} %param.14) | copy-start | bytes 4718596
  40.1 7.4 %collective-permute-start.23 = (bf16[64,1664]{1,0:T(8,128)(2,1)S(1)}, bf16[64,1664]{1,0:T(8,128)(2,1)S(1)}, u32[]{:S(2)}, u32[]{:S(2)}) collective-permute-start(bf16[64,1664]{1,0:T(8,128)(2,1)S(1)} %get-tuple-element.84.refs_4_.refs_0_), channel_id=1, source_target_pairs={{0,4},{1,5},{4,8},{5,9},{8,12},{9,13},{12,14},{13,15},{14,10},{15,... | collective-permute-start | bytes 638984 | tf_op jit(solution)/shard_map/ppermute | solution.py:165
  41.7 7.0 %collective-permute-start.24 = (bf16[64,1664]{1,0:T(8,128)(2,1)S(1)}, bf16[64,1664]{1,0:T(8,128)(2,1)S(1)}, u32[]{:S(2)}, u32[]{:S(2)}) collective-permute-start(bf16[64,1664]{1,0:T(8,128)(2,1)S(1)} %get-tuple-element.85.refs_5_.refs_1_), channel_id=1, source_target_pairs={{4,0},{5,1},{8,4},{9,5},{12,8},{13,9},{14,12},{15,13},{10,14},{11,... | collective-permute-start | bytes 638984 | tf_op jit(solution)/shard_map/ppermute | solution.py:168
  48.7 14.7 %collective-permute-start.26 = (bf16[1536,512]{1,0:T(8,128)(2,1)S(1)}, bf16[1536,512]{1,0:T(8,128)(2,1)S(1)}, u32[]{:S(2)}, u32[]{:S(2)}) collective-permute-start(bf16[1536,512]{1,0:T(8,128)(2,1)S(1)} %collective-permute-done.25.refs_7_.refs_5_.refs_3_), channel_id=1, source_target_pairs={{0,1},{1,0},{2,3},{3,2},{4,5},{5,4},{6,7},{7,6},{8,9},{9,8},{10,11... | collective-permute-start | bytes 4718600 | tf_op jit(solution)/shard_map/ppermute | solution.py:162
  48.7 8.0 %collective-permute-start.19 = (bf16[64,1664]{1,0:T(8,128)(2,1)S(1)}, bf16[64,1664]{1,0:T(8,128)(2,1)S(1)}, u32[]{:S(2)}, u32[]{:S(2)}) collective-permute-start(bf16[64,1664]{1,0:T(8,128)(2,1)S(1)} %get-tuple-element.85.refs_5_.refs_1_), channel_id=1, source_target_pairs={{0,4},{1,5},{4,8},{5,9},{8,12},{9,13},{12,14},{13,15},{14,10},{15,... | collective-permute-start | bytes 638984 | tf_op jit(solution)/shard_map/ppermute | solution.py:165
  50.3 8.1 %collective-permute-start.21 = (bf16[64,1664]{1,0:T(8,128)(2,1)S(1)}, bf16[64,1664]{1,0:T(8,128)(2,1)S(1)}, u32[]{:S(2)}, u32[]{:S(2)}) collective-permute-start(bf16[64,1664]{1,0:T(8,128)(2,1)S(1)} %get-tuple-element.84.refs_4_.refs_0_), channel_id=1, source_target_pairs={{4,0},{5,1},{8,4},{9,5},{12,8},{13,9},{14,12},{15,13},{10,14},{11,... | collective-permute-start | bytes 638984 | tf_op jit(solution)/shard_map/ppermute | solution.py:168
  50.7 10.6 %collective-permute-start.27 = (bf16[64,1664]{1,0:T(8,128)(2,1)S(1)}, bf16[64,1664]{1,0:T(8,128)(2,1)S(1)}, u32[]{:S(2)}, u32[]{:S(2)}) collective-permute-start(bf16[64,1664]{1,0:T(8,128)(2,1)S(1)} %collective-permute-done.23.refs_0_), channel_id=1, source_target_pairs={{0,4},{1,5},{4,8},{5,9},{8,12},{9,13},{12,14},{13,15},{14,10},{15,... | collective-permute-start | bytes 638984 | tf_op jit(solution)/shard_map/ppermute | solution.py:165
  52.3 10.6 %collective-permute-start.29 = (bf16[64,1664]{1,0:T(8,128)(2,1)S(1)}, bf16[64,1664]{1,0:T(8,128)(2,1)S(1)}, u32[]{:S(2)}, u32[]{:S(2)}) collective-permute-start(bf16[64,1664]{1,0:T(8,128)(2,1)S(1)} %collective-permute-done.24.refs_3_), channel_id=1, source_target_pairs={{4,0},{5,1},{8,4},{9,5},{12,8},{13,9},{14,12},{15,13},{10,14},{11,... | collective-permute-start | bytes 638984 | tf_op jit(solution)/shard_map/ppermute | solution.py:168
  56.8 11.1 %collective-permute-start.20 = (bf16[64,1664]{1,0:T(8,128)(2,1)S(1)}, bf16[64,1664]{1,0:T(8,128)(2,1)S(1)}, u32[]{:S(2)}, u32[]{:S(2)}) collective-permute-start(bf16[64,1664]{1,0:T(8,128)(2,1)S(1)} %collective-permute-done.19.refs_1_), channel_id=1, source_target_pairs={{0,4},{1,5},{4,8},{5,9},{8,12},{9,13},{12,14},{13,15},{14,10},{15,... | collective-permute-start | bytes 638984 | tf_op jit(solution)/shard_map/ppermute | solution.py:165
  58.4 9.5 %collective-permute-start.22 = (bf16[64,1664]{1,0:T(8,128)(2,1)S(1)}, bf16[64,1664]{1,0:T(8,128)(2,1)S(1)}, u32[]{:S(2)}, u32[]{:S(2)}) collective-permute-start(bf16[64,1664]{1,0:T(8,128)(2,1)S(1)} %collective-permute-done.21.refs_2_), channel_id=1, source_target_pairs={{4,0},{5,1},{8,4},{9,5},{12,8},{13,9},{14,12},{15,13},{10,14},{11,... | collective-permute-start | bytes 638984 | tf_op jit(solution)/shard_map/ppermute | solution.py:168
  61.3 12.0 %collective-permute-start.28 = (bf16[64,1664]{1,0:T(8,128)(2,1)S(1)}, bf16[64,1664]{1,0:T(8,128)(2,1)S(1)}, u32[]{:S(2)}, u32[]{:S(2)}) collective-permute-start(bf16[64,1664]{1,0:T(8,128)(2,1)S(1)} %collective-permute-done.27.refs_0_), channel_id=1, source_target_pairs={{0,4},{1,5},{4,8},{5,9},{8,12},{9,13},{12,14},{13,15},{14,10},{15,... | collective-permute-start | bytes 638984 | tf_op jit(solution)/shard_map/ppermute | solution.py:165
  62.9 10.4 %collective-permute-start.30 = (bf16[64,1664]{1,0:T(8,128)(2,1)S(1)}, bf16[64,1664]{1,0:T(8,128)(2,1)S(1)}, u32[]{:S(2)}, u32[]{:S(2)}) collective-permute-start(bf16[64,1664]{1,0:T(8,128)(2,1)S(1)} %collective-permute-done.29.refs_3_), channel_id=1, source_target_pairs={{4,0},{5,1},{8,4},{9,5},{12,8},{13,9},{14,12},{15,13},{10,14},{11,... | collective-permute-start | bytes 638984 | tf_op jit(solution)/shard_map/ppermute | solution.py:168
  67.9 7.5 %collective-permute-start.31 = (bf16[64,1664]{1,0:T(8,128)(2,1)S(1)}, bf16[64,1664]{1,0:T(8,128)(2,1)S(1)}, u32[]{:S(2)}, u32[]{:S(2)}) collective-permute-start(bf16[64,1664]{1,0:T(8,128)(2,1)S(1)} %collective-permute-done.20.refs_1_), channel_id=1, source_target_pairs={{0,4},{1,5},{4,8},{5,9},{8,12},{9,13},{12,14},{13,15},{14,10},{15,... | collective-permute-start | bytes 638984 | tf_op jit(solution)/shard_map/ppermute | solution.py:165
  69.5 6.8 %collective-permute-start.32 = (bf16[64,1664]{1,0:T(8,128)(2,1)S(1)}, bf16[64,1664]{1,0:T(8,128)(2,1)S(1)}, u32[]{:S(2)}, u32[]{:S(2)}) collective-permute-start(bf16[64,1664]{1,0:T(8,128)(2,1)S(1)} %collective-permute-done.22.refs_2_), channel_id=1, source_target_pairs={{4,0},{5,1},{8,4},{9,5},{12,8},{13,9},{14,12},{15,13},{10,14},{11,... | collective-permute-start | bytes 638984 | tf_op jit(solution)/shard_map/ppermute | solution.py:168
  73.4 8.4 %collective-permute-start.33 = (bf16[64,1664]{1,0:T(8,128)(2,1)S(1)}, bf16[64,1664]{1,0:T(8,128)(2,1)S(1)}, u32[]{:S(2)}, u32[]{:S(2)}) collective-permute-start(bf16[64,1664]{1,0:T(8,128)(2,1)S(1)} %collective-permute-done.28.refs_0_), channel_id=1, source_target_pairs={{0,4},{1,5},{4,8},{5,9},{8,12},{9,13},{12,14},{13,15},{14,10},{15,... | collective-permute-start | bytes 638984 | tf_op jit(solution)/shard_map/ppermute | solution.py:165
  75.0 6.8 %collective-permute-start.34 = (bf16[64,1664]{1,0:T(8,128)(2,1)S(1)}, bf16[64,1664]{1,0:T(8,128)(2,1)S(1)}, u32[]{:S(2)}, u32[]{:S(2)}) collective-permute-start(bf16[64,1664]{1,0:T(8,128)(2,1)S(1)} %collective-permute-done.30.refs_3_), channel_id=1, source_target_pairs={{4,0},{5,1},{8,4},{9,5},{12,8},{13,9},{14,12},{15,13},{10,14},{11,... | collective-permute-start | bytes 638984 | tf_op jit(solution)/shard_map/ppermute | solution.py:168
  79.7 7.1 %collective-permute-start.38 = (bf16[64,1536]{1,0:T(8,128)(2,1)S(1)}, bf16[64,1536]{1,0:T(8,128)(2,1)S(1)}, u32[]{:S(2)}, u32[]{:S(2)}) collective-permute-start(bf16[64,1536]{1,0:T(8,128)(2,1)S(1)} %convert_element_type.87), channel_id=1, source_target_pairs={{4,0},{5,1},{8,4},{9,5},{12,8},{13,9},{14,12},{15,13},{10,14},{11,... | collective-permute-start | bytes 589832 | tf_op jit(solution)/shard_map/ppermute | solution.py:168
  80.2 7.4 %collective-permute-start.37 = (bf16[64,1536]{1,0:T(8,128)(2,1)S(1)}, bf16[64,1536]{1,0:T(8,128)(2,1)S(1)}, u32[]{:S(2)}, u32[]{:S(2)}) collective-permute-start(bf16[64,1536]{1,0:T(8,128)(2,1)S(1)} %convert_element_type.86), channel_id=1, source_target_pairs={{0,4},{1,5},{4,8},{5,9},{8,12},{9,13},{12,14},{13,15},{14,10},{15,... | collective-permute-start | bytes 589832 | tf_op jit(solution)/shard_map/ppermute | solution.py:165
  84.0 7.9 %collective-permute-start.36 = (bf16[64,1536]{1,0:T(8,128)(2,1)S(1)}, bf16[64,1536]{1,0:T(8,128)(2,1)S(1)}, u32[]{:S(2)}, u32[]{:S(2)}) collective-permute-start(bf16[64,1536]{1,0:T(8,128)(2,1)S(1)} %convert_element_type.81), channel_id=1, source_target_pairs={{4,0},{5,1},{8,4},{9,5},{12,8},{13,9},{14,12},{15,13},{10,14},{11,... | collective-permute-start | bytes 589832 | tf_op jit(solution)/shard_map/ppermute | solution.py:168
  84.6 7.8 %collective-permute-start.35 = (bf16[64,1536]{1,0:T(8,128)(2,1)S(1)}, bf16[64,1536]{1,0:T(8,128)(2,1)S(1)}, u32[]{:S(2)}, u32[]{:S(2)}) collective-permute-start(bf16[64,1536]{1,0:T(8,128)(2,1)S(1)} %convert_element_type.80), channel_id=1, source_target_pairs={{0,4},{1,5},{4,8},{5,9},{8,12},{9,13},{12,14},{13,15},{14,10},{15,... | collective-permute-start | bytes 589832 | tf_op jit(solution)/shard_map/ppermute | solution.py:165
  87.6 8.3 %collective-permute-start.42 = (bf16[64,1536]{1,0:T(8,128)(2,1)S(1)}, bf16[64,1536]{1,0:T(8,128)(2,1)S(1)}, u32[]{:S(2)}, u32[]{:S(2)}) collective-permute-start(bf16[64,1536]{1,0:T(8,128)(2,1)S(1)} %add_convert_fusion.6), channel_id=1, source_target_pairs={{4,0},{5,1},{8,4},{9,5},{12,8},{13,9},{14,12},{15,13},{10,14},{11,... | collective-permute-start | bytes 589832 | tf_op jit(solution)/shard_map/ppermute | solution.py:168
  88.4 8.0 %collective-permute-start.41 = (bf16[64,1536]{1,0:T(8,128)(2,1)S(1)}, bf16[64,1536]{1,0:T(8,128)(2,1)S(1)}, u32[]{:S(2)}, u32[]{:S(2)}) collective-permute-start(bf16[64,1536]{1,0:T(8,128)(2,1)S(1)} %add_convert_fusion.7), channel_id=1, source_target_pairs={{0,4},{1,5},{4,8},{5,9},{8,12},{9,13},{12,14},{13,15},{14,10},{15,... | collective-permute-start | bytes 589832 | tf_op jit(solution)/shard_map/ppermute | solution.py:165
  92.4 5.7 %collective-permute-start.40 = (bf16[64,1536]{1,0:T(8,128)(2,1)S(1)}, bf16[64,1536]{1,0:T(8,128)(2,1)S(1)}, u32[]{:S(2)}, u32[]{:S(2)}) collective-permute-start(bf16[64,1536]{1,0:T(8,128)(2,1)S(1)} %add_convert_fusion.8), channel_id=1, source_target_pairs={{4,0},{5,1},{8,4},{9,5},{12,8},{13,9},{14,12},{15,13},{10,14},{11,... | collective-permute-start | bytes 589832 | tf_op jit(solution)/shard_map/ppermute | solution.py:168
  92.9 5.7 %collective-permute-start.39 = (bf16[64,1536]{1,0:T(8,128)(2,1)S(1)}, bf16[64,1536]{1,0:T(8,128)(2,1)S(1)}, u32[]{:S(2)}, u32[]{:S(2)}) collective-permute-start(bf16[64,1536]{1,0:T(8,128)(2,1)S(1)} %add_convert_fusion.9), channel_id=1, source_target_pairs={{0,4},{1,5},{4,8},{5,9},{8,12},{9,13},{12,14},{13,15},{14,10},{15,... | collective-permute-start | bytes 589832 | tf_op jit(solution)/shard_map/ppermute | solution.py:165
  96.5 13.6 %copy-start.4 = (f32[1536]{0:T(1024)S(1)}, f32[1536]{0:T(1024)}, u32[]{:S(2)}) copy-start(f32[1536]{0:T(1024)} %param.17) | copy-start | bytes 18436
  98.6 7.7 %collective-permute-start.44 = (bf16[64,1536]{1,0:T(8,128)(2,1)S(1)}, bf16[64,1536]{1,0:T(8,128)(2,1)S(1)}, u32[]{:S(2)}, u32[]{:S(2)}) collective-permute-start(bf16[64,1536]{1,0:T(8,128)(2,1)S(1)} %add_convert_fusion.4), channel_id=1, source_target_pairs={{4,0},{5,1},{8,4},{9,5},{12,8},{13,9},{14,12},{15,13},{10,14},{11,... | collective-permute-start | bytes 589832 | tf_op jit(solution)/shard_map/ppermute | solution.py:168
  100.3 7.6 %collective-permute-start.43 = (bf16[64,1536]{1,0:T(8,128)(2,1)S(1)}, bf16[64,1536]{1,0:T(8,128)(2,1)S(1)}, u32[]{:S(2)}, u32[]{:S(2)}) collective-permute-start(bf16[64,1536]{1,0:T(8,128)(2,1)S(1)} %add_convert_fusion.5), channel_id=1, source_target_pairs={{0,4},{1,5},{4,8},{5,9},{8,12},{9,13},{12,14},{13,15},{14,10},{15,... | collective-permute-start | bytes 589832 | tf_op jit(solution)/shard_map/ppermute | solution.py:165
  100.7 9.3 %collective-permute-start.46 = (bf16[64,1536]{1,0:T(8,128)(2,1)S(1)}, bf16[64,1536]{1,0:T(8,128)(2,1)S(1)}, u32[]{:S(2)}, u32[]{:S(2)}) collective-permute-start(bf16[64,1536]{1,0:T(8,128)(2,1)S(1)} %add_convert_fusion.3), channel_id=1, source_target_pairs={{0,4},{1,5},{4,8},{5,9},{8,12},{9,13},{12,14},{13,15},{14,10},{15,... | collective-permute-start | bytes 589832 | tf_op jit(solution)/shard_map/ppermute | solution.py:165
  102.3 7.9 %collective-permute-start.47 = (bf16[64,1536]{1,0:T(8,128)(2,1)S(1)}, bf16[64,1536]{1,0:T(8,128)(2,1)S(1)}, u32[]{:S(2)}, u32[]{:S(2)}) collective-permute-start(bf16[64,1536]{1,0:T(8,128)(2,1)S(1)} %add_convert_fusion.2), channel_id=1, source_target_pairs={{4,0},{5,1},{8,4},{9,5},{12,8},{13,9},{14,12},{15,13},{10,14},{11,... | collective-permute-start | bytes 589832 | tf_op jit(solution)/shard_map/ppermute | solution.py:168
  107.9 5.7 %collective-permute-start.45 = (bf16[64,1536]{1,0:T(8,128)(2,1)S(1)}, bf16[64,1536]{1,0:T(8,128)(2,1)S(1)}, u32[]{:S(2)}, u32[]{:S(2)}) collective-permute-start(bf16[64,1536]{1,0:T(8,128)(2,1)S(1)} %add_convert_fusion.1), channel_id=1, source_target_pairs={{0,4},{1,5},{4,8},{5,9},{8,12},{9,13},{12,14},{13,15},{14,10},{15,... | collective-permute-start | bytes 589832 | tf_op jit(solution)/shard_map/ppermute | solution.py:165
  108.6 5.7 %collective-permute-start.48 = (bf16[64,1536]{1,0:T(8,128)(2,1)S(1)}, bf16[64,1536]{1,0:T(8,128)(2,1)S(1)}, u32[]{:S(2)}, u32[]{:S(2)}) collective-permute-start(bf16[64,1536]{1,0:T(8,128)(2,1)S(1)} %add_convert_fusion), channel_id=1, source_target_pairs={{4,0},{5,1},{8,4},{9,5},{12,8},{13,9},{14,12},{15,13},{10,14},{11,... | collective-permute-start | bytes 589832 | tf_op jit(solution)/shard_map/ppermute | solution.py:168
